TPU v7x, 32 devices: a whole 2x2x4 slice. The times are simulated.
32 devices in a mesh: ctx: 8 (over z, x), fsdp: 4 (over y, core).
Axes of the slice: x: 2, y: 2, z: 4, core: 2. Of those that a mesh axis runs over, the one named last changes fastest.
Arguments:
- projected: bfloat16 [3, 2048, 8192], P(None, 'ctx', 'fsdp'), may hold values from -6 to 6
- short_weight: bfloat16 [3, 3, 8192], P(None, None, 'fsdp'), may hold values from -3 to 3
- rates: float32 [512, 16], P('fsdp'), may hold values from 0.00014648438 to 0.03
- residues: float32 [512, 16], P('fsdp'), may hold values from -0.12 to 0.12
- skip: float32 [8192], P('fsdp'), may hold values from -1 to 1
- residual: bfloat16 [2048, 8192], P('ctx', 'fsdp'), may hold values from -40 to 40
- gain: float32 [8192], P('fsdp'), may hold values from 0.5 to 1.5
Outputs:
- new_residual: bfloat16 [2048, 8192], P('ctx', 'fsdp')
- normed: bfloat16 [2048, 8192], P('ctx', 'fsdp')
All inputs are finite; a program needn't handle non-finite values.
Results may differ from a plain program's by a relative error of at most 0.0047.
Values may be sent and summed in bfloat16 or wider, within the bound.
No kernel may reach another device: no remote copies, remote signals or barrier semaphores. Data moves between devices by JAX's collectives and lax.ppermute only.
A program may use at most 64 MiB of HBM per device.

v0:
```python
import jax
import jax.numpy as jnp
from jax import lax
from jax.experimental import pallas as pl
from jax.experimental.pallas import tpu as pltpu
from jax.sharding import PartitionSpec as P

CHANNELS_PER_GRP = 16
MODES = 16
CHUNK = 32
LANES = 128
WIDE = 256
GROUPS = LANES // CHANNELS_PER_GRP
VMEM_LIMIT = 16 * 1024 * 1024
F32 = jnp.float32
BF16 = jnp.bfloat16


def index_of(shape, dim):
    return lax.broadcasted_iota(jnp.int32, shape, dim)


def lanes_of(tile, width=LANES):
    return slice(tile * width, (tile + 1) * width)


def per_channel(table):
    groups = table.shape[1]
    width = groups * CHANNELS_PER_GRP
    high = table.astype(BF16)
    rest = table - high.astype(F32)
    middle = rest.astype(BF16)
    low = (rest - middle.astype(F32)).astype(BF16)
    terms = jnp.concatenate([high, middle, low], axis=0)
    parts = []
    for tile in range(width // WIDE):
        shape = (groups, WIDE)
        own = index_of(shape, 0) == index_of(shape, 1) // CHANNELS_PER_GRP + tile * (WIDE // CHANNELS_PER_GRP)
        three = jnp.dot(terms, jnp.where(own, 1.0, 0.0).astype(BF16), preferred_element_type=F32)
        parts.append(three[:MODES] + three[MODES : 2 * MODES] + three[2 * MODES :])
    return jnp.concatenate(parts, axis=1)


def mode_row(channel_table):
    own = index_of(channel_table.shape, 0) == (index_of(channel_table.shape, 1) & (MODES - 1))
    return jnp.sum(jnp.where(own, channel_table, 0.0), axis=0, keepdims=True)


def mode_column(row):
    return jnp.transpose(jnp.broadcast_to(row, (LANES, LANES)))


def group_mask(dtype):
    shape = (GROUPS, MODES, LANES)
    own = index_of(shape, 0) == index_of(shape, 2) // CHANNELS_PER_GRP
    return jnp.where(own, 1.0, 0.0).astype(dtype)


def spread(rows, mask):
    size = rows.shape[0]
    copies = rows.reshape(1, size // MODES, MODES, LANES) * mask.reshape(GROUPS, 1, MODES, LANES)
    return copies.reshape(GROUPS * size, LANES)


def shifted(block, before):
    one = pltpu.roll(block, 1, 0)
    two = pltpu.roll(block, 2, 0)
    first = index_of((8, block.shape[1]), 0)
    near, far = (0.0, 0.0) if before is None else (before[1:2], before[0:1])
    head_one = jnp.where(first == 0, near, one[:8])
    head_two = jnp.where(first == 0, far, jnp.where(first == 1, near, two[:8]))
    if block.shape[0] == 8:
        return head_one, head_two
    return jnp.concatenate([head_one, one[8:]], axis=0), jnp.concatenate([head_two, two[8:]], axis=0)


def short_conv(block, before, weights):
    one, two = shifted(block, before)
    return weights[0] * block + weights[1] * one + weights[2] * two


def taps_of(weights, feature, lanes):
    return [weights[tap, feature : feature + 1, lanes] for tap in range(weights.shape[0])]


def state_kernel(
    projected_ref, weight_ref, rate_ref, product_ref, state_ref, mode_rate_ref, head_ref, buffer_ref, sems
):
    rows, width = product_ref.shape
    copies = []
    for tile in range(width // WIDE):
        here = pl.ds(tile * WIDE, WIDE)
        copies.append(
            pltpu.make_async_copy(projected_ref.at[pl.ds(1, 2), :, here], buffer_ref.at[:, :, here], sems.at[tile])
        )
        copies[-1].start()
    weights = weight_ref[...].astype(F32)
    mode_rate = per_channel(rate_ref[...])
    mode_rate_ref[...] = mode_rate
    mask = group_mask(F32)
    left = (rows - 1 - index_of((1, rows), 1)).astype(F32)
    left = jnp.where(left > rows - 2.5, 1e30, left)
    for tile in range(width // WIDE):
        here = lanes_of(tile, WIDE)
        row = mode_row(mode_rate[:, here])
        pieces = []
        for half in range(WIDE // LANES):
            rate = mode_column(row[:, lanes_of(half)])
            rate = jnp.concatenate([rate] * (rows // LANES), axis=1)
            pieces.append(jnp.exp(-rate * left).astype(BF16))
        ending = jnp.concatenate(pieces, axis=0)
        copies[tile].wait()
        parts = []
        for c in (0, 1):
            block = buffer_ref[c, :, here].astype(F32)
            head_ref[c, :, here] = block[:8]
            parts.append(short_conv(block, None, taps_of(weights, c + 1, here)))
        product = (parts[0] * parts[1]).astype(BF16)
        product_ref[:, here] = product
        every = jnp.dot(ending, product, preferred_element_type=F32)
        for half in range(WIDE // LANES):
            own = every[lanes_of(half), lanes_of(half)].reshape(GROUPS, MODES, LANES)
            state_ref[:, lanes_of((WIDE // LANES) * tile + half)] = jnp.sum(own * mask, axis=0)


def head_kernel(rows, before_ref, head_ref, weight_ref, state_ref, mode_rate_ref, full_ref, first_ref):
    weights = weight_ref[...].astype(F32)
    before = before_ref[...].astype(F32)
    everything = slice(0, head_ref.shape[2])
    parts = [short_conv(head_ref[c], before[c + 1], taps_of(weights, c + 1, everything)) for c in (0, 1)]
    first = (parts[0] * parts[1]).astype(BF16).astype(F32)
    first_ref[...] = first
    rate = mode_rate_ref[...]
    early = jnp.exp(-float(rows - 1) * rate) * first[0:1] + jnp.exp(-float(rows - 2) * rate) * first[1:2]
    full_ref[...] = (state_ref[...] + early).astype(BF16)


def split(x):
    high = x.astype(BF16)
    return high, (x - high.astype(F32)).astype(BF16)


def table_kernel(rows, mode_rate_ref, residue_ref, inner_ref, entering_ref, carry_ref):
    width = mode_rate_ref.shape[1]
    residue = per_channel(residue_ref[...])
    wide = GROUPS * CHUNK
    step = index_of((CHUNK, LANES), 0).astype(F32)
    source = (index_of((LANES, wide), 1) & (CHUNK - 1)).astype(F32)
    own = index_of((LANES, wide), 0) // MODES == index_of((LANES, wide), 1) // CHUNK
    causal = (index_of((CHUNK, wide), 1) & (CHUNK - 1)) <= index_of((CHUNK, wide), 0)
    for tile in range(width // LANES):
        here = lanes_of(tile)
        rate_row = mode_row(mode_rate_ref[:, here])
        rate = mode_column(rate_row)
        rate = jnp.concatenate([rate] * (wide // LANES), axis=1)
        falling = mode_row(residue[:, here]) * jnp.exp(-rate_row * step)
        rising = jnp.where(own, jnp.exp(rate * source), 0.0)
        fall_high, fall_low = split(falling)
        rise_high, rise_low = split(rising)
        taps = jnp.dot(jnp.concatenate([fall_high, fall_low], axis=0), rise_high, preferred_element_type=F32)
        taps = taps[:CHUNK] + taps[CHUNK:] + jnp.dot(fall_high, rise_low, preferred_element_type=F32)
        taps = jnp.where(causal, taps, 0.0)
        ending = rising * jnp.exp(-float(CHUNK - 1) * rate)
        ending = jnp.sum(ending.reshape(GROUPS, MODES, wide), axis=0)
        inner_ref[tile] = jnp.concatenate([taps.astype(BF16), ending.astype(BF16)], axis=0)
        half = tile % (WIDE // LANES)
        for chunk in range(rows // CHUNK):
            entering = (falling * jnp.exp(-float(CHUNK * chunk + 1) * rate_row)).astype(BF16)
            carry_ref[tile // (WIDE // LANES), chunk * CHUNK : (chunk + 1) * CHUNK, lanes_of(half)] = entering
            if chunk == 0:
                entering_ref[tile] = entering


def local_kernel(
    projected_ref,
    residual_hbm,
    before_ref,
    weight_ref,
    product_ref,
    first_ref,
    mode_rate_ref,
    inner_ref,
    entering_ref,
    skip_ref,
    base_ref,
    gate_ref,
    query_ref,
    residual_ref,
    sems,
):
    rows, width = product_ref.shape
    copies = []
    for part in range(width // WIDE):
        here = pl.ds(part * WIDE, WIDE)
        copies.append(
            (
                pltpu.make_async_copy(projected_ref.at[0, :, here], query_ref.at[:, here], sems.at[0, part]),
                pltpu.make_async_copy(residual_hbm.at[:, here], residual_ref.at[:, here], sems.at[1, part]),
            )
        )
        for copy in copies[-1]:
            copy.start()
    weights = weight_ref[...].astype(F32)
    before = before_ref[0].astype(F32)
    mask = group_mask(BF16)
    top = index_of((8, LANES), 0) < 2
    for tile in range(width // LANES):
        here = lanes_of(tile)
        if tile % (WIDE // LANES) == 0:
            for copy in copies[tile // (WIDE // LANES)]:
                copy.wait()
        pieces = []
        for chunk in range(rows // CHUNK):
            piece = product_ref[chunk * CHUNK : (chunk + 1) * CHUNK, here]
            if chunk == 0:
                wide = piece.astype(F32)
                head = jnp.where(top, first_ref[:, here], wide[:8])
                piece = jnp.concatenate([head, wide[8:]], axis=0).astype(BF16)
            pieces.append(piece)
        table = inner_ref[tile]
        inner = []
        for pair in range(rows // (2 * CHUNK)):
            sources = jnp.concatenate([spread(pieces[2 * pair + k], mask) for k in (0, 1)], axis=1)
            inner.append(jnp.dot(table, sources, preferred_element_type=F32))
        query = short_conv(query_ref[:, here].astype(F32), before[:, here], taps_of(weights, 0, here))
        gate_ref[:, here] = query
        decay = jnp.exp(-float(CHUNK) * mode_rate_ref[:, here])
        state = jnp.zeros((MODES, LANES), F32)
        states = []
        for chunk in range(rows // CHUNK):
            states.append(spread(state.astype(BF16), mask))
            state = decay * state + inner[chunk // 2][CHUNK:, lanes_of(chunk % 2)]
        entering = entering_ref[tile]
        skip = skip_ref[:, here]
        for pair in range(rows // (2 * CHUNK)):
            two = jnp.concatenate(states[2 * pair : 2 * pair + 2], axis=1)
            conv = inner[pair][:CHUNK] + jnp.dot(entering, two, preferred_element_type=F32)
            for k in (0, 1):
                chunk = 2 * pair + k
                span = slice(chunk * CHUNK, (chunk + 1) * CHUNK)
                whole = conv[:, lanes_of(k)] + skip * pieces[chunk].astype(F32)
                base_ref[span, here] = residual_ref[span, here].astype(F32) + query[span] * whole


def carry_kernel(stride, received, place_ref, base_ref, gate_ref, carry_ref, mode_rate_ref, inner_entry_ref, *refs):
    entry_refs, (summed_ref, squares_ref) = refs[:received], refs[received:]
    rows, width = base_ref.shape
    place = place_ref[0].astype(F32) * float(rows)
    mask = group_mask(BF16)
    total = jnp.zeros((rows, LANES), F32)
    nothing = jnp.zeros((LANES, LANES), BF16)
    for tile in range(width // WIDE):
        here = lanes_of(tile, WIDE)
        rate = mode_rate_ref[:, here]
        decay = jnp.exp(-float(rows * stride) * rate)
        outer = entry_refs[-1][:, here].astype(F32)
        for ref in entry_refs[-2::-1]:
            outer = decay * outer + ref[:, here].astype(F32)
        entry = (inner_entry_ref[:, here].astype(F32) + jnp.exp(-place * rate) * outer).astype(BF16)
        left, right = spread(entry[:, :LANES], mask), spread(entry[:, LANES:], mask)
        both = jnp.concatenate(
            [jnp.concatenate([left, nothing], axis=1), jnp.concatenate([nothing, right], axis=1)], axis=0
        )
        carry = jnp.dot(carry_ref[tile], both, preferred_element_type=F32)
        summed = base_ref[:, here] + gate_ref[:, here] * carry
        summed_ref[:, here] = summed
        square = summed * summed
        total = total + (square[:, :LANES] + square[:, LANES:])
    squares = lax.dot_general(
        jnp.ones((8, LANES), F32),
        total,
        (((1,), (1,)), ((), ())),
        precision=lax.Precision.HIGHEST,
        preferred_element_type=F32,
    )
    squares_ref[...] = squares[0:1]


def params():
    return pltpu.CompilerParams(vmem_limit_bytes=VMEM_LIMIT)


def cost(microseconds):
    return pl.CostEstimate(flops=0, bytes_accessed=int(microseconds * 3.0e6), transcendentals=0)


def radices(count):
    found = []
    for radix in (2, 4, 4, 4):
        if count % radix == 0 and count > 1:
            found.append(radix)
            count //= radix
    for radix in (3, 2, 5, 7):
        while count % radix == 0 and count > 1:
            found.append(radix)
            count //= radix
    return found + ([count] if count > 1 else [])


def decayed(value, rate, tokens):
    return jnp.exp(-tokens * rate) * value


def per_device(projected, short_weight, rates, residues, skip, residual, gain):
    rows, width = projected.shape[1:]
    taps = short_weight.shape[0]
    peers = lax.axis_size("ctx")
    here = lax.axis_index("ctx")
    full_width = width * lax.axis_size("fsdp")
    any_spec = pl.BlockSpec(memory_space=pl.ANY)
    vmem_spec = pl.BlockSpec(memory_space=pltpu.VMEM)
    smem_spec = pl.BlockSpec(memory_space=pltpu.SMEM)
    tiles = width // LANES
    wides = width // WIDE

    route = [(i, i + 1) for i in range(peers - 1)]
    before = lax.ppermute(projected[:, rows - (taps - 1) :, :], "ctx", route)

    product, state, mode_rate, head = pl.pallas_call(
        state_kernel,
        in_specs=[any_spec, vmem_spec, vmem_spec],
        out_shape=[
            jax.ShapeDtypeStruct((rows, width), BF16),
            jax.ShapeDtypeStruct((MODES, width), F32),
            jax.ShapeDtypeStruct((MODES, width), F32),
            jax.ShapeDtypeStruct((2, 8, width), F32),
        ],
        scratch_shapes=[pltpu.VMEM((2, rows, width), BF16), pltpu.SemaphoreType.DMA((wides,))],
        compiler_params=params(),
        cost_estimate=cost(3),
        name="block_state",
    )(projected, short_weight, rates.T)

    inner, entering, carry_table = pl.pallas_call(
        lambda *refs: table_kernel(rows, *refs),
        out_shape=[
            jax.ShapeDtypeStruct((tiles, CHUNK + MODES, GROUPS * CHUNK), BF16),
            jax.ShapeDtypeStruct((tiles, CHUNK, LANES), BF16),
            jax.ShapeDtypeStruct((wides, rows, WIDE), BF16),
        ],
        compiler_params=params(),
        cost_estimate=cost(3),
        name="tables",
    )(mode_rate, residues.T)

    full_state, first = pl.pallas_call(
        lambda *refs: head_kernel(rows, *refs),
        out_shape=[jax.ShapeDtypeStruct((MODES, width), BF16), jax.ShapeDtypeStruct((8, width), F32)],
        compiler_params=params(),
        cost_estimate=cost(1),
        name="head_tokens",
    )(before, head, short_weight, state, mode_rate)

    base, gate = pl.pallas_call(
        local_kernel,
        in_specs=[any_spec, any_spec] + [vmem_spec] * 8,
        out_shape=[jax.ShapeDtypeStruct((rows, width), F32)] * 2,
        scratch_shapes=[
            pltpu.VMEM((rows, width), BF16),
            pltpu.VMEM((rows, width), BF16),
            pltpu.SemaphoreType.DMA((2, wides)),
        ],
        compiler_params=params(),
        cost_estimate=cost(6),
        name="local_conv",
    )(projected, residual, before, short_weight, product, first, mode_rate, inner, entering, skip[None])

    group, entry, stride = full_state, jnp.zeros((MODES, width), F32), 1
    levels = radices(peers)
    for level, radix in enumerate(levels):
        last = level == len(levels) - 1
        size = stride * radix
        if last:
            shifts = [[(i, i + stride * k) for i in range(peers - stride * k)] for k in range(1, radix)]
            received = [lax.ppermute(group, "ctx", shift) for shift in shifts]
            break
        cycles = [
            [(i, i // size * size + (i + stride * k) % size) for i in range(peers)] for k in range(1, radix)
        ]
        others = [lax.ppermute(group, "ctx", cycle).astype(F32) for cycle in cycles]
        run = here % size // stride
        own = group.astype(F32)
        found = jnp.zeros_like(own)
        span = float(rows * stride)
        for k, other in enumerate(others, 1):
            earlier = run >= k
            lag = jnp.where(earlier, k - 1, 0).astype(F32) * span
            found = found + jnp.where(earlier, decayed(other, mode_rate, lag), 0.0)
        total = decayed(own, mode_rate, (radix - 1 - run).astype(F32) * span)
        for k, other in enumerate(others, 1):
            source = (run - k) % radix
            total = total + decayed(other, mode_rate, (radix - 1 - source).astype(F32) * span)
        entry = entry + decayed(found, mode_rate, (here % stride).astype(F32) * float(rows))
        group, stride = total.astype(BF16), size

    place = (here % stride).astype(jnp.int32).reshape(1)
    summed, squares = pl.pallas_call(
        lambda *refs: carry_kernel(stride, len(received), *refs),
        in_specs=[smem_spec] + [vmem_spec] * (5 + len(received)),
        out_shape=[jax.ShapeDtypeStruct((rows, width), F32), jax.ShapeDtypeStruct((1, rows), F32)],
        compiler_params=params(),
        cost_estimate=cost(2),
        name="add_carry",
    )(place, base, gate, carry_table, mode_rate, entry, *received)

    peers = lax.axis_size("fsdp")
    rings = [[(i, (i + k) % peers) for i in range(peers)] for k in range(1, peers)]
    parts = [lax.ppermute(squares, "fsdp", ring) for ring in rings]
    new_residual = summed.astype(BF16)
    for part in parts:
        squares = squares + part
    scale = lax.rsqrt(squares[0][:, None] / full_width + 1e-05)
    normed = (summed * scale * gain[None, :]).astype(BF16)
    return (new_residual, normed)


def solution(mesh):
    return jax.shard_map(
        per_device,
        mesh=mesh,
        in_specs=(
            P(None, "ctx", "fsdp"),
            P(None, None, "fsdp"),
            P("fsdp", None),
            P("fsdp", None),
            P("fsdp"),
            P("ctx", "fsdp"),
            P("fsdp"),
        ),
        out_specs=(P("ctx", "fsdp"), P("ctx", "fsdp")),
        check_vma=False,
    )
```

profile of v0, /device:TPU:0, one launch (start us, length us, event | category | flops | bytes accessed | tf_op | source)
XLA Modules:
  0.0 45.7 jit_solution(1827570996029778917)
XLA Ops:
  0.6 0.9 %slice.3 = bf16[3,2,2048]{2,1,0:T(2,128)(2,1)S(1)} slice(bf16[3,256,2048]{2,1,0:T(8,128)(2,1)} %projected_ref.3), slice={[0:3], [254:256], [0:2048]} | slice | bytes 49152 | tf_op jit(solution)/shard_map/slice | solution.py:317
  1.6 4.8 %collective-permute-start = (bf16[3,2,2048]{2,1,0:T(2,128)(2,1)S(1)}, bf16[3,2,2048]{2,1,0:T(2,128)(2,1)S(1)}, u32[]{:S(2)}, u32[]{:S(2)}) collective-permute-start(bf16[3,2,2048]{2,1,0:T(2,128)(2,1)S(1)} %slice.3), channel_id=1, source_target_pairs={{0,4},{4,8},{8,12},{12,16},{16,20},{20,24},{24,28},{1,5},{5,9},{9,... | collective-permute-start | bytes 73736 | tf_op jit(solution)/shard_map/ppermute | solution.py:317
  6.4 0.0 copy-start
  6.4 1.9 %copy-done = bf16[3,256,2048]{2,1,0:T(8,128)(2,1)S(1)} copy-done((bf16[3,256,2048]{2,1,0:T(8,128)(2,1)S(1)}, bf16[3,256,2048]{2,1,0:T(8,128)(2,1)}, u32[]{:S(2)}) %copy-start) | copy-done | bytes 3145752
  8.3 0.0 copy-start.5
  8.3 0.8 %copy-done.5 = bf16[3,3,2048]{2,1,0:T(4,128)(2,1)S(1)} copy-done((bf16[3,3,2048]{2,1,0:T(4,128)(2,1)S(1)}, bf16[3,3,2048]{2,1,0:T(4,128)(2,1)}, u32[]{:S(2)}) %copy-start.5) | copy-done | bytes 36888
  9.1 0.0 copy-start.7
  9.1 0.7 %copy-done.7 = f32[128,16]{0,1:T(8,128)S(1)} copy-done((f32[128,16]{0,1:T(8,128)S(1)}, f32[128,16]{0,1:T(8,128)}, u32[]{:S(2)}) %copy-start.7) | copy-done | bytes 8216
  9.8 0.0 copy-start.9
  9.8 0.0 copy-start.1
  9.8 0.0 copy-start.6
  9.8 0.0 copy-start.8
  9.8 4.1 %block_state.1 = (bf16[256,2048]{1,0:T(8,128)(2,1)S(1)}, f32[16,2048]{1,0:T(8,128)S(1)}, f32[16,2048]{1,0:T(8,128)S(1)}, f32[2,8,2048]{2,1,0:T(8,128)S(1)}) custom-call(bf16[3,256,2048]{2,1,0:T(8,128)(2,1)S(1)} %copy-done, bf16[3,3,2048]{2,1,0:T(4,128)(2,1)S(1)} %copy-done.5, f32[16,128]{1,0:T(8,128)S(1)} %bitcast.5), custom_call_target="tpu_custom_call" | custom-call | bytes 9000000 | tf_op jit(solution)/shard_map/block_state/pallas_call | solution.py:319
  13.9 0.0 copy-start.3
  13.9 1.0 %copy-done.3 = bf16[256,2048]{1,0:T(8,128)(2,1)} copy-done((bf16[256,2048]{1,0:T(8,128)(2,1)}, bf16[256,2048]{1,0:T(8,128)(2,1)S(1)}, u32[]{:S(2)}) %copy-start.3) | copy-done | bytes 1048600
  14.8 0.0 collective-permute-done.refs_0_.before_ref
  14.9 0.2 head_tokens.1
  15.0 1.6 %collective-permute-start.1 = (bf16[16,2048]{1,0:T(8,128)(2,1)S(1)}, bf16[16,2048]{1,0:T(8,128)(2,1)}, u32[]{:S(2)}, u32[]{:S(2)}) collective-permute-start(bf16[16,2048]{1,0:T(8,128)(2,1)S(1)} %get-tuple-element.25), channel_id=1, source_target_pairs={{0,4},{4,0},{8,12},{12,8},{16,20},{20,16},{24,28},{28,24},{1,5},{5... | collective-permute-start | bytes 196616 | tf_op jit(solution)/shard_map/ppermute | solution.py:380
  16.6 2.8 %collective-permute-done.1 = bf16[16,2048]{1,0:T(8,128)(2,1)} collective-permute-done((bf16[16,2048]{1,0:T(8,128)(2,1)S(1)}, bf16[16,2048]{1,0:T(8,128)(2,1)}, u32[]{:S(2)}, u32[]{:S(2)}) %collective-permute-start.1) | collective-permute-done | bytes 65568 | tf_op jit(solution)/shard_map/ppermute | solution.py:380
  19.4 0.9 %fusion.3 = (bf16[16,2048]{1,0:T(8,128)(2,1)S(1)}, f32[16,2048]{1,0:T(8,128)S(1)}) fusion(bf16[16,2048]{1,0:T(8,128)(2,1)} %collective-permute-done.1, f32[16,2048]{1,0:T(8,128)S(1)} %get-tuple-element.18.refs_4_.refs_0_.mode_rate_ref, bf16[16,2048]{1,0:T(8,128)(2,1)S(1)} %get-tuple-element.25, f32[]{:T(128)S(6)} %neg.9, f32[]{:T(128)S(6)} %neg.8, pred[]{:T(512)S(6)} %ge.3), kind=kLoop, calls=%fused_computation.6 | loop fusion | flops 393216 | bytes 458761 | tf_op jit(solution)/shard_map/convert_element_type | solution.py:394
  20.4 5.5 %collective-permute-start.4 = (bf16[16,2048]{1,0:T(8,128)(2,1)S(1)}, bf16[16,2048]{1,0:T(8,128)(2,1)S(1)}, u32[]{:S(2)}, u32[]{:S(2)}) collective-permute-start(bf16[16,2048]{1,0:T(8,128)(2,1)S(1)} %get-tuple-element.30), channel_id=1, source_target_pairs={{0,24},{4,28},{1,25},{5,29},{2,26},{6,30},{3,27},{7,31}} | collective-permute-start | bytes 196616 | tf_op jit(solution)/shard_map/ppermute | solution.py:375
  25.9 1.3 %collective-permute-start.3 = (bf16[16,2048]{1,0:T(8,128)(2,1)S(1)}, bf16[16,2048]{1,0:T(8,128)(2,1)S(1)}, u32[]{:S(2)}, u32[]{:S(2)}) collective-permute-start(bf16[16,2048]{1,0:T(8,128)(2,1)S(1)} %get-tuple-element.30), channel_id=1, source_target_pairs={{0,16},{4,20},{8,24},{12,28},{1,17},{5,21},{9,25},{13,29},{2,18},{... | collective-permute-start | bytes 196616 | tf_op jit(solution)/shard_map/ppermute | solution.py:375
  27.2 2.5 %collective-permute-start.2 = (bf16[16,2048]{1,0:T(8,128)(2,1)S(1)}, bf16[16,2048]{1,0:T(8,128)(2,1)S(1)}, u32[]{:S(2)}, u32[]{:S(2)}) collective-permute-start(bf16[16,2048]{1,0:T(8,128)(2,1)S(1)} %get-tuple-element.30), channel_id=1, source_target_pairs={{0,8},{4,12},{8,16},{12,20},{16,24},{20,28},{1,9},{5,13},{9,17},{1... | collective-permute-start | bytes 196616 | tf_op jit(solution)/shard_map/ppermute | solution.py:375
  29.7 0.0 copy-done.9
  29.7 1.3 %tables.1 = (bf16[16,48,256]{2,1,0:T(8,128)(2,1)S(1)}, bf16[16,32,128]{2,1,0:T(8,128)(2,1)S(1)}, bf16[8,256,256]{2,1,0:T(8,128)(2,1)S(1)}) custom-call(f32[16,2048]{1,0:T(8,128)S(1)} %get-tuple-element.18.refs_4_.refs_0_.mode_rate_ref, f32[16,128]{1,0:T(8,128)S(1)} %bitcast.7), custom_call_target="tpu_custom_call" | custom-call | bytes 9000000 | tf_op jit(solution)/shard_map/tables/pallas_call | solution.py:334
  30.9 0.0 copy-done.1
  30.9 0.0 copy-done.6
  30.9 0.0 copy-done.8
  31.0 0.0 copy-start.2
  31.0 1.2 %copy-done.2 = bf16[256,2048]{1,0:T(8,128)(2,1)S(1)} copy-done((bf16[256,2048]{1,0:T(8,128)(2,1)S(1)}, bf16[256,2048]{1,0:T(8,128)(2,1)}, u32[]{:S(2)}) %copy-start.2) | copy-done | bytes 1048600
  32.2 0.0 copy-start.4
  32.2 1.2 %copy-done.4 = bf16[256,2048]{1,0:T(8,128)(2,1)S(1)} copy-done((bf16[256,2048]{1,0:T(8,128)(2,1)S(1)}, bf16[256,2048]{1,0:T(8,128)(2,1)}, u32[]{:S(2)}) %copy-start.4) | copy-done | bytes 1048600
  33.4 5.2 %local_conv.1 = (f32[256,2048]{1,0:T(8,128)S(1)}, f32[256,2048]{1,0:T(8,128)S(1)}) custom-call(bf16[3,256,2048]{2,1,0:T(8,128)(2,1)S(1)} %copy-done.1, bf16[256,2048]{1,0:T(8,128)(2,1)S(1)} %copy-done.2, bf16[3,2,2048]{2,1,0:T(2,128)(2,1)S(1)} %collective-permute-done.refs_0_.before_ref, bf16[3,3,2048]{2,1,0:T(4,128)(2,1)S(1)} %copy-done.6, ...), custom_call_target="tpu_custom_call" | custom-call | bytes 18000000 | tf_op jit(solution)/shard_map/local_conv/pallas_call | solution.py:354
  38.6 0.0 collective-permute-done.4.refs_8_
  38.6 0.0 collective-permute-done.3.refs_7_
  38.6 0.0 collective-permute-done.2.refs_6_
  38.7 0.0 copy-start.10
  38.7 0.9 %add_carry.1 = (f32[256,2048]{1,0:T(8,128)S(1)}, f32[1,256]{1,0:T(1,128)S(1)}) custom-call(s32[1]{0:T(128)} %bitcast.refs_0_, f32[256,2048]{1,0:T(8,128)S(1)} %get-tuple-element.22.refs_1_, f32[256,2048]{1,0:T(8,128)S(1)} %get-tuple-element.23.refs_2_, bf16[8,256,256]{2,1,0:T(8,128)(2,1)S(1)} %get-tuple-element.24.refs_3_, ...), custom_call_target="tpu_custom_call" | custom-call | bytes 6000000 | tf_op jit(solution)/shard_map/add_carry/pallas_call | solution.py:397
  39.5 0.0 collective-permute-start.7
  39.5 1.5 %collective-permute-start.6 = (f32[1,256]{1,0:T(1,128)S(1)}, f32[1,256]{1,0:T(1,128)S(1)}, u32[]{:S(2)}, u32[]{:S(2)}) collective-permute-start(f32[1,256]{1,0:T(1,128)S(1)} %get-tuple-element.27), channel_id=1, source_target_pairs={{0,2},{1,3},{2,0},{3,1},{4,6},{5,7},{6,4},{7,5},{8,10},{9,11},{10,... | collective-permute-start | bytes 3080 | tf_op jit(solution)/shard_map/ppermute | solution.py:408
  41.1 0.2 collective-permute-start.5
  41.3 0.0 collective-permute-done.7
  41.3 1.8 %collective-permute-done.6 = f32[1,256]{1,0:T(1,128)S(1)} collective-permute-done((f32[1,256]{1,0:T(1,128)S(1)}, f32[1,256]{1,0:T(1,128)S(1)}, u32[]{:S(2)}, u32[]{:S(2)}) %collective-permute-start.6) | collective-permute-done | bytes 1056 | tf_op jit(solution)/shard_map/ppermute | solution.py:408
  43.1 0.9 %collective-permute-done.5 = f32[1,256]{1,0:T(1,128)S(1)} collective-permute-done((f32[1,256]{1,0:T(1,128)S(1)}, f32[1,256]{1,0:T(1,128)S(1)}, u32[]{:S(2)}, u32[]{:S(2)}) %collective-permute-start.5) | collective-permute-done | bytes 1056 | tf_op jit(solution)/shard_map/ppermute | solution.py:408
  44.1 0.0 copy-done.10
  44.1 1.6 %multiply_convert_fusion = (bf16[256,2048]{1,0:T(8,128)(2,1)}, bf16[256,2048]{1,0:T(8,128)(2,1)}) fusion(f32[256,2048]{1,0:T(8,128)S(1)} %get-tuple-element.26, f32[2048]{0:T(1024)S(1)} %copy-done.10, f32[256]{0:T(256)S(1)} %bitcast.8), kind=kLoop, calls=%fused_computation | loop fusion | flops 2097152 | bytes 4203520 | tf_op jit(solution)/shard_map/convert_element_type | solution.py:413
  (1 shorter events, 0.0 us)
Async XLA Ops:
  1.6 13.3 %collective-permute-start = (bf16[3,2,2048]{2,1,0:T(2,128)(2,1)S(1)}, bf16[3,2,2048]{2,1,0:T(2,128)(2,1)S(1)}, u32[]{:S(2)}, u32[]{:S(2)}) collective-permute-start(bf16[3,2,2048]{2,1,0:T(2,128)(2,1)S(1)} %slice.3), channel_id=1, source_target_pairs={{0,4},{4,8},{8,12},{12,16},{16,20},{20,24},{24,28},{1,5},{5,9},{9,... | collective-permute-start | bytes 73736 | tf_op jit(solution)/shard_map/ppermute | solution.py:317
  6.4 1.9 %copy-start = (bf16[3,256,2048]{2,1,0:T(8,128)(2,1)S(1)}, bf16[3,256,2048]{2,1,0:T(8,128)(2,1)}, u32[]{:S(2)}) copy-start(bf16[3,256,2048]{2,1,0:T(8,128)(2,1)} %projected_ref.3) | copy-start | bytes 9437188
  8.3 0.8 %copy-start.5 = (bf16[3,3,2048]{2,1,0:T(4,128)(2,1)S(1)}, bf16[3,3,2048]{2,1,0:T(4,128)(2,1)}, u32[]{:S(2)}) copy-start(bf16[3,3,2048]{2,1,0:T(4,128)(2,1)} %weight_ref.3) | copy-start | bytes 110596
  9.1 0.7 %copy-start.7 = (f32[128,16]{0,1:T(8,128)S(1)}, f32[128,16]{0,1:T(8,128)}, u32[]{:S(2)}) copy-start(f32[128,16]{0,1:T(8,128)} %param.9) | copy-start | bytes 24580
  9.8 19.9 %copy-start.9 = (f32[128,16]{0,1:T(8,128)S(1)}, f32[128,16]{0,1:T(8,128)}, u32[]{:S(2)}) copy-start(f32[128,16]{0,1:T(8,128)} %param.10) | copy-start | bytes 24580
  9.8 21.1 %copy-start.1 = (bf16[3,256,2048]{2,1,0:T(8,128)(2,1)S(1)}, bf16[3,256,2048]{2,1,0:T(8,128)(2,1)}, u32[]{:S(2)}) copy-start(bf16[3,256,2048]{2,1,0:T(8,128)(2,1)} %projected_ref.3) | copy-start | bytes 9437188
  9.8 21.1 %copy-start.6 = (bf16[3,3,2048]{2,1,0:T(4,128)(2,1)S(1)}, bf16[3,3,2048]{2,1,0:T(4,128)(2,1)}, u32[]{:S(2)}) copy-start(bf16[3,3,2048]{2,1,0:T(4,128)(2,1)} %weight_ref.3) | copy-start | bytes 110596
  9.8 21.1 %copy-start.8 = (f32[2048]{0:T(1024)S(1)}, f32[2048]{0:T(1024)}, u32[]{:S(2)}) copy-start(f32[2048]{0:T(1024)} %param.11) | copy-start | bytes 24580
  13.9 1.0 %copy-start.3 = (bf16[256,2048]{1,0:T(8,128)(2,1)}, bf16[256,2048]{1,0:T(8,128)(2,1)S(1)}, u32[]{:S(2)}) copy-start(bf16[256,2048]{1,0:T(8,128)(2,1)S(1)} %get-tuple-element.15.product_ref) | copy-start | bytes 3145732
  15.0 4.4 %collective-permute-start.1 = (bf16[16,2048]{1,0:T(8,128)(2,1)S(1)}, bf16[16,2048]{1,0:T(8,128)(2,1)}, u32[]{:S(2)}, u32[]{:S(2)}) collective-permute-start(bf16[16,2048]{1,0:T(8,128)(2,1)S(1)} %get-tuple-element.25), channel_id=1, source_target_pairs={{0,4},{4,0},{8,12},{12,8},{16,20},{20,16},{24,28},{28,24},{1,5},{5... | collective-permute-start | bytes 196616 | tf_op jit(solution)/shard_map/ppermute | solution.py:380
  20.4 18.3 %collective-permute-start.4 = (bf16[16,2048]{1,0:T(8,128)(2,1)S(1)}, bf16[16,2048]{1,0:T(8,128)(2,1)S(1)}, u32[]{:S(2)}, u32[]{:S(2)}) collective-permute-start(bf16[16,2048]{1,0:T(8,128)(2,1)S(1)} %get-tuple-element.30), channel_id=1, source_target_pairs={{0,24},{4,28},{1,25},{5,29},{2,26},{6,30},{3,27},{7,31}} | collective-permute-start | bytes 196616 | tf_op jit(solution)/shard_map/ppermute | solution.py:375
  25.9 12.7 %collective-permute-start.3 = (bf16[16,2048]{1,0:T(8,128)(2,1)S(1)}, bf16[16,2048]{1,0:T(8,128)(2,1)S(1)}, u32[]{:S(2)}, u32[]{:S(2)}) collective-permute-start(bf16[16,2048]{1,0:T(8,128)(2,1)S(1)} %get-tuple-element.30), channel_id=1, source_target_pairs={{0,16},{4,20},{8,24},{12,28},{1,17},{5,21},{9,25},{13,29},{2,18},{... | collective-permute-start | bytes 196616 | tf_op jit(solution)/shard_map/ppermute | solution.py:375
  27.2 11.5 %collective-permute-start.2 = (bf16[16,2048]{1,0:T(8,128)(2,1)S(1)}, bf16[16,2048]{1,0:T(8,128)(2,1)S(1)}, u32[]{:S(2)}, u32[]{:S(2)}) collective-permute-start(bf16[16,2048]{1,0:T(8,128)(2,1)S(1)} %get-tuple-element.30), channel_id=1, source_target_pairs={{0,8},{4,12},{8,16},{12,20},{16,24},{20,28},{1,9},{5,13},{9,17},{1... | collective-permute-start | bytes 196616 | tf_op jit(solution)/shard_map/ppermute | solution.py:375
  31.0 1.2 %copy-start.2 = (bf16[256,2048]{1,0:T(8,128)(2,1)S(1)}, bf16[256,2048]{1,0:T(8,128)(2,1)}, u32[]{:S(2)}) copy-start(bf16[256,2048]{1,0:T(8,128)(2,1)} %residual_hbm.1) | copy-start | bytes 3145732
  32.2 1.2 %copy-start.4 = (bf16[256,2048]{1,0:T(8,128)(2,1)S(1)}, bf16[256,2048]{1,0:T(8,128)(2,1)}, u32[]{:S(2)}) copy-start(bf16[256,2048]{1,0:T(8,128)(2,1)} %copy-done.3) | copy-start | bytes 3145732
  38.7 5.4 %copy-start.10 = (f32[2048]{0:T(1024)S(1)}, f32[2048]{0:T(1024)}, u32[]{:S(2)}) copy-start(f32[2048]{0:T(1024)} %param.13) | copy-start | bytes 24580
  39.5 1.8 %collective-permute-start.7 = (f32[1,256]{1,0:T(1,128)S(1)}, f32[1,256]{1,0:T(1,128)S(1)}, u32[]{:S(2)}, u32[]{:S(2)}) collective-permute-start(f32[1,256]{1,0:T(1,128)S(1)} %get-tuple-element.27), channel_id=1, source_target_pairs={{0,3},{1,0},{2,1},{3,2},{4,7},{5,4},{6,5},{7,6},{8,11},{9,8},{10,9... | collective-permute-start | bytes 3080 | tf_op jit(solution)/shard_map/ppermute | solution.py:408
  39.5 3.6 %collective-permute-start.6 = (f32[1,256]{1,0:T(1,128)S(1)}, f32[1,256]{1,0:T(1,128)S(1)}, u32[]{:S(2)}, u32[]{:S(2)}) collective-permute-start(f32[1,256]{1,0:T(1,128)S(1)} %get-tuple-element.27), channel_id=1, source_target_pairs={{0,2},{1,3},{2,0},{3,1},{4,6},{5,7},{6,4},{7,5},{8,10},{9,11},{10,... | collective-permute-start | bytes 3080 | tf_op jit(solution)/shard_map/ppermute | solution.py:408
  41.1 3.0 %collective-permute-start.5 = (f32[1,256]{1,0:T(1,128)S(1)}, f32[1,256]{1,0:T(1,128)S(1)}, u32[]{:S(2)}, u32[]{:S(2)}) collective-permute-start(f32[1,256]{1,0:T(1,128)S(1)} %get-tuple-element.27), channel_id=1, source_target_pairs={{0,1},{1,2},{2,3},{3,0},{4,5},{5,6},{6,7},{7,4},{8,9},{9,10},{10,1... | collective-permute-start | bytes 3080 | tf_op jit(solution)/shard_map/ppermute | solution.py:408
where the time goes:
time: 46.2 us; the launch traced here: 45.7 us
  starting transfers between devices  17.5 us (38%)
  Pallas kernels  11.5 us (25%)
  local copies, waits for them, and re-layouts  7.73 us (17%)
  waiting for transfers between devices  5.6 us (12%)
  other arithmetic  2.57 us (6%)
  between operations  0.8 us (2%)
    ppermute x3, starting transfers between devices, per_device(): received = [lax.ppermute(group, 'ctx', shift) for shift in shifts]  9.28 us
    unnamed x22, local copies, waits for them, and re-layouts  6.81 us
    pallas_call x1, Pallas kernels, per_device(): pl.pallas_call(local_kernel, in_specs=[any_spec, any_spec] + [vmem_spec]...  5.2 us
    ppermute x1, starting transfers between devices, per_device(): before = lax.ppermute(projected[:, rows - (taps - 1):, :], 'ctx', route)  4.84 us
    pallas_call x1, Pallas kernels, per_device(): pl.pallas_call(state_kernel, in_specs=[any_spec, vmem_spec, vmem_spec], o...  4.06 us
    ppermute x1, waiting for transfers between devices, per_device(): others = [lax.ppermute(group, 'ctx', cycle).astype(F32) for cycle in cycles]  2.82 us
    ppermute x3, waiting for transfers between devices, per_device(): parts = [lax.ppermute(squares, 'fsdp', ring) for ring in rings]  2.77 us
    ppermute x3, starting transfers between devices, per_device(): parts = [lax.ppermute(squares, 'fsdp', ring) for ring in rings]  1.77 us
  transfers between devices with their start and end apart: 8, of which 3 were waited for; matrix products, arithmetic and copies ran while one was open for 0% of the time, Pallas kernels for 23%

commit v1 on v0

v1 whole, which is shorter than its diff:
```python
import jax
import jax.numpy as jnp
from jax import lax
from jax.experimental import pallas as pl
from jax.experimental.pallas import tpu as pltpu
from jax.sharding import PartitionSpec as P

CHANNELS_PER_GRP = 16
MODES = 16
CHUNK = 32
LANES = 128
WIDE = 256
GROUPS = LANES // CHANNELS_PER_GRP
VMEM_LIMIT = 16 * 1024 * 1024
F32 = jnp.float32
BF16 = jnp.bfloat16


def index_of(shape, dim):
    return lax.broadcasted_iota(jnp.int32, shape, dim)


def lanes_of(tile, width=LANES):
    return slice(tile * width, (tile + 1) * width)


def per_channel(table):
    groups = table.shape[1]
    width = groups * CHANNELS_PER_GRP
    high = table.astype(BF16)
    rest = table - high.astype(F32)
    middle = rest.astype(BF16)
    low = (rest - middle.astype(F32)).astype(BF16)
    terms = jnp.concatenate([high, middle, low], axis=0)
    parts = []
    for tile in range(width // WIDE):
        shape = (groups, WIDE)
        own = index_of(shape, 0) == index_of(shape, 1) // CHANNELS_PER_GRP + tile * (WIDE // CHANNELS_PER_GRP)
        three = jnp.dot(terms, jnp.where(own, 1.0, 0.0).astype(BF16), preferred_element_type=F32)
        parts.append(three[:MODES] + three[MODES : 2 * MODES] + three[2 * MODES :])
    return jnp.concatenate(parts, axis=1)


def mode_row(channel_table):
    own = index_of(channel_table.shape, 0) == (index_of(channel_table.shape, 1) & (MODES - 1))
    return jnp.sum(jnp.where(own, channel_table, 0.0), axis=0, keepdims=True)


def mode_column(row):
    return jnp.transpose(jnp.broadcast_to(row, (LANES, LANES)))


def group_mask(dtype):
    shape = (GROUPS, MODES, LANES)
    own = index_of(shape, 0) == index_of(shape, 2) // CHANNELS_PER_GRP
    return jnp.where(own, 1.0, 0.0).astype(dtype)


def spread(rows, mask):
    size = rows.shape[0]
    copies = rows.reshape(1, size // MODES, MODES, LANES) * mask.reshape(GROUPS, 1, MODES, LANES)
    return copies.reshape(GROUPS * size, LANES)


def shifted(block, before):
    one = pltpu.roll(block, 1, 0)
    two = pltpu.roll(block, 2, 0)
    first = index_of((8, block.shape[1]), 0)
    near, far = (0.0, 0.0) if before is None else (before[1:2], before[0:1])
    head_one = jnp.where(first == 0, near, one[:8])
    head_two = jnp.where(first == 0, far, jnp.where(first == 1, near, two[:8]))
    if block.shape[0] == 8:
        return head_one, head_two
    return jnp.concatenate([head_one, one[8:]], axis=0), jnp.concatenate([head_two, two[8:]], axis=0)


def short_conv(block, before, weights):
    one, two = shifted(block, before)
    return weights[0] * block + weights[1] * one + weights[2] * two


def taps_of(weights, feature, lanes):
    return [weights[tap, feature : feature + 1, lanes] for tap in range(weights.shape[0])]


def state_kernel(
    projected_ref,
    weight_hbm,
    rate_hbm,
    product_ref,
    state_ref,
    mode_rate_ref,
    head_ref,
    weight_ref,
    buffer_ref,
    ending_ref,
    short_ref,
    rate_ref,
    sems,
    small_sems,
):
    rows, width = product_ref.shape
    wides = width // WIDE
    rate_copy = pltpu.make_async_copy(rate_hbm, rate_ref, small_sems.at[0])
    rate_copy.start()
    weight_copy = pltpu.make_async_copy(weight_hbm, short_ref, small_sems.at[1])
    weight_copy.start()
    copies = []
    for tile in range(wides):
        here = pl.ds(tile * WIDE, WIDE)
        copies.append(
            pltpu.make_async_copy(projected_ref.at[pl.ds(1, 2), :, here], buffer_ref.at[:, :, here], sems.at[tile])
        )
        copies[-1].start()
    rate_copy.wait()
    mode_rate = per_channel(rate_ref[...])
    mode_rate_ref[...] = mode_rate
    left = (rows - 1 - index_of((1, rows), 1)).astype(F32)
    left = jnp.where(left > rows - 2.5, 1e30, left)
    for tile in range(width // LANES):
        rate = mode_column(mode_row(mode_rate[:, lanes_of(tile)]))
        rate = jnp.concatenate([rate] * (rows // LANES), axis=1)
        ending_ref[tile // 2, lanes_of(tile % 2), :] = jnp.exp(-rate * left).astype(BF16)
    weight_copy.wait()
    weights = short_ref[...].astype(F32)
    weight_ref[...] = weights
    mask = group_mask(F32)

    def leave_state(tile, product):
        every = jnp.dot(ending_ref[tile], product, preferred_element_type=F32)
        for half in range(WIDE // LANES):
            own = every[lanes_of(half), lanes_of(half)].reshape(GROUPS, MODES, LANES)
            state_ref[:, lanes_of((WIDE // LANES) * tile + half)] = jnp.sum(own * mask, axis=0)

    previous = None
    for tile in range(wides):
        here = lanes_of(tile, WIDE)
        copies[tile].wait()
        if previous is not None:
            leave_state(tile - 1, previous)
        parts = []
        for c in (0, 1):
            block = buffer_ref[c, :, here].astype(F32)
            head_ref[c, :, here] = block[:8]
            parts.append(short_conv(block, None, taps_of(weights, c + 1, here)))
        previous = (parts[0] * parts[1]).astype(BF16)
        product_ref[:, here] = previous
    leave_state(wides - 1, previous)


def halo(before_ref, place_ref):
    return jnp.where(place_ref[0] > 0, before_ref[...].astype(F32), 0.0)


def head_kernel(rows, place_ref, before_ref, head_ref, weight_ref, state_ref, mode_rate_ref, full_ref, first_ref):
    before = halo(before_ref, place_ref)
    everything = slice(0, head_ref.shape[2])
    parts = [short_conv(head_ref[c], before[c + 1], taps_of(weight_ref, c + 1, everything)) for c in (0, 1)]
    first = (parts[0] * parts[1]).astype(BF16).astype(F32)
    first_ref[...] = first
    rate = mode_rate_ref[...]
    early = jnp.exp(-float(rows - 1) * rate) * first[0:1] + jnp.exp(-float(rows - 2) * rate) * first[1:2]
    full_ref[...] = (state_ref[...] + early).astype(BF16)


def split(x):
    high = x.astype(BF16)
    return high, (x - high.astype(F32)).astype(BF16)


def prepare_kernel(
    place_ref,
    projected_ref,
    residual_hbm,
    residue_hbm,
    before_ref,
    weight_ref,
    mode_rate_ref,
    inner_ref,
    entering_ref,
    carry_ref,
    gate_ref,
    residual_ref,
    query_ref,
    residue_ref,
    sems,
):
    rows, width = gate_ref.shape
    copies = [
        pltpu.make_async_copy(residue_hbm, residue_ref, sems.at[0]),
        pltpu.make_async_copy(projected_ref.at[0], query_ref, sems.at[1]),
        pltpu.make_async_copy(residual_hbm, residual_ref, sems.at[2]),
    ]
    for copy in copies:
        copy.start()
    copies[0].wait()
    residue = per_channel(residue_ref[...])
    wide = GROUPS * CHUNK
    step = index_of((CHUNK, LANES), 0).astype(F32)
    source = (index_of((LANES, wide), 1) & (CHUNK - 1)).astype(F32)
    own = index_of((LANES, wide), 0) // MODES == index_of((LANES, wide), 1) // CHUNK
    causal = (index_of((CHUNK, wide), 1) & (CHUNK - 1)) <= index_of((CHUNK, wide), 0)
    for tile in range(width // LANES):
        here = lanes_of(tile)
        rate_row = mode_row(mode_rate_ref[:, here])
        rate = mode_column(rate_row)
        rate = jnp.concatenate([rate] * (wide // LANES), axis=1)
        falling = mode_row(residue[:, here]) * jnp.exp(-rate_row * step)
        rising = jnp.where(own, jnp.exp(rate * source), 0.0)
        fall_high, fall_low = split(falling)
        rise_high, rise_low = split(rising)
        taps = jnp.dot(jnp.concatenate([fall_high, fall_low], axis=0), rise_high, preferred_element_type=F32)
        taps = taps[:CHUNK] + taps[CHUNK:] + jnp.dot(fall_high, rise_low, preferred_element_type=F32)
        taps = jnp.where(causal, taps, 0.0)
        ending = rising * jnp.exp(-float(CHUNK - 1) * rate)
        ending = jnp.sum(ending.reshape(GROUPS, MODES, wide), axis=0)
        inner_ref[tile] = jnp.concatenate([taps.astype(BF16), ending.astype(BF16)], axis=0)
        half = tile % (WIDE // LANES)
        for chunk in range(rows // CHUNK):
            entering = (falling * jnp.exp(-float(CHUNK * chunk + 1) * rate_row)).astype(BF16)
            carry_ref[tile // (WIDE // LANES), chunk * CHUNK : (chunk + 1) * CHUNK, lanes_of(half)] = entering
            if chunk == 0:
                entering_ref[tile] = entering
    before = halo(before_ref, place_ref)
    copies[1].wait()
    for tile in range(width // LANES):
        here = lanes_of(tile)
        gate_ref[:, here] = short_conv(
            query_ref[:, here].astype(F32), before[0, :, here], taps_of(weight_ref, 0, here)
        )
    copies[2].wait()


def local_kernel(
    gate_ref,
    residual_ref,
    product_ref,
    first_ref,
    mode_rate_ref,
    inner_ref,
    entering_ref,
    skip_ref,
    base_ref,
):
    rows, width = product_ref.shape
    mask = group_mask(BF16)
    top = index_of((8, LANES), 0) < 2
    for tile in range(width // LANES):
        here = lanes_of(tile)
        pieces = []
        for chunk in range(rows // CHUNK):
            piece = product_ref[chunk * CHUNK : (chunk + 1) * CHUNK, here]
            if chunk == 0:
                wide = piece.astype(F32)
                head = jnp.where(top, first_ref[:, here], wide[:8])
                piece = jnp.concatenate([head, wide[8:]], axis=0).astype(BF16)
            pieces.append(piece)
        table = inner_ref[tile]
        inner = []
        for pair in range(rows // (2 * CHUNK)):
            sources = jnp.concatenate([spread(pieces[2 * pair + k], mask) for k in (0, 1)], axis=1)
            inner.append(jnp.dot(table, sources, preferred_element_type=F32))
        decay = jnp.exp(-float(CHUNK) * mode_rate_ref[:, here])
        state = jnp.zeros((MODES, LANES), F32)
        states = []
        for chunk in range(rows // CHUNK):
            states.append(spread(state.astype(BF16), mask))
            state = decay * state + inner[chunk // 2][CHUNK:, lanes_of(chunk % 2)]
        entering = entering_ref[tile]
        skip = skip_ref[:, here]
        for pair in range(rows // (2 * CHUNK)):
            two = jnp.concatenate(states[2 * pair : 2 * pair + 2], axis=1)
            conv = inner[pair][:CHUNK] + jnp.dot(entering, two, preferred_element_type=F32)
            for k in (0, 1):
                chunk = 2 * pair + k
                span = slice(chunk * CHUNK, (chunk + 1) * CHUNK)
                whole = conv[:, lanes_of(k)] + skip * pieces[chunk].astype(F32)
                base_ref[span, here] = residual_ref[span, here].astype(F32) + gate_ref[span, here] * whole


def join_kernel(tokens, radix, stride, place_ref, own_ref, mode_rate_ref, entry_ref, *refs):
    others, (found_ref, group_ref) = refs[: radix - 1], refs[radix - 1 :]
    rate = mode_rate_ref[...]
    run = lax.rem(place_ref[0] // stride, radix)
    step = float(tokens * stride)

    def decayed(value, runs):
        return jnp.exp(-step * runs.astype(F32) * rate) * value

    found = jnp.zeros_like(rate)
    total = decayed(own_ref[...].astype(F32), radix - 1 - run)
    for k, ref in enumerate(others, 1):
        other = ref[...].astype(F32)
        found = found + jnp.where(run >= k, decayed(other, jnp.full((), k - 1, jnp.int32)), 0.0)
        source = lax.rem(run - k + radix, radix)
        total = total + decayed(other, radix - 1 - source)
    within = lax.rem(place_ref[0], stride).astype(F32) * float(tokens)
    found_ref[...] = entry_ref[...] + jnp.exp(-within * rate) * found
    group_ref[...] = total.astype(BF16)


def carry_kernel(stride, received, place_ref, base_ref, gate_ref, carry_ref, mode_rate_ref, inner_entry_ref, *refs):
    entry_refs, (summed_ref, squares_ref) = refs[:received], refs[received:]
    rows, width = base_ref.shape
    run = place_ref[0] // stride
    within = lax.rem(place_ref[0], stride).astype(F32) * float(rows)
    mask = group_mask(BF16)
    total = jnp.zeros((rows, LANES), F32)
    nothing = jnp.zeros((LANES, LANES), BF16)
    for tile in range(width // WIDE):
        here = lanes_of(tile, WIDE)
        rate = mode_rate_ref[:, here]
        decay = jnp.exp(-float(rows * stride) * rate)
        outer = jnp.zeros_like(rate)
        for k in range(received, 0, -1):
            outer = decay * outer + jnp.where(run >= k, entry_refs[k - 1][:, here].astype(F32), 0.0)
        entry = (inner_entry_ref[:, here] + jnp.exp(-within * rate) * outer).astype(BF16)
        left, right = spread(entry[:, :LANES], mask), spread(entry[:, LANES:], mask)
        both = jnp.concatenate(
            [jnp.concatenate([left, nothing], axis=1), jnp.concatenate([nothing, right], axis=1)], axis=0
        )
        carry = jnp.dot(carry_ref[tile], both, preferred_element_type=F32)
        summed = base_ref[:, here] + gate_ref[:, here] * carry
        summed_ref[:, here] = summed
        square = summed * summed
        total = total + (square[:, :LANES] + square[:, LANES:])
    squares = lax.dot_general(
        jnp.ones((8, LANES), F32),
        total,
        (((1,), (1,)), ((), ())),
        precision=lax.Precision.HIGHEST,
        preferred_element_type=F32,
    )
    squares_ref[...] = squares[0:1]


def write_kernel(summed_ref, out_hbm, rounded_ref, sems):
    width = summed_ref.shape[1]
    copies = []
    for tile in range(width // WIDE):
        here = lanes_of(tile, WIDE)
        rounded_ref[:, here] = summed_ref[:, here].astype(BF16)
        span = pl.ds(tile * WIDE, WIDE)
        copies.append(pltpu.make_async_copy(rounded_ref.at[:, span], out_hbm.at[:, span], sems.at[tile]))
        copies[-1].start()
    for copy in copies:
        copy.wait()


def norm_kernel(full_width, parts, summed_ref, gain_ref, *refs):
    squares_refs, (out_hbm, rounded_ref, sems) = refs[:parts], refs[parts:]
    rows, width = summed_ref.shape
    squares = squares_refs[0][...]
    for ref in squares_refs[1:]:
        squares = squares + ref[...]
    scale_row = lax.rsqrt(squares / full_width + 1e-05)
    scale = jnp.concatenate([mode_column(scale_row[:, lanes_of(k)]) for k in range(rows // LANES)], axis=0)
    copies = []
    for tile in range(width // WIDE):
        for half in range(WIDE // LANES):
            here = lanes_of(tile * (WIDE // LANES) + half)
            rounded_ref[:, here] = (summed_ref[:, here] * scale * gain_ref[:, here]).astype(BF16)
        span = pl.ds(tile * WIDE, WIDE)
        copies.append(pltpu.make_async_copy(rounded_ref.at[:, span], out_hbm.at[:, span], sems.at[tile]))
        copies[-1].start()
    for copy in copies:
        copy.wait()


def params():
    return pltpu.CompilerParams(vmem_limit_bytes=VMEM_LIMIT)


def cost(microseconds):
    return pl.CostEstimate(flops=0, bytes_accessed=int(microseconds * 3.0e6), transcendentals=0)


def radices(count):
    found = []
    for radix in (2, 4, 4, 4):
        if count % radix == 0 and count > 1:
            found.append(radix)
            count //= radix
    for radix in (3, 2, 5, 7):
        while count % radix == 0 and count > 1:
            found.append(radix)
            count //= radix
    return found + ([count] if count > 1 else [])


def ring(count, shift):
    return [(i, (i + shift) % count) for i in range(count)]


def per_device(projected, short_weight, rates, residues, skip, residual, gain):
    rows, width = projected.shape[1:]
    taps = short_weight.shape[0]
    peers = lax.axis_size("ctx")
    full_width = width * lax.axis_size("fsdp")
    place = lax.axis_index("ctx").astype(jnp.int32).reshape(1)
    hbm_spec = pl.BlockSpec(memory_space=pltpu.HBM)
    vmem_spec = pl.BlockSpec(memory_space=pltpu.VMEM)
    smem_spec = pl.BlockSpec(memory_space=pltpu.SMEM)
    tiles = width // LANES
    wides = width // WIDE

    def kept(array):
        return pltpu.with_memory_space_constraint(array, pltpu.HBM)

    def f32(*shape):
        return jax.ShapeDtypeStruct(shape, F32)

    def bf16(*shape):
        return jax.ShapeDtypeStruct(shape, BF16)

    before = lax.ppermute(projected[:, rows - (taps - 1) :, :], "ctx", ring(peers, 1))

    product, state, mode_rate, head, weights = pl.pallas_call(
        state_kernel,
        in_specs=[hbm_spec] * 3,
        out_shape=[
            bf16(rows, width),
            f32(MODES, width),
            f32(MODES, width),
            f32(2, 8, width),
            f32(*short_weight.shape),
        ],
        scratch_shapes=[
            pltpu.VMEM((2, rows, width), BF16),
            pltpu.VMEM((wides, WIDE, rows), BF16),
            pltpu.VMEM(short_weight.shape, BF16),
            pltpu.VMEM((MODES, rates.shape[0]), F32),
            pltpu.SemaphoreType.DMA((wides,)),
            pltpu.SemaphoreType.DMA((2,)),
        ],
        compiler_params=params(),
        cost_estimate=cost(3),
        name="block_state",
    )(kept(projected), kept(short_weight), kept(rates.T))

    full_state, first = pl.pallas_call(
        lambda *refs: head_kernel(rows, *refs),
        in_specs=[smem_spec] + [vmem_spec] * 5,
        out_shape=[bf16(MODES, width), f32(8, width)],
        compiler_params=params(),
        cost_estimate=cost(0.2),
        name="head_tokens",
    )(place, before, head, weights, state, mode_rate)

    inner, entering, carry_table, gate, residual_here = pl.pallas_call(
        prepare_kernel,
        in_specs=[smem_spec] + [hbm_spec] * 3 + [vmem_spec] * 3,
        out_shape=[
            bf16(tiles, CHUNK + MODES, GROUPS * CHUNK),
            bf16(tiles, CHUNK, LANES),
            bf16(wides, rows, WIDE),
            f32(rows, width),
            bf16(rows, width),
        ],
        scratch_shapes=[
            pltpu.VMEM((rows, width), BF16),
            pltpu.VMEM((MODES, rates.shape[0]), F32),
            pltpu.SemaphoreType.DMA((3,)),
        ],
        compiler_params=params(),
        cost_estimate=cost(2),
        name="prepare",
    )(place, kept(projected), kept(residual), kept(residues.T), before, weights, mode_rate)

    group, entry, stride = full_state, jnp.zeros((MODES, width), F32), 1
    levels = radices(peers)
    for level, radix in enumerate(levels):
        size = stride * radix
        if level == len(levels) - 1:
            break
        cycles = [
            [(i, i // size * size + (i + stride * k) % size) for i in range(peers)] for k in range(1, radix)
        ]
        others = [lax.ppermute(group, "ctx", cycle) for cycle in cycles]
        if level == 0:
            others[0], inner = lax.optimization_barrier((others[0], inner))
        entry, group = pl.pallas_call(
            lambda *refs, radix=radix, stride=stride: join_kernel(rows, radix, stride, *refs),
            in_specs=[smem_spec] + [vmem_spec] * (2 + radix),
            out_shape=[f32(MODES, width), bf16(MODES, width)],
            compiler_params=params(),
            cost_estimate=cost(0.2),
            name="join",
        )(place, group, mode_rate, entry, *others)
        stride = size
    received = [lax.ppermute(group, "ctx", ring(peers, stride * k)) for k in range(1, levels[-1])]

    base = pl.pallas_call(
        local_kernel,
        out_shape=f32(rows, width),
        compiler_params=params(),
        cost_estimate=cost(5),
        name="local_conv",
    )(gate, residual_here, product, first, mode_rate, inner, entering, skip[None])

    summed, squares = pl.pallas_call(
        lambda *refs: carry_kernel(stride, len(received), *refs),
        in_specs=[smem_spec] + [vmem_spec] * (5 + len(received)),
        out_shape=[f32(rows, width), f32(1, rows)],
        compiler_params=params(),
        cost_estimate=cost(1),
        name="add_carry",
    )(place, base, gate, carry_table, mode_rate, entry, *received)

    count = lax.axis_size("fsdp")
    parts = [lax.ppermute(squares, "fsdp", ring(count, k)) for k in range(1, count)]

    def write(kernel, operands, name):
        return pl.pallas_call(
            kernel,
            out_specs=hbm_spec,
            out_shape=bf16(rows, width),
            scratch_shapes=[pltpu.VMEM((rows, width), BF16), pltpu.SemaphoreType.DMA((wides,))],
            compiler_params=params(),
            cost_estimate=cost(1),
            name=name,
        )(*operands)

    new_residual = write(write_kernel, (summed,), "new_residual")
    normed = write(
        lambda *refs: norm_kernel(full_width, count, *refs), (summed, gain[None], squares, *parts), "normed"
    )
    return (new_residual, normed)


def solution(mesh):
    return jax.shard_map(
        per_device,
        mesh=mesh,
        in_specs=(
            P(None, "ctx", "fsdp"),
            P(None, None, "fsdp"),
            P("fsdp", None),
            P("fsdp", None),
            P("fsdp"),
            P("ctx", "fsdp"),
            P("fsdp"),
        ),
        out_specs=(P("ctx", "fsdp"), P("ctx", "fsdp")),
        check_vma=False,
    )
```

time: 46.2 us -> 30.5 us (0.66)
  local copies, waits for them, and re-layouts: 7.73 us -> 0.94 us
  waiting for transfers between devices: 5.6 us -> 0.25 us
  starting transfers between devices: 17.5 us -> 13.2 us
  Pallas kernels: 11.5 us -> 15.1 us
  other arithmetic: 2.57 us -> 0 us
    unnamed x22 -> x4, local copies, waits for them, and re-layouts: 6.81 us -> 0.01 us
    ppermute x8, waiting for transfers between devices: 5.6 us -> 0.25 us  [the longest x3 0.23 us: per_device(): lax.ppermute(squares, 'fsdp', ring(count, k))]
    ppermute x8, starting transfers between devices: 17.5 us -> 13.2 us  [the longest x3 5.57 us: per_device(): lax.ppermute(group, 'ctx', ring(peers, stride * k))]
    pallas_call x4 -> x7, Pallas kernels: 10.7 us -> 14.2 us  [the longest x1 5.12 us: per_device(): pl.pallas_call(state_kernel, in_specs=[hbm_spec] * 3, out_shape=[bf16(row...]
    convert_element_type x2 -> x0, other arithmetic: 2.56 us -> none  [the longest x1 1.64 us: per_device(): normed = (summed * scale * gain[None, :]).astype(BF16)]
  transfers between devices with their start and end apart: 8 -> 8, of which waited for: 3 -> 1; matrix products, arithmetic and copies ran while one was open for 0% -> 0% of each run, Pallas kernels for 23% -> 42%
where the time goes in v1:
time: 30.5 us; the launch traced here: 30.2 us
  Pallas kernels  15.1 us (50%)
  starting transfers between devices  13.2 us (43%)
  local copies, waits for them, and re-layouts  0.94 us (3%)
  between operations  0.74 us (2%)
    ppermute x3, starting transfers between devices, per_device(): lax.ppermute(group, 'ctx', ring(peers, stride * k))  5.57 us
    pallas_call x1, Pallas kernels, per_device(): pl.pallas_call(state_kernel, in_specs=[hbm_spec] * 3, out_shape=[bf16(row...  5.12 us
    pallas_call x1, Pallas kernels, per_device(): pl.pallas_call(local_kernel, out_shape=f32(rows, width), compiler_params=...  3.81 us
    ppermute x3, starting transfers between devices, per_device(): lax.ppermute(squares, 'fsdp', ring(count, k))  3.01 us
    ppermute x1, starting transfers between devices, per_device(): lax.ppermute(projected[:, rows - (taps - 1):, :], 'ctx', ring(peers, 1))  2.99 us
    pallas_call x1, Pallas kernels, per_device(): pl.pallas_call(prepare_kernel, in_specs=[smem_spec] + [hbm_spec] * 3 + [v...  2.7 us
    pallas_call x2, Pallas kernels, write(): pl.pallas_call(kernel, out_specs=hbm_spec, out_shape=bf16(rows, width), s...  2.32 us
    ppermute x1, starting transfers between devices, per_device(): others = [lax.ppermute(group, 'ctx', cycle) for cycle in cycles]  1.61 us
  transfers between devices with their start and end apart: 8, of which 1 were waited for; matrix products, arithmetic and copies ran while one was open for 0% of the time, Pallas kernels for 42%

profile of v1, /device:TPU:0, one launch (start us, length us, event | category | flops | bytes accessed | tf_op | source)
XLA Modules:
  0.0 30.2 jit_solution(12276281531565252053)
XLA Ops:
  0.6 0.9 %slice.3 = bf16[3,2,2048]{2,1,0:T(2,128)(2,1)S(1)} slice(bf16[3,256,2048]{2,1,0:T(8,128)(2,1)} %projected_ref.3), slice={[0:3], [254:256], [0:2048]} | slice | bytes 49152 | tf_op jit(solution)/shard_map/slice | solution.py:416
  1.6 3.0 %collective-permute-start = (bf16[3,2,2048]{2,1,0:T(2,128)(2,1)S(1)}, bf16[3,2,2048]{2,1,0:T(2,128)(2,1)S(1)}, u32[]{:S(2)}, u32[]{:S(2)}) collective-permute-start(bf16[3,2,2048]{2,1,0:T(2,128)(2,1)S(1)} %slice.3), channel_id=1, source_target_pairs={{0,4},{4,8},{8,12},{12,16},{16,20},{20,24},{24,28},{28,0},{1,5},{5... | collective-permute-start | bytes 73736 | tf_op jit(solution)/shard_map/ppermute | solution.py:416
  4.5 5.1 %block_state.1 = (bf16[256,2048]{1,0:T(8,128)(2,1)S(1)}, f32[16,2048]{1,0:T(8,128)S(1)}, f32[16,2048]{1,0:T(8,128)S(1)}, f32[2,8,2048]{2,1,0:T(8,128)S(1)}, f32[3,3,2048]{2,1,0:T(4,128)S(1)}) custom-call(bf16[3,256,2048]{2,1,0:T(8,128)(2,1)} %projected_ref.3, bf16[3,3,2048]{2,1,0:T(4,128)(2,1)} %weight_hbm.1, f32[16,128]{1,0:T(8,128)} %bitcast.7), custom_call_target="tpu_custom_call" | custom-call | bytes 9000000 | tf_op jit(solution)/shard_map/block_state/pallas_call | solution.py:418
  9.7 0.0 collective-permute-done.before_ref.refs_1_
  9.7 0.1 head_tokens.1
  9.8 1.6 %collective-permute-start.1 = (bf16[16,2048]{1,0:T(8,128)(2,1)S(1)}, bf16[16,2048]{1,0:T(8,128)(2,1)S(1)}, u32[]{:S(2)}, u32[]{:S(2)}) collective-permute-start(bf16[16,2048]{1,0:T(8,128)(2,1)S(1)} %get-tuple-element.28.refs_1_), channel_id=1, source_target_pairs={{0,4},{4,0},{8,12},{12,8},{16,20},{20,16},{24,28},{28,24},{1,5},{5... | collective-permute-start | bytes 196616 | tf_op jit(solution)/shard_map/ppermute | solution.py:479
  11.4 0.0 copy-start
  11.4 2.7 %prepare.1 = (bf16[16,48,256]{2,1,0:T(8,128)(2,1)S(1)}, bf16[16,32,128]{2,1,0:T(8,128)(2,1)S(1)}, bf16[8,256,256]{2,1,0:T(8,128)(2,1)S(1)}, f32[256,2048]{1,0:T(8,128)S(1)}, bf16[256,2048]{1,0:T(8,128)(2,1)S(1)}) custom-call(s32[1]{0:T(128)} %bitcast.place_ref.refs_0_, bf16[3,256,2048]{2,1,0:T(8,128)(2,1)} %projected_ref.3, bf16[256,2048]{1,0:T(8,128)(2,1)} %residual_hbm.1, ...), custom_call_target="tpu_custom_call" | custom-call | bytes 6000000 | tf_op jit(solution)/shard_map/prepare/pallas_call | solution.py:450
  14.2 0.0 collective-permute-done.1.refs_4_
  14.2 0.1 join.1
  14.3 1.6 %collective-permute-start.2 = (bf16[16,2048]{1,0:T(8,128)(2,1)S(1)}, bf16[16,2048]{1,0:T(8,128)(2,1)S(1)}, u32[]{:S(2)}, u32[]{:S(2)}) collective-permute-start(bf16[16,2048]{1,0:T(8,128)(2,1)S(1)} %get-tuple-element.35), channel_id=1, source_target_pairs={{0,8},{4,12},{8,16},{12,20},{16,24},{20,28},{24,0},{28,4},{1,9},{5... | collective-permute-start | bytes 196616 | tf_op jit(solution)/shard_map/ppermute | solution.py:491
  15.9 2.6 %collective-permute-start.3 = (bf16[16,2048]{1,0:T(8,128)(2,1)S(1)}, bf16[16,2048]{1,0:T(8,128)(2,1)S(1)}, u32[]{:S(2)}, u32[]{:S(2)}) collective-permute-start(bf16[16,2048]{1,0:T(8,128)(2,1)S(1)} %get-tuple-element.35), channel_id=1, source_target_pairs={{0,16},{4,20},{8,24},{12,28},{16,0},{20,4},{24,8},{28,12},{1,17},{... | collective-permute-start | bytes 196616 | tf_op jit(solution)/shard_map/ppermute | solution.py:491
  18.5 1.4 %collective-permute-start.4 = (bf16[16,2048]{1,0:T(8,128)(2,1)S(1)}, bf16[16,2048]{1,0:T(8,128)(2,1)S(1)}, u32[]{:S(2)}, u32[]{:S(2)}) collective-permute-start(bf16[16,2048]{1,0:T(8,128)(2,1)S(1)} %get-tuple-element.35), channel_id=1, source_target_pairs={{0,24},{4,28},{8,0},{12,4},{16,8},{20,12},{24,16},{28,20},{1,25},{... | collective-permute-start | bytes 196616 | tf_op jit(solution)/shard_map/ppermute | solution.py:491
  19.9 0.0 copy-done
  19.9 3.8 %local_conv.1.refs_1_ = f32[256,2048]{1,0:T(8,128)S(1)} custom-call(f32[256,2048]{1,0:T(8,128)S(1)} %get-tuple-element.22.gate_ref.refs_2_, bf16[256,2048]{1,0:T(8,128)(2,1)S(1)} %get-tuple-element.23.residual_ref, bf16[256,2048]{1,0:T(8,128)(2,1)S(1)} %get-tuple-element.24.product_ref, f32[8,2048]{1,0:T(8,128)S(1)} %get-tuple-element.27.first_ref, ...), custom_call_target="tpu_custom_call" | custom-call | bytes 15000000 | tf_op jit(solution)/shard_map/local_conv/pallas_call | solution.py:493
  23.7 0.0 collective-permute-done.2.refs_6_
  23.7 0.0 collective-permute-done.3.refs_7_
  23.7 0.0 collective-permute-done.4.refs_8_
  23.7 0.9 %add_carry.1 = (f32[256,2048]{1,0:T(8,128)S(1)}, f32[1,256]{1,0:T(1,128)S(1)}) custom-call(s32[1]{0:T(128)} %bitcast.place_ref.refs_0_, f32[256,2048]{1,0:T(8,128)S(1)} %local_conv.1.refs_1_, f32[256,2048]{1,0:T(8,128)S(1)} %get-tuple-element.22.gate_ref.refs_2_, bf16[8,256,256]{2,1,0:T(8,128)(2,1)S(1)} %get-tuple-element.32.refs_3_, ...), custom_call_target="tpu_custom_call" | custom-call | bytes 3000000 | tf_op jit(solution)/shard_map/add_carry/pallas_call | solution.py:501
  24.6 0.0 copy-start.1
  24.6 0.0 collective-permute-start.5
  24.6 1.6 %collective-permute-start.6 = (f32[1,256]{1,0:T(1,128)S(1)}, f32[1,256]{1,0:T(1,128)S(1)}, u32[]{:S(2)}, u32[]{:S(2)}) collective-permute-start(f32[1,256]{1,0:T(1,128)S(1)} %get-tuple-element.37.refs_2_), channel_id=1, source_target_pairs={{0,2},{1,3},{2,0},{3,1},{4,6},{5,7},{6,4},{7,5},{8,10},{9,11},{10,... | collective-permute-start | bytes 3080 | tf_op jit(solution)/shard_map/ppermute | solution.py:511
  26.2 1.4 %collective-permute-start.7 = (f32[1,256]{1,0:T(1,128)S(1)}, f32[1,256]{1,0:T(1,128)S(1)}, u32[]{:S(2)}, u32[]{:S(2)}) collective-permute-start(f32[1,256]{1,0:T(1,128)S(1)} %get-tuple-element.37.refs_2_), channel_id=1, source_target_pairs={{0,3},{1,0},{2,1},{3,2},{4,7},{5,4},{6,5},{7,6},{8,11},{9,8},{10,9... | collective-permute-start | bytes 3080 | tf_op jit(solution)/shard_map/ppermute | solution.py:511
  27.6 1.0 %new_residual.1 = bf16[256,2048]{1,0:T(8,128)(2,1)} custom-call(f32[256,2048]{1,0:T(8,128)S(1)} %get-tuple-element.36.summed_ref.refs_0_), custom_call_target="tpu_custom_call" | custom-call | bytes 3000000 | tf_op jit(solution)/shard_map/new_residual/pallas_call | solution.py:514
  28.6 0.0 collective-permute-done.5.refs_3_
  28.7 0.0 collective-permute-done.6.refs_4_
  28.7 0.2 collective-permute-done.7.refs_5_
  28.9 0.0 copy-done.1
  28.9 1.3 %normed.1 = bf16[256,2048]{1,0:T(8,128)(2,1)} custom-call(f32[256,2048]{1,0:T(8,128)S(1)} %get-tuple-element.36.summed_ref.refs_0_, f32[1,2048]{1,0:T(1,128)S(1)} %bitcast.6, f32[1,256]{1,0:T(1,128)S(1)} %get-tuple-element.37.refs_2_, f32[1,256]{1,0:T(1,128)S(1)} %collective-permute-done.5.refs_3_, f32[1,256]{1,0:T(1,128)S(1)} %collective-permute-done.6.refs_4_, ...), custom_call_target="tpu_custom_call" | custom-call | bytes 3000000 | tf_op jit(solution)/shard_map/normed/pallas_call | solution.py:514
  (1 shorter events, 0.0 us)
Async XLA Ops:
  1.6 8.1 %collective-permute-start = (bf16[3,2,2048]{2,1,0:T(2,128)(2,1)S(1)}, bf16[3,2,2048]{2,1,0:T(2,128)(2,1)S(1)}, u32[]{:S(2)}, u32[]{:S(2)}) collective-permute-start(bf16[3,2,2048]{2,1,0:T(2,128)(2,1)S(1)} %slice.3), channel_id=1, source_target_pairs={{0,4},{4,8},{8,12},{12,16},{16,20},{20,24},{24,28},{28,0},{1,5},{5... | collective-permute-start | bytes 73736 | tf_op jit(solution)/shard_map/ppermute | solution.py:416
  9.8 4.3 %collective-permute-start.1 = (bf16[16,2048]{1,0:T(8,128)(2,1)S(1)}, bf16[16,2048]{1,0:T(8,128)(2,1)S(1)}, u32[]{:S(2)}, u32[]{:S(2)}) collective-permute-start(bf16[16,2048]{1,0:T(8,128)(2,1)S(1)} %get-tuple-element.28.refs_1_), channel_id=1, source_target_pairs={{0,4},{4,0},{8,12},{12,8},{16,20},{20,16},{24,28},{28,24},{1,5},{5... | collective-permute-start | bytes 196616 | tf_op jit(solution)/shard_map/ppermute | solution.py:479
  11.4 8.4 %copy-start = (f32[2048]{0:T(1024)S(1)}, f32[2048]{0:T(1024)}, u32[]{:S(2)}) copy-start(f32[2048]{0:T(1024)} %param.11) | copy-start | bytes 24580
  14.3 9.4 %collective-permute-start.2 = (bf16[16,2048]{1,0:T(8,128)(2,1)S(1)}, bf16[16,2048]{1,0:T(8,128)(2,1)S(1)}, u32[]{:S(2)}, u32[]{:S(2)}) collective-permute-start(bf16[16,2048]{1,0:T(8,128)(2,1)S(1)} %get-tuple-element.35), channel_id=1, source_target_pairs={{0,8},{4,12},{8,16},{12,20},{16,24},{20,28},{24,0},{28,4},{1,9},{5... | collective-permute-start | bytes 196616 | tf_op jit(solution)/shard_map/ppermute | solution.py:491
  15.9 7.8 %collective-permute-start.3 = (bf16[16,2048]{1,0:T(8,128)(2,1)S(1)}, bf16[16,2048]{1,0:T(8,128)(2,1)S(1)}, u32[]{:S(2)}, u32[]{:S(2)}) collective-permute-start(bf16[16,2048]{1,0:T(8,128)(2,1)S(1)} %get-tuple-element.35), channel_id=1, source_target_pairs={{0,16},{4,20},{8,24},{12,28},{16,0},{20,4},{24,8},{28,12},{1,17},{... | collective-permute-start | bytes 196616 | tf_op jit(solution)/shard_map/ppermute | solution.py:491
  18.5 5.2 %collective-permute-start.4 = (bf16[16,2048]{1,0:T(8,128)(2,1)S(1)}, bf16[16,2048]{1,0:T(8,128)(2,1)S(1)}, u32[]{:S(2)}, u32[]{:S(2)}) collective-permute-start(bf16[16,2048]{1,0:T(8,128)(2,1)S(1)} %get-tuple-element.35), channel_id=1, source_target_pairs={{0,24},{4,28},{8,0},{12,4},{16,8},{20,12},{24,16},{28,20},{1,25},{... | collective-permute-start | bytes 196616 | tf_op jit(solution)/shard_map/ppermute | solution.py:491
  24.6 4.3 %copy-start.1 = (f32[2048]{0:T(1024)S(1)}, f32[2048]{0:T(1024)}, u32[]{:S(2)}) copy-start(f32[2048]{0:T(1024)} %param.13) | copy-start | bytes 24580
  24.6 4.1 %collective-permute-start.5 = (f32[1,256]{1,0:T(1,128)S(1)}, f32[1,256]{1,0:T(1,128)S(1)}, u32[]{:S(2)}, u32[]{:S(2)}) collective-permute-start(f32[1,256]{1,0:T(1,128)S(1)} %get-tuple-element.37.refs_2_), channel_id=1, source_target_pairs={{0,1},{1,2},{2,3},{3,0},{4,5},{5,6},{6,7},{7,4},{8,9},{9,10},{10,1... | collective-permute-start | bytes 3080 | tf_op jit(solution)/shard_map/ppermute | solution.py:511
  24.6 4.1 %collective-permute-start.6 = (f32[1,256]{1,0:T(1,128)S(1)}, f32[1,256]{1,0:T(1,128)S(1)}, u32[]{:S(2)}, u32[]{:S(2)}) collective-permute-start(f32[1,256]{1,0:T(1,128)S(1)} %get-tuple-element.37.refs_2_), channel_id=1, source_target_pairs={{0,2},{1,3},{2,0},{3,1},{4,6},{5,7},{6,4},{7,5},{8,10},{9,11},{10,... | collective-permute-start | bytes 3080 | tf_op jit(solution)/shard_map/ppermute | solution.py:511
  26.2 2.7 %collective-permute-start.7 = (f32[1,256]{1,0:T(1,128)S(1)}, f32[1,256]{1,0:T(1,128)S(1)}, u32[]{:S(2)}, u32[]{:S(2)}) collective-permute-start(f32[1,256]{1,0:T(1,128)S(1)} %get-tuple-element.37.refs_2_), channel_id=1, source_target_pairs={{0,3},{1,0},{2,1},{3,2},{4,7},{5,4},{6,5},{7,6},{8,11},{9,8},{10,9... | collective-permute-start | bytes 3080 | tf_op jit(solution)/shard_map/ppermute | solution.py:511

commit v2 on v1

--- a/solution.py
+++ b/solution.py
@@ -8,6 +8,7 @@
 CHANNELS_PER_GRP = 16
 MODES = 16
 CHUNK = 32
+PIECE = 64
 LANES = 128
 WIDE = 256
 GROUPS = LANES // CHANNELS_PER_GRP
@@ -46,8 +47,19 @@
     return jnp.sum(jnp.where(own, channel_table, 0.0), axis=0, keepdims=True)
 
 
-def mode_column(row):
+def as_column(row):
     return jnp.transpose(jnp.broadcast_to(row, (LANES, LANES)))
+
+
+def own_mode(dtype):
+    shape = (GROUPS, MODES, LANES)
+    own = index_of(shape, 0) * MODES + index_of(shape, 1) == index_of(shape, 2)
+    return jnp.where(own, 1.0, 0.0).astype(dtype)
+
+
+def split(x):
+    high = x.astype(BF16)
+    return high, (x - high.astype(F32)).astype(BF16)
 
 
 def group_mask(dtype):
@@ -77,6 +89,15 @@
 def short_conv(block, before, weights):
     one, two = shifted(block, before)
     return weights[0] * block + weights[1] * one + weights[2] * two
+
+
+def conv_piece(load, start, before, weights):
+    if start == 0:
+        return short_conv(load(0, PIECE), before, weights)
+    block = load(start - 16, start + PIECE)[8:]
+    one = pltpu.roll(block, 1, 0)[8:]
+    two = pltpu.roll(block, 2, 0)[8:]
+    return weights[0] * block[8:] + weights[1] * one + weights[2] * two
 
 
 def taps_of(weights, feature, lanes):
@@ -115,37 +136,43 @@
     rate_copy.wait()
     mode_rate = per_channel(rate_ref[...])
     mode_rate_ref[...] = mode_rate
-    left = (rows - 1 - index_of((1, rows), 1)).astype(F32)
-    left = jnp.where(left > rows - 2.5, 1e30, left)
+    eye = own_mode(BF16)
+    token = index_of((2 * LANES, rows), 1)
+    left = jnp.where(token < 2, -1e30, (token - (rows - 1)).astype(F32)).astype(BF16)
     for tile in range(width // LANES):
-        rate = mode_column(mode_row(mode_rate[:, lanes_of(tile)]))
-        rate = jnp.concatenate([rate] * (rows // LANES), axis=1)
-        ending_ref[tile // 2, lanes_of(tile % 2), :] = jnp.exp(-rate * left).astype(BF16)
+        high, low = split(mode_rate[:, lanes_of(tile)])
+        diagonal = jnp.concatenate([spread(high, eye), spread(low, eye)], axis=1)
+        exponent = jnp.dot(diagonal, left, preferred_element_type=F32)
+        ending_ref[tile // 2, lanes_of(tile % 2), :] = jnp.exp(exponent).astype(BF16)
     weight_copy.wait()
     weights = short_ref[...].astype(F32)
     weight_ref[...] = weights
     mask = group_mask(F32)
 
-    def leave_state(tile, product):
-        every = jnp.dot(ending_ref[tile], product, preferred_element_type=F32)
+    def leave_state(tile):
+        every = jnp.dot(ending_ref[tile], product_ref[:, lanes_of(tile, WIDE)], preferred_element_type=F32)
         for half in range(WIDE // LANES):
             own = every[lanes_of(half), lanes_of(half)].reshape(GROUPS, MODES, LANES)
             state_ref[:, lanes_of((WIDE // LANES) * tile + half)] = jnp.sum(own * mask, axis=0)
 
-    previous = None
-    for tile in range(wides):
-        here = lanes_of(tile, WIDE)
-        copies[tile].wait()
-        if previous is not None:
-            leave_state(tile - 1, previous)
-        parts = []
-        for c in (0, 1):
-            block = buffer_ref[c, :, here].astype(F32)
-            head_ref[c, :, here] = block[:8]
-            parts.append(short_conv(block, None, taps_of(weights, c + 1, here)))
-        previous = (parts[0] * parts[1]).astype(BF16)
-        product_ref[:, here] = previous
-    leave_state(wides - 1, previous)
+    for wide in range(wides):
+        copies[wide].wait()
+        if wide > 0:
+            leave_state(wide - 1)
+        for tile in range(wide * (WIDE // LANES), (wide + 1) * (WIDE // LANES)):
+            here = lanes_of(tile)
+            for c in (0, 1):
+                head_ref[c, :, here] = buffer_ref[c, 0:16, here].astype(F32)[:8]
+            for start in range(0, rows, PIECE):
+                parts = []
+                for c in (0, 1):
+
+                    def load(first, last):
+                        return buffer_ref[c, first:last, here].astype(F32)
+
+                    parts.append(conv_piece(load, start, None, taps_of(weights, c + 1, here)))
+                product_ref[start : start + PIECE, here] = (parts[0] * parts[1]).astype(BF16)
+    leave_state(wides - 1)
 
 
 def halo(before_ref, place_ref):
@@ -161,11 +188,6 @@
     rate = mode_rate_ref[...]
     early = jnp.exp(-float(rows - 1) * rate) * first[0:1] + jnp.exp(-float(rows - 2) * rate) * first[1:2]
     full_ref[...] = (state_ref[...] + early).astype(BF16)
-
-
-def split(x):
-    high = x.astype(BF16)
-    return high, (x - high.astype(F32)).astype(BF16)
 
 
 def prepare_kernel(
@@ -197,23 +219,30 @@
     residue = per_channel(residue_ref[...])
     wide = GROUPS * CHUNK
     step = index_of((CHUNK, LANES), 0).astype(F32)
-    source = (index_of((LANES, wide), 1) & (CHUNK - 1)).astype(F32)
-    own = index_of((LANES, wide), 0) // MODES == index_of((LANES, wide), 1) // CHUNK
     causal = (index_of((CHUNK, wide), 1) & (CHUNK - 1)) <= index_of((CHUNK, wide), 0)
+    eye = own_mode(BF16)
+    flat_eye = jnp.where((index_of((MODES, LANES), 1) & (MODES - 1)) == index_of((MODES, LANES), 0), 1.0, 0.0)
+    flat_eye = flat_eye.astype(BF16)
+    shape = (2 * LANES, wide)
+    source = (index_of(shape, 1) & (CHUNK - 1)).astype(F32)
+    own = (index_of(shape, 0) & (LANES - 1)) // MODES == index_of(shape, 1) // CHUNK
+    risen = jnp.where(own, source, -1e30).astype(BF16)
+    left = jnp.where(own, source - (CHUNK - 1), 0.0).astype(BF16)
     for tile in range(width // LANES):
         here = lanes_of(tile)
-        rate_row = mode_row(mode_rate_ref[:, here])
-        rate = mode_column(rate_row)
-        rate = jnp.concatenate([rate] * (wide // LANES), axis=1)
+        rate = mode_rate_ref[:, here]
+        high, low = split(rate)
+        diagonal = jnp.concatenate([spread(high, eye), spread(low, eye)], axis=1)
+        rising = jnp.exp(jnp.dot(diagonal, risen, preferred_element_type=F32))
+        each = jnp.concatenate([high * flat_eye, low * flat_eye], axis=1)
+        ending = jnp.exp(jnp.dot(each, left, preferred_element_type=F32))
+        rate_row = mode_row(rate)
         falling = mode_row(residue[:, here]) * jnp.exp(-rate_row * step)
-        rising = jnp.where(own, jnp.exp(rate * source), 0.0)
         fall_high, fall_low = split(falling)
         rise_high, rise_low = split(rising)
         taps = jnp.dot(jnp.concatenate([fall_high, fall_low], axis=0), rise_high, preferred_element_type=F32)
         taps = taps[:CHUNK] + taps[CHUNK:] + jnp.dot(fall_high, rise_low, preferred_element_type=F32)
         taps = jnp.where(causal, taps, 0.0)
-        ending = rising * jnp.exp(-float(CHUNK - 1) * rate)
-        ending = jnp.sum(ending.reshape(GROUPS, MODES, wide), axis=0)
         inner_ref[tile] = jnp.concatenate([taps.astype(BF16), ending.astype(BF16)], axis=0)
         half = tile % (WIDE // LANES)
         for chunk in range(rows // CHUNK):
@@ -225,9 +254,14 @@
     copies[1].wait()
     for tile in range(width // LANES):
         here = lanes_of(tile)
-        gate_ref[:, here] = short_conv(
-            query_ref[:, here].astype(F32), before[0, :, here], taps_of(weight_ref, 0, here)
-        )
+
+        def load(first, last):
+            return query_ref[first:last, here].astype(F32)
+
+        for start in range(0, rows, PIECE):
+            gate_ref[start : start + PIECE, here] = conv_piece(
+                load, start, before[0, :, here], taps_of(weight_ref, 0, here)
+            )
     copies[2].wait()
 
 
@@ -280,6 +314,7 @@
 
 def join_kernel(tokens, radix, stride, place_ref, own_ref, mode_rate_ref, entry_ref, *refs):
     others, (found_ref, group_ref) = refs[: radix - 1], refs[radix - 1 :]
+    own = own_ref[0] if len(own_ref.shape) == 3 else own_ref[...]
     rate = mode_rate_ref[...]
     run = lax.rem(place_ref[0] // stride, radix)
     step = float(tokens * stride)
@@ -288,19 +323,30 @@
         return jnp.exp(-step * runs.astype(F32) * rate) * value
 
     found = jnp.zeros_like(rate)
-    total = decayed(own_ref[...].astype(F32), radix - 1 - run)
+    total = decayed(own.astype(F32), radix - 1 - run)
     for k, ref in enumerate(others, 1):
-        other = ref[...].astype(F32)
+        other = ref[...].reshape(rate.shape).astype(F32)
         found = found + jnp.where(run >= k, decayed(other, jnp.full((), k - 1, jnp.int32)), 0.0)
         source = lax.rem(run - k + radix, radix)
         total = total + decayed(other, radix - 1 - source)
     within = lax.rem(place_ref[0], stride).astype(F32) * float(tokens)
     found_ref[...] = entry_ref[...] + jnp.exp(-within * rate) * found
-    group_ref[...] = total.astype(BF16)
-
-
-def carry_kernel(stride, received, place_ref, base_ref, gate_ref, carry_ref, mode_rate_ref, inner_entry_ref, *refs):
-    entry_refs, (summed_ref, squares_ref) = refs[:received], refs[received:]
+    for copy in range(group_ref.shape[0]):
+        group_ref[copy] = total.astype(BF16)
+
+
+def carry_kernel(
+    stride,
+    place_ref,
+    base_ref,
+    gate_ref,
+    carry_ref,
+    mode_rate_ref,
+    inner_entry_ref,
+    received_ref,
+    summed_ref,
+    squares_ref,
+):
     rows, width = base_ref.shape
     run = place_ref[0] // stride
     within = lax.rem(place_ref[0], stride).astype(F32) * float(rows)
@@ -312,8 +358,8 @@
         rate = mode_rate_ref[:, here]
         decay = jnp.exp(-float(rows * stride) * rate)
         outer = jnp.zeros_like(rate)
-        for k in range(received, 0, -1):
-            outer = decay * outer + jnp.where(run >= k, entry_refs[k - 1][:, here].astype(F32), 0.0)
+        for k in range(received_ref.shape[0] - 1):
+            outer = jnp.where(k < run, decay * outer + received_ref[k, :, here].astype(F32), outer)
         entry = (inner_entry_ref[:, here] + jnp.exp(-within * rate) * outer).astype(BF16)
         left, right = spread(entry[:, :LANES], mask), spread(entry[:, LANES:], mask)
         both = jnp.concatenate(
@@ -331,7 +377,8 @@
         precision=lax.Precision.HIGHEST,
         preferred_element_type=F32,
     )
-    squares_ref[...] = squares[0:1]
+    for copy in range(squares_ref.shape[0]):
+        squares_ref[copy] = squares[0:1]
 
 
 def write_kernel(summed_ref, out_hbm, rounded_ref, sems):
@@ -347,14 +394,13 @@
         copy.wait()
 
 
-def norm_kernel(full_width, parts, summed_ref, gain_ref, *refs):
-    squares_refs, (out_hbm, rounded_ref, sems) = refs[:parts], refs[parts:]
+def norm_kernel(full_width, summed_ref, gain_ref, squares_ref, out_hbm, rounded_ref, sems):
     rows, width = summed_ref.shape
-    squares = squares_refs[0][...]
-    for ref in squares_refs[1:]:
-        squares = squares + ref[...]
+    squares = squares_ref[0]
+    for part in range(1, squares_ref.shape[0]):
+        squares = squares + squares_ref[part]
     scale_row = lax.rsqrt(squares / full_width + 1e-05)
-    scale = jnp.concatenate([mode_column(scale_row[:, lanes_of(k)]) for k in range(rows // LANES)], axis=0)
+    scale = jnp.concatenate([as_column(scale_row[:, lanes_of(k)]) for k in range(rows // LANES)], axis=0)
     copies = []
     for tile in range(width // WIDE):
         for half in range(WIDE // LANES):
@@ -479,16 +525,20 @@
         others = [lax.ppermute(group, "ctx", cycle) for cycle in cycles]
         if level == 0:
             others[0], inner = lax.optimization_barrier((others[0], inner))
+        copies = levels[-1] if level == len(levels) - 2 else 1
         entry, group = pl.pallas_call(
             lambda *refs, radix=radix, stride=stride: join_kernel(rows, radix, stride, *refs),
             in_specs=[smem_spec] + [vmem_spec] * (2 + radix),
-            out_shape=[f32(MODES, width), bf16(MODES, width)],
+            out_shape=[f32(MODES, width), bf16(copies, MODES, width)],
             compiler_params=params(),
             cost_estimate=cost(0.2),
             name="join",
         )(place, group, mode_rate, entry, *others)
         stride = size
-    received = [lax.ppermute(group, "ctx", ring(peers, stride * k)) for k in range(1, levels[-1])]
+    if len(levels) == 1:
+        group = jnp.broadcast_to(group[None], (levels[0], MODES, width))
+    runs = [[first + stride * k for k in range(levels[-1])] for first in range(stride)]
+    received = lax.all_to_all(group, "ctx", 0, 0, axis_index_groups=runs, tiled=True)
 
     base = pl.pallas_call(
         local_kernel,
@@ -498,17 +548,17 @@
         name="local_conv",
     )(gate, residual_here, product, first, mode_rate, inner, entering, skip[None])
 
+    count = lax.axis_size("fsdp")
     summed, squares = pl.pallas_call(
-        lambda *refs: carry_kernel(stride, len(received), *refs),
-        in_specs=[smem_spec] + [vmem_spec] * (5 + len(received)),
-        out_shape=[f32(rows, width), f32(1, rows)],
+        lambda *refs: carry_kernel(stride, *refs),
+        in_specs=[smem_spec] + [vmem_spec] * 6,
+        out_shape=[f32(rows, width), f32(count, 1, rows)],
         compiler_params=params(),
         cost_estimate=cost(1),
         name="add_carry",
-    )(place, base, gate, carry_table, mode_rate, entry, *received)
-
-    count = lax.axis_size("fsdp")
-    parts = [lax.ppermute(squares, "fsdp", ring(count, k)) for k in range(1, count)]
+    )(place, base, gate, carry_table, mode_rate, entry, received)
+
+    squares = lax.all_to_all(squares, "fsdp", 0, 0, tiled=True)
 
     def write(kernel, operands, name):
         return pl.pallas_call(
@@ -523,7 +573,7 @@
 
     new_residual = write(write_kernel, (summed,), "new_residual")
     normed = write(
-        lambda *refs: norm_kernel(full_width, count, *refs), (summed, gain[None], squares, *parts), "normed"
+        lambda *refs: norm_kernel(full_width, *refs), (summed, gain[None], squares), "normed"
     )
     return (new_residual, normed)
 

time: 30.5 us -> 48.4 us (1.59)
  local copies, waits for them, and re-layouts: 0.94 us -> 16.9 us
  waiting for transfers between devices: 0.25 us -> 2.71 us
  starting transfers between devices: 13.2 us -> 11.8 us
  Pallas kernels: 15.1 us -> 15.6 us
    unnamed x4 -> x38, local copies, waits for them, and re-layouts: 0.01 us -> 16 us
    ppermute x6 -> x0, starting transfers between devices: 8.58 us -> none  [the longest x3 5.57 us: per_device(): lax.ppermute(group, 'ctx', ring(peers, stride * k))]
    all_to_all x0 -> x2, starting transfers between devices: none -> 7.24 us  [the longest x1 3.86 us: per_device(): lax.all_to_all(group, 'ctx', 0, 0, axis_index_groups=runs, tiled=True)]
    all_to_all x0 -> x2, waiting for transfers between devices: none -> 2.7 us  [the longest x1 2.7 us: per_device(): squares = lax.all_to_all(squares, 'fsdp', 0, 0, tiled=True)]
    pallas_call x1, Pallas kernels: 0.86 us -> 1.4 us  [per_device(): pl.pallas_call(lambda *refs: carry_kernel(stride, *refs), in_specs=[smem_...]
  transfers between devices with their start and end apart: 8 -> 4, of which waited for: 1 -> 1; matrix products, arithmetic and copies ran while one was open for 0% -> 0% of each run, Pallas kernels for 42% -> 27%
where the time goes in v2:
time: 48.4 us; the launch traced here: 47.8 us
  local copies, waits for them, and re-layouts  16.9 us (35%)
  Pallas kernels  15.6 us (32%)
  starting transfers between devices  11.8 us (24%)
  waiting for transfers between devices  2.71 us (6%)
  between operations  0.76 us (2%)
    unnamed x38, local copies, waits for them, and re-layouts  16 us
    pallas_call x1, Pallas kernels, per_device(): pl.pallas_call(state_kernel, in_specs=[hbm_spec] * 3, out_shape=[bf16(row...  5.03 us
    all_to_all x1, starting transfers between devices, per_device(): lax.all_to_all(group, 'ctx', 0, 0, axis_index_groups=runs, tiled=True)  3.86 us
    pallas_call x1, Pallas kernels, per_device(): pl.pallas_call(local_kernel, out_shape=f32(rows, width), compiler_params=...  3.8 us
    all_to_all x1, starting transfers between devices, per_device(): squares = lax.all_to_all(squares, 'fsdp', 0, 0, tiled=True)  3.38 us
    ppermute x1, starting transfers between devices, per_device(): lax.ppermute(projected[:, rows - (taps - 1):, :], 'ctx', ring(peers, 1))  2.99 us
    pallas_call x1, Pallas kernels, per_device(): pl.pallas_call(prepare_kernel, in_specs=[smem_spec] + [hbm_spec] * 3 + [v...  2.83 us
    all_to_all x1, waiting for transfers between devices, per_device(): squares = lax.all_to_all(squares, 'fsdp', 0, 0, tiled=True)  2.7 us
  transfers between devices with their start and end apart: 4, of which 1 were waited for; matrix products, arithmetic and copies ran while one was open for 0% of the time, Pallas kernels for 27%

profile of v2, /device:TPU:0, one launch (start us, length us, event | category | flops | bytes accessed | tf_op | source)
XLA Modules:
  0.0 47.8 jit_solution(9468887791894936955)
XLA Ops:
  0.6 0.9 %slice.3 = bf16[3,2,2048]{2,1,0:T(2,128)(2,1)S(1)} slice(bf16[3,256,2048]{2,1,0:T(8,128)(2,1)} %projected_ref.3), slice={[0:3], [254:256], [0:2048]} | slice | bytes 49152 | tf_op jit(solution)/shard_map/slice | solution.py:462
  1.6 3.0 %collective-permute-start = (bf16[3,2,2048]{2,1,0:T(2,128)(2,1)S(1)}, bf16[3,2,2048]{2,1,0:T(2,128)(2,1)S(1)}, u32[]{:S(2)}, u32[]{:S(2)}) collective-permute-start(bf16[3,2,2048]{2,1,0:T(2,128)(2,1)S(1)} %slice.3), channel_id=1, source_target_pairs={{0,4},{4,8},{8,12},{12,16},{16,20},{20,24},{24,28},{28,0},{1,5},{5... | collective-permute-start | bytes 73736 | tf_op jit(solution)/shard_map/ppermute | solution.py:462
  4.5 5.0 %block_state.1 = (bf16[256,2048]{1,0:T(8,128)(2,1)S(1)}, f32[16,2048]{1,0:T(8,128)S(1)}, f32[16,2048]{1,0:T(8,128)S(1)}, f32[2,8,2048]{2,1,0:T(8,128)S(1)}, f32[3,3,2048]{2,1,0:T(4,128)S(1)}) custom-call(bf16[3,256,2048]{2,1,0:T(8,128)(2,1)} %projected_ref.3, bf16[3,3,2048]{2,1,0:T(4,128)(2,1)} %weight_hbm.1, f32[16,128]{1,0:T(8,128)} %bitcast.7), custom_call_target="tpu_custom_call" | custom-call | bytes 9000000 | tf_op jit(solution)/shard_map/block_state/pallas_call | solution.py:464
  9.6 0.0 collective-permute-done.before_ref.refs_1_
  9.6 0.1 head_tokens.1
  9.7 0.0 copy-start.15
  9.7 0.6 %copy-done.15 = f32[8,2048]{1,0:T(8,128)} copy-done((f32[8,2048]{1,0:T(8,128)}, f32[8,2048]{1,0:T(8,128)S(1)}, u32[]{:S(2)}) %copy-start.15) | copy-done | bytes 65560
  10.4 1.5 %collective-permute-start.1 = (bf16[16,2048]{1,0:T(8,128)(2,1)S(1)}, bf16[16,2048]{1,0:T(8,128)(2,1)S(1)}, u32[]{:S(2)}, u32[]{:S(2)}) collective-permute-start(bf16[16,2048]{1,0:T(8,128)(2,1)S(1)} %get-tuple-element.28.refs_1_), channel_id=1, source_target_pairs={{0,4},{4,0},{8,12},{12,8},{16,20},{20,16},{24,28},{28,24},{1,5},{5... | collective-permute-start | bytes 196616 | tf_op jit(solution)/shard_map/ppermute | solution.py:525
  11.9 0.0 copy-start.17
  11.9 2.8 %prepare.1 = (bf16[16,48,256]{2,1,0:T(8,128)(2,1)S(1)}, bf16[16,32,128]{2,1,0:T(8,128)(2,1)S(1)}, bf16[8,256,256]{2,1,0:T(8,128)(2,1)S(1)}, f32[256,2048]{1,0:T(8,128)S(1)}, bf16[256,2048]{1,0:T(8,128)(2,1)S(1)}) custom-call(s32[1]{0:T(128)} %bitcast.place_ref.refs_0_, bf16[3,256,2048]{2,1,0:T(8,128)(2,1)} %projected_ref.3, bf16[256,2048]{1,0:T(8,128)(2,1)} %residual_hbm.1, ...), custom_call_target="tpu_custom_call" | custom-call | bytes 6000000 | tf_op jit(solution)/shard_map/prepare/pallas_call | solution.py:496
  14.7 0.0 copy-start.4
  14.8 1.0 %copy-done.4 = bf16[8,256,256]{2,1,0:T(8,128)(2,1)} copy-done((bf16[8,256,256]{2,1,0:T(8,128)(2,1)}, bf16[8,256,256]{2,1,0:T(8,128)(2,1)S(1)}, u32[]{:S(2)}) %copy-start.4) | copy-done | bytes 1048600
  15.7 0.0 copy-start.6
  15.7 1.0 %copy-done.6 = bf16[256,2048]{1,0:T(8,128)(2,1)} copy-done((bf16[256,2048]{1,0:T(8,128)(2,1)}, bf16[256,2048]{1,0:T(8,128)(2,1)S(1)}, u32[]{:S(2)}) %copy-start.6) | copy-done | bytes 1048600
  16.7 0.0 copy-start.8
  16.7 0.7 %copy-done.8 = bf16[16,48,256]{2,1,0:T(8,128)(2,1)} copy-done((bf16[16,48,256]{2,1,0:T(8,128)(2,1)}, bf16[16,48,256]{2,1,0:T(8,128)(2,1)S(1)}, u32[]{:S(2)}) %copy-start.8) | copy-done | bytes 393240
  17.4 0.0 copy-start.13
  17.4 0.7 %copy-done.13 = bf16[16,32,128]{2,1,0:T(8,128)(2,1)} copy-done((bf16[16,32,128]{2,1,0:T(8,128)(2,1)}, bf16[16,32,128]{2,1,0:T(8,128)(2,1)S(1)}, u32[]{:S(2)}) %copy-start.13) | copy-done | bytes 131096
  18.1 0.0 copy-start
  18.1 0.0 collective-permute-done.1.refs_4_
  18.1 0.1 join.1
  18.2 0.0 copy-start.10
  18.2 0.8 %copy-done.10 = bf16[4,16,2048]{2,1,0:T(8,128)(2,1)} copy-done((bf16[4,16,2048]{2,1,0:T(8,128)(2,1)}, bf16[4,16,2048]{2,1,0:T(8,128)(2,1)S(1)}, u32[]{:S(2)}) %copy-start.10) | copy-done | bytes 262168
  19.0 0.0 copy-start.11
  19.0 0.6 %copy-done.11 = f32[16,2048]{1,0:T(8,128)} copy-done((f32[16,2048]{1,0:T(8,128)}, f32[16,2048]{1,0:T(8,128)S(1)}, u32[]{:S(2)}) %copy-start.11) | copy-done | bytes 131096
  19.7 3.9 %all-to-all-start = ((bf16[4,16,2048]{2,1,0:T(8,128)(2,1)}), bf16[4,16,2048]{2,1,0:T(8,128)(2,1)S(1)}, u32[]{:S(2)}, u32[]{:S(2)}) async-start(bf16[4,16,2048]{2,1,0:T(8,128)(2,1)} %copy-done.10), calls=%async_computation | async-start | bytes 524288 | tf_op jit(solution)/shard_map/all_to_all | solution.py:541
  23.5 0.0 copy-done.17
  23.5 0.0 copy-start.7
  23.6 1.2 %copy-done.7 = bf16[256,2048]{1,0:T(8,128)(2,1)S(1)} copy-done((bf16[256,2048]{1,0:T(8,128)(2,1)S(1)}, bf16[256,2048]{1,0:T(8,128)(2,1)}, u32[]{:S(2)}) %copy-start.7) | copy-done | bytes 1048600
  24.8 0.0 copy-start.9
  24.8 1.0 %copy-done.9 = bf16[16,48,256]{2,1,0:T(8,128)(2,1)S(1)} copy-done((bf16[16,48,256]{2,1,0:T(8,128)(2,1)S(1)}, bf16[16,48,256]{2,1,0:T(8,128)(2,1)}, u32[]{:S(2)}) %copy-start.9) | copy-done | bytes 393240
  25.8 0.9 %copy-done.14 = bf16[16,32,128]{2,1,0:T(8,128)(2,1)S(1)} copy-done((bf16[16,32,128]{2,1,0:T(8,128)(2,1)S(1)}, bf16[16,32,128]{2,1,0:T(8,128)(2,1)}, u32[]{:S(2)}) %copy-start.14) | copy-done | bytes 131096
  26.7 0.8 %copy-done.16 = f32[8,2048]{1,0:T(8,128)S(1)} copy-done((f32[8,2048]{1,0:T(8,128)S(1)}, f32[8,2048]{1,0:T(8,128)}, u32[]{:S(2)}) %copy-start.16) | copy-done | bytes 65560
  27.5 3.8 %local_conv.1.refs_1_ = f32[256,2048]{1,0:T(8,128)S(1)} custom-call(f32[256,2048]{1,0:T(8,128)S(1)} %get-tuple-element.22.gate_ref.refs_2_, bf16[256,2048]{1,0:T(8,128)(2,1)S(1)} %copy-done.7, bf16[256,2048]{1,0:T(8,128)(2,1)S(1)} %get-tuple-element.24.product_ref, f32[8,2048]{1,0:T(8,128)S(1)} %copy-done.16, ...), custom_call_target="tpu_custom_call" | custom-call | bytes 15000000 | tf_op jit(solution)/shard_map/local_conv/pallas_call | solution.py:543
  31.3 0.0 copy-done
  31.3 0.0 copy-start.2
  31.3 1.3 %copy-done.2 = f32[256,2048]{1,0:T(8,128)} copy-done((f32[256,2048]{1,0:T(8,128)}, f32[256,2048]{1,0:T(8,128)S(1)}, u32[]{:S(2)}) %copy-start.2) | copy-done | bytes 2097176
  32.6 0.0 all-to-all-done.refs_6_
  32.6 1.6 %copy-done.1 = f32[256,2048]{1,0:T(8,128)S(1)} copy-done((f32[256,2048]{1,0:T(8,128)S(1)}, f32[256,2048]{1,0:T(8,128)}, u32[]{:S(2)}) %copy-start.1) | copy-done | bytes 2097176
  34.2 1.6 %copy-done.3 = f32[256,2048]{1,0:T(8,128)S(1)} copy-done((f32[256,2048]{1,0:T(8,128)S(1)}, f32[256,2048]{1,0:T(8,128)}, u32[]{:S(2)}) %copy-start.3) | copy-done | bytes 2097176
  35.8 1.2 %copy-done.5 = bf16[8,256,256]{2,1,0:T(8,128)(2,1)S(1)} copy-done((bf16[8,256,256]{2,1,0:T(8,128)(2,1)S(1)}, bf16[8,256,256]{2,1,0:T(8,128)(2,1)}, u32[]{:S(2)}) %copy-start.5) | copy-done | bytes 1048600
  37.1 0.9 %copy-done.12 = f32[16,2048]{1,0:T(8,128)S(1)} copy-done((f32[16,2048]{1,0:T(8,128)S(1)}, f32[16,2048]{1,0:T(8,128)}, u32[]{:S(2)}) %copy-start.12) | copy-done | bytes 131096
  38.0 1.4 %add_carry.1 = (f32[256,2048]{1,0:T(8,128)S(1)}, f32[4,1,256]{2,1,0:T(1,128)}) custom-call(s32[1]{0:T(128)} %bitcast.place_ref.refs_0_, f32[256,2048]{1,0:T(8,128)S(1)} %copy-done.3, f32[256,2048]{1,0:T(8,128)S(1)} %copy-done.1, bf16[8,256,256]{2,1,0:T(8,128)(2,1)S(1)} %copy-done.5, f32[16,2048]{1,0:T(8,128)S(1)} %get-tuple-element.21.mode_rate_ref.refs_5_.refs_2_.refs_4_, ...), custom_call_target="tpu_custom_call" | custom-call | bytes 3000000 | tf_op jit(solution)/shard_map/add_carry/pallas_call | solution.py:552
  39.4 3.4 %all-to-all-start.1 = ((f32[4,1,256]{2,1,0:T(1,128)}), f32[4,1,256]{2,1,0:T(1,128)S(1)}, u32[]{:S(2)}, u32[]{:S(2)}) async-start(f32[4,1,256]{2,1,0:T(1,128)} %get-tuple-element.37), calls=%async_computation.1 | async-start | bytes 8192 | tf_op jit(solution)/shard_map/all_to_all | solution.py:561
  42.7 1.0 %new_residual.1 = bf16[256,2048]{1,0:T(8,128)(2,1)} custom-call(f32[256,2048]{1,0:T(8,128)S(1)} %get-tuple-element.36.summed_ref.refs_0_), custom_call_target="tpu_custom_call" | custom-call | bytes 3000000 | tf_op jit(solution)/shard_map/new_residual/pallas_call | solution.py:564
  43.8 2.7 %all-to-all-done.1.refs_2_ = f32[4,1,256]{2,1,0:T(1,128)S(1)} async-done(((f32[4,1,256]{2,1,0:T(1,128)}), f32[4,1,256]{2,1,0:T(1,128)S(1)}, u32[]{:S(2)}, u32[]{:S(2)}) %all-to-all-start.1) | async-done | bytes 4128 | tf_op jit(solution)/shard_map/all_to_all | solution.py:561
  46.5 0.0 copy-done.18
  46.5 1.3 %normed.1 = bf16[256,2048]{1,0:T(8,128)(2,1)} custom-call(f32[256,2048]{1,0:T(8,128)S(1)} %get-tuple-element.36.summed_ref.refs_0_, f32[1,2048]{1,0:T(1,128)S(1)} %bitcast.6, f32[4,1,256]{2,1,0:T(1,128)S(1)} %all-to-all-done.1.refs_2_), custom_call_target="tpu_custom_call" | custom-call | bytes 3000000 | tf_op jit(solution)/shard_map/normed/pallas_call | solution.py:564
  (8 shorter events, 0.0 us)
Async XLA Ops:
  1.6 8.0 %collective-permute-start = (bf16[3,2,2048]{2,1,0:T(2,128)(2,1)S(1)}, bf16[3,2,2048]{2,1,0:T(2,128)(2,1)S(1)}, u32[]{:S(2)}, u32[]{:S(2)}) collective-permute-start(bf16[3,2,2048]{2,1,0:T(2,128)(2,1)S(1)} %slice.3), channel_id=1, source_target_pairs={{0,4},{4,8},{8,12},{12,16},{16,20},{20,24},{24,28},{28,0},{1,5},{5... | collective-permute-start | bytes 73736 | tf_op jit(solution)/shard_map/ppermute | solution.py:462
  9.7 0.6 %copy-start.15 = (f32[8,2048]{1,0:T(8,128)}, f32[8,2048]{1,0:T(8,128)S(1)}, u32[]{:S(2)}) copy-start(f32[8,2048]{1,0:T(8,128)S(1)} %get-tuple-element.27.first_ref) | copy-start | bytes 196612
  10.4 7.7 %collective-permute-start.1 = (bf16[16,2048]{1,0:T(8,128)(2,1)S(1)}, bf16[16,2048]{1,0:T(8,128)(2,1)S(1)}, u32[]{:S(2)}, u32[]{:S(2)}) collective-permute-start(bf16[16,2048]{1,0:T(8,128)(2,1)S(1)} %get-tuple-element.28.refs_1_), channel_id=1, source_target_pairs={{0,4},{4,0},{8,12},{12,8},{16,20},{20,16},{24,28},{28,24},{1,5},{5... | collective-permute-start | bytes 196616 | tf_op jit(solution)/shard_map/ppermute | solution.py:525
  11.9 11.6 %copy-start.17 = (f32[2048]{0:T(1024)S(1)}, f32[2048]{0:T(1024)}, u32[]{:S(2)}) copy-start(f32[2048]{0:T(1024)} %param.11) | copy-start | bytes 24580
  14.7 1.0 %copy-start.4 = (bf16[8,256,256]{2,1,0:T(8,128)(2,1)}, bf16[8,256,256]{2,1,0:T(8,128)(2,1)S(1)}, u32[]{:S(2)}) copy-start(bf16[8,256,256]{2,1,0:T(8,128)(2,1)S(1)} %get-tuple-element.32.refs_3_) | copy-start | bytes 3145732
  15.7 1.0 %copy-start.6 = (bf16[256,2048]{1,0:T(8,128)(2,1)}, bf16[256,2048]{1,0:T(8,128)(2,1)S(1)}, u32[]{:S(2)}) copy-start(bf16[256,2048]{1,0:T(8,128)(2,1)S(1)} %get-tuple-element.23.residual_ref) | copy-start | bytes 3145732
  16.7 0.7 %copy-start.8 = (bf16[16,48,256]{2,1,0:T(8,128)(2,1)}, bf16[16,48,256]{2,1,0:T(8,128)(2,1)S(1)}, u32[]{:S(2)}) copy-start(bf16[16,48,256]{2,1,0:T(8,128)(2,1)S(1)} %get-tuple-element.30.inner_ref) | copy-start | bytes 1179652
  17.4 0.7 %copy-start.13 = (bf16[16,32,128]{2,1,0:T(8,128)(2,1)}, bf16[16,32,128]{2,1,0:T(8,128)(2,1)S(1)}, u32[]{:S(2)}) copy-start(bf16[16,32,128]{2,1,0:T(8,128)(2,1)S(1)} %get-tuple-element.31.entering_ref) | copy-start | bytes 393220
  18.1 13.2 %copy-start = (f32[256,2048]{1,0:T(8,128)}, f32[256,2048]{1,0:T(8,128)S(1)}, u32[]{:S(2)}) copy-start(f32[256,2048]{1,0:T(8,128)S(1)} %get-tuple-element.22.gate_ref.refs_2_) | copy-start | bytes 6291460
  18.2 0.8 %copy-start.10 = (bf16[4,16,2048]{2,1,0:T(8,128)(2,1)}, bf16[4,16,2048]{2,1,0:T(8,128)(2,1)S(1)}, u32[]{:S(2)}) copy-start(bf16[4,16,2048]{2,1,0:T(8,128)(2,1)S(1)} %get-tuple-element.35) | copy-start | bytes 786436
  19.0 0.7 %copy-start.11 = (f32[16,2048]{1,0:T(8,128)}, f32[16,2048]{1,0:T(8,128)S(1)}, u32[]{:S(2)}) copy-start(f32[16,2048]{1,0:T(8,128)S(1)} %get-tuple-element.34.refs_5_) | copy-start | bytes 393220
  19.7 13.0 %all-to-all-start = ((bf16[4,16,2048]{2,1,0:T(8,128)(2,1)}), bf16[4,16,2048]{2,1,0:T(8,128)(2,1)S(1)}, u32[]{:S(2)}, u32[]{:S(2)}) async-start(bf16[4,16,2048]{2,1,0:T(8,128)(2,1)} %copy-done.10), calls=%async_computation | async-start | bytes 524288 | tf_op jit(solution)/shard_map/all_to_all | solution.py:541
  23.5 1.2 %copy-start.7 = (bf16[256,2048]{1,0:T(8,128)(2,1)S(1)}, bf16[256,2048]{1,0:T(8,128)(2,1)}, u32[]{:S(2)}) copy-start(bf16[256,2048]{1,0:T(8,128)(2,1)} %copy-done.6) | copy-start | bytes 3145732
  24.8 1.0 %copy-start.9 = (bf16[16,48,256]{2,1,0:T(8,128)(2,1)S(1)}, bf16[16,48,256]{2,1,0:T(8,128)(2,1)}, u32[]{:S(2)}) copy-start(bf16[16,48,256]{2,1,0:T(8,128)(2,1)} %copy-done.8) | copy-start | bytes 1179652
  25.8 0.9 %copy-start.14 = (bf16[16,32,128]{2,1,0:T(8,128)(2,1)S(1)}, bf16[16,32,128]{2,1,0:T(8,128)(2,1)}, u32[]{:S(2)}) copy-start(bf16[16,32,128]{2,1,0:T(8,128)(2,1)} %copy-done.13) | copy-start | bytes 393220
  26.7 0.8 %copy-start.16 = (f32[8,2048]{1,0:T(8,128)S(1)}, f32[8,2048]{1,0:T(8,128)}, u32[]{:S(2)}) copy-start(f32[8,2048]{1,0:T(8,128)} %copy-done.15) | copy-start | bytes 196612
  31.3 1.3 %copy-start.2 = (f32[256,2048]{1,0:T(8,128)}, f32[256,2048]{1,0:T(8,128)S(1)}, u32[]{:S(2)}) copy-start(f32[256,2048]{1,0:T(8,128)S(1)} %local_conv.1.refs_1_) | copy-start | bytes 6291460
  32.6 1.6 %copy-start.1 = (f32[256,2048]{1,0:T(8,128)S(1)}, f32[256,2048]{1,0:T(8,128)}, u32[]{:S(2)}) copy-start(f32[256,2048]{1,0:T(8,128)} %copy-done) | copy-start | bytes 6291460
  34.2 1.6 %copy-start.3 = (f32[256,2048]{1,0:T(8,128)S(1)}, f32[256,2048]{1,0:T(8,128)}, u32[]{:S(2)}) copy-start(f32[256,2048]{1,0:T(8,128)} %copy-done.2) | copy-start | bytes 6291460
  35.8 1.2 %copy-start.5 = (bf16[8,256,256]{2,1,0:T(8,128)(2,1)S(1)}, bf16[8,256,256]{2,1,0:T(8,128)(2,1)}, u32[]{:S(2)}) copy-start(bf16[8,256,256]{2,1,0:T(8,128)(2,1)} %copy-done.4) | copy-start | bytes 3145732
  37.0 0.9 %copy-start.12 = (f32[16,2048]{1,0:T(8,128)S(1)}, f32[16,2048]{1,0:T(8,128)}, u32[]{:S(2)}) copy-start(f32[16,2048]{1,0:T(8,128)} %copy-done.11) | copy-start | bytes 393220
  39.4 7.1 %copy-start.18 = (f32[2048]{0:T(1024)S(1)}, f32[2048]{0:T(1024)}, u32[]{:S(2)}) copy-start(f32[2048]{0:T(1024)} %param.13) | copy-start | bytes 24580
  39.4 7.1 %all-to-all-start.1 = ((f32[4,1,256]{2,1,0:T(1,128)}), f32[4,1,256]{2,1,0:T(1,128)S(1)}, u32[]{:S(2)}, u32[]{:S(2)}) async-start(f32[4,1,256]{2,1,0:T(1,128)} %get-tuple-element.37), calls=%async_computation.1 | async-start | bytes 8192 | tf_op jit(solution)/shard_map/all_to_all | solution.py:561

commit v3 on v2

--- a/solution.py
+++ b/solution.py
@@ -8,7 +8,6 @@
 CHANNELS_PER_GRP = 16
 MODES = 16
 CHUNK = 32
-PIECE = 64
 LANES = 128
 WIDE = 256
 GROUPS = LANES // CHANNELS_PER_GRP
@@ -91,13 +90,18 @@
     return weights[0] * block + weights[1] * one + weights[2] * two
 
 
-def conv_piece(load, start, before, weights):
-    if start == 0:
-        return short_conv(load(0, PIECE), before, weights)
-    block = load(start - 16, start + PIECE)[8:]
-    one = pltpu.roll(block, 1, 0)[8:]
-    two = pltpu.roll(block, 2, 0)[8:]
-    return weights[0] * block[8:] + weights[1] * one + weights[2] * two
+def shift_matrix(rows):
+    shape = (2 * rows, rows)
+    target = index_of(shape, 0)
+    source = index_of(shape, 1)
+    taken = jnp.where(target < rows, target - 1, target - (rows + 2))
+    return jnp.where(source == taken, 1.0, 0.0).astype(BF16)
+
+
+def wide_conv(block, shift, weights):
+    rows = block.shape[0]
+    earlier = jnp.dot(shift, block, preferred_element_type=F32)
+    return weights[0] * block.astype(F32) + weights[1] * earlier[:rows] + weights[2] * earlier[rows:]
 
 
 def taps_of(weights, feature, lanes):
@@ -115,6 +119,7 @@
     weight_ref,
     buffer_ref,
     ending_ref,
+    shift_ref,
     short_ref,
     rate_ref,
     sems,
@@ -133,6 +138,7 @@
             pltpu.make_async_copy(projected_ref.at[pl.ds(1, 2), :, here], buffer_ref.at[:, :, here], sems.at[tile])
         )
         copies[-1].start()
+    shift_ref[...] = shift_matrix(rows)
     rate_copy.wait()
     mode_rate = per_channel(rate_ref[...])
     mode_rate_ref[...] = mode_rate
@@ -159,19 +165,12 @@
         copies[wide].wait()
         if wide > 0:
             leave_state(wide - 1)
-        for tile in range(wide * (WIDE // LANES), (wide + 1) * (WIDE // LANES)):
-            here = lanes_of(tile)
-            for c in (0, 1):
-                head_ref[c, :, here] = buffer_ref[c, 0:16, here].astype(F32)[:8]
-            for start in range(0, rows, PIECE):
-                parts = []
-                for c in (0, 1):
-
-                    def load(first, last):
-                        return buffer_ref[c, first:last, here].astype(F32)
-
-                    parts.append(conv_piece(load, start, None, taps_of(weights, c + 1, here)))
-                product_ref[start : start + PIECE, here] = (parts[0] * parts[1]).astype(BF16)
+        here = lanes_of(wide, WIDE)
+        parts = []
+        for c in (0, 1):
+            head_ref[c, :, here] = buffer_ref[c, 0:16, here].astype(F32)[:8]
+            parts.append(wide_conv(buffer_ref[c, :, here], shift_ref[...], taps_of(weights, c + 1, here)))
+        product_ref[:, here] = (parts[0] * parts[1]).astype(BF16)
     leave_state(wides - 1)
 
 
@@ -204,6 +203,7 @@
     gate_ref,
     residual_ref,
     query_ref,
+    shift_ref,
     residue_ref,
     sems,
 ):
@@ -252,16 +252,13 @@
                 entering_ref[tile] = entering
     before = halo(before_ref, place_ref)
     copies[1].wait()
-    for tile in range(width // LANES):
-        here = lanes_of(tile)
-
-        def load(first, last):
-            return query_ref[first:last, here].astype(F32)
-
-        for start in range(0, rows, PIECE):
-            gate_ref[start : start + PIECE, here] = conv_piece(
-                load, start, before[0, :, here], taps_of(weight_ref, 0, here)
-            )
+    shift_ref[...] = shift_matrix(rows)
+    for tile in range(width // WIDE):
+        here = lanes_of(tile, WIDE)
+        weights = taps_of(weight_ref, 0, here)
+        gate_ref[:, here] = wide_conv(query_ref[:, here], shift_ref[...], weights)
+        head = query_ref[0:16, here].astype(F32)[:8]
+        gate_ref[0:8, here] = short_conv(head, before[0, :, here], weights)
     copies[2].wait()
 
 
@@ -314,7 +311,6 @@
 
 def join_kernel(tokens, radix, stride, place_ref, own_ref, mode_rate_ref, entry_ref, *refs):
     others, (found_ref, group_ref) = refs[: radix - 1], refs[radix - 1 :]
-    own = own_ref[0] if len(own_ref.shape) == 3 else own_ref[...]
     rate = mode_rate_ref[...]
     run = lax.rem(place_ref[0] // stride, radix)
     step = float(tokens * stride)
@@ -323,30 +319,19 @@
         return jnp.exp(-step * runs.astype(F32) * rate) * value
 
     found = jnp.zeros_like(rate)
-    total = decayed(own.astype(F32), radix - 1 - run)
+    total = decayed(own_ref[...].astype(F32), radix - 1 - run)
     for k, ref in enumerate(others, 1):
-        other = ref[...].reshape(rate.shape).astype(F32)
+        other = ref[...].astype(F32)
         found = found + jnp.where(run >= k, decayed(other, jnp.full((), k - 1, jnp.int32)), 0.0)
         source = lax.rem(run - k + radix, radix)
         total = total + decayed(other, radix - 1 - source)
     within = lax.rem(place_ref[0], stride).astype(F32) * float(tokens)
     found_ref[...] = entry_ref[...] + jnp.exp(-within * rate) * found
-    for copy in range(group_ref.shape[0]):
-        group_ref[copy] = total.astype(BF16)
-
-
-def carry_kernel(
-    stride,
-    place_ref,
-    base_ref,
-    gate_ref,
-    carry_ref,
-    mode_rate_ref,
-    inner_entry_ref,
-    received_ref,
-    summed_ref,
-    squares_ref,
-):
+    group_ref[...] = total.astype(BF16)
+
+
+def carry_kernel(stride, place_ref, base_ref, gate_ref, carry_ref, mode_rate_ref, inner_entry_ref, *refs):
+    entry_refs, (summed_ref, squares_ref) = refs[:-2], refs[-2:]
     rows, width = base_ref.shape
     run = place_ref[0] // stride
     within = lax.rem(place_ref[0], stride).astype(F32) * float(rows)
@@ -358,8 +343,8 @@
         rate = mode_rate_ref[:, here]
         decay = jnp.exp(-float(rows * stride) * rate)
         outer = jnp.zeros_like(rate)
-        for k in range(received_ref.shape[0] - 1):
-            outer = jnp.where(k < run, decay * outer + received_ref[k, :, here].astype(F32), outer)
+        for k in range(len(entry_refs), 0, -1):
+            outer = decay * outer + jnp.where(run >= k, entry_refs[k - 1][:, here].astype(F32), 0.0)
         entry = (inner_entry_ref[:, here] + jnp.exp(-within * rate) * outer).astype(BF16)
         left, right = spread(entry[:, :LANES], mask), spread(entry[:, LANES:], mask)
         both = jnp.concatenate(
@@ -377,8 +362,7 @@
         precision=lax.Precision.HIGHEST,
         preferred_element_type=F32,
     )
-    for copy in range(squares_ref.shape[0]):
-        squares_ref[copy] = squares[0:1]
+    squares_ref[...] = squares[0:1]
 
 
 def write_kernel(summed_ref, out_hbm, rounded_ref, sems):
@@ -394,11 +378,12 @@
         copy.wait()
 
 
-def norm_kernel(full_width, summed_ref, gain_ref, squares_ref, out_hbm, rounded_ref, sems):
+def norm_kernel(full_width, summed_ref, gain_ref, *refs):
+    squares_refs, (out_hbm, rounded_ref, sems) = refs[:-3], refs[-3:]
     rows, width = summed_ref.shape
-    squares = squares_ref[0]
-    for part in range(1, squares_ref.shape[0]):
-        squares = squares + squares_ref[part]
+    squares = squares_refs[0][...]
+    for ref in squares_refs[1:]:
+        squares = squares + ref[...]
     scale_row = lax.rsqrt(squares / full_width + 1e-05)
     scale = jnp.concatenate([as_column(scale_row[:, lanes_of(k)]) for k in range(rows // LANES)], axis=0)
     copies = []
@@ -474,6 +459,7 @@
         scratch_shapes=[
             pltpu.VMEM((2, rows, width), BF16),
             pltpu.VMEM((wides, WIDE, rows), BF16),
+            pltpu.VMEM((2 * rows, rows), BF16),
             pltpu.VMEM(short_weight.shape, BF16),
             pltpu.VMEM((MODES, rates.shape[0]), F32),
             pltpu.SemaphoreType.DMA((wides,)),
@@ -505,6 +491,7 @@
         ],
         scratch_shapes=[
             pltpu.VMEM((rows, width), BF16),
+            pltpu.VMEM((2 * rows, rows), BF16),
             pltpu.VMEM((MODES, rates.shape[0]), F32),
             pltpu.SemaphoreType.DMA((3,)),
         ],
@@ -525,20 +512,16 @@
         others = [lax.ppermute(group, "ctx", cycle) for cycle in cycles]
         if level == 0:
             others[0], inner = lax.optimization_barrier((others[0], inner))
-        copies = levels[-1] if level == len(levels) - 2 else 1
         entry, group = pl.pallas_call(
             lambda *refs, radix=radix, stride=stride: join_kernel(rows, radix, stride, *refs),
             in_specs=[smem_spec] + [vmem_spec] * (2 + radix),
-            out_shape=[f32(MODES, width), bf16(copies, MODES, width)],
+            out_shape=[f32(MODES, width), bf16(MODES, width)],
             compiler_params=params(),
             cost_estimate=cost(0.2),
             name="join",
         )(place, group, mode_rate, entry, *others)
         stride = size
-    if len(levels) == 1:
-        group = jnp.broadcast_to(group[None], (levels[0], MODES, width))
-    runs = [[first + stride * k for k in range(levels[-1])] for first in range(stride)]
-    received = lax.all_to_all(group, "ctx", 0, 0, axis_index_groups=runs, tiled=True)
+    received = [lax.ppermute(group, "ctx", ring(peers, stride * k)) for k in range(1, levels[-1])]
 
     base = pl.pallas_call(
         local_kernel,
@@ -551,14 +534,14 @@
     count = lax.axis_size("fsdp")
     summed, squares = pl.pallas_call(
         lambda *refs: carry_kernel(stride, *refs),
-        in_specs=[smem_spec] + [vmem_spec] * 6,
-        out_shape=[f32(rows, width), f32(count, 1, rows)],
+        in_specs=[smem_spec] + [vmem_spec] * (5 + len(received)),
+        out_shape=[f32(rows, width), f32(1, rows)],
         compiler_params=params(),
         cost_estimate=cost(1),
         name="add_carry",
-    )(place, base, gate, carry_table, mode_rate, entry, received)
-
-    squares = lax.all_to_all(squares, "fsdp", 0, 0, tiled=True)
+    )(place, base, gate, carry_table, mode_rate, entry, *received)
+
+    parts = [lax.ppermute(squares, "fsdp", ring(count, k)) for k in range(1, count)]
 
     def write(kernel, operands, name):
         return pl.pallas_call(
@@ -573,7 +556,7 @@
 
     new_residual = write(write_kernel, (summed,), "new_residual")
     normed = write(
-        lambda *refs: norm_kernel(full_width, *refs), (summed, gain[None], squares), "normed"
+        lambda *refs: norm_kernel(full_width, *refs), (summed, gain[None], squares, *parts), "normed"
     )
     return (new_residual, normed)
 

time: 48.4 us -> 30.7 us (0.63)
  local copies, waits for them, and re-layouts: 16.9 us -> 0.94 us
  waiting for transfers between devices: 2.71 us -> 0.25 us
  starting transfers between devices: 11.8 us -> 13.2 us
    unnamed x38 -> x4, local copies, waits for them, and re-layouts: 16 us -> 0.01 us
    ppermute x0 -> x6, starting transfers between devices: none -> 8.58 us  [the longest x3 5.57 us: per_device(): lax.ppermute(group, 'ctx', ring(peers, stride * k))]
    all_to_all x2 -> x0, starting transfers between devices: 7.24 us -> none  [the longest x1 3.86 us: per_device(): lax.all_to_all(group, 'ctx', 0, 0, axis_index_groups=runs, tiled=True)]
    all_to_all x2 -> x0, waiting for transfers between devices: 2.7 us -> none  [the longest x1 2.7 us: per_device(): squares = lax.all_to_all(squares, 'fsdp', 0, 0, tiled=True)]
    pallas_call x1, Pallas kernels: 1.4 us -> 0.86 us  [per_device(): pl.pallas_call(lambda *refs: carry_kernel(stride, *refs), in_specs=[smem_...]
  transfers between devices with their start and end apart: 4 -> 8, of which waited for: 1 -> 1; matrix products, arithmetic and copies ran while one was open for 0% -> 0% of each run, Pallas kernels for 27% -> 43%
where the time goes in v3:
time: 30.7 us; the launch traced here: 30.4 us
  Pallas kernels  15.3 us (50%)
  starting transfers between devices  13.2 us (43%)
  local copies, waits for them, and re-layouts  0.94 us (3%)
  between operations  0.75 us (2%)
    ppermute x3, starting transfers between devices, per_device(): lax.ppermute(group, 'ctx', ring(peers, stride * k))  5.57 us
    pallas_call x1, Pallas kernels, per_device(): pl.pallas_call(state_kernel, in_specs=[hbm_spec] * 3, out_shape=[bf16(row...  5.18 us
    pallas_call x1, Pallas kernels, per_device(): pl.pallas_call(local_kernel, out_shape=f32(rows, width), compiler_params=...  3.81 us
    ppermute x3, starting transfers between devices, per_device(): lax.ppermute(squares, 'fsdp', ring(count, k))  3.01 us
    ppermute x1, starting transfers between devices, per_device(): lax.ppermute(projected[:, rows - (taps - 1):, :], 'ctx', ring(peers, 1))  2.99 us
    pallas_call x1, Pallas kernels, per_device(): pl.pallas_call(prepare_kernel, in_specs=[smem_spec] + [hbm_spec] * 3 + [v...  2.91 us
    pallas_call x2, Pallas kernels, write(): pl.pallas_call(kernel, out_specs=hbm_spec, out_shape=bf16(rows, width), s...  2.32 us
    ppermute x1, starting transfers between devices, per_device(): others = [lax.ppermute(group, 'ctx', cycle) for cycle in cycles]  1.61 us
  transfers between devices with their start and end apart: 8, of which 1 were waited for; matrix products, arithmetic and copies ran while one was open for 0% of the time, Pallas kernels for 43%

profile of v3, /device:TPU:0, one launch (start us, length us, event | category | flops | bytes accessed | tf_op | source)
XLA Modules:
  0.0 30.4 jit_solution(5905527871123673529)
XLA Ops:
  0.6 0.9 %slice.3 = bf16[3,2,2048]{2,1,0:T(2,128)(2,1)S(1)} slice(bf16[3,256,2048]{2,1,0:T(8,128)(2,1)} %projected_ref.3), slice={[0:3], [254:256], [0:2048]} | slice | bytes 49152 | tf_op jit(solution)/shard_map/slice | solution.py:447
  1.6 3.0 %collective-permute-start = (bf16[3,2,2048]{2,1,0:T(2,128)(2,1)S(1)}, bf16[3,2,2048]{2,1,0:T(2,128)(2,1)S(1)}, u32[]{:S(2)}, u32[]{:S(2)}) collective-permute-start(bf16[3,2,2048]{2,1,0:T(2,128)(2,1)S(1)} %slice.3), channel_id=1, source_target_pairs={{0,4},{4,8},{8,12},{12,16},{16,20},{20,24},{24,28},{28,0},{1,5},{5... | collective-permute-start | bytes 73736 | tf_op jit(solution)/shard_map/ppermute | solution.py:447
  4.5 5.2 %block_state.1 = (bf16[256,2048]{1,0:T(8,128)(2,1)S(1)}, f32[16,2048]{1,0:T(8,128)S(1)}, f32[16,2048]{1,0:T(8,128)S(1)}, f32[2,8,2048]{2,1,0:T(8,128)S(1)}, f32[3,3,2048]{2,1,0:T(4,128)S(1)}) custom-call(bf16[3,256,2048]{2,1,0:T(8,128)(2,1)} %projected_ref.3, bf16[3,3,2048]{2,1,0:T(4,128)(2,1)} %weight_hbm.1, f32[16,128]{1,0:T(8,128)} %bitcast.7), custom_call_target="tpu_custom_call" | custom-call | bytes 9000000 | tf_op jit(solution)/shard_map/block_state/pallas_call | solution.py:449
  9.7 0.0 collective-permute-done.before_ref.refs_1_
  9.8 0.1 head_tokens.1
  9.9 1.6 %collective-permute-start.1 = (bf16[16,2048]{1,0:T(8,128)(2,1)S(1)}, bf16[16,2048]{1,0:T(8,128)(2,1)S(1)}, u32[]{:S(2)}, u32[]{:S(2)}) collective-permute-start(bf16[16,2048]{1,0:T(8,128)(2,1)S(1)} %get-tuple-element.28.refs_1_), channel_id=1, source_target_pairs={{0,4},{4,0},{8,12},{12,8},{16,20},{20,16},{24,28},{28,24},{1,5},{5... | collective-permute-start | bytes 196616 | tf_op jit(solution)/shard_map/ppermute | solution.py:512
  11.5 0.0 copy-start
  11.5 2.9 %prepare.1 = (bf16[16,48,256]{2,1,0:T(8,128)(2,1)S(1)}, bf16[16,32,128]{2,1,0:T(8,128)(2,1)S(1)}, bf16[8,256,256]{2,1,0:T(8,128)(2,1)S(1)}, f32[256,2048]{1,0:T(8,128)S(1)}, bf16[256,2048]{1,0:T(8,128)(2,1)S(1)}) custom-call(s32[1]{0:T(128)} %bitcast.place_ref.refs_0_, bf16[3,256,2048]{2,1,0:T(8,128)(2,1)} %projected_ref.3, bf16[256,2048]{1,0:T(8,128)(2,1)} %residual_hbm.1, ...), custom_call_target="tpu_custom_call" | custom-call | bytes 6000000 | tf_op jit(solution)/shard_map/prepare/pallas_call | solution.py:482
  14.4 0.0 collective-permute-done.1.refs_4_
  14.4 0.1 join.1
  14.6 1.6 %collective-permute-start.2 = (bf16[16,2048]{1,0:T(8,128)(2,1)S(1)}, bf16[16,2048]{1,0:T(8,128)(2,1)S(1)}, u32[]{:S(2)}, u32[]{:S(2)}) collective-permute-start(bf16[16,2048]{1,0:T(8,128)(2,1)S(1)} %get-tuple-element.35), channel_id=1, source_target_pairs={{0,8},{4,12},{8,16},{12,20},{16,24},{20,28},{24,0},{28,4},{1,9},{5... | collective-permute-start | bytes 196616 | tf_op jit(solution)/shard_map/ppermute | solution.py:524
  16.2 2.4 %collective-permute-start.3 = (bf16[16,2048]{1,0:T(8,128)(2,1)S(1)}, bf16[16,2048]{1,0:T(8,128)(2,1)S(1)}, u32[]{:S(2)}, u32[]{:S(2)}) collective-permute-start(bf16[16,2048]{1,0:T(8,128)(2,1)S(1)} %get-tuple-element.35), channel_id=1, source_target_pairs={{0,16},{4,20},{8,24},{12,28},{16,0},{20,4},{24,8},{28,12},{1,17},{... | collective-permute-start | bytes 196616 | tf_op jit(solution)/shard_map/ppermute | solution.py:524
  18.6 1.6 %collective-permute-start.4 = (bf16[16,2048]{1,0:T(8,128)(2,1)S(1)}, bf16[16,2048]{1,0:T(8,128)(2,1)S(1)}, u32[]{:S(2)}, u32[]{:S(2)}) collective-permute-start(bf16[16,2048]{1,0:T(8,128)(2,1)S(1)} %get-tuple-element.35), channel_id=1, source_target_pairs={{0,24},{4,28},{8,0},{12,4},{16,8},{20,12},{24,16},{28,20},{1,25},{... | collective-permute-start | bytes 196616 | tf_op jit(solution)/shard_map/ppermute | solution.py:524
  20.1 0.0 copy-done
  20.1 3.8 %local_conv.1.refs_1_ = f32[256,2048]{1,0:T(8,128)S(1)} custom-call(f32[256,2048]{1,0:T(8,128)S(1)} %get-tuple-element.22.gate_ref.refs_2_, bf16[256,2048]{1,0:T(8,128)(2,1)S(1)} %get-tuple-element.23.residual_ref, bf16[256,2048]{1,0:T(8,128)(2,1)S(1)} %get-tuple-element.24.product_ref, f32[8,2048]{1,0:T(8,128)S(1)} %get-tuple-element.27.first_ref, ...), custom_call_target="tpu_custom_call" | custom-call | bytes 15000000 | tf_op jit(solution)/shard_map/local_conv/pallas_call | solution.py:526
  23.9 0.0 collective-permute-done.2.refs_6_
  24.0 0.0 collective-permute-done.3.refs_7_
  24.0 0.0 collective-permute-done.4.refs_8_
  24.0 0.9 %add_carry.1 = (f32[256,2048]{1,0:T(8,128)S(1)}, f32[1,256]{1,0:T(1,128)S(1)}) custom-call(s32[1]{0:T(128)} %bitcast.place_ref.refs_0_, f32[256,2048]{1,0:T(8,128)S(1)} %local_conv.1.refs_1_, f32[256,2048]{1,0:T(8,128)S(1)} %get-tuple-element.22.gate_ref.refs_2_, bf16[8,256,256]{2,1,0:T(8,128)(2,1)S(1)} %get-tuple-element.32.refs_3_, ...), custom_call_target="tpu_custom_call" | custom-call | bytes 3000000 | tf_op jit(solution)/shard_map/add_carry/pallas_call | solution.py:535
  24.8 0.0 copy-start.1
  24.8 0.0 collective-permute-start.5
  24.9 1.6 %collective-permute-start.6 = (f32[1,256]{1,0:T(1,128)S(1)}, f32[1,256]{1,0:T(1,128)S(1)}, u32[]{:S(2)}, u32[]{:S(2)}) collective-permute-start(f32[1,256]{1,0:T(1,128)S(1)} %get-tuple-element.37.refs_2_), channel_id=1, source_target_pairs={{0,2},{1,3},{2,0},{3,1},{4,6},{5,7},{6,4},{7,5},{8,10},{9,11},{10,... | collective-permute-start | bytes 3080 | tf_op jit(solution)/shard_map/ppermute | solution.py:544
  26.4 1.4 %collective-permute-start.7 = (f32[1,256]{1,0:T(1,128)S(1)}, f32[1,256]{1,0:T(1,128)S(1)}, u32[]{:S(2)}, u32[]{:S(2)}) collective-permute-start(f32[1,256]{1,0:T(1,128)S(1)} %get-tuple-element.37.refs_2_), channel_id=1, source_target_pairs={{0,3},{1,0},{2,1},{3,2},{4,7},{5,4},{6,5},{7,6},{8,11},{9,8},{10,9... | collective-permute-start | bytes 3080 | tf_op jit(solution)/shard_map/ppermute | solution.py:544
  27.9 1.0 %new_residual.1 = bf16[256,2048]{1,0:T(8,128)(2,1)} custom-call(f32[256,2048]{1,0:T(8,128)S(1)} %get-tuple-element.36.summed_ref.refs_0_), custom_call_target="tpu_custom_call" | custom-call | bytes 3000000 | tf_op jit(solution)/shard_map/new_residual/pallas_call | solution.py:547
  28.9 0.0 collective-permute-done.5.refs_3_
  28.9 0.0 collective-permute-done.6.refs_4_
  28.9 0.2 collective-permute-done.7.refs_5_
  29.2 0.0 copy-done.1
  29.2 1.3 %normed.1 = bf16[256,2048]{1,0:T(8,128)(2,1)} custom-call(f32[256,2048]{1,0:T(8,128)S(1)} %get-tuple-element.36.summed_ref.refs_0_, f32[1,2048]{1,0:T(1,128)S(1)} %bitcast.6, f32[1,256]{1,0:T(1,128)S(1)} %get-tuple-element.37.refs_2_, f32[1,256]{1,0:T(1,128)S(1)} %collective-permute-done.5.refs_3_, f32[1,256]{1,0:T(1,128)S(1)} %collective-permute-done.6.refs_4_, ...), custom_call_target="tpu_custom_call" | custom-call | bytes 3000000 | tf_op jit(solution)/shard_map/normed/pallas_call | solution.py:547
  (1 shorter events, 0.0 us)
Async XLA Ops:
  1.6 8.2 %collective-permute-start = (bf16[3,2,2048]{2,1,0:T(2,128)(2,1)S(1)}, bf16[3,2,2048]{2,1,0:T(2,128)(2,1)S(1)}, u32[]{:S(2)}, u32[]{:S(2)}) collective-permute-start(bf16[3,2,2048]{2,1,0:T(2,128)(2,1)S(1)} %slice.3), channel_id=1, source_target_pairs={{0,4},{4,8},{8,12},{12,16},{16,20},{20,24},{24,28},{28,0},{1,5},{5... | collective-permute-start | bytes 73736 | tf_op jit(solution)/shard_map/ppermute | solution.py:447
  9.9 4.5 %collective-permute-start.1 = (bf16[16,2048]{1,0:T(8,128)(2,1)S(1)}, bf16[16,2048]{1,0:T(8,128)(2,1)S(1)}, u32[]{:S(2)}, u32[]{:S(2)}) collective-permute-start(bf16[16,2048]{1,0:T(8,128)(2,1)S(1)} %get-tuple-element.28.refs_1_), channel_id=1, source_target_pairs={{0,4},{4,0},{8,12},{12,8},{16,20},{20,16},{24,28},{28,24},{1,5},{5... | collective-permute-start | bytes 196616 | tf_op jit(solution)/shard_map/ppermute | solution.py:512
  11.5 8.6 %copy-start = (f32[2048]{0:T(1024)S(1)}, f32[2048]{0:T(1024)}, u32[]{:S(2)}) copy-start(f32[2048]{0:T(1024)} %param.11) | copy-start | bytes 24580
  14.6 9.4 %collective-permute-start.2 = (bf16[16,2048]{1,0:T(8,128)(2,1)S(1)}, bf16[16,2048]{1,0:T(8,128)(2,1)S(1)}, u32[]{:S(2)}, u32[]{:S(2)}) collective-permute-start(bf16[16,2048]{1,0:T(8,128)(2,1)S(1)} %get-tuple-element.35), channel_id=1, source_target_pairs={{0,8},{4,12},{8,16},{12,20},{16,24},{20,28},{24,0},{28,4},{1,9},{5... | collective-permute-start | bytes 196616 | tf_op jit(solution)/shard_map/ppermute | solution.py:524
  16.2 7.8 %collective-permute-start.3 = (bf16[16,2048]{1,0:T(8,128)(2,1)S(1)}, bf16[16,2048]{1,0:T(8,128)(2,1)S(1)}, u32[]{:S(2)}, u32[]{:S(2)}) collective-permute-start(bf16[16,2048]{1,0:T(8,128)(2,1)S(1)} %get-tuple-element.35), channel_id=1, source_target_pairs={{0,16},{4,20},{8,24},{12,28},{16,0},{20,4},{24,8},{28,12},{1,17},{... | collective-permute-start | bytes 196616 | tf_op jit(solution)/shard_map/ppermute | solution.py:524
  18.6 5.4 %collective-permute-start.4 = (bf16[16,2048]{1,0:T(8,128)(2,1)S(1)}, bf16[16,2048]{1,0:T(8,128)(2,1)S(1)}, u32[]{:S(2)}, u32[]{:S(2)}) collective-permute-start(bf16[16,2048]{1,0:T(8,128)(2,1)S(1)} %get-tuple-element.35), channel_id=1, source_target_pairs={{0,24},{4,28},{8,0},{12,4},{16,8},{20,12},{24,16},{28,20},{1,25},{... | collective-permute-start | bytes 196616 | tf_op jit(solution)/shard_map/ppermute | solution.py:524
  24.8 4.3 %copy-start.1 = (f32[2048]{0:T(1024)S(1)}, f32[2048]{0:T(1024)}, u32[]{:S(2)}) copy-start(f32[2048]{0:T(1024)} %param.13) | copy-start | bytes 24580
  24.8 4.1 %collective-permute-start.5 = (f32[1,256]{1,0:T(1,128)S(1)}, f32[1,256]{1,0:T(1,128)S(1)}, u32[]{:S(2)}, u32[]{:S(2)}) collective-permute-start(f32[1,256]{1,0:T(1,128)S(1)} %get-tuple-element.37.refs_2_), channel_id=1, source_target_pairs={{0,1},{1,2},{2,3},{3,0},{4,5},{5,6},{6,7},{7,4},{8,9},{9,10},{10,1... | collective-permute-start | bytes 3080 | tf_op jit(solution)/shard_map/ppermute | solution.py:544
  24.9 4.1 %collective-permute-start.6 = (f32[1,256]{1,0:T(1,128)S(1)}, f32[1,256]{1,0:T(1,128)S(1)}, u32[]{:S(2)}, u32[]{:S(2)}) collective-permute-start(f32[1,256]{1,0:T(1,128)S(1)} %get-tuple-element.37.refs_2_), channel_id=1, source_target_pairs={{0,2},{1,3},{2,0},{3,1},{4,6},{5,7},{6,4},{7,5},{8,10},{9,11},{10,... | collective-permute-start | bytes 3080 | tf_op jit(solution)/shard_map/ppermute | solution.py:544
  26.4 2.7 %collective-permute-start.7 = (f32[1,256]{1,0:T(1,128)S(1)}, f32[1,256]{1,0:T(1,128)S(1)}, u32[]{:S(2)}, u32[]{:S(2)}) collective-permute-start(f32[1,256]{1,0:T(1,128)S(1)} %get-tuple-element.37.refs_2_), channel_id=1, source_target_pairs={{0,3},{1,0},{2,1},{3,2},{4,7},{5,4},{6,5},{7,6},{8,11},{9,8},{10,9... | collective-permute-start | bytes 3080 | tf_op jit(solution)/shard_map/ppermute | solution.py:544

commit v4 on v3

--- a/solution.py
+++ b/solution.py
@@ -108,38 +108,33 @@
     return [weights[tap, feature : feature + 1, lanes] for tap in range(weights.shape[0])]
 
 
-def state_kernel(
+def fetch_kernel(
     projected_ref,
     weight_hbm,
     rate_hbm,
-    product_ref,
-    state_ref,
+    block_ref,
+    tail_ref,
+    weight_ref,
     mode_rate_ref,
-    head_ref,
-    weight_ref,
-    buffer_ref,
     ending_ref,
     shift_ref,
+    last_ref,
     short_ref,
     rate_ref,
     sems,
-    small_sems,
 ):
-    rows, width = product_ref.shape
-    wides = width // WIDE
-    rate_copy = pltpu.make_async_copy(rate_hbm, rate_ref, small_sems.at[0])
-    rate_copy.start()
-    weight_copy = pltpu.make_async_copy(weight_hbm, short_ref, small_sems.at[1])
-    weight_copy.start()
-    copies = []
-    for tile in range(wides):
-        here = pl.ds(tile * WIDE, WIDE)
-        copies.append(
-            pltpu.make_async_copy(projected_ref.at[pl.ds(1, 2), :, here], buffer_ref.at[:, :, here], sems.at[tile])
-        )
-        copies[-1].start()
+    rows, width = block_ref.shape[1:]
+    copies = [
+        pltpu.make_async_copy(rate_hbm, rate_ref, sems.at[0]),
+        pltpu.make_async_copy(projected_ref.at[:, pl.ds(rows - 16, 16), :], last_ref, sems.at[1]),
+        pltpu.make_async_copy(weight_hbm, short_ref, sems.at[2]),
+        pltpu.make_async_copy(projected_ref.at[1], block_ref.at[0], sems.at[3]),
+        pltpu.make_async_copy(projected_ref.at[2], block_ref.at[1], sems.at[4]),
+    ]
+    for copy in copies:
+        copy.start()
     shift_ref[...] = shift_matrix(rows)
-    rate_copy.wait()
+    copies[0].wait()
     mode_rate = per_channel(rate_ref[...])
     mode_rate_ref[...] = mode_rate
     eye = own_mode(BF16)
@@ -150,38 +145,47 @@
         diagonal = jnp.concatenate([spread(high, eye), spread(low, eye)], axis=1)
         exponent = jnp.dot(diagonal, left, preferred_element_type=F32)
         ending_ref[tile // 2, lanes_of(tile % 2), :] = jnp.exp(exponent).astype(BF16)
-    weight_copy.wait()
-    weights = short_ref[...].astype(F32)
-    weight_ref[...] = weights
+    copies[1].wait()
+    for c in range(3):
+        tail_ref[c] = last_ref[c].astype(F32)[14:16].astype(BF16)
+    copies[2].wait()
+    weight_ref[...] = short_ref[...].astype(F32)
+    copies[3].wait()
+    copies[4].wait()
+
+
+def state_kernel(block_ref, weight_ref, ending_ref, shift_ref, product_ref, state_ref):
+    width = product_ref.shape[1]
     mask = group_mask(F32)
 
-    def leave_state(tile):
-        every = jnp.dot(ending_ref[tile], product_ref[:, lanes_of(tile, WIDE)], preferred_element_type=F32)
+    def leave_state(wide, product):
+        every = jnp.dot(ending_ref[wide], product, preferred_element_type=F32)
         for half in range(WIDE // LANES):
             own = every[lanes_of(half), lanes_of(half)].reshape(GROUPS, MODES, LANES)
-            state_ref[:, lanes_of((WIDE // LANES) * tile + half)] = jnp.sum(own * mask, axis=0)
-
-    for wide in range(wides):
-        copies[wide].wait()
+            state_ref[:, lanes_of((WIDE // LANES) * wide + half)] = jnp.sum(own * mask, axis=0)
+
+    previous = None
+    for wide in range(width // WIDE):
+        here = lanes_of(wide, WIDE)
+        parts = [wide_conv(block_ref[c, :, here], shift_ref[...], taps_of(weight_ref, c + 1, here)) for c in (0, 1)]
+        product = (parts[0] * parts[1]).astype(BF16)
+        product_ref[:, here] = product
         if wide > 0:
-            leave_state(wide - 1)
-        here = lanes_of(wide, WIDE)
-        parts = []
-        for c in (0, 1):
-            head_ref[c, :, here] = buffer_ref[c, 0:16, here].astype(F32)[:8]
-            parts.append(wide_conv(buffer_ref[c, :, here], shift_ref[...], taps_of(weights, c + 1, here)))
-        product_ref[:, here] = (parts[0] * parts[1]).astype(BF16)
-    leave_state(wides - 1)
+            leave_state(wide - 1, previous)
+        previous = product
+    leave_state(width // WIDE - 1, previous)
 
 
 def halo(before_ref, place_ref):
     return jnp.where(place_ref[0] > 0, before_ref[...].astype(F32), 0.0)
 
 
-def head_kernel(rows, place_ref, before_ref, head_ref, weight_ref, state_ref, mode_rate_ref, full_ref, first_ref):
+def head_kernel(place_ref, before_ref, block_ref, weight_ref, state_ref, mode_rate_ref, full_ref, first_ref):
     before = halo(before_ref, place_ref)
-    everything = slice(0, head_ref.shape[2])
-    parts = [short_conv(head_ref[c], before[c + 1], taps_of(weight_ref, c + 1, everything)) for c in (0, 1)]
+    rows, width = block_ref.shape[1:]
+    everything = slice(0, width)
+    heads = [block_ref[c, 0:16, :].astype(F32)[:8] for c in (0, 1)]
+    parts = [short_conv(heads[c], before[c + 1], taps_of(weight_ref, c + 1, everything)) for c in (0, 1)]
     first = (parts[0] * parts[1]).astype(BF16).astype(F32)
     first_ref[...] = first
     rate = mode_rate_ref[...]
@@ -197,13 +201,13 @@
     before_ref,
     weight_ref,
     mode_rate_ref,
+    shift_ref,
     inner_ref,
     entering_ref,
     carry_ref,
     gate_ref,
     residual_ref,
     query_ref,
-    shift_ref,
     residue_ref,
     sems,
 ):
@@ -252,7 +256,6 @@
                 entering_ref[tile] = entering
     before = halo(before_ref, place_ref)
     copies[1].wait()
-    shift_ref[...] = shift_matrix(rows)
     for tile in range(width // WIDE):
         here = lanes_of(tile, WIDE)
         weights = taps_of(weight_ref, 0, here)
@@ -444,44 +447,50 @@
     def bf16(*shape):
         return jax.ShapeDtypeStruct(shape, BF16)
 
-    before = lax.ppermute(projected[:, rows - (taps - 1) :, :], "ctx", ring(peers, 1))
-
-    product, state, mode_rate, head, weights = pl.pallas_call(
-        state_kernel,
+    block, tail, weights, mode_rate, ending, shift = pl.pallas_call(
+        fetch_kernel,
         in_specs=[hbm_spec] * 3,
         out_shape=[
-            bf16(rows, width),
+            bf16(2, rows, width),
+            bf16(3, taps - 1, width),
+            f32(*short_weight.shape),
             f32(MODES, width),
-            f32(MODES, width),
-            f32(2, 8, width),
-            f32(*short_weight.shape),
+            bf16(wides, WIDE, rows),
+            bf16(2 * rows, rows),
         ],
         scratch_shapes=[
-            pltpu.VMEM((2, rows, width), BF16),
-            pltpu.VMEM((wides, WIDE, rows), BF16),
-            pltpu.VMEM((2 * rows, rows), BF16),
+            pltpu.VMEM((3, 16, width), BF16),
             pltpu.VMEM(short_weight.shape, BF16),
             pltpu.VMEM((MODES, rates.shape[0]), F32),
-            pltpu.SemaphoreType.DMA((wides,)),
-            pltpu.SemaphoreType.DMA((2,)),
+            pltpu.SemaphoreType.DMA((5,)),
         ],
+        compiler_params=params(),
+        cost_estimate=cost(2),
+        name="fetch",
+    )(kept(projected), kept(short_weight), kept(rates.T))
+
+    before = lax.ppermute(tail, "ctx", ring(peers, 1))
+
+    product, state = pl.pallas_call(
+        state_kernel,
+        out_shape=[bf16(rows, width), f32(MODES, width)],
         compiler_params=params(),
         cost_estimate=cost(3),
         name="block_state",
-    )(kept(projected), kept(short_weight), kept(rates.T))
+    )(block, weights, ending, shift)
 
     full_state, first = pl.pallas_call(
-        lambda *refs: head_kernel(rows, *refs),
+        head_kernel,
         in_specs=[smem_spec] + [vmem_spec] * 5,
         out_shape=[bf16(MODES, width), f32(8, width)],
         compiler_params=params(),
         cost_estimate=cost(0.2),
         name="head_tokens",
-    )(place, before, head, weights, state, mode_rate)
+    )(place, before, block, weights, state, mode_rate)
 
     inner, entering, carry_table, gate, residual_here = pl.pallas_call(
         prepare_kernel,
-        in_specs=[smem_spec] + [hbm_spec] * 3 + [vmem_spec] * 3,
+        in_specs=[smem_spec] + [hbm_spec] * 3 + [vmem_spec] * 4,
         out_shape=[
             bf16(tiles, CHUNK + MODES, GROUPS * CHUNK),
             bf16(tiles, CHUNK, LANES),
@@ -491,14 +500,13 @@
         ],
         scratch_shapes=[
             pltpu.VMEM((rows, width), BF16),
-            pltpu.VMEM((2 * rows, rows), BF16),
             pltpu.VMEM((MODES, rates.shape[0]), F32),
             pltpu.SemaphoreType.DMA((3,)),
         ],
         compiler_params=params(),
         cost_estimate=cost(2),
         name="prepare",
-    )(place, kept(projected), kept(residual), kept(residues.T), before, weights, mode_rate)
+    )(place, kept(projected), kept(residual), kept(residues.T), before, weights, mode_rate, shift)
 
     group, entry, stride = full_state, jnp.zeros((MODES, width), F32), 1
     levels = radices(peers)

time: 30.7 us -> 32.4 us (1.055)
  waiting for transfers between devices: 0.25 us -> 6.01 us
  starting transfers between devices: 13.2 us -> 8.08 us
  local copies, waits for them, and re-layouts: 0.94 us -> 1.55 us
  Pallas kernels: 15.3 us -> 15.7 us
    ppermute x1, waiting for transfers between devices: 0.01 us -> 2.5 us  [per_device(): before = lax.ppermute(tail, 'ctx', ring(peers, 1))]
    ppermute x3, starting transfers between devices: 5.57 us -> 3.13 us  [per_device(): lax.ppermute(group, 'ctx', ring(peers, stride * k))]
    ppermute x1, starting transfers between devices: 1.61 us -> 0.07 us  [per_device(): others = [lax.ppermute(group, 'ctx', cycle) for cycle in cycles]]
    unnamed x4 -> x8, local copies, waits for them, and re-layouts: 0.01 us -> 1.54 us
    ppermute x3, waiting for transfers between devices: 0.23 us -> 1.75 us  [per_device(): lax.ppermute(squares, 'fsdp', ring(count, k))]
    ppermute x3, waiting for transfers between devices: 0.01 us -> 1.16 us  [per_device(): lax.ppermute(group, 'ctx', ring(peers, stride * k))]
    ppermute x3, starting transfers between devices: 3.01 us -> 1.94 us  [per_device(): lax.ppermute(squares, 'fsdp', ring(count, k))]
    slice x1 -> x0, local copies, waits for them, and re-layouts: 0.92 us -> none  [per_device(): projected[:, rows - (taps - 1):, :]]
  transfers between devices with their start and end apart: 8 -> 8, of which waited for: 1 -> 6; matrix products, arithmetic and copies ran while one was open for 0% -> 0% of each run, Pallas kernels for 43% -> 32%
where the time goes in v4:
time: 32.4 us; the launch traced here: 32.1 us
  Pallas kernels  15.7 us (48%)
  starting transfers between devices  8.08 us (25%)
  waiting for transfers between devices  6.01 us (19%)
  local copies, waits for them, and re-layouts  1.55 us (5%)
  between operations  0.73 us (2%)
    pallas_call x1, Pallas kernels, per_device(): pl.pallas_call(local_kernel, out_shape=f32(rows, width), compiler_params=...  3.81 us
    pallas_call x1, Pallas kernels, per_device(): pl.pallas_call(prepare_kernel, in_specs=[smem_spec] + [hbm_spec] * 3 + [v...  3.63 us
    ppermute x3, starting transfers between devices, per_device(): lax.ppermute(group, 'ctx', ring(peers, stride * k))  3.13 us
    ppermute x1, starting transfers between devices, per_device(): before = lax.ppermute(tail, 'ctx', ring(peers, 1))  2.94 us
    ppermute x1, waiting for transfers between devices, per_device(): before = lax.ppermute(tail, 'ctx', ring(peers, 1))  2.5 us
    pallas_call x1, Pallas kernels, per_device(): pl.pallas_call(fetch_kernel, in_specs=[hbm_spec] * 3, out_shape=[bf16(2,...  2.35 us
    pallas_call x2, Pallas kernels, write(): pl.pallas_call(kernel, out_specs=hbm_spec, out_shape=bf16(rows, width), s...  2.32 us
    ppermute x3, starting transfers between devices, per_device(): lax.ppermute(squares, 'fsdp', ring(count, k))  1.94 us
  transfers between devices with their start and end apart: 8, of which 6 were waited for; matrix products, arithmetic and copies ran while one was open for 0% of the time, Pallas kernels for 32%

profile of v4, /device:TPU:0, one launch (start us, length us, event | category | flops | bytes accessed | tf_op | source)
XLA Modules:
  0.0 32.1 jit_solution(3931637116245497899)
XLA Ops:
  0.6 2.4 %fetch.1 = (bf16[2,256,2048]{2,1,0:T(8,128)(2,1)S(1)}, bf16[3,2,2048]{2,1,0:T(2,128)(2,1)}, f32[3,3,2048]{2,1,0:T(4,128)S(1)}, f32[16,2048]{1,0:T(8,128)S(1)}, b...) custom-call(bf16[3,256,2048]{2,1,0:T(8,128)(2,1)} %projected_ref.3, bf16[3,3,2048]{2,1,0:T(4,128)(2,1)} %weight_hbm.1, ...), custom_call_target="tpu_custom_call" | custom-call | bytes 6000000 | tf_op jit(solution)/shard_map/fetch/pallas_call | solution.py:450
  3.0 0.0 copy-start
  3.0 0.6 %copy-done = f32[3,3,2048]{2,1,0:T(4,128)} copy-done((f32[3,3,2048]{2,1,0:T(4,128)}, f32[3,3,2048]{2,1,0:T(4,128)S(1)}, u32[]{:S(2)}) %copy-start) | copy-done | bytes 73752
  3.6 2.9 %collective-permute-start = (bf16[3,2,2048]{2,1,0:T(2,128)(2,1)}, bf16[3,2,2048]{2,1,0:T(2,128)(2,1)}, u32[]{:S(2)}, u32[]{:S(2)}) collective-permute-start(bf16[3,2,2048]{2,1,0:T(2,128)(2,1)} %get-tuple-element.23), channel_id=1, source_target_pairs={{0,4},{4,8},{8,12},{12,16},{16,20},{20,24},{24,28},{28,0},{1,5},{5... | collective-permute-start | bytes 73736 | tf_op jit(solution)/shard_map/ppermute | solution.py:472
  6.6 0.0 copy-start.1
  6.6 0.9 %copy-done.1 = f32[3,3,2048]{2,1,0:T(4,128)S(1)} copy-done((f32[3,3,2048]{2,1,0:T(4,128)S(1)}, f32[3,3,2048]{2,1,0:T(4,128)}, u32[]{:S(2)}) %copy-start.1) | copy-done | bytes 73752
  7.5 1.8 %block_state.1 = (bf16[256,2048]{1,0:T(8,128)(2,1)S(1)}, f32[16,2048]{1,0:T(8,128)S(1)}) custom-call(bf16[2,256,2048]{2,1,0:T(8,128)(2,1)S(1)} %get-tuple-element.29.block_ref, f32[3,3,2048]{2,1,0:T(4,128)S(1)} %copy-done.1, bf16[8,256,256]{2,1,0:T(8,128)(2,1)S(1)} %get-tuple-element.30.ending_ref, bf16[512,256]{1,0:T(8,128)(2,1)S(1)} %get-tuple-element.26.shift_ref), custom_call_target="tpu_custom_call" | custom-call | bytes 9000000 | tf_op jit(solution)/shard_map/block_state/pallas_call | solution.py:474
  9.2 2.5 %collective-permute-done.before_ref = bf16[3,2,2048]{2,1,0:T(2,128)(2,1)} collective-permute-done((bf16[3,2,2048]{2,1,0:T(2,128)(2,1)}, bf16[3,2,2048]{2,1,0:T(2,128)(2,1)}, u32[]{:S(2)}, u32[]{:S(2)}) %collective-permute-start) | collective-permute-done | bytes 24608 | tf_op jit(solution)/shard_map/ppermute | solution.py:472
  11.7 0.9 %head_tokens.1 = (bf16[16,2048]{1,0:T(8,128)(2,1)S(1)}, f32[8,2048]{1,0:T(8,128)S(1)}) custom-call(s32[1]{0:T(128)} %bitcast.place_ref.refs_0_, bf16[3,2,2048]{2,1,0:T(2,128)(2,1)} %collective-permute-done.before_ref, bf16[2,256,2048]{2,1,0:T(8,128)(2,1)S(1)} %get-tuple-element.29.block_ref, f32[3,3,2048]{2,1,0:T(4,128)S(1)} %copy-done.1, ...), custom_call_target="tpu_custom_call" | custom-call | bytes 600000 | tf_op jit(solution)/shard_map/head_tokens/pallas_call | solution.py:482
  12.6 0.1 collective-permute-start.1
  12.7 0.0 copy-start.2
  12.7 3.6 %prepare.1 = (bf16[16,48,256]{2,1,0:T(8,128)(2,1)S(1)}, bf16[16,32,128]{2,1,0:T(8,128)(2,1)S(1)}, bf16[8,256,256]{2,1,0:T(8,128)(2,1)S(1)}, f32[256,2048]{1,0:T(8,128)S(1)}, bf16[256,2048]{1,0:T(8,128)(2,1)S(1)}) custom-call(s32[1]{0:T(128)} %bitcast.place_ref.refs_0_, bf16[3,256,2048]{2,1,0:T(8,128)(2,1)} %projected_ref.3, bf16[256,2048]{1,0:T(8,128)(2,1)} %residual_hbm.1, ...), custom_call_target="tpu_custom_call" | custom-call | bytes 6000000 | tf_op jit(solution)/shard_map/prepare/pallas_call | solution.py:491
  16.3 0.6 %collective-permute-done.1.refs_4_ = bf16[16,2048]{1,0:T(8,128)(2,1)S(1)} collective-permute-done((bf16[16,2048]{1,0:T(8,128)(2,1)S(1)}, bf16[16,2048]{1,0:T(8,128)(2,1)S(1)}, u32[]{:S(2)}, u32[]{:S(2)}) %collective-permute-start.1) | collective-permute-done | bytes 65568 | tf_op jit(solution)/shard_map/ppermute | solution.py:520
  16.9 0.1 join.1
  17.1 2.0 %collective-permute-start.4 = (bf16[16,2048]{1,0:T(8,128)(2,1)S(1)}, bf16[16,2048]{1,0:T(8,128)(2,1)S(1)}, u32[]{:S(2)}, u32[]{:S(2)}) collective-permute-start(bf16[16,2048]{1,0:T(8,128)(2,1)S(1)} %get-tuple-element.41), channel_id=1, source_target_pairs={{0,24},{4,28},{8,0},{12,4},{16,8},{20,12},{24,16},{28,20},{1,25},{... | collective-permute-start | bytes 196616 | tf_op jit(solution)/shard_map/ppermute | solution.py:532
  19.1 0.0 collective-permute-start.3
  19.1 1.1 %collective-permute-start.2 = (bf16[16,2048]{1,0:T(8,128)(2,1)S(1)}, bf16[16,2048]{1,0:T(8,128)(2,1)S(1)}, u32[]{:S(2)}, u32[]{:S(2)}) collective-permute-start(bf16[16,2048]{1,0:T(8,128)(2,1)S(1)} %get-tuple-element.41), channel_id=1, source_target_pairs={{0,8},{4,12},{8,16},{12,20},{16,24},{20,28},{24,0},{28,4},{1,9},{5... | collective-permute-start | bytes 196616 | tf_op jit(solution)/shard_map/ppermute | solution.py:532
  20.2 0.0 copy-done.2
  20.2 3.8 %local_conv.1.refs_1_ = f32[256,2048]{1,0:T(8,128)S(1)} custom-call(f32[256,2048]{1,0:T(8,128)S(1)} %get-tuple-element.27.gate_ref.refs_2_, bf16[256,2048]{1,0:T(8,128)(2,1)S(1)} %get-tuple-element.28.residual_ref, bf16[256,2048]{1,0:T(8,128)(2,1)S(1)} %get-tuple-element.31.product_ref, f32[8,2048]{1,0:T(8,128)S(1)} %get-tuple-element.33.first_ref, ...), custom_call_target="tpu_custom_call" | custom-call | bytes 15000000 | tf_op jit(solution)/shard_map/local_conv/pallas_call | solution.py:534
  24.0 0.0 collective-permute-done.4.refs_8_
  24.0 0.4 %collective-permute-done.3.refs_7_ = bf16[16,2048]{1,0:T(8,128)(2,1)S(1)} collective-permute-done((bf16[16,2048]{1,0:T(8,128)(2,1)S(1)}, bf16[16,2048]{1,0:T(8,128)(2,1)S(1)}, u32[]{:S(2)}, u32[]{:S(2)}) %collective-permute-start.3) | collective-permute-done | bytes 65568 | tf_op jit(solution)/shard_map/ppermute | solution.py:532
  24.4 0.7 %collective-permute-done.2.refs_6_ = bf16[16,2048]{1,0:T(8,128)(2,1)S(1)} collective-permute-done((bf16[16,2048]{1,0:T(8,128)(2,1)S(1)}, bf16[16,2048]{1,0:T(8,128)(2,1)S(1)}, u32[]{:S(2)}, u32[]{:S(2)}) %collective-permute-start.2) | collective-permute-done | bytes 65568 | tf_op jit(solution)/shard_map/ppermute | solution.py:532
  25.2 0.8 %add_carry.1 = (f32[256,2048]{1,0:T(8,128)S(1)}, f32[1,256]{1,0:T(1,128)S(1)}) custom-call(s32[1]{0:T(128)} %bitcast.place_ref.refs_0_, f32[256,2048]{1,0:T(8,128)S(1)} %local_conv.1.refs_1_, f32[256,2048]{1,0:T(8,128)S(1)} %get-tuple-element.27.gate_ref.refs_2_, bf16[8,256,256]{2,1,0:T(8,128)(2,1)S(1)} %get-tuple-element.38.refs_3_, ...), custom_call_target="tpu_custom_call" | custom-call | bytes 3000000 | tf_op jit(solution)/shard_map/add_carry/pallas_call | solution.py:543
  26.0 0.0 copy-start.3
  26.0 0.0 collective-permute-start.7
  26.0 1.8 %collective-permute-start.6 = (f32[1,256]{1,0:T(1,128)S(1)}, f32[1,256]{1,0:T(1,128)S(1)}, u32[]{:S(2)}, u32[]{:S(2)}) collective-permute-start(f32[1,256]{1,0:T(1,128)S(1)} %get-tuple-element.43.refs_2_), channel_id=1, source_target_pairs={{0,2},{1,3},{2,0},{3,1},{4,6},{5,7},{6,4},{7,5},{8,10},{9,11},{10,... | collective-permute-start | bytes 3080 | tf_op jit(solution)/shard_map/ppermute | solution.py:552
  27.8 0.2 collective-permute-start.5
  28.0 1.0 %new_residual.1 = bf16[256,2048]{1,0:T(8,128)(2,1)} custom-call(f32[256,2048]{1,0:T(8,128)S(1)} %get-tuple-element.42.summed_ref.refs_0_), custom_call_target="tpu_custom_call" | custom-call | bytes 3000000 | tf_op jit(solution)/shard_map/new_residual/pallas_call | solution.py:555
  29.0 0.0 collective-permute-done.7.refs_5_
  29.0 0.6 %collective-permute-done.6.refs_4_ = f32[1,256]{1,0:T(1,128)S(1)} collective-permute-done((f32[1,256]{1,0:T(1,128)S(1)}, f32[1,256]{1,0:T(1,128)S(1)}, u32[]{:S(2)}, u32[]{:S(2)}) %collective-permute-start.6) | collective-permute-done | bytes 1056 | tf_op jit(solution)/shard_map/ppermute | solution.py:552
  29.7 1.1 %collective-permute-done.5.refs_3_ = f32[1,256]{1,0:T(1,128)S(1)} collective-permute-done((f32[1,256]{1,0:T(1,128)S(1)}, f32[1,256]{1,0:T(1,128)S(1)}, u32[]{:S(2)}, u32[]{:S(2)}) %collective-permute-start.5) | collective-permute-done | bytes 1056 | tf_op jit(solution)/shard_map/ppermute | solution.py:552
  30.8 0.0 copy-done.3
  30.8 1.3 %normed.1 = bf16[256,2048]{1,0:T(8,128)(2,1)} custom-call(f32[256,2048]{1,0:T(8,128)S(1)} %get-tuple-element.42.summed_ref.refs_0_, f32[1,2048]{1,0:T(1,128)S(1)} %bitcast.6, f32[1,256]{1,0:T(1,128)S(1)} %get-tuple-element.43.refs_2_, f32[1,256]{1,0:T(1,128)S(1)} %collective-permute-done.5.refs_3_, f32[1,256]{1,0:T(1,128)S(1)} %collective-permute-done.6.refs_4_, ...), custom_call_target="tpu_custom_call" | custom-call | bytes 3000000 | tf_op jit(solution)/shard_map/normed/pallas_call | solution.py:555
  (1 shorter events, 0.0 us)
Async XLA Ops:
  3.0 0.6 %copy-start = (f32[3,3,2048]{2,1,0:T(4,128)}, f32[3,3,2048]{2,1,0:T(4,128)S(1)}, u32[]{:S(2)}) copy-start(f32[3,3,2048]{2,1,0:T(4,128)S(1)} %get-tuple-element.24.weight_ref) | copy-start | bytes 221188
  3.6 8.1 %collective-permute-start = (bf16[3,2,2048]{2,1,0:T(2,128)(2,1)}, bf16[3,2,2048]{2,1,0:T(2,128)(2,1)}, u32[]{:S(2)}, u32[]{:S(2)}) collective-permute-start(bf16[3,2,2048]{2,1,0:T(2,128)(2,1)} %get-tuple-element.23), channel_id=1, source_target_pairs={{0,4},{4,8},{8,12},{12,16},{16,20},{20,24},{24,28},{28,0},{1,5},{5... | collective-permute-start | bytes 73736 | tf_op jit(solution)/shard_map/ppermute | solution.py:472
  6.6 0.9 %copy-start.1 = (f32[3,3,2048]{2,1,0:T(4,128)S(1)}, f32[3,3,2048]{2,1,0:T(4,128)}, u32[]{:S(2)}) copy-start(f32[3,3,2048]{2,1,0:T(4,128)} %copy-done) | copy-start | bytes 221188
  12.6 4.3 %collective-permute-start.1 = (bf16[16,2048]{1,0:T(8,128)(2,1)S(1)}, bf16[16,2048]{1,0:T(8,128)(2,1)S(1)}, u32[]{:S(2)}, u32[]{:S(2)}) collective-permute-start(bf16[16,2048]{1,0:T(8,128)(2,1)S(1)} %get-tuple-element.34.refs_1_), channel_id=1, source_target_pairs={{0,4},{4,0},{8,12},{12,8},{16,20},{20,16},{24,28},{28,24},{1,5},{5... | collective-permute-start | bytes 196616 | tf_op jit(solution)/shard_map/ppermute | solution.py:520
  12.7 7.5 %copy-start.2 = (f32[2048]{0:T(1024)S(1)}, f32[2048]{0:T(1024)}, u32[]{:S(2)}) copy-start(f32[2048]{0:T(1024)} %param.11) | copy-start | bytes 24580
  17.1 6.9 %collective-permute-start.4 = (bf16[16,2048]{1,0:T(8,128)(2,1)S(1)}, bf16[16,2048]{1,0:T(8,128)(2,1)S(1)}, u32[]{:S(2)}, u32[]{:S(2)}) collective-permute-start(bf16[16,2048]{1,0:T(8,128)(2,1)S(1)} %get-tuple-element.41), channel_id=1, source_target_pairs={{0,24},{4,28},{8,0},{12,4},{16,8},{20,12},{24,16},{28,20},{1,25},{... | collective-permute-start | bytes 196616 | tf_op jit(solution)/shard_map/ppermute | solution.py:532
  19.1 5.3 %collective-permute-start.3 = (bf16[16,2048]{1,0:T(8,128)(2,1)S(1)}, bf16[16,2048]{1,0:T(8,128)(2,1)S(1)}, u32[]{:S(2)}, u32[]{:S(2)}) collective-permute-start(bf16[16,2048]{1,0:T(8,128)(2,1)S(1)} %get-tuple-element.41), channel_id=1, source_target_pairs={{0,16},{4,20},{8,24},{12,28},{16,0},{20,4},{24,8},{28,12},{1,17},{... | collective-permute-start | bytes 196616 | tf_op jit(solution)/shard_map/ppermute | solution.py:532
  19.1 6.1 %collective-permute-start.2 = (bf16[16,2048]{1,0:T(8,128)(2,1)S(1)}, bf16[16,2048]{1,0:T(8,128)(2,1)S(1)}, u32[]{:S(2)}, u32[]{:S(2)}) collective-permute-start(bf16[16,2048]{1,0:T(8,128)(2,1)S(1)} %get-tuple-element.41), channel_id=1, source_target_pairs={{0,8},{4,12},{8,16},{12,20},{16,24},{20,28},{24,0},{28,4},{1,9},{5... | collective-permute-start | bytes 196616 | tf_op jit(solution)/shard_map/ppermute | solution.py:532
  26.0 4.8 %copy-start.3 = (f32[2048]{0:T(1024)S(1)}, f32[2048]{0:T(1024)}, u32[]{:S(2)}) copy-start(f32[2048]{0:T(1024)} %param.13) | copy-start | bytes 24580
  26.0 3.0 %collective-permute-start.7 = (f32[1,256]{1,0:T(1,128)S(1)}, f32[1,256]{1,0:T(1,128)S(1)}, u32[]{:S(2)}, u32[]{:S(2)}) collective-permute-start(f32[1,256]{1,0:T(1,128)S(1)} %get-tuple-element.43.refs_2_), channel_id=1, source_target_pairs={{0,3},{1,0},{2,1},{3,2},{4,7},{5,4},{6,5},{7,6},{8,11},{9,8},{10,9... | collective-permute-start | bytes 3080 | tf_op jit(solution)/shard_map/ppermute | solution.py:552
  26.0 3.6 %collective-permute-start.6 = (f32[1,256]{1,0:T(1,128)S(1)}, f32[1,256]{1,0:T(1,128)S(1)}, u32[]{:S(2)}, u32[]{:S(2)}) collective-permute-start(f32[1,256]{1,0:T(1,128)S(1)} %get-tuple-element.43.refs_2_), channel_id=1, source_target_pairs={{0,2},{1,3},{2,0},{3,1},{4,6},{5,7},{6,4},{7,5},{8,10},{9,11},{10,... | collective-permute-start | bytes 3080 | tf_op jit(solution)/shard_map/ppermute | solution.py:552
  27.8 3.0 %collective-permute-start.5 = (f32[1,256]{1,0:T(1,128)S(1)}, f32[1,256]{1,0:T(1,128)S(1)}, u32[]{:S(2)}, u32[]{:S(2)}) collective-permute-start(f32[1,256]{1,0:T(1,128)S(1)} %get-tuple-element.43.refs_2_), channel_id=1, source_target_pairs={{0,1},{1,2},{2,3},{3,0},{4,5},{5,6},{6,7},{7,4},{8,9},{9,10},{10,1... | collective-permute-start | bytes 3080 | tf_op jit(solution)/shard_map/ppermute | solution.py:552

commit v5 on v3

--- a/solution.py
+++ b/solution.py
@@ -18,6 +18,15 @@
 
 def index_of(shape, dim):
     return lax.broadcasted_iota(jnp.int32, shape, dim)
+
+
+def pipelined(count, *stages):
+    held = {}
+    for step in range(count + len(stages) - 1):
+        for k, stage in enumerate(stages):
+            item = step - k
+            if 0 <= item < count:
+                held[item] = stage(item, *held.get(item, ()))
 
 
 def lanes_of(tile, width=LANES):
@@ -98,9 +107,12 @@
     return jnp.where(source == taken, 1.0, 0.0).astype(BF16)
 
 
-def wide_conv(block, shift, weights):
+def earlier_tokens(shift, block):
+    return jnp.dot(shift, block, preferred_element_type=F32)
+
+
+def wide_conv(block, earlier, weights):
     rows = block.shape[0]
-    earlier = jnp.dot(shift, block, preferred_element_type=F32)
     return weights[0] * block.astype(F32) + weights[1] * earlier[:rows] + weights[2] * earlier[rows:]
 
 
@@ -131,13 +143,9 @@
     rate_copy.start()
     weight_copy = pltpu.make_async_copy(weight_hbm, short_ref, small_sems.at[1])
     weight_copy.start()
-    copies = []
-    for tile in range(wides):
-        here = pl.ds(tile * WIDE, WIDE)
-        copies.append(
-            pltpu.make_async_copy(projected_ref.at[pl.ds(1, 2), :, here], buffer_ref.at[:, :, here], sems.at[tile])
-        )
-        copies[-1].start()
+    copies = [pltpu.make_async_copy(projected_ref.at[1 + c], buffer_ref.at[c], sems.at[c]) for c in (0, 1)]
+    for copy in copies:
+        copy.start()
     shift_ref[...] = shift_matrix(rows)
     rate_copy.wait()
     mode_rate = per_channel(rate_ref[...])
@@ -145,33 +153,42 @@
     eye = own_mode(BF16)
     token = index_of((2 * LANES, rows), 1)
     left = jnp.where(token < 2, -1e30, (token - (rows - 1)).astype(F32)).astype(BF16)
-    for tile in range(width // LANES):
+
+    def exponents(tile):
         high, low = split(mode_rate[:, lanes_of(tile)])
         diagonal = jnp.concatenate([spread(high, eye), spread(low, eye)], axis=1)
-        exponent = jnp.dot(diagonal, left, preferred_element_type=F32)
+        return (jnp.dot(diagonal, left, preferred_element_type=F32),)
+
+    def endings(tile, exponent):
         ending_ref[tile // 2, lanes_of(tile % 2), :] = jnp.exp(exponent).astype(BF16)
+
+    pipelined(width // LANES, exponents, endings)
     weight_copy.wait()
     weights = short_ref[...].astype(F32)
     weight_ref[...] = weights
     mask = group_mask(F32)
-
-    def leave_state(tile):
-        every = jnp.dot(ending_ref[tile], product_ref[:, lanes_of(tile, WIDE)], preferred_element_type=F32)
-        for half in range(WIDE // LANES):
-            own = every[lanes_of(half), lanes_of(half)].reshape(GROUPS, MODES, LANES)
-            state_ref[:, lanes_of((WIDE // LANES) * tile + half)] = jnp.sum(own * mask, axis=0)
-
-    for wide in range(wides):
-        copies[wide].wait()
-        if wide > 0:
-            leave_state(wide - 1)
+    for copy in copies:
+        copy.wait()
+
+    def fetch(wide):
+        return [earlier_tokens(shift_ref[...], buffer_ref[c, :, lanes_of(wide, WIDE)]) for c in (0, 1)]
+
+    def multiply(wide, *earlier):
         here = lanes_of(wide, WIDE)
         parts = []
         for c in (0, 1):
             head_ref[c, :, here] = buffer_ref[c, 0:16, here].astype(F32)[:8]
-            parts.append(wide_conv(buffer_ref[c, :, here], shift_ref[...], taps_of(weights, c + 1, here)))
-        product_ref[:, here] = (parts[0] * parts[1]).astype(BF16)
-    leave_state(wides - 1)
+            parts.append(wide_conv(buffer_ref[c, :, here], earlier[c], taps_of(weights, c + 1, here)))
+        product = (parts[0] * parts[1]).astype(BF16)
+        product_ref[:, here] = product
+        return (jnp.dot(ending_ref[wide], product, preferred_element_type=F32),)
+
+    def leave(wide, every):
+        for half in range(WIDE // LANES):
+            own = every[lanes_of(half), lanes_of(half)].reshape(GROUPS, MODES, LANES)
+            state_ref[:, lanes_of((WIDE // LANES) * wide + half)] = jnp.sum(own * mask, axis=0)
+
+    pipelined(wides, fetch, multiply, leave)
 
 
 def halo(before_ref, place_ref):
@@ -226,39 +243,60 @@
     shape = (2 * LANES, wide)
     source = (index_of(shape, 1) & (CHUNK - 1)).astype(F32)
     own = (index_of(shape, 0) & (LANES - 1)) // MODES == index_of(shape, 1) // CHUNK
-    risen = jnp.where(own, source, -1e30).astype(BF16)
+    own_chunk = jnp.where(own[:LANES], 1.0, 0.0).astype(BF16)
+    risen = source[:, :LANES].astype(BF16)
     left = jnp.where(own, source - (CHUNK - 1), 0.0).astype(BF16)
-    for tile in range(width // LANES):
-        here = lanes_of(tile)
-        rate = mode_rate_ref[:, here]
+
+    def exponents(tile):
+        rate = mode_rate_ref[:, lanes_of(tile)]
         high, low = split(rate)
         diagonal = jnp.concatenate([spread(high, eye), spread(low, eye)], axis=1)
-        rising = jnp.exp(jnp.dot(diagonal, risen, preferred_element_type=F32))
         each = jnp.concatenate([high * flat_eye, low * flat_eye], axis=1)
-        ending = jnp.exp(jnp.dot(each, left, preferred_element_type=F32))
-        rate_row = mode_row(rate)
+        return (
+            jnp.dot(diagonal, risen, preferred_element_type=F32),
+            jnp.dot(each, left, preferred_element_type=F32),
+        )
+
+    def products(tile, rise, end):
+        here = lanes_of(tile)
+        rise_high, rise_low = [
+            jnp.concatenate([part] * (wide // LANES), axis=1) * own_chunk for part in split(jnp.exp(rise))
+        ]
+        rate_row = mode_row(mode_rate_ref[:, here])
         falling = mode_row(residue[:, here]) * jnp.exp(-rate_row * step)
         fall_high, fall_low = split(falling)
-        rise_high, rise_low = split(rising)
-        taps = jnp.dot(jnp.concatenate([fall_high, fall_low], axis=0), rise_high, preferred_element_type=F32)
-        taps = taps[:CHUNK] + taps[CHUNK:] + jnp.dot(fall_high, rise_low, preferred_element_type=F32)
-        taps = jnp.where(causal, taps, 0.0)
-        inner_ref[tile] = jnp.concatenate([taps.astype(BF16), ending.astype(BF16)], axis=0)
         half = tile % (WIDE // LANES)
         for chunk in range(rows // CHUNK):
             entering = (falling * jnp.exp(-float(CHUNK * chunk + 1) * rate_row)).astype(BF16)
             carry_ref[tile // (WIDE // LANES), chunk * CHUNK : (chunk + 1) * CHUNK, lanes_of(half)] = entering
             if chunk == 0:
                 entering_ref[tile] = entering
+        return (
+            jnp.dot(jnp.concatenate([fall_high, fall_low], axis=0), rise_high, preferred_element_type=F32),
+            jnp.dot(fall_high, rise_low, preferred_element_type=F32),
+            jnp.exp(end),
+        )
+
+    def finish(tile, taps, rest, ending):
+        taps = jnp.where(causal, taps[:CHUNK] + taps[CHUNK:] + rest, 0.0)
+        inner_ref[tile] = jnp.concatenate([taps.astype(BF16), ending.astype(BF16)], axis=0)
+
+    pipelined(width // LANES, exponents, products, finish)
     before = halo(before_ref, place_ref)
     copies[1].wait()
     shift_ref[...] = shift_matrix(rows)
-    for tile in range(width // WIDE):
-        here = lanes_of(tile, WIDE)
+
+    def fetch(part):
+        return (earlier_tokens(shift_ref[...], query_ref[:, lanes_of(part, WIDE)]),)
+
+    def convolve(part, earlier):
+        here = lanes_of(part, WIDE)
         weights = taps_of(weight_ref, 0, here)
-        gate_ref[:, here] = wide_conv(query_ref[:, here], shift_ref[...], weights)
+        gate_ref[:, here] = wide_conv(query_ref[:, here], earlier, weights)
         head = query_ref[0:16, here].astype(F32)[:8]
         gate_ref[0:8, here] = short_conv(head, before[0, :, here], weights)
+
+    pipelined(width // WIDE, fetch, convolve)
     copies[2].wait()
 
 
@@ -276,37 +314,48 @@
     rows, width = product_ref.shape
     mask = group_mask(BF16)
     top = index_of((8, LANES), 0) < 2
-    for tile in range(width // LANES):
+    chunks = range(rows // CHUNK)
+
+    def inside(tile):
         here = lanes_of(tile)
         pieces = []
-        for chunk in range(rows // CHUNK):
+        for chunk in chunks:
             piece = product_ref[chunk * CHUNK : (chunk + 1) * CHUNK, here]
             if chunk == 0:
                 wide = piece.astype(F32)
                 head = jnp.where(top, first_ref[:, here], wide[:8])
                 piece = jnp.concatenate([head, wide[8:]], axis=0).astype(BF16)
             pieces.append(piece)
-        table = inner_ref[tile]
-        inner = []
-        for pair in range(rows // (2 * CHUNK)):
-            sources = jnp.concatenate([spread(pieces[2 * pair + k], mask) for k in (0, 1)], axis=1)
-            inner.append(jnp.dot(table, sources, preferred_element_type=F32))
-        decay = jnp.exp(-float(CHUNK) * mode_rate_ref[:, here])
+        found = []
+        for pair in chunks[::2]:
+            sources = jnp.concatenate([spread(pieces[pair + k], mask) for k in (0, 1)], axis=1)
+            found.append(jnp.dot(inner_ref[tile], sources, preferred_element_type=F32))
+        return found, pieces[0]
+
+    def across(tile, inner, first):
+        decay = jnp.exp(-float(CHUNK) * mode_rate_ref[:, lanes_of(tile)])
         state = jnp.zeros((MODES, LANES), F32)
         states = []
-        for chunk in range(rows // CHUNK):
+        for chunk in chunks:
             states.append(spread(state.astype(BF16), mask))
             state = decay * state + inner[chunk // 2][CHUNK:, lanes_of(chunk % 2)]
-        entering = entering_ref[tile]
+        outer = []
+        for pair in chunks[::2]:
+            two = jnp.concatenate(states[pair : pair + 2], axis=1)
+            outer.append(jnp.dot(entering_ref[tile], two, preferred_element_type=F32))
+        return [part[:CHUNK] for part in inner], outer, first
+
+    def finish(tile, inner, outer, first):
+        here = lanes_of(tile)
         skip = skip_ref[:, here]
-        for pair in range(rows // (2 * CHUNK)):
-            two = jnp.concatenate(states[2 * pair : 2 * pair + 2], axis=1)
-            conv = inner[pair][:CHUNK] + jnp.dot(entering, two, preferred_element_type=F32)
-            for k in (0, 1):
-                chunk = 2 * pair + k
-                span = slice(chunk * CHUNK, (chunk + 1) * CHUNK)
-                whole = conv[:, lanes_of(k)] + skip * pieces[chunk].astype(F32)
-                base_ref[span, here] = residual_ref[span, here].astype(F32) + gate_ref[span, here] * whole
+        for chunk in chunks:
+            span = slice(chunk * CHUNK, (chunk + 1) * CHUNK)
+            piece = first if chunk == 0 else product_ref[span, here]
+            conv = (inner[chunk // 2] + outer[chunk // 2])[:, lanes_of(chunk % 2)]
+            whole = conv + skip * piece.astype(F32)
+            base_ref[span, here] = residual_ref[span, here].astype(F32) + gate_ref[span, here] * whole
+
+    pipelined(width // LANES, inside, across, finish)
 
 
 def join_kernel(tokens, radix, stride, place_ref, own_ref, mode_rate_ref, entry_ref, *refs):
@@ -336,9 +385,10 @@
     run = place_ref[0] // stride
     within = lax.rem(place_ref[0], stride).astype(F32) * float(rows)
     mask = group_mask(BF16)
-    total = jnp.zeros((rows, LANES), F32)
+    totals = [jnp.zeros((rows, LANES), F32)]
     nothing = jnp.zeros((LANES, LANES), BF16)
-    for tile in range(width // WIDE):
+
+    def enter(tile):
         here = lanes_of(tile, WIDE)
         rate = mode_rate_ref[:, here]
         decay = jnp.exp(-float(rows * stride) * rate)
@@ -350,11 +400,17 @@
         both = jnp.concatenate(
             [jnp.concatenate([left, nothing], axis=1), jnp.concatenate([nothing, right], axis=1)], axis=0
         )
-        carry = jnp.dot(carry_ref[tile], both, preferred_element_type=F32)
+        return (jnp.dot(carry_ref[tile], both, preferred_element_type=F32),)
+
+    def add(tile, carry):
+        here = lanes_of(tile, WIDE)
         summed = base_ref[:, here] + gate_ref[:, here] * carry
         summed_ref[:, here] = summed
         square = summed * summed
-        total = total + (square[:, :LANES] + square[:, LANES:])
+        totals[0] = totals[0] + (square[:, :LANES] + square[:, LANES:])
+
+    pipelined(width // WIDE, enter, add)
+    total = totals[0]
     squares = lax.dot_general(
         jnp.ones((8, LANES), F32),
         total,
@@ -462,7 +518,7 @@
             pltpu.VMEM((2 * rows, rows), BF16),
             pltpu.VMEM(short_weight.shape, BF16),
             pltpu.VMEM((MODES, rates.shape[0]), F32),
-            pltpu.SemaphoreType.DMA((wides,)),
+            pltpu.SemaphoreType.DMA((2,)),
             pltpu.SemaphoreType.DMA((2,)),
         ],
         compiler_params=params(),

time: 30.7 us -> 28.4 us (0.925)
  waiting for transfers between devices: 0.25 us -> 3.22 us
  Pallas kernels: 15.3 us -> 12.4 us
  starting transfers between devices: 13.2 us -> 10.8 us
    pallas_call x1, Pallas kernels: 5.18 us -> 3.43 us  [per_device(): pl.pallas_call(state_kernel, in_specs=[hbm_spec] * 3, out_shape=[bf16(row...]
    ppermute x1, waiting for transfers between devices: 0.01 us -> 1.41 us  [per_device(): lax.ppermute(projected[:, rows - (taps - 1):, :], 'ctx', ring(peers, 1))]
    ppermute x1, starting transfers between devices: 1.61 us -> 0.22 us  [per_device(): others = [lax.ppermute(group, 'ctx', cycle) for cycle in cycles]]
    pallas_call x1, Pallas kernels: 3.81 us -> 2.44 us  [per_device(): pl.pallas_call(local_kernel, out_shape=f32(rows, width), compiler_params=...]
    ppermute x3, starting transfers between devices: 5.57 us -> 4.61 us  [per_device(): lax.ppermute(group, 'ctx', ring(peers, stride * k))]
    ppermute x1, waiting for transfers between devices: 0.01 us -> 0.96 us  [per_device(): others = [lax.ppermute(group, 'ctx', cycle) for cycle in cycles]]
    ppermute x3, waiting for transfers between devices: 0.01 us -> 0.62 us  [per_device(): lax.ppermute(group, 'ctx', ring(peers, stride * k))]
  transfers between devices with their start and end apart: 8 -> 8, of which waited for: 1 -> 4; matrix products, arithmetic and copies ran while one was open for 0% -> 0% of each run, Pallas kernels for 43% -> 36%
where the time goes in v5:
time: 28.4 us; the launch traced here: 28.1 us
  Pallas kernels  12.4 us (44%)
  starting transfers between devices  10.8 us (38%)
  waiting for transfers between devices  3.22 us (11%)
  local copies, waits for them, and re-layouts  0.94 us (3%)
  between operations  0.71 us (2%)
    ppermute x3, starting transfers between devices, per_device(): lax.ppermute(group, 'ctx', ring(peers, stride * k))  4.61 us
    pallas_call x1, Pallas kernels, per_device(): pl.pallas_call(state_kernel, in_specs=[hbm_spec] * 3, out_shape=[bf16(row...  3.43 us
    pallas_call x1, Pallas kernels, per_device(): pl.pallas_call(prepare_kernel, in_specs=[smem_spec] + [hbm_spec] * 3 + [v...  3.14 us
    ppermute x3, starting transfers between devices, per_device(): lax.ppermute(squares, 'fsdp', ring(count, k))  3.01 us
    ppermute x1, starting transfers between devices, per_device(): lax.ppermute(projected[:, rows - (taps - 1):, :], 'ctx', ring(peers, 1))  2.99 us
    pallas_call x1, Pallas kernels, per_device(): pl.pallas_call(local_kernel, out_shape=f32(rows, width), compiler_params=...  2.44 us
    pallas_call x2, Pallas kernels, write(): pl.pallas_call(kernel, out_specs=hbm_spec, out_shape=bf16(rows, width), s...  2.32 us
    ppermute x1, waiting for transfers between devices, per_device(): lax.ppermute(projected[:, rows - (taps - 1):, :], 'ctx', ring(peers, 1))  1.41 us
  transfers between devices with their start and end apart: 8, of which 4 were waited for; matrix products, arithmetic and copies ran while one was open for 0% of the time, Pallas kernels for 36%

profile of v5, /device:TPU:0, one launch (start us, length us, event | category | flops | bytes accessed | tf_op | source)
XLA Modules:
  0.0 28.1 jit_solution(351475353568392268)
XLA Ops:
  0.6 0.9 %slice.3 = bf16[3,2,2048]{2,1,0:T(2,128)(2,1)S(1)} slice(bf16[3,256,2048]{2,1,0:T(8,128)(2,1)} %projected_ref.3), slice={[0:3], [254:256], [0:2048]} | slice | bytes 49152 | tf_op jit(solution)/shard_map/slice | solution.py:503
  1.6 3.0 %collective-permute-start = (bf16[3,2,2048]{2,1,0:T(2,128)(2,1)S(1)}, bf16[3,2,2048]{2,1,0:T(2,128)(2,1)S(1)}, u32[]{:S(2)}, u32[]{:S(2)}) collective-permute-start(bf16[3,2,2048]{2,1,0:T(2,128)(2,1)S(1)} %slice.3), channel_id=1, source_target_pairs={{0,4},{4,8},{8,12},{12,16},{16,20},{20,24},{24,28},{28,0},{1,5},{5... | collective-permute-start | bytes 73736 | tf_op jit(solution)/shard_map/ppermute | solution.py:503
  4.5 3.4 %block_state.1 = (bf16[256,2048]{1,0:T(8,128)(2,1)S(1)}, f32[16,2048]{1,0:T(8,128)S(1)}, f32[16,2048]{1,0:T(8,128)S(1)}, f32[2,8,2048]{2,1,0:T(8,128)S(1)}, f32[3,3,2048]{2,1,0:T(4,128)S(1)}) custom-call(bf16[3,256,2048]{2,1,0:T(8,128)(2,1)} %projected_ref.3, bf16[3,3,2048]{2,1,0:T(4,128)(2,1)} %weight_hbm.1, f32[16,128]{1,0:T(8,128)} %bitcast.7), custom_call_target="tpu_custom_call" | custom-call | bytes 9000000 | tf_op jit(solution)/shard_map/block_state/pallas_call | solution.py:505
  8.0 1.4 %collective-permute-done.before_ref.refs_1_ = bf16[3,2,2048]{2,1,0:T(2,128)(2,1)S(1)} collective-permute-done((bf16[3,2,2048]{2,1,0:T(2,128)(2,1)S(1)}, bf16[3,2,2048]{2,1,0:T(2,128)(2,1)S(1)}, u32[]{:S(2)}, u32[]{:S(2)}) %collective-permute-start) | collective-permute-done | bytes 24608 | tf_op jit(solution)/shard_map/ppermute | solution.py:503
  9.4 0.1 head_tokens.1
  9.5 0.2 collective-permute-start.1
  9.7 0.0 copy-start
  9.7 3.1 %prepare.1 = (bf16[16,48,256]{2,1,0:T(8,128)(2,1)S(1)}, bf16[16,32,128]{2,1,0:T(8,128)(2,1)S(1)}, bf16[8,256,256]{2,1,0:T(8,128)(2,1)S(1)}, f32[256,2048]{1,0:T(8,128)S(1)}, bf16[256,2048]{1,0:T(8,128)(2,1)S(1)}) custom-call(s32[1]{0:T(128)} %bitcast.place_ref.refs_0_, bf16[3,256,2048]{2,1,0:T(8,128)(2,1)} %projected_ref.3, bf16[256,2048]{1,0:T(8,128)(2,1)} %residual_hbm.1, ...), custom_call_target="tpu_custom_call" | custom-call | bytes 6000000 | tf_op jit(solution)/shard_map/prepare/pallas_call | solution.py:538
  12.9 1.0 %collective-permute-done.1.refs_4_ = bf16[16,2048]{1,0:T(8,128)(2,1)S(1)} collective-permute-done((bf16[16,2048]{1,0:T(8,128)(2,1)S(1)}, bf16[16,2048]{1,0:T(8,128)(2,1)S(1)}, u32[]{:S(2)}, u32[]{:S(2)}) %collective-permute-start.1) | collective-permute-done | bytes 65568 | tf_op jit(solution)/shard_map/ppermute | solution.py:568
  13.9 0.1 join.1
  14.0 0.7 %collective-permute-start.2 = (bf16[16,2048]{1,0:T(8,128)(2,1)S(1)}, bf16[16,2048]{1,0:T(8,128)(2,1)S(1)}, u32[]{:S(2)}, u32[]{:S(2)}) collective-permute-start(bf16[16,2048]{1,0:T(8,128)(2,1)S(1)} %get-tuple-element.35), channel_id=1, source_target_pairs={{0,8},{4,12},{8,16},{12,20},{16,24},{20,28},{24,0},{28,4},{1,9},{5... | collective-permute-start | bytes 196616 | tf_op jit(solution)/shard_map/ppermute | solution.py:580
  14.7 2.1 %collective-permute-start.3 = (bf16[16,2048]{1,0:T(8,128)(2,1)S(1)}, bf16[16,2048]{1,0:T(8,128)(2,1)S(1)}, u32[]{:S(2)}, u32[]{:S(2)}) collective-permute-start(bf16[16,2048]{1,0:T(8,128)(2,1)S(1)} %get-tuple-element.35), channel_id=1, source_target_pairs={{0,16},{4,20},{8,24},{12,28},{16,0},{20,4},{24,8},{28,12},{1,17},{... | collective-permute-start | bytes 196616 | tf_op jit(solution)/shard_map/ppermute | solution.py:580
  16.8 1.8 %collective-permute-start.4 = (bf16[16,2048]{1,0:T(8,128)(2,1)S(1)}, bf16[16,2048]{1,0:T(8,128)(2,1)S(1)}, u32[]{:S(2)}, u32[]{:S(2)}) collective-permute-start(bf16[16,2048]{1,0:T(8,128)(2,1)S(1)} %get-tuple-element.35), channel_id=1, source_target_pairs={{0,24},{4,28},{8,0},{12,4},{16,8},{20,12},{24,16},{28,20},{1,25},{... | collective-permute-start | bytes 196616 | tf_op jit(solution)/shard_map/ppermute | solution.py:580
  18.6 0.0 copy-done
  18.6 2.4 %local_conv.1.refs_1_ = f32[256,2048]{1,0:T(8,128)S(1)} custom-call(f32[256,2048]{1,0:T(8,128)S(1)} %get-tuple-element.22.gate_ref.refs_2_, bf16[256,2048]{1,0:T(8,128)(2,1)S(1)} %get-tuple-element.23.residual_ref, bf16[256,2048]{1,0:T(8,128)(2,1)S(1)} %get-tuple-element.24.product_ref, f32[8,2048]{1,0:T(8,128)S(1)} %get-tuple-element.27.first_ref, ...), custom_call_target="tpu_custom_call" | custom-call | bytes 15000000 | tf_op jit(solution)/shard_map/local_conv/pallas_call | solution.py:582
  21.0 0.0 collective-permute-done.2.refs_6_
  21.1 0.6 %collective-permute-done.3.refs_7_ = bf16[16,2048]{1,0:T(8,128)(2,1)S(1)} collective-permute-done((bf16[16,2048]{1,0:T(8,128)(2,1)S(1)}, bf16[16,2048]{1,0:T(8,128)(2,1)S(1)}, u32[]{:S(2)}, u32[]{:S(2)}) %collective-permute-start.3) | collective-permute-done | bytes 65568 | tf_op jit(solution)/shard_map/ppermute | solution.py:580
  21.7 0.0 collective-permute-done.4.refs_8_
  21.7 0.9 %add_carry.1 = (f32[256,2048]{1,0:T(8,128)S(1)}, f32[1,256]{1,0:T(1,128)S(1)}) custom-call(s32[1]{0:T(128)} %bitcast.place_ref.refs_0_, f32[256,2048]{1,0:T(8,128)S(1)} %local_conv.1.refs_1_, f32[256,2048]{1,0:T(8,128)S(1)} %get-tuple-element.22.gate_ref.refs_2_, bf16[8,256,256]{2,1,0:T(8,128)(2,1)S(1)} %get-tuple-element.32.refs_3_, ...), custom_call_target="tpu_custom_call" | custom-call | bytes 3000000 | tf_op jit(solution)/shard_map/add_carry/pallas_call | solution.py:591
  22.5 0.0 copy-start.1
  22.5 0.0 collective-permute-start.5
  22.5 1.6 %collective-permute-start.6 = (f32[1,256]{1,0:T(1,128)S(1)}, f32[1,256]{1,0:T(1,128)S(1)}, u32[]{:S(2)}, u32[]{:S(2)}) collective-permute-start(f32[1,256]{1,0:T(1,128)S(1)} %get-tuple-element.37.refs_2_), channel_id=1, source_target_pairs={{0,2},{1,3},{2,0},{3,1},{4,6},{5,7},{6,4},{7,5},{8,10},{9,11},{10,... | collective-permute-start | bytes 3080 | tf_op jit(solution)/shard_map/ppermute | solution.py:600
  24.1 1.4 %collective-permute-start.7 = (f32[1,256]{1,0:T(1,128)S(1)}, f32[1,256]{1,0:T(1,128)S(1)}, u32[]{:S(2)}, u32[]{:S(2)}) collective-permute-start(f32[1,256]{1,0:T(1,128)S(1)} %get-tuple-element.37.refs_2_), channel_id=1, source_target_pairs={{0,3},{1,0},{2,1},{3,2},{4,7},{5,4},{6,5},{7,6},{8,11},{9,8},{10,9... | collective-permute-start | bytes 3080 | tf_op jit(solution)/shard_map/ppermute | solution.py:600
  25.5 1.0 %new_residual.1 = bf16[256,2048]{1,0:T(8,128)(2,1)} custom-call(f32[256,2048]{1,0:T(8,128)S(1)} %get-tuple-element.36.summed_ref.refs_0_), custom_call_target="tpu_custom_call" | custom-call | bytes 3000000 | tf_op jit(solution)/shard_map/new_residual/pallas_call | solution.py:603
  26.6 0.0 collective-permute-done.5.refs_3_
  26.6 0.0 collective-permute-done.6.refs_4_
  26.6 0.2 collective-permute-done.7.refs_5_
  26.8 0.0 copy-done.1
  26.8 1.3 %normed.1 = bf16[256,2048]{1,0:T(8,128)(2,1)} custom-call(f32[256,2048]{1,0:T(8,128)S(1)} %get-tuple-element.36.summed_ref.refs_0_, f32[1,2048]{1,0:T(1,128)S(1)} %bitcast.6, f32[1,256]{1,0:T(1,128)S(1)} %get-tuple-element.37.refs_2_, f32[1,256]{1,0:T(1,128)S(1)} %collective-permute-done.5.refs_3_, f32[1,256]{1,0:T(1,128)S(1)} %collective-permute-done.6.refs_4_, ...), custom_call_target="tpu_custom_call" | custom-call | bytes 3000000 | tf_op jit(solution)/shard_map/normed/pallas_call | solution.py:603
  (1 shorter events, 0.0 us)
Async XLA Ops:
  1.6 7.8 %collective-permute-start = (bf16[3,2,2048]{2,1,0:T(2,128)(2,1)S(1)}, bf16[3,2,2048]{2,1,0:T(2,128)(2,1)S(1)}, u32[]{:S(2)}, u32[]{:S(2)}) collective-permute-start(bf16[3,2,2048]{2,1,0:T(2,128)(2,1)S(1)} %slice.3), channel_id=1, source_target_pairs={{0,4},{4,8},{8,12},{12,16},{16,20},{20,24},{24,28},{28,0},{1,5},{5... | collective-permute-start | bytes 73736 | tf_op jit(solution)/shard_map/ppermute | solution.py:503
  9.5 4.3 %collective-permute-start.1 = (bf16[16,2048]{1,0:T(8,128)(2,1)S(1)}, bf16[16,2048]{1,0:T(8,128)(2,1)S(1)}, u32[]{:S(2)}, u32[]{:S(2)}) collective-permute-start(bf16[16,2048]{1,0:T(8,128)(2,1)S(1)} %get-tuple-element.28.refs_1_), channel_id=1, source_target_pairs={{0,4},{4,0},{8,12},{12,8},{16,20},{20,16},{24,28},{28,24},{1,5},{5... | collective-permute-start | bytes 196616 | tf_op jit(solution)/shard_map/ppermute | solution.py:568
  9.7 8.8 %copy-start = (f32[2048]{0:T(1024)S(1)}, f32[2048]{0:T(1024)}, u32[]{:S(2)}) copy-start(f32[2048]{0:T(1024)} %param.11) | copy-start | bytes 24580
  14.0 7.1 %collective-permute-start.2 = (bf16[16,2048]{1,0:T(8,128)(2,1)S(1)}, bf16[16,2048]{1,0:T(8,128)(2,1)S(1)}, u32[]{:S(2)}, u32[]{:S(2)}) collective-permute-start(bf16[16,2048]{1,0:T(8,128)(2,1)S(1)} %get-tuple-element.35), channel_id=1, source_target_pairs={{0,8},{4,12},{8,16},{12,20},{16,24},{20,28},{24,0},{28,4},{1,9},{5... | collective-permute-start | bytes 196616 | tf_op jit(solution)/shard_map/ppermute | solution.py:580
  14.7 7.0 %collective-permute-start.3 = (bf16[16,2048]{1,0:T(8,128)(2,1)S(1)}, bf16[16,2048]{1,0:T(8,128)(2,1)S(1)}, u32[]{:S(2)}, u32[]{:S(2)}) collective-permute-start(bf16[16,2048]{1,0:T(8,128)(2,1)S(1)} %get-tuple-element.35), channel_id=1, source_target_pairs={{0,16},{4,20},{8,24},{12,28},{16,0},{20,4},{24,8},{28,12},{1,17},{... | collective-permute-start | bytes 196616 | tf_op jit(solution)/shard_map/ppermute | solution.py:580
  16.8 4.9 %collective-permute-start.4 = (bf16[16,2048]{1,0:T(8,128)(2,1)S(1)}, bf16[16,2048]{1,0:T(8,128)(2,1)S(1)}, u32[]{:S(2)}, u32[]{:S(2)}) collective-permute-start(bf16[16,2048]{1,0:T(8,128)(2,1)S(1)} %get-tuple-element.35), channel_id=1, source_target_pairs={{0,24},{4,28},{8,0},{12,4},{16,8},{20,12},{24,16},{28,20},{1,25},{... | collective-permute-start | bytes 196616 | tf_op jit(solution)/shard_map/ppermute | solution.py:580
  22.5 4.3 %copy-start.1 = (f32[2048]{0:T(1024)S(1)}, f32[2048]{0:T(1024)}, u32[]{:S(2)}) copy-start(f32[2048]{0:T(1024)} %param.13) | copy-start | bytes 24580
  22.5 4.1 %collective-permute-start.5 = (f32[1,256]{1,0:T(1,128)S(1)}, f32[1,256]{1,0:T(1,128)S(1)}, u32[]{:S(2)}, u32[]{:S(2)}) collective-permute-start(f32[1,256]{1,0:T(1,128)S(1)} %get-tuple-element.37.refs_2_), channel_id=1, source_target_pairs={{0,1},{1,2},{2,3},{3,0},{4,5},{5,6},{6,7},{7,4},{8,9},{9,10},{10,1... | collective-permute-start | bytes 3080 | tf_op jit(solution)/shard_map/ppermute | solution.py:600
  22.5 4.1 %collective-permute-start.6 = (f32[1,256]{1,0:T(1,128)S(1)}, f32[1,256]{1,0:T(1,128)S(1)}, u32[]{:S(2)}, u32[]{:S(2)}) collective-permute-start(f32[1,256]{1,0:T(1,128)S(1)} %get-tuple-element.37.refs_2_), channel_id=1, source_target_pairs={{0,2},{1,3},{2,0},{3,1},{4,6},{5,7},{6,4},{7,5},{8,10},{9,11},{10,... | collective-permute-start | bytes 3080 | tf_op jit(solution)/shard_map/ppermute | solution.py:600
  24.1 2.7 %collective-permute-start.7 = (f32[1,256]{1,0:T(1,128)S(1)}, f32[1,256]{1,0:T(1,128)S(1)}, u32[]{:S(2)}, u32[]{:S(2)}) collective-permute-start(f32[1,256]{1,0:T(1,128)S(1)} %get-tuple-element.37.refs_2_), channel_id=1, source_target_pairs={{0,3},{1,0},{2,1},{3,2},{4,7},{5,4},{6,5},{7,6},{8,11},{9,8},{10,9... | collective-permute-start | bytes 3080 | tf_op jit(solution)/shard_map/ppermute | solution.py:600

commit v6 on v5

--- a/solution.py
+++ b/solution.py
@@ -124,11 +124,16 @@
     projected_ref,
     weight_hbm,
     rate_hbm,
+    residue_hbm,
+    residual_hbm,
     product_ref,
     state_ref,
     mode_rate_ref,
     head_ref,
     weight_ref,
+    query_ref,
+    residue_ref,
+    residual_ref,
     buffer_ref,
     ending_ref,
     shift_ref,
@@ -144,7 +149,12 @@
     weight_copy = pltpu.make_async_copy(weight_hbm, short_ref, small_sems.at[1])
     weight_copy.start()
     copies = [pltpu.make_async_copy(projected_ref.at[1 + c], buffer_ref.at[c], sems.at[c]) for c in (0, 1)]
-    for copy in copies:
+    later = [
+        pltpu.make_async_copy(residue_hbm, residue_ref, sems.at[2]),
+        pltpu.make_async_copy(projected_ref.at[0], query_ref, sems.at[3]),
+        pltpu.make_async_copy(residual_hbm, residual_ref, sems.at[4]),
+    ]
+    for copy in copies + later:
         copy.start()
     shift_ref[...] = shift_matrix(rows)
     rate_copy.wait()
@@ -189,13 +199,22 @@
             state_ref[:, lanes_of((WIDE // LANES) * wide + half)] = jnp.sum(own * mask, axis=0)
 
     pipelined(wides, fetch, multiply, leave)
+    for copy in later:
+        copy.wait()
 
 
 def halo(before_ref, place_ref):
     return jnp.where(place_ref[0] > 0, before_ref[...].astype(F32), 0.0)
 
 
-def head_kernel(rows, place_ref, before_ref, head_ref, weight_ref, state_ref, mode_rate_ref, full_ref, first_ref):
+def halves(table, place_ref):
+    half = table.shape[1] // 2
+    left, right = table[:, :half], table[:, half:]
+    even = lax.rem(place_ref[0], 2) == 0
+    return jnp.where(even, left, right), jnp.where(even, right, left)
+
+
+def head_kernel(rows, place_ref, before_ref, head_ref, weight_ref, state_ref, mode_rate_ref, keep_ref, send_ref, first_ref):
     before = halo(before_ref, place_ref)
     everything = slice(0, head_ref.shape[2])
     parts = [short_conv(head_ref[c], before[c + 1], taps_of(weight_ref, c + 1, everything)) for c in (0, 1)]
@@ -203,14 +222,15 @@
     first_ref[...] = first
     rate = mode_rate_ref[...]
     early = jnp.exp(-float(rows - 1) * rate) * first[0:1] + jnp.exp(-float(rows - 2) * rate) * first[1:2]
-    full_ref[...] = (state_ref[...] + early).astype(BF16)
+    keep, send = halves(state_ref[...] + early, place_ref)
+    keep_ref[...] = keep
+    send_ref[...] = send.astype(BF16)
 
 
 def prepare_kernel(
     place_ref,
-    projected_ref,
-    residual_hbm,
-    residue_hbm,
+    query_ref,
+    residue_ref,
     before_ref,
     weight_ref,
     mode_rate_ref,
@@ -218,21 +238,10 @@
     entering_ref,
     carry_ref,
     gate_ref,
-    residual_ref,
-    query_ref,
     shift_ref,
-    residue_ref,
-    sems,
 ):
     rows, width = gate_ref.shape
-    copies = [
-        pltpu.make_async_copy(residue_hbm, residue_ref, sems.at[0]),
-        pltpu.make_async_copy(projected_ref.at[0], query_ref, sems.at[1]),
-        pltpu.make_async_copy(residual_hbm, residual_ref, sems.at[2]),
-    ]
-    for copy in copies:
-        copy.start()
-    copies[0].wait()
+    shift_ref[...] = shift_matrix(rows)
     residue = per_channel(residue_ref[...])
     wide = GROUPS * CHUNK
     step = index_of((CHUNK, LANES), 0).astype(F32)
@@ -283,8 +292,6 @@
 
     pipelined(width // LANES, exponents, products, finish)
     before = halo(before_ref, place_ref)
-    copies[1].wait()
-    shift_ref[...] = shift_matrix(rows)
 
     def fetch(part):
         return (earlier_tokens(shift_ref[...], query_ref[:, lanes_of(part, WIDE)]),)
@@ -297,10 +304,10 @@
         gate_ref[0:8, here] = short_conv(head, before[0, :, here], weights)
 
     pipelined(width // WIDE, fetch, convolve)
-    copies[2].wait()
 
 
 def local_kernel(
+    start,
     gate_ref,
     residual_ref,
     product_ref,
@@ -311,12 +318,13 @@
     skip_ref,
     base_ref,
 ):
-    rows, width = product_ref.shape
+    rows, width = base_ref.shape
     mask = group_mask(BF16)
     top = index_of((8, LANES), 0) < 2
     chunks = range(rows // CHUNK)
 
-    def inside(tile):
+    def inside(item):
+        tile = start + item
         here = lanes_of(tile)
         pieces = []
         for chunk in chunks:
@@ -332,7 +340,8 @@
             found.append(jnp.dot(inner_ref[tile], sources, preferred_element_type=F32))
         return found, pieces[0]
 
-    def across(tile, inner, first):
+    def across(item, inner, first):
+        tile = start + item
         decay = jnp.exp(-float(CHUNK) * mode_rate_ref[:, lanes_of(tile)])
         state = jnp.zeros((MODES, LANES), F32)
         states = []
@@ -345,22 +354,31 @@
             outer.append(jnp.dot(entering_ref[tile], two, preferred_element_type=F32))
         return [part[:CHUNK] for part in inner], outer, first
 
-    def finish(tile, inner, outer, first):
-        here = lanes_of(tile)
+    def finish(item, inner, outer, first):
+        here = lanes_of(start + item)
         skip = skip_ref[:, here]
         for chunk in chunks:
             span = slice(chunk * CHUNK, (chunk + 1) * CHUNK)
             piece = first if chunk == 0 else product_ref[span, here]
             conv = (inner[chunk // 2] + outer[chunk // 2])[:, lanes_of(chunk % 2)]
             whole = conv + skip * piece.astype(F32)
-            base_ref[span, here] = residual_ref[span, here].astype(F32) + gate_ref[span, here] * whole
+            base_ref[span, lanes_of(item)] = residual_ref[span, here].astype(F32) + gate_ref[span, here] * whole
 
     pipelined(width // LANES, inside, across, finish)
+
+
+def pair_kernel(tokens, place_ref, keep_ref, got_ref, mode_rate_ref, even_ref, group_ref):
+    rate, _ = halves(mode_rate_ref[...], place_ref)
+    first = lax.rem(place_ref[0], 2) == 0
+    keep, got = keep_ref[...], got_ref[...].astype(F32)
+    even, odd = jnp.where(first, keep, got), jnp.where(first, got, keep)
+    even_ref[...] = even
+    group_ref[...] = (jnp.exp(-float(tokens) * rate) * even + odd).astype(BF16)
 
 
 def join_kernel(tokens, radix, stride, place_ref, own_ref, mode_rate_ref, entry_ref, *refs):
     others, (found_ref, group_ref) = refs[: radix - 1], refs[radix - 1 :]
-    rate = mode_rate_ref[...]
+    rate, _ = halves(mode_rate_ref[...], place_ref)
     run = lax.rem(place_ref[0] // stride, radix)
     step = float(tokens * stride)
 
@@ -374,28 +392,45 @@
         found = found + jnp.where(run >= k, decayed(other, jnp.full((), k - 1, jnp.int32)), 0.0)
         source = lax.rem(run - k + radix, radix)
         total = total + decayed(other, radix - 1 - source)
-    within = lax.rem(place_ref[0], stride).astype(F32) * float(tokens)
-    found_ref[...] = entry_ref[...] + jnp.exp(-within * rate) * found
+    found_ref[...] = entry_ref[...] + jnp.exp(-before_pair(stride, tokens, place_ref) * rate) * found
     group_ref[...] = total.astype(BF16)
 
 
-def carry_kernel(stride, place_ref, base_ref, gate_ref, carry_ref, mode_rate_ref, inner_entry_ref, *refs):
-    entry_refs, (summed_ref, squares_ref) = refs[:-2], refs[-2:]
-    rows, width = base_ref.shape
+def before_pair(stride, tokens, place_ref):
+    within = lax.rem(place_ref[0], stride)
+    return (within - lax.rem(within, 2)).astype(F32) * float(tokens)
+
+
+def hand_kernel(tokens, stride, place_ref, mode_rate_ref, entry_ref, even_ref, *refs):
+    received, (keep_ref, send_ref) = refs[:-2], refs[-2:]
+    rate, _ = halves(mode_rate_ref[...], place_ref)
     run = place_ref[0] // stride
-    within = lax.rem(place_ref[0], stride).astype(F32) * float(rows)
+    decay = jnp.exp(-float(tokens * stride) * rate)
+    outer = jnp.zeros_like(rate)
+    for k in range(len(received), 0, -1):
+        outer = decay * outer + jnp.where(run >= k, received[k - 1][...].astype(F32), 0.0)
+    entry = entry_ref[...] + jnp.exp(-before_pair(stride, tokens, place_ref) * rate) * outer
+    second = jnp.exp(-float(tokens) * rate) * entry + even_ref[...]
+    first = lax.rem(place_ref[0], 2) == 0
+    keep_ref[...] = jnp.where(first, entry, second).astype(BF16)
+    send_ref[...] = jnp.where(first, second, entry).astype(BF16)
+
+
+def carry_kernel(
+    place_ref, left_ref, right_ref, gate_ref, carry_ref, keep_ref, got_ref, summed_ref, squares_ref
+):
+    rows, width = gate_ref.shape
+    half = width // 2
+    even = lax.rem(place_ref[0], 2) == 0
     mask = group_mask(BF16)
     totals = [jnp.zeros((rows, LANES), F32)]
     nothing = jnp.zeros((LANES, LANES), BF16)
 
     def enter(tile):
-        here = lanes_of(tile, WIDE)
-        rate = mode_rate_ref[:, here]
-        decay = jnp.exp(-float(rows * stride) * rate)
-        outer = jnp.zeros_like(rate)
-        for k in range(len(entry_refs), 0, -1):
-            outer = decay * outer + jnp.where(run >= k, entry_refs[k - 1][:, here].astype(F32), 0.0)
-        entry = (inner_entry_ref[:, here] + jnp.exp(-within * rate) * outer).astype(BF16)
+        there = lanes_of(tile % (half // WIDE), WIDE)
+        keep, got = keep_ref[:, there].astype(F32), got_ref[:, there].astype(F32)
+        own_half = even if tile < half // WIDE else jnp.logical_not(even)
+        entry = jnp.where(own_half, keep, got).astype(BF16)
         left, right = spread(entry[:, :LANES], mask), spread(entry[:, LANES:], mask)
         both = jnp.concatenate(
             [jnp.concatenate([left, nothing], axis=1), jnp.concatenate([nothing, right], axis=1)], axis=0
@@ -404,7 +439,9 @@
 
     def add(tile, carry):
         here = lanes_of(tile, WIDE)
-        summed = base_ref[:, here] + gate_ref[:, here] * carry
+        base_ref = left_ref if tile < half // WIDE else right_ref
+        base = base_ref[:, lanes_of(tile % (half // WIDE), WIDE)]
+        summed = base + gate_ref[:, here] * carry
         summed_ref[:, here] = summed
         square = summed * summed
         totals[0] = totals[0] + (square[:, :LANES] + square[:, LANES:])
@@ -412,10 +449,9 @@
     pipelined(width // WIDE, enter, add)
     total = totals[0]
     squares = lax.dot_general(
-        jnp.ones((8, LANES), F32),
-        total,
+        jnp.ones((8, 2 * LANES), BF16),
+        jnp.concatenate(split(total), axis=1),
         (((1,), (1,)), ((), ())),
-        precision=lax.Precision.HIGHEST,
         preferred_element_type=F32,
     )
     squares_ref[...] = squares[0:1]
@@ -464,12 +500,8 @@
 
 def radices(count):
     found = []
-    for radix in (2, 4, 4, 4):
-        if count % radix == 0 and count > 1:
-            found.append(radix)
-            count //= radix
-    for radix in (3, 2, 5, 7):
-        while count % radix == 0 and count > 1:
+    for radix in (4, 3, 2, 5, 7):
+        while count % radix == 0:
             found.append(radix)
             count //= radix
     return found + ([count] if count > 1 else [])
@@ -502,15 +534,18 @@
 
     before = lax.ppermute(projected[:, rows - (taps - 1) :, :], "ctx", ring(peers, 1))
 
-    product, state, mode_rate, head, weights = pl.pallas_call(
+    product, state, mode_rate, head, weights, query, residue, residual_here = pl.pallas_call(
         state_kernel,
-        in_specs=[hbm_spec] * 3,
+        in_specs=[hbm_spec] * 5,
         out_shape=[
             bf16(rows, width),
             f32(MODES, width),
             f32(MODES, width),
             f32(2, 8, width),
             f32(*short_weight.shape),
+            bf16(rows, width),
+            f32(MODES, residues.shape[0]),
+            bf16(rows, width),
         ],
         scratch_shapes=[
             pltpu.VMEM((2, rows, width), BF16),
@@ -518,86 +553,100 @@
             pltpu.VMEM((2 * rows, rows), BF16),
             pltpu.VMEM(short_weight.shape, BF16),
             pltpu.VMEM((MODES, rates.shape[0]), F32),
-            pltpu.SemaphoreType.DMA((2,)),
+            pltpu.SemaphoreType.DMA((5,)),
             pltpu.SemaphoreType.DMA((2,)),
         ],
         compiler_params=params(),
         cost_estimate=cost(3),
         name="block_state",
-    )(kept(projected), kept(short_weight), kept(rates.T))
-
-    full_state, first = pl.pallas_call(
+    )(kept(projected), kept(short_weight), kept(rates.T), kept(residues.T), kept(residual))
+
+    half = width // 2
+
+    def place_call(kernel, count, out_shape, microseconds, name, scratch=()):
+        return pl.pallas_call(
+            kernel,
+            in_specs=[smem_spec] + [vmem_spec] * count,
+            out_shape=out_shape,
+            scratch_shapes=scratch,
+            compiler_params=params(),
+            cost_estimate=cost(microseconds),
+            name=name,
+        )
+
+    keep, send, first = place_call(
         lambda *refs: head_kernel(rows, *refs),
-        in_specs=[smem_spec] + [vmem_spec] * 5,
-        out_shape=[bf16(MODES, width), f32(8, width)],
-        compiler_params=params(),
-        cost_estimate=cost(0.2),
-        name="head_tokens",
+        5,
+        [f32(MODES, half), bf16(MODES, half), f32(8, width)],
+        0.2,
+        "head_tokens",
     )(place, before, head, weights, state, mode_rate)
 
-    inner, entering, carry_table, gate, residual_here = pl.pallas_call(
+    inner, entering, carry_table, gate = place_call(
         prepare_kernel,
-        in_specs=[smem_spec] + [hbm_spec] * 3 + [vmem_spec] * 3,
-        out_shape=[
+        5,
+        [
             bf16(tiles, CHUNK + MODES, GROUPS * CHUNK),
             bf16(tiles, CHUNK, LANES),
             bf16(wides, rows, WIDE),
             f32(rows, width),
-            bf16(rows, width),
         ],
-        scratch_shapes=[
-            pltpu.VMEM((rows, width), BF16),
-            pltpu.VMEM((2 * rows, rows), BF16),
-            pltpu.VMEM((MODES, rates.shape[0]), F32),
-            pltpu.SemaphoreType.DMA((3,)),
-        ],
-        compiler_params=params(),
-        cost_estimate=cost(2),
-        name="prepare",
-    )(place, kept(projected), kept(residual), kept(residues.T), before, weights, mode_rate)
-
-    group, entry, stride = full_state, jnp.zeros((MODES, width), F32), 1
-    levels = radices(peers)
-    for level, radix in enumerate(levels):
+        2,
+        "prepare",
+        [pltpu.VMEM((2 * rows, rows), BF16)],
+    )(place, query, residue, before, weights, mode_rate)
+
+    swap = [(i, i ^ 1) for i in range(peers)]
+    got = lax.ppermute(send, "ctx", swap)
+    got, inner = lax.optimization_barrier((got, inner))
+    even, group = place_call(
+        lambda *refs: pair_kernel(rows, *refs), 3, [f32(MODES, half), bf16(MODES, half)], 0.2, "pair"
+    )(place, keep, got, mode_rate)
+
+    entry, stride = jnp.zeros((MODES, half), F32), 2
+    levels = radices(peers // 2)
+    for radix in levels[:-1]:
         size = stride * radix
-        if level == len(levels) - 1:
-            break
         cycles = [
             [(i, i // size * size + (i + stride * k) % size) for i in range(peers)] for k in range(1, radix)
         ]
         others = [lax.ppermute(group, "ctx", cycle) for cycle in cycles]
-        if level == 0:
-            others[0], inner = lax.optimization_barrier((others[0], inner))
-        entry, group = pl.pallas_call(
+        entry, group = place_call(
             lambda *refs, radix=radix, stride=stride: join_kernel(rows, radix, stride, *refs),
-            in_specs=[smem_spec] + [vmem_spec] * (2 + radix),
-            out_shape=[f32(MODES, width), bf16(MODES, width)],
-            compiler_params=params(),
-            cost_estimate=cost(0.2),
-            name="join",
+            2 + radix,
+            [f32(MODES, half), bf16(MODES, half)],
+            0.2,
+            "join",
         )(place, group, mode_rate, entry, *others)
         stride = size
     received = [lax.ppermute(group, "ctx", ring(peers, stride * k)) for k in range(1, levels[-1])]
 
-    base = pl.pallas_call(
-        local_kernel,
-        out_shape=f32(rows, width),
-        compiler_params=params(),
-        cost_estimate=cost(5),
-        name="local_conv",
-    )(gate, residual_here, product, first, mode_rate, inner, entering, skip[None])
+    def local(start, entering):
+        return pl.pallas_call(
+            lambda *refs: local_kernel(start, *refs),
+            out_shape=f32(rows, half),
+            compiler_params=params(),
+            cost_estimate=cost(1.3),
+            name="local_conv",
+        )(gate, residual_here, product, first, mode_rate, inner, entering, skip[None])
+
+    left = local(0, entering)
+    received[0], left = lax.optimization_barrier((received[0], left))
+    keep, send = place_call(
+        lambda *refs: hand_kernel(rows, stride, *refs), 3 + len(received), [bf16(MODES, half)] * 2, 0.2, "hand"
+    )(place, mode_rate, entry, even, *received)
+    got = lax.ppermute(send, "ctx", swap)
+    keep, entering = lax.optimization_barrier((keep, entering))
+    right = local(tiles // 2, entering)
+
+    summed, squares = place_call(carry_kernel, 6, [f32(rows, width), f32(1, rows)], 1, "add_carry")(
+        place, left, right, gate, carry_table, keep, got
+    )
 
     count = lax.axis_size("fsdp")
-    summed, squares = pl.pallas_call(
-        lambda *refs: carry_kernel(stride, *refs),
-        in_specs=[smem_spec] + [vmem_spec] * (5 + len(received)),
-        out_shape=[f32(rows, width), f32(1, rows)],
-        compiler_params=params(),
-        cost_estimate=cost(1),
-        name="add_carry",
-    )(place, base, gate, carry_table, mode_rate, entry, *received)
-
-    parts = [lax.ppermute(squares, "fsdp", ring(count, k)) for k in range(1, count)]
+    paired = count & (count - 1) == 0
+    routes = [[(i, i ^ k if paired else (i + k) % count) for i in range(count)] for k in range(1, count)]
+    parts = [lax.ppermute(squares, "fsdp", route) for route in routes]
 
     def write(kernel, operands, name):
         return pl.pallas_call(

time: 28.4 us -> 32.2 us (1.13)
  waiting for transfers between devices: 3.22 us -> 8.12 us
  starting transfers between devices: 10.8 us -> 10.2 us
  Pallas kernels: 12.4 us -> 12 us
    ppermute x3, waiting for transfers between devices: 0.62 us -> 3.48 us  [per_device(): lax.ppermute(group, 'ctx', ring(peers, stride * k))]
    ppermute x4 -> x5, waiting for transfers between devices: 1.19 us -> 3.71 us  [the longest x2 3 us: per_device(): got = lax.ppermute(send, 'ctx', swap)]
    ppermute x3, starting transfers between devices: 4.61 us -> 3.88 us  [per_device(): lax.ppermute(group, 'ctx', ring(peers, stride * k))]
    ppermute x1, waiting for transfers between devices: 1.41 us -> 0.93 us  [per_device(): lax.ppermute(projected[:, rows - (taps - 1):, :], 'ctx', ring(peers, 1))]
    pallas_call x6 -> x8, Pallas kernels: 10.1 us -> 9.64 us  [the longest x1 3.91 us: per_device(): pl.pallas_call(state_kernel, in_specs=[hbm_spec] * 5, out_shape=[bf16(row...]
    ppermute x4 -> x5, starting transfers between devices: 3.23 us -> 3.28 us  [the longest x3 1.87 us: per_device(): parts = [lax.ppermute(squares, 'fsdp', route) for route in routes]]
  transfers between devices with their start and end apart: 8 -> 9, of which waited for: 4 -> 7; matrix products, arithmetic and copies ran while one was open for 0% -> 0% of each run, Pallas kernels for 36% -> 31%
where the time goes in v6:
time: 32.2 us; the launch traced here: 31.9 us
  Pallas kernels  12 us (37%)
  starting transfers between devices  10.2 us (32%)
  waiting for transfers between devices  8.12 us (25%)
  local copies, waits for them, and re-layouts  0.94 us (3%)
  between operations  0.69 us (2%)
    pallas_call x1, Pallas kernels, per_device(): pl.pallas_call(state_kernel, in_specs=[hbm_spec] * 5, out_shape=[bf16(row...  3.91 us
    ppermute x3, starting transfers between devices, per_device(): lax.ppermute(group, 'ctx', ring(peers, stride * k))  3.88 us
    ppermute x3, waiting for transfers between devices, per_device(): lax.ppermute(group, 'ctx', ring(peers, stride * k))  3.48 us
    ppermute x2, waiting for transfers between devices, per_device(): got = lax.ppermute(send, 'ctx', swap)  3 us
    ppermute x1, starting transfers between devices, per_device(): lax.ppermute(projected[:, rows - (taps - 1):, :], 'ctx', ring(peers, 1))  2.99 us
    pallas_call x2, Pallas kernels, local(): pl.pallas_call(lambda *refs: local_kernel(start, *refs), out_shape=f32(ro...  2.64 us
    pallas_call x2, Pallas kernels, write(): pl.pallas_call(kernel, out_specs=hbm_spec, out_shape=bf16(rows, width), s...  2.32 us
    pallas_call x1, Pallas kernels, per_device(): place_call(prepare_kernel, 5, [bf16(tiles, CHUNK + MODES, GROUPS * CHUNK)...  2.22 us
  transfers between devices with their start and end apart: 9, of which 7 were waited for; matrix products, arithmetic and copies ran while one was open for 0% of the time, Pallas kernels for 31%

profile of v6, /device:TPU:0, one launch (start us, length us, event | category | flops | bytes accessed | tf_op | source)
XLA Modules:
  0.0 31.9 jit_solution(6737393310592610857)
XLA Ops:
  0.6 0.9 %slice.3 = bf16[3,2,2048]{2,1,0:T(2,128)(2,1)S(1)} slice(bf16[3,256,2048]{2,1,0:T(8,128)(2,1)} %projected_ref.1), slice={[0:3], [254:256], [0:2048]} | slice | bytes 49152 | tf_op jit(solution)/shard_map/slice | solution.py:535
  1.6 3.0 %collective-permute-start = (bf16[3,2,2048]{2,1,0:T(2,128)(2,1)S(1)}, bf16[3,2,2048]{2,1,0:T(2,128)(2,1)S(1)}, u32[]{:S(2)}, u32[]{:S(2)}) collective-permute-start(bf16[3,2,2048]{2,1,0:T(2,128)(2,1)S(1)} %slice.3), channel_id=1, source_target_pairs={{0,4},{4,8},{8,12},{12,16},{16,20},{20,24},{24,28},{28,0},{1,5},{5... | collective-permute-start | bytes 73736 | tf_op jit(solution)/shard_map/ppermute | solution.py:535
  4.5 0.0 copy-start
  4.5 3.9 %block_state.1 = (bf16[256,2048]{1,0:T(8,128)(2,1)S(1)}, f32[16,2048]{1,0:T(8,128)S(1)}, f32[16,2048]{1,0:T(8,128)S(1)}, f32[2,8,2048]{2,1,0:T(8,128)S(1)}, f32[...) custom-call(bf16[3,256,2048]{2,1,0:T(8,128)(2,1)} %projected_ref.1, ...), custom_call_target="tpu_custom_call" | custom-call | bytes 9000000 | tf_op jit(solution)/shard_map/block_state/pallas_call | solution.py:537
  8.5 0.9 %collective-permute-done.refs_1_.before_ref = bf16[3,2,2048]{2,1,0:T(2,128)(2,1)S(1)} collective-permute-done((bf16[3,2,2048]{2,1,0:T(2,128)(2,1)S(1)}, bf16[3,2,2048]{2,1,0:T(2,128)(2,1)S(1)}, u32[]{:S(2)}, u32[]{:S(2)}) %collective-permute-start) | collective-permute-done | bytes 24608 | tf_op jit(solution)/shard_map/ppermute | solution.py:535
  9.4 0.1 head_tokens.1
  9.5 0.7 %collective-permute-start.1 = (bf16[16,1024]{1,0:T(8,128)(2,1)S(1)}, bf16[16,1024]{1,0:T(8,128)(2,1)S(1)}, u32[]{:S(2)}, u32[]{:S(2)}) collective-permute-start(bf16[16,1024]{1,0:T(8,128)(2,1)S(1)} %get-tuple-element.34), channel_id=1, source_target_pairs={{0,4},{4,0},{8,12},{12,8},{16,20},{20,16},{24,28},{28,24},{1,5},{5... | collective-permute-start | bytes 98312 | tf_op jit(solution)/shard_map/ppermute | solution.py:600
  10.2 2.2 %prepare.1 = (bf16[16,48,256]{2,1,0:T(8,128)(2,1)S(1)}, bf16[16,32,128]{2,1,0:T(8,128)(2,1)S(1)}, bf16[8,256,256]{2,1,0:T(8,128)(2,1)S(1)}, f32[256,2048]{1,0:T(8,128)S(1)}) custom-call(s32[1]{0:T(128)} %bitcast.refs_0_.place_ref, bf16[256,2048]{1,0:T(8,128)(2,1)S(1)} %get-tuple-element.35.query_ref, f32[16,128]{1,0:T(8,128)S(1)} %get-tuple-element.36.residue_ref, ...), custom_call_target="tpu_custom_call" | custom-call | bytes 6000000 | tf_op jit(solution)/shard_map/prepare/pallas_call | solution.py:585
  12.5 1.0 %collective-permute-done.1.refs_2_ = bf16[16,1024]{1,0:T(8,128)(2,1)S(1)} collective-permute-done((bf16[16,1024]{1,0:T(8,128)(2,1)S(1)}, bf16[16,1024]{1,0:T(8,128)(2,1)S(1)}, u32[]{:S(2)}, u32[]{:S(2)}) %collective-permute-start.1) | collective-permute-done | bytes 32800 | tf_op jit(solution)/shard_map/ppermute | solution.py:600
  13.5 0.7 %collective-permute-start.2 = (bf16[16,1024]{1,0:T(8,128)(2,1)S(1)}, bf16[16,1024]{1,0:T(8,128)(2,1)S(1)}, u32[]{:S(2)}, u32[]{:S(2)}) collective-permute-start(bf16[16,1024]{1,0:T(8,128)(2,1)S(1)} %get-tuple-element.39), channel_id=1, source_target_pairs={{0,8},{4,12},{8,16},{12,20},{16,24},{20,28},{24,0},{28,4},{1,9},{5... | collective-permute-start | bytes 98312 | tf_op jit(solution)/shard_map/ppermute | solution.py:622
  14.3 3.2 %collective-permute-start.4 = (bf16[16,1024]{1,0:T(8,128)(2,1)S(1)}, bf16[16,1024]{1,0:T(8,128)(2,1)S(1)}, u32[]{:S(2)}, u32[]{:S(2)}) collective-permute-start(bf16[16,1024]{1,0:T(8,128)(2,1)S(1)} %get-tuple-element.39), channel_id=1, source_target_pairs={{0,24},{4,28},{8,0},{12,4},{16,8},{20,12},{24,16},{28,20},{1,25},{... | collective-permute-start | bytes 98312 | tf_op jit(solution)/shard_map/ppermute | solution.py:622
  17.4 0.0 collective-permute-start.3
  17.4 0.0 copy-done
  17.4 1.3 %local_conv.2.left_ref = f32[256,1024]{1,0:T(8,128)S(1)} custom-call(f32[256,2048]{1,0:T(8,128)S(1)} %get-tuple-element.40.refs_0_.gate_ref, bf16[256,2048]{1,0:T(8,128)(2,1)S(1)} %get-tuple-element.41.refs_1_, bf16[256,2048]{1,0:T(8,128)(2,1)S(1)} %get-tuple-element.42.refs_2_, f32[8,2048]{1,0:T(8,128)S(1)} %get-tuple-element.43.refs_3_, ...), custom_call_target="tpu_custom_call" | custom-call | bytes 3900000 | tf_op jit(solution)/shard_map/local_conv/pallas_call | solution.py:625
  18.7 0.7 %collective-permute-done.2.refs_4_ = bf16[16,1024]{1,0:T(8,128)(2,1)S(1)} collective-permute-done((bf16[16,1024]{1,0:T(8,128)(2,1)S(1)}, bf16[16,1024]{1,0:T(8,128)(2,1)S(1)}, u32[]{:S(2)}, u32[]{:S(2)}) %collective-permute-start.2) | collective-permute-done | bytes 32800 | tf_op jit(solution)/shard_map/ppermute | solution.py:622
  19.4 0.0 collective-permute-done.4.refs_6_
  19.4 2.8 %collective-permute-done.3.refs_5_ = bf16[16,1024]{1,0:T(8,128)(2,1)S(1)} collective-permute-done((bf16[16,1024]{1,0:T(8,128)(2,1)S(1)}, bf16[16,1024]{1,0:T(8,128)(2,1)S(1)}, u32[]{:S(2)}, u32[]{:S(2)}) %collective-permute-start.3) | collective-permute-done | bytes 32800 | tf_op jit(solution)/shard_map/ppermute | solution.py:622
  22.2 0.1 hand.1
  22.3 0.7 %collective-permute-start.5 = (bf16[16,1024]{1,0:T(8,128)(2,1)S(1)}, bf16[16,1024]{1,0:T(8,128)(2,1)S(1)}, u32[]{:S(2)}, u32[]{:S(2)}) collective-permute-start(bf16[16,1024]{1,0:T(8,128)(2,1)S(1)} %get-tuple-element.53), channel_id=1, source_target_pairs={{0,4},{4,0},{8,12},{12,8},{16,20},{20,16},{24,28},{28,24},{1,5},{5... | collective-permute-start | bytes 98312 | tf_op jit(solution)/shard_map/ppermute | solution.py:638
  23.0 1.3 %local_conv.3.right_ref = f32[256,1024]{1,0:T(8,128)S(1)} custom-call(f32[256,2048]{1,0:T(8,128)S(1)} %get-tuple-element.40.refs_0_.gate_ref, bf16[256,2048]{1,0:T(8,128)(2,1)S(1)} %get-tuple-element.41.refs_1_, bf16[256,2048]{1,0:T(8,128)(2,1)S(1)} %get-tuple-element.42.refs_2_, f32[8,2048]{1,0:T(8,128)S(1)} %get-tuple-element.43.refs_3_, ...), custom_call_target="tpu_custom_call" | custom-call | bytes 3900000 | tf_op jit(solution)/shard_map/local_conv/pallas_call | solution.py:625
  24.3 2.0 %collective-permute-done.5.got_ref = bf16[16,1024]{1,0:T(8,128)(2,1)S(1)} collective-permute-done((bf16[16,1024]{1,0:T(8,128)(2,1)S(1)}, bf16[16,1024]{1,0:T(8,128)(2,1)S(1)}, u32[]{:S(2)}, u32[]{:S(2)}) %collective-permute-start.5) | collective-permute-done | bytes 32800 | tf_op jit(solution)/shard_map/ppermute | solution.py:638
  26.3 0.6 %add_carry.1 = (f32[256,2048]{1,0:T(8,128)S(1)}, f32[1,256]{1,0:T(1,128)S(1)}) custom-call(s32[1]{0:T(128)} %bitcast.refs_0_.place_ref, f32[256,1024]{1,0:T(8,128)S(1)} %local_conv.2.left_ref, f32[256,1024]{1,0:T(8,128)S(1)} %local_conv.3.right_ref, f32[256,2048]{1,0:T(8,128)S(1)} %get-tuple-element.40.refs_0_.gate_ref, ...), custom_call_target="tpu_custom_call" | custom-call | bytes 3000000 | tf_op jit(solution)/shard_map/add_carry/pallas_call | solution.py:642
  26.9 0.0 copy-start.1
  26.9 0.0 collective-permute-start.8
  26.9 1.8 %collective-permute-start.7 = (f32[1,256]{1,0:T(1,128)S(1)}, f32[1,256]{1,0:T(1,128)S(1)}, u32[]{:S(2)}, u32[]{:S(2)}) collective-permute-start(f32[1,256]{1,0:T(1,128)S(1)} %get-tuple-element.55.refs_2_), channel_id=1, source_target_pairs={{0,2},{1,3},{2,0},{3,1},{4,6},{5,7},{6,4},{7,5},{8,10},{9,11},{10,... | collective-permute-start | bytes 3080 | tf_op jit(solution)/shard_map/ppermute | solution.py:649
  28.7 0.1 collective-permute-start.6
  28.8 1.0 %new_residual.1 = bf16[256,2048]{1,0:T(8,128)(2,1)} custom-call(f32[256,2048]{1,0:T(8,128)S(1)} %get-tuple-element.54.summed_ref.refs_0_), custom_call_target="tpu_custom_call" | custom-call | bytes 3000000 | tf_op jit(solution)/shard_map/new_residual/pallas_call | solution.py:652
  29.9 0.1 collective-permute-done.8.refs_5_
  30.0 0.6 %collective-permute-done.7.refs_4_ = f32[1,256]{1,0:T(1,128)S(1)} collective-permute-done((f32[1,256]{1,0:T(1,128)S(1)}, f32[1,256]{1,0:T(1,128)S(1)}, u32[]{:S(2)}, u32[]{:S(2)}) %collective-permute-start.7) | collective-permute-done | bytes 1056 | tf_op jit(solution)/shard_map/ppermute | solution.py:649
  30.6 0.0 collective-permute-done.6.refs_3_
  30.6 0.0 copy-done.1
  30.6 1.3 %normed.1 = bf16[256,2048]{1,0:T(8,128)(2,1)} custom-call(f32[256,2048]{1,0:T(8,128)S(1)} %get-tuple-element.54.summed_ref.refs_0_, f32[1,2048]{1,0:T(1,128)S(1)} %bitcast.7, f32[1,256]{1,0:T(1,128)S(1)} %get-tuple-element.55.refs_2_, f32[1,256]{1,0:T(1,128)S(1)} %collective-permute-done.6.refs_3_, f32[1,256]{1,0:T(1,128)S(1)} %collective-permute-done.7.refs_4_, ...), custom_call_target="tpu_custom_call" | custom-call | bytes 3000000 | tf_op jit(solution)/shard_map/normed/pallas_call | solution.py:652
  (2 shorter events, 0.0 us)
Async XLA Ops:
  1.6 7.8 %collective-permute-start = (bf16[3,2,2048]{2,1,0:T(2,128)(2,1)S(1)}, bf16[3,2,2048]{2,1,0:T(2,128)(2,1)S(1)}, u32[]{:S(2)}, u32[]{:S(2)}) collective-permute-start(bf16[3,2,2048]{2,1,0:T(2,128)(2,1)S(1)} %slice.3), channel_id=1, source_target_pairs={{0,4},{4,8},{8,12},{12,16},{16,20},{20,24},{24,28},{28,0},{1,5},{5... | collective-permute-start | bytes 73736 | tf_op jit(solution)/shard_map/ppermute | solution.py:535
  4.5 12.9 %copy-start = (f32[2048]{0:T(1024)S(1)}, f32[2048]{0:T(1024)}, u32[]{:S(2)}) copy-start(f32[2048]{0:T(1024)} %param.11) | copy-start | bytes 24580
  9.5 4.0 %collective-permute-start.1 = (bf16[16,1024]{1,0:T(8,128)(2,1)S(1)}, bf16[16,1024]{1,0:T(8,128)(2,1)S(1)}, u32[]{:S(2)}, u32[]{:S(2)}) collective-permute-start(bf16[16,1024]{1,0:T(8,128)(2,1)S(1)} %get-tuple-element.34), channel_id=1, source_target_pairs={{0,4},{4,0},{8,12},{12,8},{16,20},{20,16},{24,28},{28,24},{1,5},{5... | collective-permute-start | bytes 98312 | tf_op jit(solution)/shard_map/ppermute | solution.py:600
  13.5 5.9 %collective-permute-start.2 = (bf16[16,1024]{1,0:T(8,128)(2,1)S(1)}, bf16[16,1024]{1,0:T(8,128)(2,1)S(1)}, u32[]{:S(2)}, u32[]{:S(2)}) collective-permute-start(bf16[16,1024]{1,0:T(8,128)(2,1)S(1)} %get-tuple-element.39), channel_id=1, source_target_pairs={{0,8},{4,12},{8,16},{12,20},{16,24},{20,28},{24,0},{28,4},{1,9},{5... | collective-permute-start | bytes 98312 | tf_op jit(solution)/shard_map/ppermute | solution.py:622
  14.3 5.1 %collective-permute-start.4 = (bf16[16,1024]{1,0:T(8,128)(2,1)S(1)}, bf16[16,1024]{1,0:T(8,128)(2,1)S(1)}, u32[]{:S(2)}, u32[]{:S(2)}) collective-permute-start(bf16[16,1024]{1,0:T(8,128)(2,1)S(1)} %get-tuple-element.39), channel_id=1, source_target_pairs={{0,24},{4,28},{8,0},{12,4},{16,8},{20,12},{24,16},{28,20},{1,25},{... | collective-permute-start | bytes 98312 | tf_op jit(solution)/shard_map/ppermute | solution.py:622
  17.4 4.8 %collective-permute-start.3 = (bf16[16,1024]{1,0:T(8,128)(2,1)S(1)}, bf16[16,1024]{1,0:T(8,128)(2,1)S(1)}, u32[]{:S(2)}, u32[]{:S(2)}) collective-permute-start(bf16[16,1024]{1,0:T(8,128)(2,1)S(1)} %get-tuple-element.39), channel_id=1, source_target_pairs={{0,16},{4,20},{8,24},{12,28},{16,0},{20,4},{24,8},{28,12},{1,17},{... | collective-permute-start | bytes 98312 | tf_op jit(solution)/shard_map/ppermute | solution.py:622
  22.3 4.0 %collective-permute-start.5 = (bf16[16,1024]{1,0:T(8,128)(2,1)S(1)}, bf16[16,1024]{1,0:T(8,128)(2,1)S(1)}, u32[]{:S(2)}, u32[]{:S(2)}) collective-permute-start(bf16[16,1024]{1,0:T(8,128)(2,1)S(1)} %get-tuple-element.53), channel_id=1, source_target_pairs={{0,4},{4,0},{8,12},{12,8},{16,20},{20,16},{24,28},{28,24},{1,5},{5... | collective-permute-start | bytes 98312 | tf_op jit(solution)/shard_map/ppermute | solution.py:638
  26.9 3.6 %copy-start.1 = (f32[2048]{0:T(1024)S(1)}, f32[2048]{0:T(1024)}, u32[]{:S(2)}) copy-start(f32[2048]{0:T(1024)} %param.13) | copy-start | bytes 24580
  26.9 3.0 %collective-permute-start.8 = (f32[1,256]{1,0:T(1,128)S(1)}, f32[1,256]{1,0:T(1,128)S(1)}, u32[]{:S(2)}, u32[]{:S(2)}) collective-permute-start(f32[1,256]{1,0:T(1,128)S(1)} %get-tuple-element.55.refs_2_), channel_id=1, source_target_pairs={{0,3},{1,2},{2,1},{3,0},{4,7},{5,6},{6,5},{7,4},{8,11},{9,10},{10,... | collective-permute-start | bytes 3080 | tf_op jit(solution)/shard_map/ppermute | solution.py:649
  26.9 3.6 %collective-permute-start.7 = (f32[1,256]{1,0:T(1,128)S(1)}, f32[1,256]{1,0:T(1,128)S(1)}, u32[]{:S(2)}, u32[]{:S(2)}) collective-permute-start(f32[1,256]{1,0:T(1,128)S(1)} %get-tuple-element.55.refs_2_), channel_id=1, source_target_pairs={{0,2},{1,3},{2,0},{3,1},{4,6},{5,7},{6,4},{7,5},{8,10},{9,11},{10,... | collective-permute-start | bytes 3080 | tf_op jit(solution)/shard_map/ppermute | solution.py:649
  28.7 1.8 %collective-permute-start.6 = (f32[1,256]{1,0:T(1,128)S(1)}, f32[1,256]{1,0:T(1,128)S(1)}, u32[]{:S(2)}, u32[]{:S(2)}) collective-permute-start(f32[1,256]{1,0:T(1,128)S(1)} %get-tuple-element.55.refs_2_), channel_id=1, source_target_pairs={{0,1},{1,0},{2,3},{3,2},{4,5},{5,4},{6,7},{7,6},{8,9},{9,8},{10,11... | collective-permute-start | bytes 3080 | tf_op jit(solution)/shard_map/ppermute | solution.py:649

commit v7 on v5

--- a/solution.py
+++ b/solution.py
@@ -124,11 +124,16 @@
     projected_ref,
     weight_hbm,
     rate_hbm,
+    residue_hbm,
+    residual_hbm,
     product_ref,
     state_ref,
     mode_rate_ref,
     head_ref,
     weight_ref,
+    query_ref,
+    residue_ref,
+    residual_ref,
     buffer_ref,
     ending_ref,
     shift_ref,
@@ -144,6 +149,11 @@
     weight_copy = pltpu.make_async_copy(weight_hbm, short_ref, small_sems.at[1])
     weight_copy.start()
     copies = [pltpu.make_async_copy(projected_ref.at[1 + c], buffer_ref.at[c], sems.at[c]) for c in (0, 1)]
+    later = [
+        pltpu.make_async_copy(residue_hbm, residue_ref, sems.at[2]),
+        pltpu.make_async_copy(projected_ref.at[0], query_ref, sems.at[3]),
+        pltpu.make_async_copy(residual_hbm, residual_ref, sems.at[4]),
+    ]
     for copy in copies:
         copy.start()
     shift_ref[...] = shift_matrix(rows)
@@ -169,6 +179,8 @@
     mask = group_mask(F32)
     for copy in copies:
         copy.wait()
+    for copy in later:
+        copy.start()
 
     def fetch(wide):
         return [earlier_tokens(shift_ref[...], buffer_ref[c, :, lanes_of(wide, WIDE)]) for c in (0, 1)]
@@ -189,6 +201,8 @@
             state_ref[:, lanes_of((WIDE // LANES) * wide + half)] = jnp.sum(own * mask, axis=0)
 
     pipelined(wides, fetch, multiply, leave)
+    for copy in later:
+        copy.wait()
 
 
 def halo(before_ref, place_ref):
@@ -208,9 +222,8 @@
 
 def prepare_kernel(
     place_ref,
-    projected_ref,
-    residual_hbm,
-    residue_hbm,
+    query_ref,
+    residue_ref,
     before_ref,
     weight_ref,
     mode_rate_ref,
@@ -218,21 +231,10 @@
     entering_ref,
     carry_ref,
     gate_ref,
-    residual_ref,
-    query_ref,
     shift_ref,
-    residue_ref,
-    sems,
 ):
     rows, width = gate_ref.shape
-    copies = [
-        pltpu.make_async_copy(residue_hbm, residue_ref, sems.at[0]),
-        pltpu.make_async_copy(projected_ref.at[0], query_ref, sems.at[1]),
-        pltpu.make_async_copy(residual_hbm, residual_ref, sems.at[2]),
-    ]
-    for copy in copies:
-        copy.start()
-    copies[0].wait()
+    shift_ref[...] = shift_matrix(rows)
     residue = per_channel(residue_ref[...])
     wide = GROUPS * CHUNK
     step = index_of((CHUNK, LANES), 0).astype(F32)
@@ -283,8 +285,6 @@
 
     pipelined(width // LANES, exponents, products, finish)
     before = halo(before_ref, place_ref)
-    copies[1].wait()
-    shift_ref[...] = shift_matrix(rows)
 
     def fetch(part):
         return (earlier_tokens(shift_ref[...], query_ref[:, lanes_of(part, WIDE)]),)
@@ -297,7 +297,6 @@
         gate_ref[0:8, here] = short_conv(head, before[0, :, here], weights)
 
     pipelined(width // WIDE, fetch, convolve)
-    copies[2].wait()
 
 
 def local_kernel(
@@ -371,15 +370,15 @@
     total = decayed(own_ref[...].astype(F32), radix - 1 - run)
     for k, ref in enumerate(others, 1):
         other = ref[...].astype(F32)
-        found = found + jnp.where(run >= k, decayed(other, jnp.full((), k - 1, jnp.int32)), 0.0)
-        source = lax.rem(run - k + radix, radix)
+        source = partner(run, k, radix)
+        found = found + jnp.where(source < run, decayed(other, jnp.maximum(run - 1 - source, 0)), 0.0)
         total = total + decayed(other, radix - 1 - source)
     within = lax.rem(place_ref[0], stride).astype(F32) * float(tokens)
     found_ref[...] = entry_ref[...] + jnp.exp(-within * rate) * found
     group_ref[...] = total.astype(BF16)
 
 
-def carry_kernel(stride, place_ref, base_ref, gate_ref, carry_ref, mode_rate_ref, inner_entry_ref, *refs):
+def carry_kernel(stride, radix, place_ref, base_ref, gate_ref, carry_ref, mode_rate_ref, inner_entry_ref, *refs):
     entry_refs, (summed_ref, squares_ref) = refs[:-2], refs[-2:]
     rows, width = base_ref.shape
     run = place_ref[0] // stride
@@ -391,10 +390,12 @@
     def enter(tile):
         here = lanes_of(tile, WIDE)
         rate = mode_rate_ref[:, here]
-        decay = jnp.exp(-float(rows * stride) * rate)
+        step = float(rows * stride)
         outer = jnp.zeros_like(rate)
-        for k in range(len(entry_refs), 0, -1):
-            outer = decay * outer + jnp.where(run >= k, entry_refs[k - 1][:, here].astype(F32), 0.0)
+        for k, ref in enumerate(entry_refs[::-1], 1):
+            source = partner(run, k, radix)
+            lag = jnp.maximum(run - 1 - source, 0).astype(F32) * step
+            outer = outer + jnp.where(source < run, jnp.exp(-lag * rate) * ref[:, here].astype(F32), 0.0)
         entry = (inner_entry_ref[:, here] + jnp.exp(-within * rate) * outer).astype(BF16)
         left, right = spread(entry[:, :LANES], mask), spread(entry[:, LANES:], mask)
         both = jnp.concatenate(
@@ -412,10 +413,9 @@
     pipelined(width // WIDE, enter, add)
     total = totals[0]
     squares = lax.dot_general(
-        jnp.ones((8, LANES), F32),
-        total,
+        jnp.ones((8, 2 * LANES), BF16),
+        jnp.concatenate(split(total), axis=1),
         (((1,), (1,)), ((), ())),
-        precision=lax.Precision.HIGHEST,
         preferred_element_type=F32,
     )
     squares_ref[...] = squares[0:1]
@@ -464,15 +464,28 @@
 
 def radices(count):
     found = []
-    for radix in (2, 4, 4, 4):
-        if count % radix == 0 and count > 1:
-            found.append(radix)
-            count //= radix
-    for radix in (3, 2, 5, 7):
-        while count % radix == 0 and count > 1:
+    for radix in (2, 4, 4, 4, 3, 2, 5, 7):
+        if count % radix == 0:
             found.append(radix)
             count //= radix
     return found + ([count] if count > 1 else [])
+
+
+def partner(run, k, radix):
+    if radix & (radix - 1) == 0:
+        return run ^ k
+    return (run - k + radix) % radix
+
+
+def routes(count, stride, radix):
+    found = []
+    for k in range(1, radix):
+        route = []
+        for i in range(count):
+            run = i // stride % radix
+            route.append((i + (partner(run, k, radix) - run) * stride, i))
+        found.append(route)
+    return found
 
 
 def ring(count, shift):
@@ -502,15 +515,18 @@
 
     before = lax.ppermute(projected[:, rows - (taps - 1) :, :], "ctx", ring(peers, 1))
 
-    product, state, mode_rate, head, weights = pl.pallas_call(
+    product, state, mode_rate, head, weights, query, residue, residual_here = pl.pallas_call(
         state_kernel,
-        in_specs=[hbm_spec] * 3,
+        in_specs=[hbm_spec] * 5,
         out_shape=[
             bf16(rows, width),
             f32(MODES, width),
             f32(MODES, width),
             f32(2, 8, width),
             f32(*short_weight.shape),
+            bf16(rows, width),
+            f32(MODES, residues.shape[0]),
+            bf16(rows, width),
         ],
         scratch_shapes=[
             pltpu.VMEM((2, rows, width), BF16),
@@ -518,13 +534,13 @@
             pltpu.VMEM((2 * rows, rows), BF16),
             pltpu.VMEM(short_weight.shape, BF16),
             pltpu.VMEM((MODES, rates.shape[0]), F32),
-            pltpu.SemaphoreType.DMA((2,)),
+            pltpu.SemaphoreType.DMA((5,)),
             pltpu.SemaphoreType.DMA((2,)),
         ],
         compiler_params=params(),
         cost_estimate=cost(3),
         name="block_state",
-    )(kept(projected), kept(short_weight), kept(rates.T))
+    )(kept(projected), kept(short_weight), kept(rates.T), kept(residues.T), kept(residual))
 
     full_state, first = pl.pallas_call(
         lambda *refs: head_kernel(rows, *refs),
@@ -535,26 +551,20 @@
         name="head_tokens",
     )(place, before, head, weights, state, mode_rate)
 
-    inner, entering, carry_table, gate, residual_here = pl.pallas_call(
+    inner, entering, carry_table, gate = pl.pallas_call(
         prepare_kernel,
-        in_specs=[smem_spec] + [hbm_spec] * 3 + [vmem_spec] * 3,
+        in_specs=[smem_spec] + [vmem_spec] * 5,
         out_shape=[
             bf16(tiles, CHUNK + MODES, GROUPS * CHUNK),
             bf16(tiles, CHUNK, LANES),
             bf16(wides, rows, WIDE),
             f32(rows, width),
-            bf16(rows, width),
         ],
-        scratch_shapes=[
-            pltpu.VMEM((rows, width), BF16),
-            pltpu.VMEM((2 * rows, rows), BF16),
-            pltpu.VMEM((MODES, rates.shape[0]), F32),
-            pltpu.SemaphoreType.DMA((3,)),
-        ],
+        scratch_shapes=[pltpu.VMEM((2 * rows, rows), BF16)],
         compiler_params=params(),
         cost_estimate=cost(2),
         name="prepare",
-    )(place, kept(projected), kept(residual), kept(residues.T), before, weights, mode_rate)
+    )(place, query, residue, before, weights, mode_rate)
 
     group, entry, stride = full_state, jnp.zeros((MODES, width), F32), 1
     levels = radices(peers)
@@ -562,10 +572,7 @@
         size = stride * radix
         if level == len(levels) - 1:
             break
-        cycles = [
-            [(i, i // size * size + (i + stride * k) % size) for i in range(peers)] for k in range(1, radix)
-        ]
-        others = [lax.ppermute(group, "ctx", cycle) for cycle in cycles]
+        others = [lax.ppermute(group, "ctx", route) for route in routes(peers, stride, radix)]
         if level == 0:
             others[0], inner = lax.optimization_barrier((others[0], inner))
         entry, group = pl.pallas_call(
@@ -577,7 +584,7 @@
             name="join",
         )(place, group, mode_rate, entry, *others)
         stride = size
-    received = [lax.ppermute(group, "ctx", ring(peers, stride * k)) for k in range(1, levels[-1])]
+    received = [lax.ppermute(group, "ctx", route) for route in routes(peers, stride, levels[-1])[::-1]]
 
     base = pl.pallas_call(
         local_kernel,
@@ -589,7 +596,7 @@
 
     count = lax.axis_size("fsdp")
     summed, squares = pl.pallas_call(
-        lambda *refs: carry_kernel(stride, *refs),
+        lambda *refs: carry_kernel(stride, levels[-1], *refs),
         in_specs=[smem_spec] + [vmem_spec] * (5 + len(received)),
         out_shape=[f32(rows, width), f32(1, rows)],
         compiler_params=params(),
@@ -597,7 +604,7 @@
         name="add_carry",
     )(place, base, gate, carry_table, mode_rate, entry, *received)
 
-    parts = [lax.ppermute(squares, "fsdp", ring(count, k)) for k in range(1, count)]
+    parts = [lax.ppermute(squares, "fsdp", route) for route in routes(count, 1, count)[::-1]]
 
     def write(kernel, operands, name):
         return pl.pallas_call(

time: 28.4 us -> 27.8 us (0.979)
  waiting for transfers between devices: 3.22 us -> 4.94 us
  starting transfers between devices: 10.8 us -> 9.59 us
  Pallas kernels: 12.4 us -> 11.4 us
    ppermute x7, waiting for transfers between devices: 1.81 us -> 3.58 us  [the longest x4 2.86 us: per_device(): lax.ppermute(group, 'ctx', route)]
    ppermute x7, starting transfers between devices: 7.84 us -> 6.59 us  [the longest x4 4.72 us: per_device(): lax.ppermute(group, 'ctx', route)]
    pallas_call x3, Pallas kernels: 7.43 us -> 6.42 us  [the longest x1 3.46 us: per_device(): pl.pallas_call(state_kernel, in_specs=[hbm_spec] * 5, out_shape=[bf16(row...]
  transfers between devices with their start and end apart: 8 -> 8, of which waited for: 4 -> 5; matrix products, arithmetic and copies ran while one was open for 0% -> 0% of each run, Pallas kernels for 36% -> 33%
where the time goes in v7:
time: 27.8 us; the launch traced here: 27.6 us
  Pallas kernels  11.4 us (41%)
  starting transfers between devices  9.59 us (34%)
  waiting for transfers between devices  4.94 us (18%)
  local copies, waits for them, and re-layouts  0.94 us (3%)
  between operations  0.7 us (3%)
    ppermute x4, starting transfers between devices, per_device(): lax.ppermute(group, 'ctx', route)  4.72 us
    pallas_call x1, Pallas kernels, per_device(): pl.pallas_call(state_kernel, in_specs=[hbm_spec] * 5, out_shape=[bf16(row...  3.46 us
    ppermute x1, starting transfers between devices, per_device(): lax.ppermute(projected[:, rows - (taps - 1):, :], 'ctx', ring(peers, 1))  2.99 us
    ppermute x4, waiting for transfers between devices, per_device(): lax.ppermute(group, 'ctx', route)  2.86 us
    pallas_call x1, Pallas kernels, per_device(): pl.pallas_call(local_kernel, out_shape=f32(rows, width), compiler_params=...  2.42 us
    pallas_call x2, Pallas kernels, write(): pl.pallas_call(kernel, out_specs=hbm_spec, out_shape=bf16(rows, width), s...  2.32 us
    pallas_call x1, Pallas kernels, per_device(): pl.pallas_call(prepare_kernel, in_specs=[smem_spec] + [vmem_spec] * 5, ou...  2.22 us
    ppermute x3, starting transfers between devices, per_device(): lax.ppermute(squares, 'fsdp', route)  1.87 us
  transfers between devices with their start and end apart: 8, of which 5 were waited for; matrix products, arithmetic and copies ran while one was open for 0% of the time, Pallas kernels for 33%

profile of v7, /device:TPU:0, one launch (start us, length us, event | category | flops | bytes accessed | tf_op | source)
XLA Modules:
  0.0 27.6 jit_solution(9823365034341142599)
XLA Ops:
  0.6 0.9 %slice.3 = bf16[3,2,2048]{2,1,0:T(2,128)(2,1)S(1)} slice(bf16[3,256,2048]{2,1,0:T(8,128)(2,1)} %projected_ref.1), slice={[0:3], [254:256], [0:2048]} | slice | bytes 49152 | tf_op jit(solution)/shard_map/slice | solution.py:516
  1.6 3.0 %collective-permute-start = (bf16[3,2,2048]{2,1,0:T(2,128)(2,1)S(1)}, bf16[3,2,2048]{2,1,0:T(2,128)(2,1)S(1)}, u32[]{:S(2)}, u32[]{:S(2)}) collective-permute-start(bf16[3,2,2048]{2,1,0:T(2,128)(2,1)S(1)} %slice.3), channel_id=1, source_target_pairs={{0,4},{4,8},{8,12},{12,16},{16,20},{20,24},{24,28},{28,0},{1,5},{5... | collective-permute-start | bytes 73736 | tf_op jit(solution)/shard_map/ppermute | solution.py:516
  4.5 3.5 %block_state.1 = (bf16[256,2048]{1,0:T(8,128)(2,1)S(1)}, f32[16,2048]{1,0:T(8,128)S(1)}, f32[16,2048]{1,0:T(8,128)S(1)}, f32[2,8,2048]{2,1,0:T(8,128)S(1)}, f32[...) custom-call(bf16[3,256,2048]{2,1,0:T(8,128)(2,1)} %projected_ref.1, ...), custom_call_target="tpu_custom_call" | custom-call | bytes 9000000 | tf_op jit(solution)/shard_map/block_state/pallas_call | solution.py:518
  8.0 0.0 copy-start
  8.0 1.4 %collective-permute-done.before_ref.refs_1_ = bf16[3,2,2048]{2,1,0:T(2,128)(2,1)S(1)} collective-permute-done((bf16[3,2,2048]{2,1,0:T(2,128)(2,1)S(1)}, bf16[3,2,2048]{2,1,0:T(2,128)(2,1)S(1)}, u32[]{:S(2)}, u32[]{:S(2)}) %collective-permute-start) | collective-permute-done | bytes 24608 | tf_op jit(solution)/shard_map/ppermute | solution.py:516
  9.4 0.1 head_tokens.1
  9.5 0.3 collective-permute-start.1
  9.8 2.2 %prepare.1 = (bf16[16,48,256]{2,1,0:T(8,128)(2,1)S(1)}, bf16[16,32,128]{2,1,0:T(8,128)(2,1)S(1)}, bf16[8,256,256]{2,1,0:T(8,128)(2,1)S(1)}, f32[256,2048]{1,0:T(8,128)S(1)}) custom-call(s32[1]{0:T(128)} %bitcast.place_ref.refs_0_, bf16[256,2048]{1,0:T(8,128)(2,1)S(1)} %get-tuple-element.22.query_ref, f32[16,128]{1,0:T(8,128)S(1)} %get-tuple-element.23.residue_ref, ...), custom_call_target="tpu_custom_call" | custom-call | bytes 6000000 | tf_op jit(solution)/shard_map/prepare/pallas_call | solution.py:554
  12.0 1.8 %collective-permute-done.1.refs_4_ = bf16[16,2048]{1,0:T(8,128)(2,1)S(1)} collective-permute-done((bf16[16,2048]{1,0:T(8,128)(2,1)S(1)}, bf16[16,2048]{1,0:T(8,128)(2,1)S(1)}, u32[]{:S(2)}, u32[]{:S(2)}) %collective-permute-start.1) | collective-permute-done | bytes 65568 | tf_op jit(solution)/shard_map/ppermute | solution.py:575
  13.9 0.1 join.1
  14.0 2.3 %collective-permute-start.2 = (bf16[16,2048]{1,0:T(8,128)(2,1)S(1)}, bf16[16,2048]{1,0:T(8,128)(2,1)S(1)}, u32[]{:S(2)}, u32[]{:S(2)}) collective-permute-start(bf16[16,2048]{1,0:T(8,128)(2,1)S(1)} %get-tuple-element.39), channel_id=1, source_target_pairs={{24,0},{28,4},{16,8},{20,12},{8,16},{12,20},{0,24},{4,28},{25,1},{... | collective-permute-start | bytes 196616 | tf_op jit(solution)/shard_map/ppermute | solution.py:587
  16.3 0.0 collective-permute-start.3
  16.3 2.1 %collective-permute-start.4 = (bf16[16,2048]{1,0:T(8,128)(2,1)S(1)}, bf16[16,2048]{1,0:T(8,128)(2,1)S(1)}, u32[]{:S(2)}, u32[]{:S(2)}) collective-permute-start(bf16[16,2048]{1,0:T(8,128)(2,1)S(1)} %get-tuple-element.39), channel_id=1, source_target_pairs={{8,0},{12,4},{0,8},{4,12},{24,16},{28,20},{16,24},{20,28},{9,1},{1... | collective-permute-start | bytes 196616 | tf_op jit(solution)/shard_map/ppermute | solution.py:587
  18.4 0.0 copy-done
  18.4 2.4 %local_conv.1.refs_1_ = f32[256,2048]{1,0:T(8,128)S(1)} custom-call(f32[256,2048]{1,0:T(8,128)S(1)} %get-tuple-element.26.gate_ref.refs_2_, bf16[256,2048]{1,0:T(8,128)(2,1)S(1)} %get-tuple-element.27.residual_ref, bf16[256,2048]{1,0:T(8,128)(2,1)S(1)} %get-tuple-element.28.product_ref, f32[8,2048]{1,0:T(8,128)S(1)} %get-tuple-element.31.first_ref, ...), custom_call_target="tpu_custom_call" | custom-call | bytes 15000000 | tf_op jit(solution)/shard_map/local_conv/pallas_call | solution.py:589
  20.9 0.0 collective-permute-done.2.refs_6_
  20.9 1.0 %collective-permute-done.3.refs_7_ = bf16[16,2048]{1,0:T(8,128)(2,1)S(1)} collective-permute-done((bf16[16,2048]{1,0:T(8,128)(2,1)S(1)}, bf16[16,2048]{1,0:T(8,128)(2,1)S(1)}, u32[]{:S(2)}, u32[]{:S(2)}) %collective-permute-start.3) | collective-permute-done | bytes 65568 | tf_op jit(solution)/shard_map/ppermute | solution.py:587
  21.9 0.0 collective-permute-done.4.refs_8_
  21.9 0.7 %add_carry.1 = (f32[256,2048]{1,0:T(8,128)S(1)}, f32[1,256]{1,0:T(1,128)S(1)}) custom-call(s32[1]{0:T(128)} %bitcast.place_ref.refs_0_, f32[256,2048]{1,0:T(8,128)S(1)} %local_conv.1.refs_1_, f32[256,2048]{1,0:T(8,128)S(1)} %get-tuple-element.26.gate_ref.refs_2_, bf16[8,256,256]{2,1,0:T(8,128)(2,1)S(1)} %get-tuple-element.36.refs_3_, ...), custom_call_target="tpu_custom_call" | custom-call | bytes 3000000 | tf_op jit(solution)/shard_map/add_carry/pallas_call | solution.py:598
  22.6 0.0 copy-start.1
  22.6 0.0 collective-permute-start.5
  22.7 1.6 %collective-permute-start.6 = (f32[1,256]{1,0:T(1,128)S(1)}, f32[1,256]{1,0:T(1,128)S(1)}, u32[]{:S(2)}, u32[]{:S(2)}) collective-permute-start(f32[1,256]{1,0:T(1,128)S(1)} %get-tuple-element.41.refs_2_), channel_id=1, source_target_pairs={{2,0},{3,1},{0,2},{1,3},{6,4},{7,5},{4,6},{5,7},{10,8},{11,9},{8,1... | collective-permute-start | bytes 3080 | tf_op jit(solution)/shard_map/ppermute | solution.py:607
  24.2 0.3 %collective-permute-start.7 = (f32[1,256]{1,0:T(1,128)S(1)}, f32[1,256]{1,0:T(1,128)S(1)}, u32[]{:S(2)}, u32[]{:S(2)}) collective-permute-start(f32[1,256]{1,0:T(1,128)S(1)} %get-tuple-element.41.refs_2_), channel_id=1, source_target_pairs={{1,0},{0,1},{3,2},{2,3},{5,4},{4,5},{7,6},{6,7},{9,8},{8,9},{11,10... | collective-permute-start | bytes 3080 | tf_op jit(solution)/shard_map/ppermute | solution.py:607
  24.5 1.0 %new_residual.1 = bf16[256,2048]{1,0:T(8,128)(2,1)} custom-call(f32[256,2048]{1,0:T(8,128)S(1)} %get-tuple-element.40.summed_ref.refs_0_), custom_call_target="tpu_custom_call" | custom-call | bytes 3000000 | tf_op jit(solution)/shard_map/new_residual/pallas_call | solution.py:610
  25.6 0.1 collective-permute-done.5.refs_3_
  25.7 0.6 %collective-permute-done.6.refs_4_ = f32[1,256]{1,0:T(1,128)S(1)} collective-permute-done((f32[1,256]{1,0:T(1,128)S(1)}, f32[1,256]{1,0:T(1,128)S(1)}, u32[]{:S(2)}, u32[]{:S(2)}) %collective-permute-start.6) | collective-permute-done | bytes 1056 | tf_op jit(solution)/shard_map/ppermute | solution.py:607
  26.3 0.0 collective-permute-done.7.refs_5_
  26.3 0.0 copy-done.1
  26.3 1.3 %normed.1 = bf16[256,2048]{1,0:T(8,128)(2,1)} custom-call(f32[256,2048]{1,0:T(8,128)S(1)} %get-tuple-element.40.summed_ref.refs_0_, f32[1,2048]{1,0:T(1,128)S(1)} %bitcast.6, f32[1,256]{1,0:T(1,128)S(1)} %get-tuple-element.41.refs_2_, f32[1,256]{1,0:T(1,128)S(1)} %collective-permute-done.5.refs_3_, f32[1,256]{1,0:T(1,128)S(1)} %collective-permute-done.6.refs_4_, ...), custom_call_target="tpu_custom_call" | custom-call | bytes 3000000 | tf_op jit(solution)/shard_map/normed/pallas_call | solution.py:610
  (1 shorter events, 0.0 us)
Async XLA Ops:
  1.6 7.8 %collective-permute-start = (bf16[3,2,2048]{2,1,0:T(2,128)(2,1)S(1)}, bf16[3,2,2048]{2,1,0:T(2,128)(2,1)S(1)}, u32[]{:S(2)}, u32[]{:S(2)}) collective-permute-start(bf16[3,2,2048]{2,1,0:T(2,128)(2,1)S(1)} %slice.3), channel_id=1, source_target_pairs={{0,4},{4,8},{8,12},{12,16},{16,20},{20,24},{24,28},{28,0},{1,5},{5... | collective-permute-start | bytes 73736 | tf_op jit(solution)/shard_map/ppermute | solution.py:516
  8.0 10.4 %copy-start = (f32[2048]{0:T(1024)S(1)}, f32[2048]{0:T(1024)}, u32[]{:S(2)}) copy-start(f32[2048]{0:T(1024)} %param.11) | copy-start | bytes 24580
  9.5 4.3 %collective-permute-start.1 = (bf16[16,2048]{1,0:T(8,128)(2,1)S(1)}, bf16[16,2048]{1,0:T(8,128)(2,1)S(1)}, u32[]{:S(2)}, u32[]{:S(2)}) collective-permute-start(bf16[16,2048]{1,0:T(8,128)(2,1)S(1)} %get-tuple-element.32.refs_1_), channel_id=1, source_target_pairs={{4,0},{0,4},{12,8},{8,12},{20,16},{16,20},{28,24},{24,28},{5,1},{1... | collective-permute-start | bytes 196616 | tf_op jit(solution)/shard_map/ppermute | solution.py:575
  14.0 6.9 %collective-permute-start.2 = (bf16[16,2048]{1,0:T(8,128)(2,1)S(1)}, bf16[16,2048]{1,0:T(8,128)(2,1)S(1)}, u32[]{:S(2)}, u32[]{:S(2)}) collective-permute-start(bf16[16,2048]{1,0:T(8,128)(2,1)S(1)} %get-tuple-element.39), channel_id=1, source_target_pairs={{24,0},{28,4},{16,8},{20,12},{8,16},{12,20},{0,24},{4,28},{25,1},{... | collective-permute-start | bytes 196616 | tf_op jit(solution)/shard_map/ppermute | solution.py:587
  16.3 5.6 %collective-permute-start.3 = (bf16[16,2048]{1,0:T(8,128)(2,1)S(1)}, bf16[16,2048]{1,0:T(8,128)(2,1)S(1)}, u32[]{:S(2)}, u32[]{:S(2)}) collective-permute-start(bf16[16,2048]{1,0:T(8,128)(2,1)S(1)} %get-tuple-element.39), channel_id=1, source_target_pairs={{16,0},{20,4},{24,8},{28,12},{0,16},{4,20},{8,24},{12,28},{17,1},{... | collective-permute-start | bytes 196616 | tf_op jit(solution)/shard_map/ppermute | solution.py:587
  16.3 5.6 %collective-permute-start.4 = (bf16[16,2048]{1,0:T(8,128)(2,1)S(1)}, bf16[16,2048]{1,0:T(8,128)(2,1)S(1)}, u32[]{:S(2)}, u32[]{:S(2)}) collective-permute-start(bf16[16,2048]{1,0:T(8,128)(2,1)S(1)} %get-tuple-element.39), channel_id=1, source_target_pairs={{8,0},{12,4},{0,8},{4,12},{24,16},{28,20},{16,24},{20,28},{9,1},{1... | collective-permute-start | bytes 196616 | tf_op jit(solution)/shard_map/ppermute | solution.py:587
  22.6 3.6 %copy-start.1 = (f32[2048]{0:T(1024)S(1)}, f32[2048]{0:T(1024)}, u32[]{:S(2)}) copy-start(f32[2048]{0:T(1024)} %param.13) | copy-start | bytes 24580
  22.6 3.0 %collective-permute-start.5 = (f32[1,256]{1,0:T(1,128)S(1)}, f32[1,256]{1,0:T(1,128)S(1)}, u32[]{:S(2)}, u32[]{:S(2)}) collective-permute-start(f32[1,256]{1,0:T(1,128)S(1)} %get-tuple-element.41.refs_2_), channel_id=1, source_target_pairs={{3,0},{2,1},{1,2},{0,3},{7,4},{6,5},{5,6},{4,7},{11,8},{10,9},{9,1... | collective-permute-start | bytes 3080 | tf_op jit(solution)/shard_map/ppermute | solution.py:607
  22.7 3.6 %collective-permute-start.6 = (f32[1,256]{1,0:T(1,128)S(1)}, f32[1,256]{1,0:T(1,128)S(1)}, u32[]{:S(2)}, u32[]{:S(2)}) collective-permute-start(f32[1,256]{1,0:T(1,128)S(1)} %get-tuple-element.41.refs_2_), channel_id=1, source_target_pairs={{2,0},{3,1},{0,2},{1,3},{6,4},{7,5},{4,6},{5,7},{10,8},{11,9},{8,1... | collective-permute-start | bytes 3080 | tf_op jit(solution)/shard_map/ppermute | solution.py:607
  24.2 2.1 %collective-permute-start.7 = (f32[1,256]{1,0:T(1,128)S(1)}, f32[1,256]{1,0:T(1,128)S(1)}, u32[]{:S(2)}, u32[]{:S(2)}) collective-permute-start(f32[1,256]{1,0:T(1,128)S(1)} %get-tuple-element.41.refs_2_), channel_id=1, source_target_pairs={{1,0},{0,1},{3,2},{2,3},{5,4},{4,5},{7,6},{6,7},{9,8},{8,9},{11,10... | collective-permute-start | bytes 3080 | tf_op jit(solution)/shard_map/ppermute | solution.py:607

commit v8 on v7

--- a/solution.py
+++ b/solution.py
@@ -100,20 +100,20 @@
 
 
 def shift_matrix(rows):
-    shape = (2 * rows, rows)
-    target = index_of(shape, 0)
-    source = index_of(shape, 1)
-    taken = jnp.where(target < rows, target - 1, target - (rows + 2))
-    return jnp.where(source == taken, 1.0, 0.0).astype(BF16)
-
-
-def earlier_tokens(shift, block):
+    own = index_of((rows, rows), 1) == index_of((rows, rows), 0) - 2
+    return jnp.where(own, 1.0, 0.0).astype(BF16)
+
+
+def two_later(shift, block):
     return jnp.dot(shift, block, preferred_element_type=F32)
 
 
-def wide_conv(block, earlier, weights):
-    rows = block.shape[0]
-    return weights[0] * block.astype(F32) + weights[1] * earlier[:rows] + weights[2] * earlier[rows:]
+def wide_conv(block, two, weights):
+    wide = block.astype(F32)
+    one = pltpu.roll(wide, 1, 0)
+    head = jnp.where(index_of((8, wide.shape[1]), 0) == 0, 0.0, one[:8])
+    one = jnp.concatenate([head, one[8:]], axis=0)
+    return weights[0] * wide + weights[1] * one + weights[2] * two
 
 
 def taps_of(weights, feature, lanes):
@@ -148,11 +148,20 @@
     rate_copy.start()
     weight_copy = pltpu.make_async_copy(weight_hbm, short_ref, small_sems.at[1])
     weight_copy.start()
-    copies = [pltpu.make_async_copy(projected_ref.at[1 + c], buffer_ref.at[c], sems.at[c]) for c in (0, 1)]
+    part = width // 2
+    copies = [
+        pltpu.make_async_copy(
+            projected_ref.at[1 + c, :, pl.ds(side * part, part)],
+            buffer_ref.at[c, :, pl.ds(side * part, part)],
+            sems.at[2 * side + c],
+        )
+        for side in (0, 1)
+        for c in (0, 1)
+    ]
     later = [
-        pltpu.make_async_copy(residue_hbm, residue_ref, sems.at[2]),
-        pltpu.make_async_copy(projected_ref.at[0], query_ref, sems.at[3]),
-        pltpu.make_async_copy(residual_hbm, residual_ref, sems.at[4]),
+        pltpu.make_async_copy(residue_hbm, residue_ref, sems.at[4]),
+        pltpu.make_async_copy(projected_ref.at[0], query_ref, sems.at[5]),
+        pltpu.make_async_copy(residual_hbm, residual_ref, sems.at[6]),
     ]
     for copy in copies:
         copy.start()
@@ -161,8 +170,8 @@
     mode_rate = per_channel(rate_ref[...])
     mode_rate_ref[...] = mode_rate
     eye = own_mode(BF16)
-    token = index_of((2 * LANES, rows), 1)
-    left = jnp.where(token < 2, -1e30, (token - (rows - 1)).astype(F32)).astype(BF16)
+    side = rows // 2
+    left = (index_of((2 * LANES, side), 1) - (side - 1)).astype(F32).astype(BF16)
 
     def exponents(tile):
         high, low = split(mode_rate[:, lanes_of(tile)])
@@ -177,28 +186,38 @@
     weights = short_ref[...].astype(F32)
     weight_ref[...] = weights
     mask = group_mask(F32)
-    for copy in copies:
-        copy.wait()
-    for copy in later:
-        copy.start()
+    middle = jnp.exp(-float(side) * mode_rate)
 
     def fetch(wide):
-        return [earlier_tokens(shift_ref[...], buffer_ref[c, :, lanes_of(wide, WIDE)]) for c in (0, 1)]
-
-    def multiply(wide, *earlier):
+        if wide % (wides // 2) == 0:
+            first = 2 * (wide // (wides // 2))
+            for copy in copies[first : first + 2]:
+                copy.wait()
+            if first > 0:
+                for copy in later:
+                    copy.start()
+        return [two_later(shift_ref[...], buffer_ref[c, :, lanes_of(wide, WIDE)]) for c in (0, 1)]
+
+    def multiply(wide, *later_two):
         here = lanes_of(wide, WIDE)
         parts = []
         for c in (0, 1):
             head_ref[c, :, here] = buffer_ref[c, 0:16, here].astype(F32)[:8]
-            parts.append(wide_conv(buffer_ref[c, :, here], earlier[c], taps_of(weights, c + 1, here)))
+            parts.append(wide_conv(buffer_ref[c, :, here], later_two[c], taps_of(weights, c + 1, here)))
         product = (parts[0] * parts[1]).astype(BF16)
         product_ref[:, here] = product
-        return (jnp.dot(ending_ref[wide], product, preferred_element_type=F32),)
+        head_ref[2, :, here] = product[:16].astype(F32)[:8]
+        sides = jnp.concatenate([product[:side], product[side:]], axis=1)
+        return (jnp.dot(ending_ref[wide], sides, preferred_element_type=F32),)
 
     def leave(wide, every):
         for half in range(WIDE // LANES):
-            own = every[lanes_of(half), lanes_of(half)].reshape(GROUPS, MODES, LANES)
-            state_ref[:, lanes_of((WIDE // LANES) * wide + half)] = jnp.sum(own * mask, axis=0)
+            there = lanes_of((WIDE // LANES) * wide + half)
+            early, late = [
+                jnp.sum(every[lanes_of(half), lanes_of(k)].reshape(GROUPS, MODES, LANES) * mask, axis=0)
+                for k in (half, WIDE // LANES + half)
+            ]
+            state_ref[:, there] = middle[:, there] * early + late
 
     pipelined(wides, fetch, multiply, leave)
     for copy in later:
@@ -216,7 +235,8 @@
     first = (parts[0] * parts[1]).astype(BF16).astype(F32)
     first_ref[...] = first
     rate = mode_rate_ref[...]
-    early = jnp.exp(-float(rows - 1) * rate) * first[0:1] + jnp.exp(-float(rows - 2) * rate) * first[1:2]
+    missing = first - head_ref[2]
+    early = jnp.exp(-float(rows - 1) * rate) * missing[0:1] + jnp.exp(-float(rows - 2) * rate) * missing[1:2]
     full_ref[...] = (state_ref[...] + early).astype(BF16)
 
 
@@ -287,7 +307,7 @@
     before = halo(before_ref, place_ref)
 
     def fetch(part):
-        return (earlier_tokens(shift_ref[...], query_ref[:, lanes_of(part, WIDE)]),)
+        return (two_later(shift_ref[...], query_ref[:, lanes_of(part, WIDE)]),)
 
     def convolve(part, earlier):
         here = lanes_of(part, WIDE)
@@ -443,12 +463,14 @@
     scale_row = lax.rsqrt(squares / full_width + 1e-05)
     scale = jnp.concatenate([as_column(scale_row[:, lanes_of(k)]) for k in range(rows // LANES)], axis=0)
     copies = []
-    for tile in range(width // WIDE):
-        for half in range(WIDE // LANES):
-            here = lanes_of(tile * (WIDE // LANES) + half)
-            rounded_ref[:, here] = (summed_ref[:, here] * scale * gain_ref[:, here]).astype(BF16)
-        span = pl.ds(tile * WIDE, WIDE)
-        copies.append(pltpu.make_async_copy(rounded_ref.at[:, span], out_hbm.at[:, span], sems.at[tile]))
+    block = rows // 8
+    for start in range(0, rows, block):
+        span = slice(start, start + block)
+        for tile in range(width // LANES):
+            here = lanes_of(tile)
+            rounded_ref[span, here] = (summed_ref[span, here] * scale[span] * gain_ref[:, here]).astype(BF16)
+        there = pl.ds(start, block)
+        copies.append(pltpu.make_async_copy(rounded_ref.at[there, :], out_hbm.at[there, :], sems.at[start // block]))
         copies[-1].start()
     for copy in copies:
         copy.wait()
@@ -522,7 +544,7 @@
             bf16(rows, width),
             f32(MODES, width),
             f32(MODES, width),
-            f32(2, 8, width),
+            f32(3, 8, width),
             f32(*short_weight.shape),
             bf16(rows, width),
             f32(MODES, residues.shape[0]),
@@ -530,11 +552,11 @@
         ],
         scratch_shapes=[
             pltpu.VMEM((2, rows, width), BF16),
-            pltpu.VMEM((wides, WIDE, rows), BF16),
-            pltpu.VMEM((2 * rows, rows), BF16),
+            pltpu.VMEM((wides, WIDE, rows // 2), BF16),
+            pltpu.VMEM((rows, rows), BF16),
             pltpu.VMEM(short_weight.shape, BF16),
             pltpu.VMEM((MODES, rates.shape[0]), F32),
-            pltpu.SemaphoreType.DMA((5,)),
+            pltpu.SemaphoreType.DMA((7,)),
             pltpu.SemaphoreType.DMA((2,)),
         ],
         compiler_params=params(),
@@ -560,7 +582,7 @@
             bf16(wides, rows, WIDE),
             f32(rows, width),
         ],
-        scratch_shapes=[pltpu.VMEM((2 * rows, rows), BF16)],
+        scratch_shapes=[pltpu.VMEM((rows, rows), BF16)],
         compiler_params=params(),
         cost_estimate=cost(2),
         name="prepare",
@@ -611,7 +633,7 @@
             kernel,
             out_specs=hbm_spec,
             out_shape=bf16(rows, width),
-            scratch_shapes=[pltpu.VMEM((rows, width), BF16), pltpu.SemaphoreType.DMA((wides,))],
+            scratch_shapes=[pltpu.VMEM((rows, width), BF16), pltpu.SemaphoreType.DMA((max(8, wides),))],
             compiler_params=params(),
             cost_estimate=cost(1),
             name=name,

time: 27.8 us -> 28.1 us (1.011)
  waiting for transfers between devices: 4.94 us -> 3.73 us
  starting transfers between devices: 9.59 us -> 10.4 us
  Pallas kernels: 11.4 us -> 12.1 us
    pallas_call x1, Pallas kernels: 3.46 us -> 4.28 us  [per_device(): pl.pallas_call(state_kernel, in_specs=[hbm_spec] * 5, out_shape=[bf16(row...]
    ppermute x1, waiting for transfers between devices: 1.36 us -> 0.55 us  [per_device(): lax.ppermute(projected[:, rows - (taps - 1):, :], 'ctx', ring(peers, 1))]
    ppermute x4, starting transfers between devices: 4.72 us -> 5.54 us  [per_device(): lax.ppermute(group, 'ctx', route)]
    ppermute x4, waiting for transfers between devices: 2.86 us -> 2.47 us  [per_device(): lax.ppermute(group, 'ctx', route)]
  transfers between devices with their start and end apart: 8 -> 8, of which waited for: 5 -> 5; matrix products, arithmetic and copies ran while one was open for 0% -> 0% of each run, Pallas kernels for 33% -> 36%
where the time goes in v8:
time: 28.1 us; the launch traced here: 27.9 us
  Pallas kernels  12.1 us (43%)
  starting transfers between devices  10.4 us (37%)
  waiting for transfers between devices  3.73 us (13%)
  local copies, waits for them, and re-layouts  0.94 us (3%)
  between operations  0.7 us (2%)
    ppermute x4, starting transfers between devices, per_device(): lax.ppermute(group, 'ctx', route)  5.54 us
    pallas_call x1, Pallas kernels, per_device(): pl.pallas_call(state_kernel, in_specs=[hbm_spec] * 5, out_shape=[bf16(row...  4.28 us
    ppermute x1, starting transfers between devices, per_device(): lax.ppermute(projected[:, rows - (taps - 1):, :], 'ctx', ring(peers, 1))  2.99 us
    ppermute x4, waiting for transfers between devices, per_device(): lax.ppermute(group, 'ctx', route)  2.47 us
    pallas_call x1, Pallas kernels, per_device(): pl.pallas_call(local_kernel, out_shape=f32(rows, width), compiler_params=...  2.43 us
    pallas_call x2, Pallas kernels, write(): pl.pallas_call(kernel, out_specs=hbm_spec, out_shape=bf16(rows, width), s...  2.21 us
    pallas_call x1, Pallas kernels, per_device(): pl.pallas_call(prepare_kernel, in_specs=[smem_spec] + [vmem_spec] * 5, ou...  2.18 us
    ppermute x3, starting transfers between devices, per_device(): lax.ppermute(squares, 'fsdp', route)  1.87 us
  transfers between devices with their start and end apart: 8, of which 5 were waited for; matrix products, arithmetic and copies ran while one was open for 0% of the time, Pallas kernels for 36%

profile of v8, /device:TPU:0, one launch (start us, length us, event | category | flops | bytes accessed | tf_op | source)
XLA Modules:
  0.0 27.9 jit_solution(4383528261474518757)
XLA Ops:
  0.6 0.9 %slice.3 = bf16[3,2,2048]{2,1,0:T(2,128)(2,1)S(1)} slice(bf16[3,256,2048]{2,1,0:T(8,128)(2,1)} %projected_ref.1), slice={[0:3], [254:256], [0:2048]} | slice | bytes 49152 | tf_op jit(solution)/shard_map/slice | solution.py:538
  1.6 3.0 %collective-permute-start = (bf16[3,2,2048]{2,1,0:T(2,128)(2,1)S(1)}, bf16[3,2,2048]{2,1,0:T(2,128)(2,1)S(1)}, u32[]{:S(2)}, u32[]{:S(2)}) collective-permute-start(bf16[3,2,2048]{2,1,0:T(2,128)(2,1)S(1)} %slice.3), channel_id=1, source_target_pairs={{0,4},{4,8},{8,12},{12,16},{16,20},{20,24},{24,28},{28,0},{1,5},{5... | collective-permute-start | bytes 73736 | tf_op jit(solution)/shard_map/ppermute | solution.py:538
  4.5 4.3 %block_state.1 = (bf16[256,2048]{1,0:T(8,128)(2,1)S(1)}, f32[16,2048]{1,0:T(8,128)S(1)}, f32[16,2048]{1,0:T(8,128)S(1)}, f32[3,8,2048]{2,1,0:T(8,128)S(1)}, f32[...) custom-call(bf16[3,256,2048]{2,1,0:T(8,128)(2,1)} %projected_ref.1, ...), custom_call_target="tpu_custom_call" | custom-call | bytes 9000000 | tf_op jit(solution)/shard_map/block_state/pallas_call | solution.py:540
  8.8 0.0 copy-start
  8.8 0.5 %collective-permute-done.before_ref.refs_1_ = bf16[3,2,2048]{2,1,0:T(2,128)(2,1)S(1)} collective-permute-done((bf16[3,2,2048]{2,1,0:T(2,128)(2,1)S(1)}, bf16[3,2,2048]{2,1,0:T(2,128)(2,1)S(1)}, u32[]{:S(2)}, u32[]{:S(2)}) %collective-permute-start) | collective-permute-done | bytes 24608 | tf_op jit(solution)/shard_map/ppermute | solution.py:538
  9.4 0.1 head_tokens.1
  9.5 1.1 %collective-permute-start.1 = (bf16[16,2048]{1,0:T(8,128)(2,1)S(1)}, bf16[16,2048]{1,0:T(8,128)(2,1)S(1)}, u32[]{:S(2)}, u32[]{:S(2)}) collective-permute-start(bf16[16,2048]{1,0:T(8,128)(2,1)S(1)} %get-tuple-element.32.refs_1_), channel_id=1, source_target_pairs={{4,0},{0,4},{12,8},{8,12},{20,16},{16,20},{28,24},{24,28},{5,1},{1... | collective-permute-start | bytes 196616 | tf_op jit(solution)/shard_map/ppermute | solution.py:597
  10.6 2.2 %prepare.1 = (bf16[16,48,256]{2,1,0:T(8,128)(2,1)S(1)}, bf16[16,32,128]{2,1,0:T(8,128)(2,1)S(1)}, bf16[8,256,256]{2,1,0:T(8,128)(2,1)S(1)}, f32[256,2048]{1,0:T(8,128)S(1)}) custom-call(s32[1]{0:T(128)} %bitcast.place_ref.refs_0_, bf16[256,2048]{1,0:T(8,128)(2,1)S(1)} %get-tuple-element.22.query_ref, f32[16,128]{1,0:T(8,128)S(1)} %get-tuple-element.23.residue_ref, ...), custom_call_target="tpu_custom_call" | custom-call | bytes 6000000 | tf_op jit(solution)/shard_map/prepare/pallas_call | solution.py:576
  12.8 1.1 %collective-permute-done.1.refs_4_ = bf16[16,2048]{1,0:T(8,128)(2,1)S(1)} collective-permute-done((bf16[16,2048]{1,0:T(8,128)(2,1)S(1)}, bf16[16,2048]{1,0:T(8,128)(2,1)S(1)}, u32[]{:S(2)}, u32[]{:S(2)}) %collective-permute-start.1) | collective-permute-done | bytes 65568 | tf_op jit(solution)/shard_map/ppermute | solution.py:597
  13.9 0.1 join.1
  14.0 3.1 %collective-permute-start.2 = (bf16[16,2048]{1,0:T(8,128)(2,1)S(1)}, bf16[16,2048]{1,0:T(8,128)(2,1)S(1)}, u32[]{:S(2)}, u32[]{:S(2)}) collective-permute-start(bf16[16,2048]{1,0:T(8,128)(2,1)S(1)} %get-tuple-element.39), channel_id=1, source_target_pairs={{24,0},{28,4},{16,8},{20,12},{8,16},{12,20},{0,24},{4,28},{25,1},{... | collective-permute-start | bytes 196616 | tf_op jit(solution)/shard_map/ppermute | solution.py:609
  17.1 0.0 collective-permute-start.3
  17.1 1.3 %collective-permute-start.4 = (bf16[16,2048]{1,0:T(8,128)(2,1)S(1)}, bf16[16,2048]{1,0:T(8,128)(2,1)S(1)}, u32[]{:S(2)}, u32[]{:S(2)}) collective-permute-start(bf16[16,2048]{1,0:T(8,128)(2,1)S(1)} %get-tuple-element.39), channel_id=1, source_target_pairs={{8,0},{12,4},{0,8},{4,12},{24,16},{28,20},{16,24},{20,28},{9,1},{1... | collective-permute-start | bytes 196616 | tf_op jit(solution)/shard_map/ppermute | solution.py:609
  18.4 0.0 copy-done
  18.4 2.4 %local_conv.1.refs_1_ = f32[256,2048]{1,0:T(8,128)S(1)} custom-call(f32[256,2048]{1,0:T(8,128)S(1)} %get-tuple-element.26.gate_ref.refs_2_, bf16[256,2048]{1,0:T(8,128)(2,1)S(1)} %get-tuple-element.27.residual_ref, bf16[256,2048]{1,0:T(8,128)(2,1)S(1)} %get-tuple-element.28.product_ref, f32[8,2048]{1,0:T(8,128)S(1)} %get-tuple-element.31.first_ref, ...), custom_call_target="tpu_custom_call" | custom-call | bytes 15000000 | tf_op jit(solution)/shard_map/local_conv/pallas_call | solution.py:611
  20.9 0.0 collective-permute-done.2.refs_6_
  20.9 1.4 %collective-permute-done.3.refs_7_ = bf16[16,2048]{1,0:T(8,128)(2,1)S(1)} collective-permute-done((bf16[16,2048]{1,0:T(8,128)(2,1)S(1)}, bf16[16,2048]{1,0:T(8,128)(2,1)S(1)}, u32[]{:S(2)}, u32[]{:S(2)}) %collective-permute-start.3) | collective-permute-done | bytes 65568 | tf_op jit(solution)/shard_map/ppermute | solution.py:609
  22.3 0.0 collective-permute-done.4.refs_8_
  22.3 0.7 %add_carry.1 = (f32[256,2048]{1,0:T(8,128)S(1)}, f32[1,256]{1,0:T(1,128)S(1)}) custom-call(s32[1]{0:T(128)} %bitcast.place_ref.refs_0_, f32[256,2048]{1,0:T(8,128)S(1)} %local_conv.1.refs_1_, f32[256,2048]{1,0:T(8,128)S(1)} %get-tuple-element.26.gate_ref.refs_2_, bf16[8,256,256]{2,1,0:T(8,128)(2,1)S(1)} %get-tuple-element.36.refs_3_, ...), custom_call_target="tpu_custom_call" | custom-call | bytes 3000000 | tf_op jit(solution)/shard_map/add_carry/pallas_call | solution.py:620
  23.0 0.0 copy-start.1
  23.0 0.0 collective-permute-start.5
  23.0 1.7 %collective-permute-start.6 = (f32[1,256]{1,0:T(1,128)S(1)}, f32[1,256]{1,0:T(1,128)S(1)}, u32[]{:S(2)}, u32[]{:S(2)}) collective-permute-start(f32[1,256]{1,0:T(1,128)S(1)} %get-tuple-element.41.refs_2_), channel_id=1, source_target_pairs={{2,0},{3,1},{0,2},{1,3},{6,4},{7,5},{4,6},{5,7},{10,8},{11,9},{8,1... | collective-permute-start | bytes 3080 | tf_op jit(solution)/shard_map/ppermute | solution.py:629
  24.7 0.2 collective-permute-start.7
  24.9 1.0 %new_residual.1 = bf16[256,2048]{1,0:T(8,128)(2,1)} custom-call(f32[256,2048]{1,0:T(8,128)S(1)} %get-tuple-element.40.summed_ref.refs_0_), custom_call_target="tpu_custom_call" | custom-call | bytes 3000000 | tf_op jit(solution)/shard_map/new_residual/pallas_call | solution.py:632
  26.0 0.1 collective-permute-done.5.refs_3_
  26.0 0.6 %collective-permute-done.6.refs_4_ = f32[1,256]{1,0:T(1,128)S(1)} collective-permute-done((f32[1,256]{1,0:T(1,128)S(1)}, f32[1,256]{1,0:T(1,128)S(1)}, u32[]{:S(2)}, u32[]{:S(2)}) %collective-permute-start.6) | collective-permute-done | bytes 1056 | tf_op jit(solution)/shard_map/ppermute | solution.py:629
  26.7 0.0 collective-permute-done.7.refs_5_
  26.7 0.0 copy-done.1
  26.7 1.2 %normed.1 = bf16[256,2048]{1,0:T(8,128)(2,1)} custom-call(f32[256,2048]{1,0:T(8,128)S(1)} %get-tuple-element.40.summed_ref.refs_0_, f32[1,2048]{1,0:T(1,128)S(1)} %bitcast.6, f32[1,256]{1,0:T(1,128)S(1)} %get-tuple-element.41.refs_2_, f32[1,256]{1,0:T(1,128)S(1)} %collective-permute-done.5.refs_3_, f32[1,256]{1,0:T(1,128)S(1)} %collective-permute-done.6.refs_4_, ...), custom_call_target="tpu_custom_call" | custom-call | bytes 3000000 | tf_op jit(solution)/shard_map/normed/pallas_call | solution.py:632
  (1 shorter events, 0.0 us)
Async XLA Ops:
  1.6 7.8 %collective-permute-start = (bf16[3,2,2048]{2,1,0:T(2,128)(2,1)S(1)}, bf16[3,2,2048]{2,1,0:T(2,128)(2,1)S(1)}, u32[]{:S(2)}, u32[]{:S(2)}) collective-permute-start(bf16[3,2,2048]{2,1,0:T(2,128)(2,1)S(1)} %slice.3), channel_id=1, source_target_pairs={{0,4},{4,8},{8,12},{12,16},{16,20},{20,24},{24,28},{28,0},{1,5},{5... | collective-permute-start | bytes 73736 | tf_op jit(solution)/shard_map/ppermute | solution.py:538
  8.8 9.6 %copy-start = (f32[2048]{0:T(1024)S(1)}, f32[2048]{0:T(1024)}, u32[]{:S(2)}) copy-start(f32[2048]{0:T(1024)} %param.11) | copy-start | bytes 24580
  9.5 4.3 %collective-permute-start.1 = (bf16[16,2048]{1,0:T(8,128)(2,1)S(1)}, bf16[16,2048]{1,0:T(8,128)(2,1)S(1)}, u32[]{:S(2)}, u32[]{:S(2)}) collective-permute-start(bf16[16,2048]{1,0:T(8,128)(2,1)S(1)} %get-tuple-element.32.refs_1_), channel_id=1, source_target_pairs={{4,0},{0,4},{12,8},{8,12},{20,16},{16,20},{28,24},{24,28},{5,1},{1... | collective-permute-start | bytes 196616 | tf_op jit(solution)/shard_map/ppermute | solution.py:597
  14.0 6.9 %collective-permute-start.2 = (bf16[16,2048]{1,0:T(8,128)(2,1)S(1)}, bf16[16,2048]{1,0:T(8,128)(2,1)S(1)}, u32[]{:S(2)}, u32[]{:S(2)}) collective-permute-start(bf16[16,2048]{1,0:T(8,128)(2,1)S(1)} %get-tuple-element.39), channel_id=1, source_target_pairs={{24,0},{28,4},{16,8},{20,12},{8,16},{12,20},{0,24},{4,28},{25,1},{... | collective-permute-start | bytes 196616 | tf_op jit(solution)/shard_map/ppermute | solution.py:609
  17.1 5.2 %collective-permute-start.3 = (bf16[16,2048]{1,0:T(8,128)(2,1)S(1)}, bf16[16,2048]{1,0:T(8,128)(2,1)S(1)}, u32[]{:S(2)}, u32[]{:S(2)}) collective-permute-start(bf16[16,2048]{1,0:T(8,128)(2,1)S(1)} %get-tuple-element.39), channel_id=1, source_target_pairs={{16,0},{20,4},{24,8},{28,12},{0,16},{4,20},{8,24},{12,28},{17,1},{... | collective-permute-start | bytes 196616 | tf_op jit(solution)/shard_map/ppermute | solution.py:609
  17.1 5.2 %collective-permute-start.4 = (bf16[16,2048]{1,0:T(8,128)(2,1)S(1)}, bf16[16,2048]{1,0:T(8,128)(2,1)S(1)}, u32[]{:S(2)}, u32[]{:S(2)}) collective-permute-start(bf16[16,2048]{1,0:T(8,128)(2,1)S(1)} %get-tuple-element.39), channel_id=1, source_target_pairs={{8,0},{12,4},{0,8},{4,12},{24,16},{28,20},{16,24},{20,28},{9,1},{1... | collective-permute-start | bytes 196616 | tf_op jit(solution)/shard_map/ppermute | solution.py:609
  23.0 3.6 %copy-start.1 = (f32[2048]{0:T(1024)S(1)}, f32[2048]{0:T(1024)}, u32[]{:S(2)}) copy-start(f32[2048]{0:T(1024)} %param.13) | copy-start | bytes 24580
  23.0 3.0 %collective-permute-start.5 = (f32[1,256]{1,0:T(1,128)S(1)}, f32[1,256]{1,0:T(1,128)S(1)}, u32[]{:S(2)}, u32[]{:S(2)}) collective-permute-start(f32[1,256]{1,0:T(1,128)S(1)} %get-tuple-element.41.refs_2_), channel_id=1, source_target_pairs={{3,0},{2,1},{1,2},{0,3},{7,4},{6,5},{5,6},{4,7},{11,8},{10,9},{9,1... | collective-permute-start | bytes 3080 | tf_op jit(solution)/shard_map/ppermute | solution.py:629
  23.0 3.6 %collective-permute-start.6 = (f32[1,256]{1,0:T(1,128)S(1)}, f32[1,256]{1,0:T(1,128)S(1)}, u32[]{:S(2)}, u32[]{:S(2)}) collective-permute-start(f32[1,256]{1,0:T(1,128)S(1)} %get-tuple-element.41.refs_2_), channel_id=1, source_target_pairs={{2,0},{3,1},{0,2},{1,3},{6,4},{7,5},{4,6},{5,7},{10,8},{11,9},{8,1... | collective-permute-start | bytes 3080 | tf_op jit(solution)/shard_map/ppermute | solution.py:629
  24.7 1.9 %collective-permute-start.7 = (f32[1,256]{1,0:T(1,128)S(1)}, f32[1,256]{1,0:T(1,128)S(1)}, u32[]{:S(2)}, u32[]{:S(2)}) collective-permute-start(f32[1,256]{1,0:T(1,128)S(1)} %get-tuple-element.41.refs_2_), channel_id=1, source_target_pairs={{1,0},{0,1},{3,2},{2,3},{5,4},{4,5},{7,6},{6,7},{9,8},{8,9},{11,10... | collective-permute-start | bytes 3080 | tf_op jit(solution)/shard_map/ppermute | solution.py:629

commit v9 on v8

--- a/solution.py
+++ b/solution.py
@@ -193,7 +193,7 @@
             first = 2 * (wide // (wides // 2))
             for copy in copies[first : first + 2]:
                 copy.wait()
-            if first > 0:
+            if first == 0:
                 for copy in later:
                     copy.start()
         return [two_later(shift_ref[...], buffer_ref[c, :, lanes_of(wide, WIDE)]) for c in (0, 1)]

time: 28.1 us -> 28.1 us (level)
  waiting for transfers between devices: 3.73 us -> 4.33 us
  Pallas kernels: 12.1 us -> 11.7 us
  starting transfers between devices: 10.4 us -> 10.1 us
    pallas_call x1, Pallas kernels: 4.28 us -> 3.93 us  [per_device(): pl.pallas_call(state_kernel, in_specs=[hbm_spec] * 5, out_shape=[bf16(row...]
    ppermute x1, waiting for transfers between devices: 0.55 us -> 0.9 us  [per_device(): lax.ppermute(projected[:, rows - (taps - 1):, :], 'ctx', ring(peers, 1))]
    ppermute x4, starting transfers between devices: 5.54 us -> 5.19 us  [per_device(): lax.ppermute(group, 'ctx', route)]
  transfers between devices with their start and end apart: 8 -> 8, of which waited for: 5 -> 5; matrix products, arithmetic and copies ran while one was open for 0% -> 0% of each run, Pallas kernels for 36% -> 34%
where the time goes in v9:
time: 28.1 us; the launch traced here: 27.8 us
  Pallas kernels  11.7 us (42%)
  starting transfers between devices  10.1 us (36%)
  waiting for transfers between devices  4.33 us (15%)
  local copies, waits for them, and re-layouts  0.94 us (3%)
  between operations  0.7 us (2%)
    ppermute x4, starting transfers between devices, per_device(): lax.ppermute(group, 'ctx', route)  5.19 us
    pallas_call x1, Pallas kernels, per_device(): pl.pallas_call(state_kernel, in_specs=[hbm_spec] * 5, out_shape=[bf16(row...  3.93 us
    ppermute x1, starting transfers between devices, per_device(): lax.ppermute(projected[:, rows - (taps - 1):, :], 'ctx', ring(peers, 1))  2.99 us
    ppermute x4, waiting for transfers between devices, per_device(): lax.ppermute(group, 'ctx', route)  2.75 us
    pallas_call x1, Pallas kernels, per_device(): pl.pallas_call(local_kernel, out_shape=f32(rows, width), compiler_params=...  2.43 us
    pallas_call x2, Pallas kernels, write(): pl.pallas_call(kernel, out_specs=hbm_spec, out_shape=bf16(rows, width), s...  2.21 us
    pallas_call x1, Pallas kernels, per_device(): pl.pallas_call(prepare_kernel, in_specs=[smem_spec] + [vmem_spec] * 5, ou...  2.18 us
    ppermute x3, starting transfers between devices, per_device(): lax.ppermute(squares, 'fsdp', route)  1.9 us
  transfers between devices with their start and end apart: 8, of which 5 were waited for; matrix products, arithmetic and copies ran while one was open for 0% of the time, Pallas kernels for 34%

profile of v9, /device:TPU:0, one launch (start us, length us, event | category | flops | bytes accessed | tf_op | source)
XLA Modules:
  0.0 27.8 jit_solution(4985036774802217544)
XLA Ops:
  0.6 0.9 %slice.3 = bf16[3,2,2048]{2,1,0:T(2,128)(2,1)S(1)} slice(bf16[3,256,2048]{2,1,0:T(8,128)(2,1)} %projected_ref.1), slice={[0:3], [254:256], [0:2048]} | slice | bytes 49152 | tf_op jit(solution)/shard_map/slice | solution.py:538
  1.6 3.0 %collective-permute-start = (bf16[3,2,2048]{2,1,0:T(2,128)(2,1)S(1)}, bf16[3,2,2048]{2,1,0:T(2,128)(2,1)S(1)}, u32[]{:S(2)}, u32[]{:S(2)}) collective-permute-start(bf16[3,2,2048]{2,1,0:T(2,128)(2,1)S(1)} %slice.3), channel_id=1, source_target_pairs={{0,4},{4,8},{8,12},{12,16},{16,20},{20,24},{24,28},{28,0},{1,5},{5... | collective-permute-start | bytes 73736 | tf_op jit(solution)/shard_map/ppermute | solution.py:538
  4.5 3.9 %block_state.1 = (bf16[256,2048]{1,0:T(8,128)(2,1)S(1)}, f32[16,2048]{1,0:T(8,128)S(1)}, f32[16,2048]{1,0:T(8,128)S(1)}, f32[3,8,2048]{2,1,0:T(8,128)S(1)}, f32[...) custom-call(bf16[3,256,2048]{2,1,0:T(8,128)(2,1)} %projected_ref.1, ...), custom_call_target="tpu_custom_call" | custom-call | bytes 9000000 | tf_op jit(solution)/shard_map/block_state/pallas_call | solution.py:540
  8.5 0.0 copy-start
  8.5 0.9 %collective-permute-done.before_ref.refs_1_ = bf16[3,2,2048]{2,1,0:T(2,128)(2,1)S(1)} collective-permute-done((bf16[3,2,2048]{2,1,0:T(2,128)(2,1)S(1)}, bf16[3,2,2048]{2,1,0:T(2,128)(2,1)S(1)}, u32[]{:S(2)}, u32[]{:S(2)}) %collective-permute-start) | collective-permute-done | bytes 24608 | tf_op jit(solution)/shard_map/ppermute | solution.py:538
  9.4 0.1 head_tokens.1
  9.5 0.7 %collective-permute-start.1 = (bf16[16,2048]{1,0:T(8,128)(2,1)S(1)}, bf16[16,2048]{1,0:T(8,128)(2,1)S(1)}, u32[]{:S(2)}, u32[]{:S(2)}) collective-permute-start(bf16[16,2048]{1,0:T(8,128)(2,1)S(1)} %get-tuple-element.32.refs_1_), channel_id=1, source_target_pairs={{4,0},{0,4},{12,8},{8,12},{20,16},{16,20},{28,24},{24,28},{5,1},{1... | collective-permute-start | bytes 196616 | tf_op jit(solution)/shard_map/ppermute | solution.py:597
  10.3 2.2 %prepare.1 = (bf16[16,48,256]{2,1,0:T(8,128)(2,1)S(1)}, bf16[16,32,128]{2,1,0:T(8,128)(2,1)S(1)}, bf16[8,256,256]{2,1,0:T(8,128)(2,1)S(1)}, f32[256,2048]{1,0:T(8,128)S(1)}) custom-call(s32[1]{0:T(128)} %bitcast.place_ref.refs_0_, bf16[256,2048]{1,0:T(8,128)(2,1)S(1)} %get-tuple-element.22.query_ref, f32[16,128]{1,0:T(8,128)S(1)} %get-tuple-element.23.residue_ref, ...), custom_call_target="tpu_custom_call" | custom-call | bytes 6000000 | tf_op jit(solution)/shard_map/prepare/pallas_call | solution.py:576
  12.4 1.4 %collective-permute-done.1.refs_4_ = bf16[16,2048]{1,0:T(8,128)(2,1)S(1)} collective-permute-done((bf16[16,2048]{1,0:T(8,128)(2,1)S(1)}, bf16[16,2048]{1,0:T(8,128)(2,1)S(1)}, u32[]{:S(2)}, u32[]{:S(2)}) %collective-permute-start.1) | collective-permute-done | bytes 65568 | tf_op jit(solution)/shard_map/ppermute | solution.py:597
  13.9 0.1 join.1
  14.0 2.8 %collective-permute-start.2 = (bf16[16,2048]{1,0:T(8,128)(2,1)S(1)}, bf16[16,2048]{1,0:T(8,128)(2,1)S(1)}, u32[]{:S(2)}, u32[]{:S(2)}) collective-permute-start(bf16[16,2048]{1,0:T(8,128)(2,1)S(1)} %get-tuple-element.39), channel_id=1, source_target_pairs={{24,0},{28,4},{16,8},{20,12},{8,16},{12,20},{0,24},{4,28},{25,1},{... | collective-permute-start | bytes 196616 | tf_op jit(solution)/shard_map/ppermute | solution.py:609
  16.8 0.0 collective-permute-start.3
  16.8 1.7 %collective-permute-start.4 = (bf16[16,2048]{1,0:T(8,128)(2,1)S(1)}, bf16[16,2048]{1,0:T(8,128)(2,1)S(1)}, u32[]{:S(2)}, u32[]{:S(2)}) collective-permute-start(bf16[16,2048]{1,0:T(8,128)(2,1)S(1)} %get-tuple-element.39), channel_id=1, source_target_pairs={{8,0},{12,4},{0,8},{4,12},{24,16},{28,20},{16,24},{20,28},{9,1},{1... | collective-permute-start | bytes 196616 | tf_op jit(solution)/shard_map/ppermute | solution.py:609
  18.4 0.0 copy-done
  18.4 2.4 %local_conv.1.refs_1_ = f32[256,2048]{1,0:T(8,128)S(1)} custom-call(f32[256,2048]{1,0:T(8,128)S(1)} %get-tuple-element.26.gate_ref.refs_2_, bf16[256,2048]{1,0:T(8,128)(2,1)S(1)} %get-tuple-element.27.residual_ref, bf16[256,2048]{1,0:T(8,128)(2,1)S(1)} %get-tuple-element.28.product_ref, f32[8,2048]{1,0:T(8,128)S(1)} %get-tuple-element.31.first_ref, ...), custom_call_target="tpu_custom_call" | custom-call | bytes 15000000 | tf_op jit(solution)/shard_map/local_conv/pallas_call | solution.py:611
  20.9 0.0 collective-permute-done.2.refs_6_
  20.9 1.3 %collective-permute-done.3.refs_7_ = bf16[16,2048]{1,0:T(8,128)(2,1)S(1)} collective-permute-done((bf16[16,2048]{1,0:T(8,128)(2,1)S(1)}, bf16[16,2048]{1,0:T(8,128)(2,1)S(1)}, u32[]{:S(2)}, u32[]{:S(2)}) %collective-permute-start.3) | collective-permute-done | bytes 65568 | tf_op jit(solution)/shard_map/ppermute | solution.py:609
  22.2 0.0 collective-permute-done.4.refs_8_
  22.2 0.7 %add_carry.1 = (f32[256,2048]{1,0:T(8,128)S(1)}, f32[1,256]{1,0:T(1,128)S(1)}) custom-call(s32[1]{0:T(128)} %bitcast.place_ref.refs_0_, f32[256,2048]{1,0:T(8,128)S(1)} %local_conv.1.refs_1_, f32[256,2048]{1,0:T(8,128)S(1)} %get-tuple-element.26.gate_ref.refs_2_, bf16[8,256,256]{2,1,0:T(8,128)(2,1)S(1)} %get-tuple-element.36.refs_3_, ...), custom_call_target="tpu_custom_call" | custom-call | bytes 3000000 | tf_op jit(solution)/shard_map/add_carry/pallas_call | solution.py:620
  23.0 0.0 copy-start.1
  23.0 0.0 collective-permute-start.5
  23.0 1.7 %collective-permute-start.6 = (f32[1,256]{1,0:T(1,128)S(1)}, f32[1,256]{1,0:T(1,128)S(1)}, u32[]{:S(2)}, u32[]{:S(2)}) collective-permute-start(f32[1,256]{1,0:T(1,128)S(1)} %get-tuple-element.41.refs_2_), channel_id=1, source_target_pairs={{2,0},{3,1},{0,2},{1,3},{6,4},{7,5},{4,6},{5,7},{10,8},{11,9},{8,1... | collective-permute-start | bytes 3080 | tf_op jit(solution)/shard_map/ppermute | solution.py:629
  24.7 0.1 collective-permute-start.7
  24.9 1.0 %new_residual.1 = bf16[256,2048]{1,0:T(8,128)(2,1)} custom-call(f32[256,2048]{1,0:T(8,128)S(1)} %get-tuple-element.40.summed_ref.refs_0_), custom_call_target="tpu_custom_call" | custom-call | bytes 3000000 | tf_op jit(solution)/shard_map/new_residual/pallas_call | solution.py:632
  25.9 0.1 collective-permute-done.5.refs_3_
  26.0 0.6 %collective-permute-done.6.refs_4_ = f32[1,256]{1,0:T(1,128)S(1)} collective-permute-done((f32[1,256]{1,0:T(1,128)S(1)}, f32[1,256]{1,0:T(1,128)S(1)}, u32[]{:S(2)}, u32[]{:S(2)}) %collective-permute-start.6) | collective-permute-done | bytes 1056 | tf_op jit(solution)/shard_map/ppermute | solution.py:629
  26.6 0.0 collective-permute-done.7.refs_5_
  26.6 0.0 copy-done.1
  26.6 1.2 %normed.1 = bf16[256,2048]{1,0:T(8,128)(2,1)} custom-call(f32[256,2048]{1,0:T(8,128)S(1)} %get-tuple-element.40.summed_ref.refs_0_, f32[1,2048]{1,0:T(1,128)S(1)} %bitcast.6, f32[1,256]{1,0:T(1,128)S(1)} %get-tuple-element.41.refs_2_, f32[1,256]{1,0:T(1,128)S(1)} %collective-permute-done.5.refs_3_, f32[1,256]{1,0:T(1,128)S(1)} %collective-permute-done.6.refs_4_, ...), custom_call_target="tpu_custom_call" | custom-call | bytes 3000000 | tf_op jit(solution)/shard_map/normed/pallas_call | solution.py:632
  (1 shorter events, 0.0 us)
Async XLA Ops:
  1.6 7.8 %collective-permute-start = (bf16[3,2,2048]{2,1,0:T(2,128)(2,1)S(1)}, bf16[3,2,2048]{2,1,0:T(2,128)(2,1)S(1)}, u32[]{:S(2)}, u32[]{:S(2)}) collective-permute-start(bf16[3,2,2048]{2,1,0:T(2,128)(2,1)S(1)} %slice.3), channel_id=1, source_target_pairs={{0,4},{4,8},{8,12},{12,16},{16,20},{20,24},{24,28},{28,0},{1,5},{5... | collective-permute-start | bytes 73736 | tf_op jit(solution)/shard_map/ppermute | solution.py:538
  8.5 10.0 %copy-start = (f32[2048]{0:T(1024)S(1)}, f32[2048]{0:T(1024)}, u32[]{:S(2)}) copy-start(f32[2048]{0:T(1024)} %param.11) | copy-start | bytes 24580
  9.5 4.3 %collective-permute-start.1 = (bf16[16,2048]{1,0:T(8,128)(2,1)S(1)}, bf16[16,2048]{1,0:T(8,128)(2,1)S(1)}, u32[]{:S(2)}, u32[]{:S(2)}) collective-permute-start(bf16[16,2048]{1,0:T(8,128)(2,1)S(1)} %get-tuple-element.32.refs_1_), channel_id=1, source_target_pairs={{4,0},{0,4},{12,8},{8,12},{20,16},{16,20},{28,24},{24,28},{5,1},{1... | collective-permute-start | bytes 196616 | tf_op jit(solution)/shard_map/ppermute | solution.py:597
  14.0 6.9 %collective-permute-start.2 = (bf16[16,2048]{1,0:T(8,128)(2,1)S(1)}, bf16[16,2048]{1,0:T(8,128)(2,1)S(1)}, u32[]{:S(2)}, u32[]{:S(2)}) collective-permute-start(bf16[16,2048]{1,0:T(8,128)(2,1)S(1)} %get-tuple-element.39), channel_id=1, source_target_pairs={{24,0},{28,4},{16,8},{20,12},{8,16},{12,20},{0,24},{4,28},{25,1},{... | collective-permute-start | bytes 196616 | tf_op jit(solution)/shard_map/ppermute | solution.py:609
  16.8 5.4 %collective-permute-start.3 = (bf16[16,2048]{1,0:T(8,128)(2,1)S(1)}, bf16[16,2048]{1,0:T(8,128)(2,1)S(1)}, u32[]{:S(2)}, u32[]{:S(2)}) collective-permute-start(bf16[16,2048]{1,0:T(8,128)(2,1)S(1)} %get-tuple-element.39), channel_id=1, source_target_pairs={{16,0},{20,4},{24,8},{28,12},{0,16},{4,20},{8,24},{12,28},{17,1},{... | collective-permute-start | bytes 196616 | tf_op jit(solution)/shard_map/ppermute | solution.py:609
  16.8 5.4 %collective-permute-start.4 = (bf16[16,2048]{1,0:T(8,128)(2,1)S(1)}, bf16[16,2048]{1,0:T(8,128)(2,1)S(1)}, u32[]{:S(2)}, u32[]{:S(2)}) collective-permute-start(bf16[16,2048]{1,0:T(8,128)(2,1)S(1)} %get-tuple-element.39), channel_id=1, source_target_pairs={{8,0},{12,4},{0,8},{4,12},{24,16},{28,20},{16,24},{20,28},{9,1},{1... | collective-permute-start | bytes 196616 | tf_op jit(solution)/shard_map/ppermute | solution.py:609
  23.0 3.6 %copy-start.1 = (f32[2048]{0:T(1024)S(1)}, f32[2048]{0:T(1024)}, u32[]{:S(2)}) copy-start(f32[2048]{0:T(1024)} %param.13) | copy-start | bytes 24580
  23.0 3.0 %collective-permute-start.5 = (f32[1,256]{1,0:T(1,128)S(1)}, f32[1,256]{1,0:T(1,128)S(1)}, u32[]{:S(2)}, u32[]{:S(2)}) collective-permute-start(f32[1,256]{1,0:T(1,128)S(1)} %get-tuple-element.41.refs_2_), channel_id=1, source_target_pairs={{3,0},{2,1},{1,2},{0,3},{7,4},{6,5},{5,6},{4,7},{11,8},{10,9},{9,1... | collective-permute-start | bytes 3080 | tf_op jit(solution)/shard_map/ppermute | solution.py:629
  23.0 3.6 %collective-permute-start.6 = (f32[1,256]{1,0:T(1,128)S(1)}, f32[1,256]{1,0:T(1,128)S(1)}, u32[]{:S(2)}, u32[]{:S(2)}) collective-permute-start(f32[1,256]{1,0:T(1,128)S(1)} %get-tuple-element.41.refs_2_), channel_id=1, source_target_pairs={{2,0},{3,1},{0,2},{1,3},{6,4},{7,5},{4,6},{5,7},{10,8},{11,9},{8,1... | collective-permute-start | bytes 3080 | tf_op jit(solution)/shard_map/ppermute | solution.py:629
  24.7 1.9 %collective-permute-start.7 = (f32[1,256]{1,0:T(1,128)S(1)}, f32[1,256]{1,0:T(1,128)S(1)}, u32[]{:S(2)}, u32[]{:S(2)}) collective-permute-start(f32[1,256]{1,0:T(1,128)S(1)} %get-tuple-element.41.refs_2_), channel_id=1, source_target_pairs={{1,0},{0,1},{3,2},{2,3},{5,4},{4,5},{7,6},{6,7},{9,8},{8,9},{11,10... | collective-permute-start | bytes 3080 | tf_op jit(solution)/shard_map/ppermute | solution.py:629

commit v10 on v7

--- a/solution.py
+++ b/solution.py
@@ -127,9 +127,9 @@
     residue_hbm,
     residual_hbm,
     product_ref,
-    state_ref,
+    swapped_ref,
     mode_rate_ref,
-    head_ref,
+    tail_ref,
     weight_ref,
     query_ref,
     residue_ref,
@@ -189,7 +189,6 @@
         here = lanes_of(wide, WIDE)
         parts = []
         for c in (0, 1):
-            head_ref[c, :, here] = buffer_ref[c, 0:16, here].astype(F32)[:8]
             parts.append(wide_conv(buffer_ref[c, :, here], earlier[c], taps_of(weights, c + 1, here)))
         product = (parts[0] * parts[1]).astype(BF16)
         product_ref[:, here] = product
@@ -198,33 +197,62 @@
     def leave(wide, every):
         for half in range(WIDE // LANES):
             own = every[lanes_of(half), lanes_of(half)].reshape(GROUPS, MODES, LANES)
-            state_ref[:, lanes_of((WIDE // LANES) * wide + half)] = jnp.sum(own * mask, axis=0)
+            there = lanes_of((WIDE // LANES) * wide + half)
+            swapped_ref[:MODES, there] = jnp.sum(own * mask, axis=0).astype(BF16)
 
     pipelined(wides, fetch, multiply, leave)
+    heads = [buffer_ref[c, 0:16, :].astype(F32)[:8] for c in (0, 1)]
+    swapped_ref[MODES:, :] = jnp.concatenate(heads, axis=0).astype(BF16)
     for copy in later:
         copy.wait()
-
-
-def halo(before_ref, place_ref):
-    return jnp.where(place_ref[0] > 0, before_ref[...].astype(F32), 0.0)
-
-
-def head_kernel(rows, place_ref, before_ref, head_ref, weight_ref, state_ref, mode_rate_ref, full_ref, first_ref):
-    before = halo(before_ref, place_ref)
-    everything = slice(0, head_ref.shape[2])
-    parts = [short_conv(head_ref[c], before[c + 1], taps_of(weight_ref, c + 1, everything)) for c in (0, 1)]
-    first = (parts[0] * parts[1]).astype(BF16).astype(F32)
-    first_ref[...] = first
+    for c, ref in enumerate((query_ref, buffer_ref.at[0], buffer_ref.at[1])):
+        tail_ref[c] = ref[rows - 16 : rows, :].astype(F32)[14:].astype(BF16)
+
+
+def pair_kernel(
+    tokens,
+    place_ref,
+    got_ref,
+    before_ref,
+    skipped_ref,
+    own_ref,
+    tail_ref,
+    query_ref,
+    weight_ref,
+    mode_rate_ref,
+    entry_ref,
+    group_ref,
+    first_ref,
+    gate_ref,
+):
+    odd = lax.rem(place_ref[0], 2) == 1
+    before = jnp.where(place_ref[0] > 0, before_ref[...].astype(F32), 0.0)
+    skipped = jnp.where(place_ref[0] > 1, skipped_ref[...].astype(F32), 0.0)
+    own, got = own_ref[...].astype(F32), got_ref[...].astype(F32)
+    everything = slice(0, own.shape[1])
     rate = mode_rate_ref[...]
-    early = jnp.exp(-float(rows - 1) * rate) * first[0:1] + jnp.exp(-float(rows - 2) * rate) * first[1:2]
-    full_ref[...] = (state_ref[...] + early).astype(BF16)
+    blocks = (
+        (jnp.where(odd, got, own), jnp.where(odd, skipped, before)),
+        (jnp.where(odd, own, got), jnp.where(odd, before, tail_ref[...].astype(F32))),
+    )
+    states, firsts = [], []
+    for block, halo in blocks:
+        heads = (block[MODES : MODES + 8], block[MODES + 8 :])
+        parts = [short_conv(heads[c], halo[c + 1], taps_of(weight_ref, c + 1, everything)) for c in (0, 1)]
+        first = (parts[0] * parts[1]).astype(BF16).astype(F32)
+        early = jnp.exp(-float(tokens - 1) * rate) * first[0:1] + jnp.exp(-float(tokens - 2) * rate) * first[1:2]
+        states.append(block[:MODES] + early)
+        firsts.append(first)
+    entry_ref[...] = jnp.where(odd, states[0], 0.0)
+    group_ref[...] = (jnp.exp(-float(tokens) * rate) * states[0] + states[1]).astype(BF16)
+    first_ref[...] = jnp.where(odd, firsts[1], firsts[0])
+    query = query_ref[0:16, :].astype(F32)[:8]
+    gate_ref[...] = short_conv(query, before[0], taps_of(weight_ref, 0, everything))
 
 
 def prepare_kernel(
-    place_ref,
     query_ref,
     residue_ref,
-    before_ref,
     weight_ref,
     mode_rate_ref,
     inner_ref,
@@ -284,7 +312,6 @@
         inner_ref[tile] = jnp.concatenate([taps.astype(BF16), ending.astype(BF16)], axis=0)
 
     pipelined(width // LANES, exponents, products, finish)
-    before = halo(before_ref, place_ref)
 
     def fetch(part):
         return (earlier_tokens(shift_ref[...], query_ref[:, lanes_of(part, WIDE)]),)
@@ -293,14 +320,17 @@
         here = lanes_of(part, WIDE)
         weights = taps_of(weight_ref, 0, here)
         gate_ref[:, here] = wide_conv(query_ref[:, here], earlier, weights)
-        head = query_ref[0:16, here].astype(F32)[:8]
-        gate_ref[0:8, here] = short_conv(head, before[0, :, here], weights)
 
     pipelined(width // WIDE, fetch, convolve)
+
+
+def with_head(block, head):
+    return jnp.concatenate([head, block[head.shape[0] :]], axis=0)
 
 
 def local_kernel(
     gate_ref,
+    gate_head_ref,
     residual_ref,
     product_ref,
     first_ref,
@@ -352,7 +382,10 @@
             piece = first if chunk == 0 else product_ref[span, here]
             conv = (inner[chunk // 2] + outer[chunk // 2])[:, lanes_of(chunk % 2)]
             whole = conv + skip * piece.astype(F32)
-            base_ref[span, here] = residual_ref[span, here].astype(F32) + gate_ref[span, here] * whole
+            gate = gate_ref[span, here]
+            if chunk == 0:
+                gate = with_head(gate, gate_head_ref[:, here])
+            base_ref[span, here] = residual_ref[span, here].astype(F32) + gate * whole
 
     pipelined(width // LANES, inside, across, finish)
 
@@ -378,7 +411,9 @@
     group_ref[...] = total.astype(BF16)
 
 
-def carry_kernel(stride, radix, place_ref, base_ref, gate_ref, carry_ref, mode_rate_ref, inner_entry_ref, *refs):
+def carry_kernel(
+    stride, radix, place_ref, base_ref, gate_ref, gate_head_ref, carry_ref, mode_rate_ref, inner_entry_ref, *refs
+):
     entry_refs, (summed_ref, squares_ref) = refs[:-2], refs[-2:]
     rows, width = base_ref.shape
     run = place_ref[0] // stride
@@ -405,7 +440,7 @@
 
     def add(tile, carry):
         here = lanes_of(tile, WIDE)
-        summed = base_ref[:, here] + gate_ref[:, here] * carry
+        summed = base_ref[:, here] + with_head(gate_ref[:, here], gate_head_ref[:, here]) * carry
         summed_ref[:, here] = summed
         square = summed * summed
         totals[0] = totals[0] + (square[:, :LANES] + square[:, LANES:])
@@ -443,12 +478,14 @@
     scale_row = lax.rsqrt(squares / full_width + 1e-05)
     scale = jnp.concatenate([as_column(scale_row[:, lanes_of(k)]) for k in range(rows // LANES)], axis=0)
     copies = []
-    for tile in range(width // WIDE):
-        for half in range(WIDE // LANES):
-            here = lanes_of(tile * (WIDE // LANES) + half)
-            rounded_ref[:, here] = (summed_ref[:, here] * scale * gain_ref[:, here]).astype(BF16)
-        span = pl.ds(tile * WIDE, WIDE)
-        copies.append(pltpu.make_async_copy(rounded_ref.at[:, span], out_hbm.at[:, span], sems.at[tile]))
+    block = rows // 8
+    for start in range(0, rows, block):
+        span = slice(start, start + block)
+        for tile in range(width // LANES):
+            here = lanes_of(tile)
+            rounded_ref[span, here] = (summed_ref[span, here] * scale[span] * gain_ref[:, here]).astype(BF16)
+        there = pl.ds(start, block)
+        copies.append(pltpu.make_async_copy(rounded_ref.at[there, :], out_hbm.at[there, :], sems.at[start // block]))
         copies[-1].start()
     for copy in copies:
         copy.wait()
@@ -513,16 +550,14 @@
     def bf16(*shape):
         return jax.ShapeDtypeStruct(shape, BF16)
 
-    before = lax.ppermute(projected[:, rows - (taps - 1) :, :], "ctx", ring(peers, 1))
-
-    product, state, mode_rate, head, weights, query, residue, residual_here = pl.pallas_call(
+    product, swapped, mode_rate, tail, weights, query, residue, residual_here = pl.pallas_call(
         state_kernel,
         in_specs=[hbm_spec] * 5,
         out_shape=[
             bf16(rows, width),
+            bf16(2 * MODES, width),
             f32(MODES, width),
-            f32(MODES, width),
-            f32(2, 8, width),
+            bf16(3, taps - 1, width),
             f32(*short_weight.shape),
             bf16(rows, width),
             f32(MODES, residues.shape[0]),
@@ -542,18 +577,14 @@
         name="block_state",
     )(kept(projected), kept(short_weight), kept(rates.T), kept(residues.T), kept(residual))
 
-    full_state, first = pl.pallas_call(
-        lambda *refs: head_kernel(rows, *refs),
-        in_specs=[smem_spec] + [vmem_spec] * 5,
-        out_shape=[bf16(MODES, width), f32(8, width)],
-        compiler_params=params(),
-        cost_estimate=cost(0.2),
-        name="head_tokens",
-    )(place, before, head, weights, state, mode_rate)
+    levels = radices(peers)
+    got = lax.ppermute(swapped, "ctx", routes(peers, 1, levels[0])[0])
+    before = lax.ppermute(tail, "ctx", ring(peers, 1))
+    skipped = lax.ppermute(tail, "ctx", ring(peers, 2))
 
     inner, entering, carry_table, gate = pl.pallas_call(
         prepare_kernel,
-        in_specs=[smem_spec] + [vmem_spec] * 5,
+        in_specs=[vmem_spec] * 4,
         out_shape=[
             bf16(tiles, CHUNK + MODES, GROUPS * CHUNK),
             bf16(tiles, CHUNK, LANES),
@@ -564,17 +595,21 @@
         compiler_params=params(),
         cost_estimate=cost(2),
         name="prepare",
-    )(place, query, residue, before, weights, mode_rate)
-
-    group, entry, stride = full_state, jnp.zeros((MODES, width), F32), 1
-    levels = radices(peers)
-    for level, radix in enumerate(levels):
-        size = stride * radix
-        if level == len(levels) - 1:
-            break
+    )(query, residue, weights, mode_rate)
+
+    got, inner = lax.optimization_barrier((got, inner))
+    entry, group, first, gate_head = pl.pallas_call(
+        lambda *refs: pair_kernel(rows, *refs),
+        in_specs=[smem_spec] + [vmem_spec] * 8,
+        out_shape=[f32(MODES, width), bf16(MODES, width), f32(8, width), f32(8, width)],
+        compiler_params=params(),
+        cost_estimate=cost(0.2),
+        name="pair",
+    )(place, got, before, skipped, swapped, tail, query, weights, mode_rate)
+
+    stride = levels[0]
+    for radix in levels[1:-1]:
         others = [lax.ppermute(group, "ctx", route) for route in routes(peers, stride, radix)]
-        if level == 0:
-            others[0], inner = lax.optimization_barrier((others[0], inner))
         entry, group = pl.pallas_call(
             lambda *refs, radix=radix, stride=stride: join_kernel(rows, radix, stride, *refs),
             in_specs=[smem_spec] + [vmem_spec] * (2 + radix),
@@ -583,7 +618,7 @@
             cost_estimate=cost(0.2),
             name="join",
         )(place, group, mode_rate, entry, *others)
-        stride = size
+        stride *= radix
     received = [lax.ppermute(group, "ctx", route) for route in routes(peers, stride, levels[-1])[::-1]]
 
     base = pl.pallas_call(
@@ -592,17 +627,17 @@
         compiler_params=params(),
         cost_estimate=cost(5),
         name="local_conv",
-    )(gate, residual_here, product, first, mode_rate, inner, entering, skip[None])
+    )(gate, gate_head, residual_here, product, first, mode_rate, inner, entering, skip[None])
 
     count = lax.axis_size("fsdp")
     summed, squares = pl.pallas_call(
         lambda *refs: carry_kernel(stride, levels[-1], *refs),
-        in_specs=[smem_spec] + [vmem_spec] * (5 + len(received)),
+        in_specs=[smem_spec] + [vmem_spec] * (6 + len(received)),
         out_shape=[f32(rows, width), f32(1, rows)],
         compiler_params=params(),
         cost_estimate=cost(1),
         name="add_carry",
-    )(place, base, gate, carry_table, mode_rate, entry, *received)
+    )(place, base, gate, gate_head, carry_table, mode_rate, entry, *received)
 
     parts = [lax.ppermute(squares, "fsdp", route) for route in routes(count, 1, count)[::-1]]
 
@@ -611,7 +646,7 @@
             kernel,
             out_specs=hbm_spec,
             out_shape=bf16(rows, width),
-            scratch_shapes=[pltpu.VMEM((rows, width), BF16), pltpu.SemaphoreType.DMA((wides,))],
+            scratch_shapes=[pltpu.VMEM((rows, width), BF16), pltpu.SemaphoreType.DMA((max(8, wides),))],
             compiler_params=params(),
             cost_estimate=cost(1),
             name=name,

time: 27.8 us -> 31.3 us (1.13)
  starting transfers between devices: 9.59 us -> 11.4 us
  Pallas kernels: 11.4 us -> 12.2 us
  waiting for transfers between devices: 4.94 us -> 5.42 us
  local copies, waits for them, and re-layouts: 0.94 us -> 1.3 us
    ppermute x4 -> x3, waiting for transfers between devices: 2.86 us -> 0.6 us  [per_device(): lax.ppermute(group, 'ctx', route)]
    ppermute x1 -> x3, starting transfers between devices: 2.99 us -> 5.05 us  [the longest x1 2.94 us: per_device(): got = lax.ppermute(swapped, 'ctx', routes(peers, 1, levels[0])[0])]
    ppermute x1 -> x3, waiting for transfers between devices: 1.36 us -> 3.18 us  [the longest x1 2.58 us: per_device(): before = lax.ppermute(tail, 'ctx', ring(peers, 1))]
    unnamed x4 -> x8, local copies, waits for them, and re-layouts: 0.01 us -> 1.3 us
    pallas_call x3 -> x2, Pallas kernels: 2.46 us -> 3.44 us  [the longest x1 2.2 us: per_device(): pl.pallas_call(prepare_kernel, in_specs=[vmem_spec] * 4, out_shape=[bf16(...]
    ppermute x3, waiting for transfers between devices: 0.71 us -> 1.65 us  [per_device(): lax.ppermute(squares, 'fsdp', route)]
    slice x1 -> x0, local copies, waits for them, and re-layouts: 0.92 us -> none  [per_device(): projected[:, rows - (taps - 1):, :]]
    ppermute x4 -> x3, starting transfers between devices: 4.72 us -> 4.44 us  [per_device(): lax.ppermute(group, 'ctx', route)]
  transfers between devices with their start and end apart: 8 -> 9, of which waited for: 5 -> 5; matrix products, arithmetic and copies ran while one was open for 0% -> 0% of each run, Pallas kernels for 33% -> 18%
where the time goes in v10:
time: 31.3 us; the launch traced here: 31 us
  Pallas kernels  12.2 us (39%)
  starting transfers between devices  11.4 us (36%)
  waiting for transfers between devices  5.42 us (17%)
  local copies, waits for them, and re-layouts  1.3 us (4%)
  between operations  0.72 us (2%)
    ppermute x3, starting transfers between devices, per_device(): lax.ppermute(group, 'ctx', route)  4.44 us
    pallas_call x1, Pallas kernels, per_device(): pl.pallas_call(state_kernel, in_specs=[hbm_spec] * 5, out_shape=[bf16(row...  3.45 us
    ppermute x1, starting transfers between devices, per_device(): got = lax.ppermute(swapped, 'ctx', routes(peers, 1, levels[0])[0])  2.94 us
    ppermute x1, waiting for transfers between devices, per_device(): before = lax.ppermute(tail, 'ctx', ring(peers, 1))  2.58 us
    pallas_call x1, Pallas kernels, per_device(): pl.pallas_call(local_kernel, out_shape=f32(rows, width), compiler_params=...  2.42 us
    pallas_call x2, Pallas kernels, write(): pl.pallas_call(kernel, out_specs=hbm_spec, out_shape=bf16(rows, width), s...  2.21 us
    pallas_call x1, Pallas kernels, per_device(): pl.pallas_call(prepare_kernel, in_specs=[vmem_spec] * 4, out_shape=[bf16(...  2.2 us
    ppermute x3, starting transfers between devices, per_device(): lax.ppermute(squares, 'fsdp', route)  1.87 us
  transfers between devices with their start and end apart: 9, of which 5 were waited for; matrix products, arithmetic and copies ran while one was open for 0% of the time, Pallas kernels for 18%

profile of v10, /device:TPU:0, one launch (start us, length us, event | category | flops | bytes accessed | tf_op | source)
XLA Modules:
  0.0 31.0 jit_solution(991551517084543750)
XLA Ops:
  0.6 3.4 %block_state.1 = (bf16[256,2048]{1,0:T(8,128)(2,1)S(1)}, bf16[32,2048]{1,0:T(8,128)(2,1)S(1)}, f32[16,2048]{1,0:T(8,128)S(1)}, bf16[3,2,2048]{2,1,0:T(2,128)(2,1...) custom-call(bf16[3,256,2048]{2,1,0:T(8,128)(2,1)} %projected_ref.1, ...), custom_call_target="tpu_custom_call" | custom-call | bytes 9000000 | tf_op jit(solution)/shard_map/block_state/pallas_call | solution.py:553
  4.1 0.0 copy-start.1
  4.1 0.6 %copy-done.1 = f32[16,128]{1,0:T(8,128)} copy-done((f32[16,128]{1,0:T(8,128)}, f32[16,128]{1,0:T(8,128)S(1)}, u32[]{:S(2)}) %copy-start.1) | copy-done | bytes 8216
  4.7 2.9 %collective-permute-start = (bf16[32,2048]{1,0:T(8,128)(2,1)S(1)}, bf16[32,2048]{1,0:T(8,128)(2,1)}, u32[]{:S(2)}, u32[]{:S(2)}) collective-permute-start(bf16[32,2048]{1,0:T(8,128)(2,1)S(1)} %get-tuple-element.27.refs_4_), channel_id=1, source_target_pairs={{4,0},{0,4},{12,8},{8,12},{20,16},{16,20},{28,24},{24,28},{5,1},{1... | collective-permute-start | bytes 393224 | tf_op jit(solution)/shard_map/ppermute | solution.py:581
  7.6 1.6 %collective-permute-start.2 = (bf16[3,2,2048]{2,1,0:T(2,128)(2,1)S(1)}, bf16[3,2,2048]{2,1,0:T(2,128)(2,1)S(1)}, u32[]{:S(2)}, u32[]{:S(2)}) collective-permute-start(bf16[3,2,2048]{2,1,0:T(2,128)(2,1)S(1)} %get-tuple-element.30.refs_5_), channel_id=1, source_target_pairs={{0,8},{4,12},{8,16},{12,20},{16,24},{20,28},{24,0},{28,4},{1,9},{5... | collective-permute-start | bytes 73736 | tf_op jit(solution)/shard_map/ppermute | solution.py:583
  9.2 0.5 %collective-permute-start.1 = (bf16[3,2,2048]{2,1,0:T(2,128)(2,1)S(1)}, bf16[3,2,2048]{2,1,0:T(2,128)(2,1)}, u32[]{:S(2)}, u32[]{:S(2)}) collective-permute-start(bf16[3,2,2048]{2,1,0:T(2,128)(2,1)S(1)} %get-tuple-element.30.refs_5_), channel_id=1, source_target_pairs={{0,4},{4,8},{8,12},{12,16},{16,20},{20,24},{24,28},{28,0},{1,5},{5... | collective-permute-start | bytes 73736 | tf_op jit(solution)/shard_map/ppermute | solution.py:582
  9.7 0.0 copy-start.2
  9.7 0.7 %copy-done.2 = f32[16,128]{1,0:T(8,128)S(1)} copy-done((f32[16,128]{1,0:T(8,128)S(1)}, f32[16,128]{1,0:T(8,128)}, u32[]{:S(2)}) %copy-start.2) | copy-done | bytes 8216
  10.4 0.0 copy-start.3
  10.4 2.2 %prepare.1 = (bf16[16,48,256]{2,1,0:T(8,128)(2,1)S(1)}, bf16[16,32,128]{2,1,0:T(8,128)(2,1)S(1)}, bf16[8,256,256]{2,1,0:T(8,128)(2,1)S(1)}, f32[256,2048]{1,0:T(8,128)S(1)}) custom-call(bf16[256,2048]{1,0:T(8,128)(2,1)S(1)} %get-tuple-element.22.query_ref.refs_6_, f32[16,128]{1,0:T(8,128)S(1)} %copy-done.2, ...), custom_call_target="tpu_custom_call" | custom-call | bytes 6000000 | tf_op jit(solution)/shard_map/prepare/pallas_call | solution.py:585
  12.6 0.0 collective-permute-done.refs_1_
  12.7 0.6 %collective-permute-done.2.refs_3_ = bf16[3,2,2048]{2,1,0:T(2,128)(2,1)S(1)} collective-permute-done((bf16[3,2,2048]{2,1,0:T(2,128)(2,1)S(1)}, bf16[3,2,2048]{2,1,0:T(2,128)(2,1)S(1)}, u32[]{:S(2)}, u32[]{:S(2)}) %collective-permute-start.2) | collective-permute-done | bytes 24608 | tf_op jit(solution)/shard_map/ppermute | solution.py:583
  13.3 2.6 %collective-permute-done.1.refs_2_ = bf16[3,2,2048]{2,1,0:T(2,128)(2,1)} collective-permute-done((bf16[3,2,2048]{2,1,0:T(2,128)(2,1)S(1)}, bf16[3,2,2048]{2,1,0:T(2,128)(2,1)}, u32[]{:S(2)}, u32[]{:S(2)}) %collective-permute-start.1) | collective-permute-done | bytes 24608 | tf_op jit(solution)/shard_map/ppermute | solution.py:582
  15.8 1.2 %pair.1 = (f32[16,2048]{1,0:T(8,128)S(1)}, bf16[16,2048]{1,0:T(8,128)(2,1)S(1)}, f32[8,2048]{1,0:T(8,128)S(1)}, f32[8,2048]{1,0:T(8,128)S(1)}) custom-call(s32[1]{0:T(128)} %bitcast.refs_0_, bf16[32,2048]{1,0:T(8,128)(2,1)} %collective-permute-done.refs_1_, bf16[3,2,2048]{2,1,0:T(2,128)(2,1)} %collective-permute-done.1.refs_2_, ...), custom_call_target="tpu_custom_call" | custom-call | bytes 600000 | tf_op jit(solution)/shard_map/pair/pallas_call | solution.py:601
  17.1 0.1 collective-permute-start.5
  17.2 1.0 %collective-permute-start.4 = (bf16[16,2048]{1,0:T(8,128)(2,1)S(1)}, bf16[16,2048]{1,0:T(8,128)(2,1)S(1)}, u32[]{:S(2)}, u32[]{:S(2)}) collective-permute-start(bf16[16,2048]{1,0:T(8,128)(2,1)S(1)} %get-tuple-element.39), channel_id=1, source_target_pairs={{16,0},{20,4},{24,8},{28,12},{0,16},{4,20},{8,24},{12,28},{17,1},{... | collective-permute-start | bytes 196616 | tf_op jit(solution)/shard_map/ppermute | solution.py:622
  18.2 3.4 %collective-permute-start.3 = (bf16[16,2048]{1,0:T(8,128)(2,1)S(1)}, bf16[16,2048]{1,0:T(8,128)(2,1)S(1)}, u32[]{:S(2)}, u32[]{:S(2)}) collective-permute-start(bf16[16,2048]{1,0:T(8,128)(2,1)S(1)} %get-tuple-element.39), channel_id=1, source_target_pairs={{24,0},{28,4},{16,8},{20,12},{8,16},{12,20},{0,24},{4,28},{25,1},{... | collective-permute-start | bytes 196616 | tf_op jit(solution)/shard_map/ppermute | solution.py:622
  21.5 0.0 copy-done.3
  21.5 2.4 %local_conv.1.refs_1_ = f32[256,2048]{1,0:T(8,128)S(1)} custom-call(f32[256,2048]{1,0:T(8,128)S(1)} %get-tuple-element.26.gate_ref.refs_2_, f32[8,2048]{1,0:T(8,128)S(1)} %get-tuple-element.31.gate_head_ref.refs_3_, bf16[256,2048]{1,0:T(8,128)(2,1)S(1)} %get-tuple-element.32.residual_ref, bf16[256,2048]{1,0:T(8,128)(2,1)S(1)} %get-tuple-element.33.product_ref, ...), custom_call_target="tpu_custom_call" | custom-call | bytes 15000000 | tf_op jit(solution)/shard_map/local_conv/pallas_call | solution.py:624
  24.0 0.0 collective-permute-done.5.refs_9_
  24.0 0.0 collective-permute-done.4.refs_8_
  24.0 0.6 %collective-permute-done.3.refs_7_ = bf16[16,2048]{1,0:T(8,128)(2,1)S(1)} collective-permute-done((bf16[16,2048]{1,0:T(8,128)(2,1)S(1)}, bf16[16,2048]{1,0:T(8,128)(2,1)S(1)}, u32[]{:S(2)}, u32[]{:S(2)}) %collective-permute-start.3) | collective-permute-done | bytes 65568 | tf_op jit(solution)/shard_map/ppermute | solution.py:622
  24.6 0.7 %add_carry.1 = (f32[256,2048]{1,0:T(8,128)S(1)}, f32[1,256]{1,0:T(1,128)S(1)}) custom-call(s32[1]{0:T(128)} %bitcast.refs_0_, f32[256,2048]{1,0:T(8,128)S(1)} %local_conv.1.refs_1_, f32[256,2048]{1,0:T(8,128)S(1)} %get-tuple-element.26.gate_ref.refs_2_, f32[8,2048]{1,0:T(8,128)S(1)} %get-tuple-element.31.gate_head_ref.refs_3_, ...), custom_call_target="tpu_custom_call" | custom-call | bytes 3000000 | tf_op jit(solution)/shard_map/add_carry/pallas_call | solution.py:633
  25.3 0.0 copy-start
  25.3 0.0 collective-permute-start.8
  25.3 1.6 %collective-permute-start.7 = (f32[1,256]{1,0:T(1,128)S(1)}, f32[1,256]{1,0:T(1,128)S(1)}, u32[]{:S(2)}, u32[]{:S(2)}) collective-permute-start(f32[1,256]{1,0:T(1,128)S(1)} %get-tuple-element.41.refs_2_), channel_id=1, source_target_pairs={{2,0},{3,1},{0,2},{1,3},{6,4},{7,5},{4,6},{5,7},{10,8},{11,9},{8,1... | collective-permute-start | bytes 3080 | tf_op jit(solution)/shard_map/ppermute | solution.py:642
  26.9 0.3 collective-permute-start.6
  27.2 1.0 %new_residual.1 = bf16[256,2048]{1,0:T(8,128)(2,1)} custom-call(f32[256,2048]{1,0:T(8,128)S(1)} %get-tuple-element.40.summed_ref.refs_0_), custom_call_target="tpu_custom_call" | custom-call | bytes 3000000 | tf_op jit(solution)/shard_map/new_residual/pallas_call | solution.py:645
  28.2 0.0 collective-permute-done.8.refs_5_
  28.2 0.7 %collective-permute-done.7.refs_4_ = f32[1,256]{1,0:T(1,128)S(1)} collective-permute-done((f32[1,256]{1,0:T(1,128)S(1)}, f32[1,256]{1,0:T(1,128)S(1)}, u32[]{:S(2)}, u32[]{:S(2)}) %collective-permute-start.7) | collective-permute-done | bytes 1056 | tf_op jit(solution)/shard_map/ppermute | solution.py:642
  28.9 0.9 %collective-permute-done.6.refs_3_ = f32[1,256]{1,0:T(1,128)S(1)} collective-permute-done((f32[1,256]{1,0:T(1,128)S(1)}, f32[1,256]{1,0:T(1,128)S(1)}, u32[]{:S(2)}, u32[]{:S(2)}) %collective-permute-start.6) | collective-permute-done | bytes 1056 | tf_op jit(solution)/shard_map/ppermute | solution.py:642
  29.9 0.0 copy-done
  29.9 1.2 %normed.1 = bf16[256,2048]{1,0:T(8,128)(2,1)} custom-call(f32[256,2048]{1,0:T(8,128)S(1)} %get-tuple-element.40.summed_ref.refs_0_, f32[1,2048]{1,0:T(1,128)S(1)} %bitcast.5, f32[1,256]{1,0:T(1,128)S(1)} %get-tuple-element.41.refs_2_, f32[1,256]{1,0:T(1,128)S(1)} %collective-permute-done.6.refs_3_, f32[1,256]{1,0:T(1,128)S(1)} %collective-permute-done.7.refs_4_, ...), custom_call_target="tpu_custom_call" | custom-call | bytes 3000000 | tf_op jit(solution)/shard_map/normed/pallas_call | solution.py:645
Async XLA Ops:
  4.1 0.6 %copy-start.1 = (f32[16,128]{1,0:T(8,128)}, f32[16,128]{1,0:T(8,128)S(1)}, u32[]{:S(2)}) copy-start(f32[16,128]{1,0:T(8,128)S(1)} %get-tuple-element.23.residue_ref) | copy-start | bytes 24580
  4.7 8.0 %collective-permute-start = (bf16[32,2048]{1,0:T(8,128)(2,1)S(1)}, bf16[32,2048]{1,0:T(8,128)(2,1)}, u32[]{:S(2)}, u32[]{:S(2)}) collective-permute-start(bf16[32,2048]{1,0:T(8,128)(2,1)S(1)} %get-tuple-element.27.refs_4_), channel_id=1, source_target_pairs={{4,0},{0,4},{12,8},{8,12},{20,16},{16,20},{28,24},{24,28},{5,1},{1... | collective-permute-start | bytes 393224 | tf_op jit(solution)/shard_map/ppermute | solution.py:581
  7.6 5.6 %collective-permute-start.2 = (bf16[3,2,2048]{2,1,0:T(2,128)(2,1)S(1)}, bf16[3,2,2048]{2,1,0:T(2,128)(2,1)S(1)}, u32[]{:S(2)}, u32[]{:S(2)}) collective-permute-start(bf16[3,2,2048]{2,1,0:T(2,128)(2,1)S(1)} %get-tuple-element.30.refs_5_), channel_id=1, source_target_pairs={{0,8},{4,12},{8,16},{12,20},{16,24},{20,28},{24,0},{28,4},{1,9},{5... | collective-permute-start | bytes 73736 | tf_op jit(solution)/shard_map/ppermute | solution.py:583
  9.2 6.6 %collective-permute-start.1 = (bf16[3,2,2048]{2,1,0:T(2,128)(2,1)S(1)}, bf16[3,2,2048]{2,1,0:T(2,128)(2,1)}, u32[]{:S(2)}, u32[]{:S(2)}) collective-permute-start(bf16[3,2,2048]{2,1,0:T(2,128)(2,1)S(1)} %get-tuple-element.30.refs_5_), channel_id=1, source_target_pairs={{0,4},{4,8},{8,12},{12,16},{16,20},{20,24},{24,28},{28,0},{1,5},{5... | collective-permute-start | bytes 73736 | tf_op jit(solution)/shard_map/ppermute | solution.py:582
  9.7 0.7 %copy-start.2 = (f32[16,128]{1,0:T(8,128)S(1)}, f32[16,128]{1,0:T(8,128)}, u32[]{:S(2)}) copy-start(f32[16,128]{1,0:T(8,128)} %copy-done.1) | copy-start | bytes 24580
  10.4 11.1 %copy-start.3 = (f32[2048]{0:T(1024)S(1)}, f32[2048]{0:T(1024)}, u32[]{:S(2)}) copy-start(f32[2048]{0:T(1024)} %param.11) | copy-start | bytes 24580
  17.1 6.9 %collective-permute-start.5 = (bf16[16,2048]{1,0:T(8,128)(2,1)S(1)}, bf16[16,2048]{1,0:T(8,128)(2,1)S(1)}, u32[]{:S(2)}, u32[]{:S(2)}) collective-permute-start(bf16[16,2048]{1,0:T(8,128)(2,1)S(1)} %get-tuple-element.39), channel_id=1, source_target_pairs={{8,0},{12,4},{0,8},{4,12},{24,16},{28,20},{16,24},{20,28},{9,1},{1... | collective-permute-start | bytes 196616 | tf_op jit(solution)/shard_map/ppermute | solution.py:622
  17.2 6.8 %collective-permute-start.4 = (bf16[16,2048]{1,0:T(8,128)(2,1)S(1)}, bf16[16,2048]{1,0:T(8,128)(2,1)S(1)}, u32[]{:S(2)}, u32[]{:S(2)}) collective-permute-start(bf16[16,2048]{1,0:T(8,128)(2,1)S(1)} %get-tuple-element.39), channel_id=1, source_target_pairs={{16,0},{20,4},{24,8},{28,12},{0,16},{4,20},{8,24},{12,28},{17,1},{... | collective-permute-start | bytes 196616 | tf_op jit(solution)/shard_map/ppermute | solution.py:622
  18.2 6.4 %collective-permute-start.3 = (bf16[16,2048]{1,0:T(8,128)(2,1)S(1)}, bf16[16,2048]{1,0:T(8,128)(2,1)S(1)}, u32[]{:S(2)}, u32[]{:S(2)}) collective-permute-start(bf16[16,2048]{1,0:T(8,128)(2,1)S(1)} %get-tuple-element.39), channel_id=1, source_target_pairs={{24,0},{28,4},{16,8},{20,12},{8,16},{12,20},{0,24},{4,28},{25,1},{... | collective-permute-start | bytes 196616 | tf_op jit(solution)/shard_map/ppermute | solution.py:622
  25.3 4.6 %copy-start = (f32[2048]{0:T(1024)S(1)}, f32[2048]{0:T(1024)}, u32[]{:S(2)}) copy-start(f32[2048]{0:T(1024)} %param.13) | copy-start | bytes 24580
  25.3 2.9 %collective-permute-start.8 = (f32[1,256]{1,0:T(1,128)S(1)}, f32[1,256]{1,0:T(1,128)S(1)}, u32[]{:S(2)}, u32[]{:S(2)}) collective-permute-start(f32[1,256]{1,0:T(1,128)S(1)} %get-tuple-element.41.refs_2_), channel_id=1, source_target_pairs={{1,0},{0,1},{3,2},{2,3},{5,4},{4,5},{7,6},{6,7},{9,8},{8,9},{11,10... | collective-permute-start | bytes 3080 | tf_op jit(solution)/shard_map/ppermute | solution.py:642
  25.3 3.6 %collective-permute-start.7 = (f32[1,256]{1,0:T(1,128)S(1)}, f32[1,256]{1,0:T(1,128)S(1)}, u32[]{:S(2)}, u32[]{:S(2)}) collective-permute-start(f32[1,256]{1,0:T(1,128)S(1)} %get-tuple-element.41.refs_2_), channel_id=1, source_target_pairs={{2,0},{3,1},{0,2},{1,3},{6,4},{7,5},{4,6},{5,7},{10,8},{11,9},{8,1... | collective-permute-start | bytes 3080 | tf_op jit(solution)/shard_map/ppermute | solution.py:642
  26.9 3.0 %collective-permute-start.6 = (f32[1,256]{1,0:T(1,128)S(1)}, f32[1,256]{1,0:T(1,128)S(1)}, u32[]{:S(2)}, u32[]{:S(2)}) collective-permute-start(f32[1,256]{1,0:T(1,128)S(1)} %get-tuple-element.41.refs_2_), channel_id=1, source_target_pairs={{3,0},{2,1},{1,2},{0,3},{7,4},{6,5},{5,6},{4,7},{11,8},{10,9},{9,1... | collective-permute-start | bytes 3080 | tf_op jit(solution)/shard_map/ppermute | solution.py:642

commit v11 on v9

--- a/solution.py
+++ b/solution.py
@@ -100,20 +100,20 @@
 
 
 def shift_matrix(rows):
-    own = index_of((rows, rows), 1) == index_of((rows, rows), 0) - 2
-    return jnp.where(own, 1.0, 0.0).astype(BF16)
-
-
-def two_later(shift, block):
+    shape = (2 * rows, rows)
+    target = index_of(shape, 0)
+    source = index_of(shape, 1)
+    taken = jnp.where(target < rows, target - 1, target - (rows + 2))
+    return jnp.where(source == taken, 1.0, 0.0).astype(BF16)
+
+
+def earlier_tokens(shift, block):
     return jnp.dot(shift, block, preferred_element_type=F32)
 
 
-def wide_conv(block, two, weights):
-    wide = block.astype(F32)
-    one = pltpu.roll(wide, 1, 0)
-    head = jnp.where(index_of((8, wide.shape[1]), 0) == 0, 0.0, one[:8])
-    one = jnp.concatenate([head, one[8:]], axis=0)
-    return weights[0] * wide + weights[1] * one + weights[2] * two
+def wide_conv(block, earlier, weights):
+    rows = block.shape[0]
+    return weights[0] * block.astype(F32) + weights[1] * earlier[:rows] + weights[2] * earlier[rows:]
 
 
 def taps_of(weights, feature, lanes):
@@ -135,7 +135,6 @@
     residue_ref,
     residual_ref,
     buffer_ref,
-    ending_ref,
     shift_ref,
     short_ref,
     rate_ref,
@@ -170,23 +169,12 @@
     mode_rate = per_channel(rate_ref[...])
     mode_rate_ref[...] = mode_rate
     eye = own_mode(BF16)
-    side = rows // 2
-    left = (index_of((2 * LANES, side), 1) - (side - 1)).astype(F32).astype(BF16)
-
-    def exponents(tile):
-        high, low = split(mode_rate[:, lanes_of(tile)])
-        diagonal = jnp.concatenate([spread(high, eye), spread(low, eye)], axis=1)
-        return (jnp.dot(diagonal, left, preferred_element_type=F32),)
-
-    def endings(tile, exponent):
-        ending_ref[tile // 2, lanes_of(tile % 2), :] = jnp.exp(exponent).astype(BF16)
-
-    pipelined(width // LANES, exponents, endings)
+    token = index_of((2 * LANES, rows), 1)
+    left = jnp.where(token < 2, -1e30, (token - (rows - 1)).astype(F32)).astype(BF16)
     weight_copy.wait()
     weights = short_ref[...].astype(F32)
     weight_ref[...] = weights
     mask = group_mask(F32)
-    middle = jnp.exp(-float(side) * mode_rate)
 
     def fetch(wide):
         if wide % (wides // 2) == 0:
@@ -196,28 +184,29 @@
             if first == 0:
                 for copy in later:
                     copy.start()
-        return [two_later(shift_ref[...], buffer_ref[c, :, lanes_of(wide, WIDE)]) for c in (0, 1)]
-
-    def multiply(wide, *later_two):
+        exponents = []
+        for half in range(WIDE // LANES):
+            high, low = split(mode_rate[:, lanes_of((WIDE // LANES) * wide + half)])
+            diagonal = jnp.concatenate([spread(high, eye), spread(low, eye)], axis=1)
+            exponents.append(jnp.dot(diagonal, left, preferred_element_type=F32))
+        earlier = [earlier_tokens(shift_ref[...], buffer_ref[c, :, lanes_of(wide, WIDE)]) for c in (0, 1)]
+        return exponents + earlier
+
+    def multiply(wide, *found):
         here = lanes_of(wide, WIDE)
+        ending = jnp.concatenate([jnp.exp(exponent).astype(BF16) for exponent in found[:-2]], axis=0)
         parts = []
         for c in (0, 1):
             head_ref[c, :, here] = buffer_ref[c, 0:16, here].astype(F32)[:8]
-            parts.append(wide_conv(buffer_ref[c, :, here], later_two[c], taps_of(weights, c + 1, here)))
+            parts.append(wide_conv(buffer_ref[c, :, here], found[c - 2], taps_of(weights, c + 1, here)))
         product = (parts[0] * parts[1]).astype(BF16)
         product_ref[:, here] = product
-        head_ref[2, :, here] = product[:16].astype(F32)[:8]
-        sides = jnp.concatenate([product[:side], product[side:]], axis=1)
-        return (jnp.dot(ending_ref[wide], sides, preferred_element_type=F32),)
+        return (jnp.dot(ending, product, preferred_element_type=F32),)
 
     def leave(wide, every):
         for half in range(WIDE // LANES):
-            there = lanes_of((WIDE // LANES) * wide + half)
-            early, late = [
-                jnp.sum(every[lanes_of(half), lanes_of(k)].reshape(GROUPS, MODES, LANES) * mask, axis=0)
-                for k in (half, WIDE // LANES + half)
-            ]
-            state_ref[:, there] = middle[:, there] * early + late
+            own = every[lanes_of(half), lanes_of(half)].reshape(GROUPS, MODES, LANES)
+            state_ref[:, lanes_of((WIDE // LANES) * wide + half)] = jnp.sum(own * mask, axis=0)
 
     pipelined(wides, fetch, multiply, leave)
     for copy in later:
@@ -235,8 +224,7 @@
     first = (parts[0] * parts[1]).astype(BF16).astype(F32)
     first_ref[...] = first
     rate = mode_rate_ref[...]
-    missing = first - head_ref[2]
-    early = jnp.exp(-float(rows - 1) * rate) * missing[0:1] + jnp.exp(-float(rows - 2) * rate) * missing[1:2]
+    early = jnp.exp(-float(rows - 1) * rate) * first[0:1] + jnp.exp(-float(rows - 2) * rate) * first[1:2]
     full_ref[...] = (state_ref[...] + early).astype(BF16)
 
 
@@ -307,7 +295,7 @@
     before = halo(before_ref, place_ref)
 
     def fetch(part):
-        return (two_later(shift_ref[...], query_ref[:, lanes_of(part, WIDE)]),)
+        return (earlier_tokens(shift_ref[...], query_ref[:, lanes_of(part, WIDE)]),)
 
     def convolve(part, earlier):
         here = lanes_of(part, WIDE)
@@ -544,7 +532,7 @@
             bf16(rows, width),
             f32(MODES, width),
             f32(MODES, width),
-            f32(3, 8, width),
+            f32(2, 8, width),
             f32(*short_weight.shape),
             bf16(rows, width),
             f32(MODES, residues.shape[0]),
@@ -552,8 +540,7 @@
         ],
         scratch_shapes=[
             pltpu.VMEM((2, rows, width), BF16),
-            pltpu.VMEM((wides, WIDE, rows // 2), BF16),
-            pltpu.VMEM((rows, rows), BF16),
+            pltpu.VMEM((2 * rows, rows), BF16),
             pltpu.VMEM(short_weight.shape, BF16),
             pltpu.VMEM((MODES, rates.shape[0]), F32),
             pltpu.SemaphoreType.DMA((7,)),
@@ -582,7 +569,7 @@
             bf16(wides, rows, WIDE),
             f32(rows, width),
         ],
-        scratch_shapes=[pltpu.VMEM((rows, rows), BF16)],
+        scratch_shapes=[pltpu.VMEM((2 * rows, rows), BF16)],
         compiler_params=params(),
         cost_estimate=cost(2),
         name="prepare",

time: 28.1 us -> 28 us (level)
  no operation moved by 1% of the time
where the time goes in v11:
time: 28 us; the launch traced here: 27.8 us
  Pallas kernels  11.6 us (41%)
  starting transfers between devices  9.95 us (36%)
  waiting for transfers between devices  4.53 us (16%)
  local copies, waits for them, and re-layouts  0.94 us (3%)
  between operations  0.7 us (2%)
    ppermute x4, starting transfers between devices, per_device(): lax.ppermute(group, 'ctx', route)  5.09 us
    pallas_call x1, Pallas kernels, per_device(): pl.pallas_call(state_kernel, in_specs=[hbm_spec] * 5, out_shape=[bf16(row...  3.83 us
    ppermute x1, starting transfers between devices, per_device(): lax.ppermute(projected[:, rows - (taps - 1):, :], 'ctx', ring(peers, 1))  2.99 us
    ppermute x4, waiting for transfers between devices, per_device(): lax.ppermute(group, 'ctx', route)  2.82 us
    pallas_call x1, Pallas kernels, per_device(): pl.pallas_call(local_kernel, out_shape=f32(rows, width), compiler_params=...  2.42 us
    pallas_call x2, Pallas kernels, write(): pl.pallas_call(kernel, out_specs=hbm_spec, out_shape=bf16(rows, width), s...  2.21 us
    pallas_call x1, Pallas kernels, per_device(): pl.pallas_call(prepare_kernel, in_specs=[smem_spec] + [vmem_spec] * 5, ou...  2.21 us
    ppermute x3, starting transfers between devices, per_device(): lax.ppermute(squares, 'fsdp', route)  1.87 us
  transfers between devices with their start and end apart: 8, of which 5 were waited for; matrix products, arithmetic and copies ran while one was open for 0% of the time, Pallas kernels for 34%

profile of v11, /device:TPU:0, one launch (start us, length us, event | category | flops | bytes accessed | tf_op | source)
XLA Modules:
  0.0 27.8 jit_solution(6920989764191846354)
XLA Ops:
  0.6 0.9 %slice.3 = bf16[3,2,2048]{2,1,0:T(2,128)(2,1)S(1)} slice(bf16[3,256,2048]{2,1,0:T(8,128)(2,1)} %projected_ref.1), slice={[0:3], [254:256], [0:2048]} | slice | bytes 49152 | tf_op jit(solution)/shard_map/slice | solution.py:526
  1.6 3.0 %collective-permute-start = (bf16[3,2,2048]{2,1,0:T(2,128)(2,1)S(1)}, bf16[3,2,2048]{2,1,0:T(2,128)(2,1)S(1)}, u32[]{:S(2)}, u32[]{:S(2)}) collective-permute-start(bf16[3,2,2048]{2,1,0:T(2,128)(2,1)S(1)} %slice.3), channel_id=1, source_target_pairs={{0,4},{4,8},{8,12},{12,16},{16,20},{20,24},{24,28},{28,0},{1,5},{5... | collective-permute-start | bytes 73736 | tf_op jit(solution)/shard_map/ppermute | solution.py:526
  4.5 3.8 %block_state.1 = (bf16[256,2048]{1,0:T(8,128)(2,1)S(1)}, f32[16,2048]{1,0:T(8,128)S(1)}, f32[16,2048]{1,0:T(8,128)S(1)}, f32[2,8,2048]{2,1,0:T(8,128)S(1)}, f32[...) custom-call(bf16[3,256,2048]{2,1,0:T(8,128)(2,1)} %projected_ref.1, ...), custom_call_target="tpu_custom_call" | custom-call | bytes 9000000 | tf_op jit(solution)/shard_map/block_state/pallas_call | solution.py:528
  8.4 0.0 copy-start
  8.4 1.0 %collective-permute-done.before_ref.refs_1_ = bf16[3,2,2048]{2,1,0:T(2,128)(2,1)S(1)} collective-permute-done((bf16[3,2,2048]{2,1,0:T(2,128)(2,1)S(1)}, bf16[3,2,2048]{2,1,0:T(2,128)(2,1)S(1)}, u32[]{:S(2)}, u32[]{:S(2)}) %collective-permute-start) | collective-permute-done | bytes 24608 | tf_op jit(solution)/shard_map/ppermute | solution.py:526
  9.4 0.1 head_tokens.1
  9.5 0.6 %collective-permute-start.1 = (bf16[16,2048]{1,0:T(8,128)(2,1)S(1)}, bf16[16,2048]{1,0:T(8,128)(2,1)S(1)}, u32[]{:S(2)}, u32[]{:S(2)}) collective-permute-start(bf16[16,2048]{1,0:T(8,128)(2,1)S(1)} %get-tuple-element.32.refs_1_), channel_id=1, source_target_pairs={{4,0},{0,4},{12,8},{8,12},{20,16},{16,20},{28,24},{24,28},{5,1},{1... | collective-permute-start | bytes 196616 | tf_op jit(solution)/shard_map/ppermute | solution.py:584
  10.2 2.2 %prepare.1 = (bf16[16,48,256]{2,1,0:T(8,128)(2,1)S(1)}, bf16[16,32,128]{2,1,0:T(8,128)(2,1)S(1)}, bf16[8,256,256]{2,1,0:T(8,128)(2,1)S(1)}, f32[256,2048]{1,0:T(8,128)S(1)}) custom-call(s32[1]{0:T(128)} %bitcast.place_ref.refs_0_, bf16[256,2048]{1,0:T(8,128)(2,1)S(1)} %get-tuple-element.22.query_ref, f32[16,128]{1,0:T(8,128)S(1)} %get-tuple-element.23.residue_ref, ...), custom_call_target="tpu_custom_call" | custom-call | bytes 6000000 | tf_op jit(solution)/shard_map/prepare/pallas_call | solution.py:563
  12.4 1.5 %collective-permute-done.1.refs_4_ = bf16[16,2048]{1,0:T(8,128)(2,1)S(1)} collective-permute-done((bf16[16,2048]{1,0:T(8,128)(2,1)S(1)}, bf16[16,2048]{1,0:T(8,128)(2,1)S(1)}, u32[]{:S(2)}, u32[]{:S(2)}) %collective-permute-start.1) | collective-permute-done | bytes 65568 | tf_op jit(solution)/shard_map/ppermute | solution.py:584
  13.9 0.1 join.1
  14.0 2.7 %collective-permute-start.2 = (bf16[16,2048]{1,0:T(8,128)(2,1)S(1)}, bf16[16,2048]{1,0:T(8,128)(2,1)S(1)}, u32[]{:S(2)}, u32[]{:S(2)}) collective-permute-start(bf16[16,2048]{1,0:T(8,128)(2,1)S(1)} %get-tuple-element.39), channel_id=1, source_target_pairs={{24,0},{28,4},{16,8},{20,12},{8,16},{12,20},{0,24},{4,28},{25,1},{... | collective-permute-start | bytes 196616 | tf_op jit(solution)/shard_map/ppermute | solution.py:596
  16.7 0.0 collective-permute-start.3
  16.7 1.8 %collective-permute-start.4 = (bf16[16,2048]{1,0:T(8,128)(2,1)S(1)}, bf16[16,2048]{1,0:T(8,128)(2,1)S(1)}, u32[]{:S(2)}, u32[]{:S(2)}) collective-permute-start(bf16[16,2048]{1,0:T(8,128)(2,1)S(1)} %get-tuple-element.39), channel_id=1, source_target_pairs={{8,0},{12,4},{0,8},{4,12},{24,16},{28,20},{16,24},{20,28},{9,1},{1... | collective-permute-start | bytes 196616 | tf_op jit(solution)/shard_map/ppermute | solution.py:596
  18.4 0.0 copy-done
  18.4 2.4 %local_conv.1.refs_1_ = f32[256,2048]{1,0:T(8,128)S(1)} custom-call(f32[256,2048]{1,0:T(8,128)S(1)} %get-tuple-element.26.gate_ref.refs_2_, bf16[256,2048]{1,0:T(8,128)(2,1)S(1)} %get-tuple-element.27.residual_ref, bf16[256,2048]{1,0:T(8,128)(2,1)S(1)} %get-tuple-element.28.product_ref, f32[8,2048]{1,0:T(8,128)S(1)} %get-tuple-element.31.first_ref, ...), custom_call_target="tpu_custom_call" | custom-call | bytes 15000000 | tf_op jit(solution)/shard_map/local_conv/pallas_call | solution.py:598
  20.9 0.0 collective-permute-done.2.refs_6_
  20.9 1.3 %collective-permute-done.3.refs_7_ = bf16[16,2048]{1,0:T(8,128)(2,1)S(1)} collective-permute-done((bf16[16,2048]{1,0:T(8,128)(2,1)S(1)}, bf16[16,2048]{1,0:T(8,128)(2,1)S(1)}, u32[]{:S(2)}, u32[]{:S(2)}) %collective-permute-start.3) | collective-permute-done | bytes 65568 | tf_op jit(solution)/shard_map/ppermute | solution.py:596
  22.2 0.0 collective-permute-done.4.refs_8_
  22.2 0.7 %add_carry.1 = (f32[256,2048]{1,0:T(8,128)S(1)}, f32[1,256]{1,0:T(1,128)S(1)}) custom-call(s32[1]{0:T(128)} %bitcast.place_ref.refs_0_, f32[256,2048]{1,0:T(8,128)S(1)} %local_conv.1.refs_1_, f32[256,2048]{1,0:T(8,128)S(1)} %get-tuple-element.26.gate_ref.refs_2_, bf16[8,256,256]{2,1,0:T(8,128)(2,1)S(1)} %get-tuple-element.36.refs_3_, ...), custom_call_target="tpu_custom_call" | custom-call | bytes 3000000 | tf_op jit(solution)/shard_map/add_carry/pallas_call | solution.py:607
  23.0 0.0 copy-start.1
  23.0 0.0 collective-permute-start.5
  23.0 1.6 %collective-permute-start.6 = (f32[1,256]{1,0:T(1,128)S(1)}, f32[1,256]{1,0:T(1,128)S(1)}, u32[]{:S(2)}, u32[]{:S(2)}) collective-permute-start(f32[1,256]{1,0:T(1,128)S(1)} %get-tuple-element.41.refs_2_), channel_id=1, source_target_pairs={{2,0},{3,1},{0,2},{1,3},{6,4},{7,5},{4,6},{5,7},{10,8},{11,9},{8,1... | collective-permute-start | bytes 3080 | tf_op jit(solution)/shard_map/ppermute | solution.py:616
  24.6 0.2 collective-permute-start.7
  24.8 1.0 %new_residual.1 = bf16[256,2048]{1,0:T(8,128)(2,1)} custom-call(f32[256,2048]{1,0:T(8,128)S(1)} %get-tuple-element.40.summed_ref.refs_0_), custom_call_target="tpu_custom_call" | custom-call | bytes 3000000 | tf_op jit(solution)/shard_map/new_residual/pallas_call | solution.py:619
  25.9 0.1 collective-permute-done.5.refs_3_
  26.0 0.6 %collective-permute-done.6.refs_4_ = f32[1,256]{1,0:T(1,128)S(1)} collective-permute-done((f32[1,256]{1,0:T(1,128)S(1)}, f32[1,256]{1,0:T(1,128)S(1)}, u32[]{:S(2)}, u32[]{:S(2)}) %collective-permute-start.6) | collective-permute-done | bytes 1056 | tf_op jit(solution)/shard_map/ppermute | solution.py:616
  26.6 0.0 collective-permute-done.7.refs_5_
  26.6 0.0 copy-done.1
  26.6 1.2 %normed.1 = bf16[256,2048]{1,0:T(8,128)(2,1)} custom-call(f32[256,2048]{1,0:T(8,128)S(1)} %get-tuple-element.40.summed_ref.refs_0_, f32[1,2048]{1,0:T(1,128)S(1)} %bitcast.6, f32[1,256]{1,0:T(1,128)S(1)} %get-tuple-element.41.refs_2_, f32[1,256]{1,0:T(1,128)S(1)} %collective-permute-done.5.refs_3_, f32[1,256]{1,0:T(1,128)S(1)} %collective-permute-done.6.refs_4_, ...), custom_call_target="tpu_custom_call" | custom-call | bytes 3000000 | tf_op jit(solution)/shard_map/normed/pallas_call | solution.py:619
  (1 shorter events, 0.0 us)
Async XLA Ops:
  1.6 7.8 %collective-permute-start = (bf16[3,2,2048]{2,1,0:T(2,128)(2,1)S(1)}, bf16[3,2,2048]{2,1,0:T(2,128)(2,1)S(1)}, u32[]{:S(2)}, u32[]{:S(2)}) collective-permute-start(bf16[3,2,2048]{2,1,0:T(2,128)(2,1)S(1)} %slice.3), channel_id=1, source_target_pairs={{0,4},{4,8},{8,12},{12,16},{16,20},{20,24},{24,28},{28,0},{1,5},{5... | collective-permute-start | bytes 73736 | tf_op jit(solution)/shard_map/ppermute | solution.py:526
  8.4 10.1 %copy-start = (f32[2048]{0:T(1024)S(1)}, f32[2048]{0:T(1024)}, u32[]{:S(2)}) copy-start(f32[2048]{0:T(1024)} %param.11) | copy-start | bytes 24580
  9.5 4.3 %collective-permute-start.1 = (bf16[16,2048]{1,0:T(8,128)(2,1)S(1)}, bf16[16,2048]{1,0:T(8,128)(2,1)S(1)}, u32[]{:S(2)}, u32[]{:S(2)}) collective-permute-start(bf16[16,2048]{1,0:T(8,128)(2,1)S(1)} %get-tuple-element.32.refs_1_), channel_id=1, source_target_pairs={{4,0},{0,4},{12,8},{8,12},{20,16},{16,20},{28,24},{24,28},{5,1},{1... | collective-permute-start | bytes 196616 | tf_op jit(solution)/shard_map/ppermute | solution.py:584
  14.0 6.9 %collective-permute-start.2 = (bf16[16,2048]{1,0:T(8,128)(2,1)S(1)}, bf16[16,2048]{1,0:T(8,128)(2,1)S(1)}, u32[]{:S(2)}, u32[]{:S(2)}) collective-permute-start(bf16[16,2048]{1,0:T(8,128)(2,1)S(1)} %get-tuple-element.39), channel_id=1, source_target_pairs={{24,0},{28,4},{16,8},{20,12},{8,16},{12,20},{0,24},{4,28},{25,1},{... | collective-permute-start | bytes 196616 | tf_op jit(solution)/shard_map/ppermute | solution.py:596
  16.7 5.5 %collective-permute-start.3 = (bf16[16,2048]{1,0:T(8,128)(2,1)S(1)}, bf16[16,2048]{1,0:T(8,128)(2,1)S(1)}, u32[]{:S(2)}, u32[]{:S(2)}) collective-permute-start(bf16[16,2048]{1,0:T(8,128)(2,1)S(1)} %get-tuple-element.39), channel_id=1, source_target_pairs={{16,0},{20,4},{24,8},{28,12},{0,16},{4,20},{8,24},{12,28},{17,1},{... | collective-permute-start | bytes 196616 | tf_op jit(solution)/shard_map/ppermute | solution.py:596
  16.7 5.5 %collective-permute-start.4 = (bf16[16,2048]{1,0:T(8,128)(2,1)S(1)}, bf16[16,2048]{1,0:T(8,128)(2,1)S(1)}, u32[]{:S(2)}, u32[]{:S(2)}) collective-permute-start(bf16[16,2048]{1,0:T(8,128)(2,1)S(1)} %get-tuple-element.39), channel_id=1, source_target_pairs={{8,0},{12,4},{0,8},{4,12},{24,16},{28,20},{16,24},{20,28},{9,1},{1... | collective-permute-start | bytes 196616 | tf_op jit(solution)/shard_map/ppermute | solution.py:596
  23.0 3.6 %copy-start.1 = (f32[2048]{0:T(1024)S(1)}, f32[2048]{0:T(1024)}, u32[]{:S(2)}) copy-start(f32[2048]{0:T(1024)} %param.13) | copy-start | bytes 24580
  23.0 3.0 %collective-permute-start.5 = (f32[1,256]{1,0:T(1,128)S(1)}, f32[1,256]{1,0:T(1,128)S(1)}, u32[]{:S(2)}, u32[]{:S(2)}) collective-permute-start(f32[1,256]{1,0:T(1,128)S(1)} %get-tuple-element.41.refs_2_), channel_id=1, source_target_pairs={{3,0},{2,1},{1,2},{0,3},{7,4},{6,5},{5,6},{4,7},{11,8},{10,9},{9,1... | collective-permute-start | bytes 3080 | tf_op jit(solution)/shard_map/ppermute | solution.py:616
  23.0 3.6 %collective-permute-start.6 = (f32[1,256]{1,0:T(1,128)S(1)}, f32[1,256]{1,0:T(1,128)S(1)}, u32[]{:S(2)}, u32[]{:S(2)}) collective-permute-start(f32[1,256]{1,0:T(1,128)S(1)} %get-tuple-element.41.refs_2_), channel_id=1, source_target_pairs={{2,0},{3,1},{0,2},{1,3},{6,4},{7,5},{4,6},{5,7},{10,8},{11,9},{8,1... | collective-permute-start | bytes 3080 | tf_op jit(solution)/shard_map/ppermute | solution.py:616
  24.6 2.0 %collective-permute-start.7 = (f32[1,256]{1,0:T(1,128)S(1)}, f32[1,256]{1,0:T(1,128)S(1)}, u32[]{:S(2)}, u32[]{:S(2)}) collective-permute-start(f32[1,256]{1,0:T(1,128)S(1)} %get-tuple-element.41.refs_2_), channel_id=1, source_target_pairs={{1,0},{0,1},{3,2},{2,3},{5,4},{4,5},{7,6},{6,7},{9,8},{8,9},{11,10... | collective-permute-start | bytes 3080 | tf_op jit(solution)/shard_map/ppermute | solution.py:616

commit v12 on v11

--- a/solution.py
+++ b/solution.py
@@ -125,15 +125,12 @@
     weight_hbm,
     rate_hbm,
     residue_hbm,
-    residual_hbm,
     product_ref,
     state_ref,
     mode_rate_ref,
     head_ref,
     weight_ref,
-    query_ref,
     residue_ref,
-    residual_ref,
     buffer_ref,
     shift_ref,
     short_ref,
@@ -157,13 +154,10 @@
         for side in (0, 1)
         for c in (0, 1)
     ]
-    later = [
-        pltpu.make_async_copy(residue_hbm, residue_ref, sems.at[4]),
-        pltpu.make_async_copy(projected_ref.at[0], query_ref, sems.at[5]),
-        pltpu.make_async_copy(residual_hbm, residual_ref, sems.at[6]),
-    ]
+    residue_copy = pltpu.make_async_copy(residue_hbm, residue_ref, sems.at[4])
     for copy in copies:
         copy.start()
+    residue_copy.start()
     shift_ref[...] = shift_matrix(rows)
     rate_copy.wait()
     mode_rate = per_channel(rate_ref[...])
@@ -181,9 +175,6 @@
             first = 2 * (wide // (wides // 2))
             for copy in copies[first : first + 2]:
                 copy.wait()
-            if first == 0:
-                for copy in later:
-                    copy.start()
         exponents = []
         for half in range(WIDE // LANES):
             high, low = split(mode_rate[:, lanes_of((WIDE // LANES) * wide + half)])
@@ -209,8 +200,7 @@
             state_ref[:, lanes_of((WIDE // LANES) * wide + half)] = jnp.sum(own * mask, axis=0)
 
     pipelined(wides, fetch, multiply, leave)
-    for copy in later:
-        copy.wait()
+    residue_copy.wait()
 
 
 def halo(before_ref, place_ref):
@@ -230,7 +220,8 @@
 
 def prepare_kernel(
     place_ref,
-    query_ref,
+    projected_ref,
+    residual_hbm,
     residue_ref,
     before_ref,
     weight_ref,
@@ -239,9 +230,16 @@
     entering_ref,
     carry_ref,
     gate_ref,
+    residual_ref,
+    query_ref,
     shift_ref,
+    sems,
 ):
     rows, width = gate_ref.shape
+    query_copy = pltpu.make_async_copy(projected_ref.at[0], query_ref, sems.at[0])
+    query_copy.start()
+    residual_copy = pltpu.make_async_copy(residual_hbm, residual_ref, sems.at[1])
+    residual_copy.start()
     shift_ref[...] = shift_matrix(rows)
     residue = per_channel(residue_ref[...])
     wide = GROUPS * CHUNK
@@ -293,6 +291,7 @@
 
     pipelined(width // LANES, exponents, products, finish)
     before = halo(before_ref, place_ref)
+    query_copy.wait()
 
     def fetch(part):
         return (earlier_tokens(shift_ref[...], query_ref[:, lanes_of(part, WIDE)]),)
@@ -305,6 +304,7 @@
         gate_ref[0:8, here] = short_conv(head, before[0, :, here], weights)
 
     pipelined(width // WIDE, fetch, convolve)
+    residual_copy.wait()
 
 
 def local_kernel(
@@ -525,31 +525,29 @@
 
     before = lax.ppermute(projected[:, rows - (taps - 1) :, :], "ctx", ring(peers, 1))
 
-    product, state, mode_rate, head, weights, query, residue, residual_here = pl.pallas_call(
+    product, state, mode_rate, head, weights, residue = pl.pallas_call(
         state_kernel,
-        in_specs=[hbm_spec] * 5,
+        in_specs=[hbm_spec] * 4,
         out_shape=[
             bf16(rows, width),
             f32(MODES, width),
             f32(MODES, width),
             f32(2, 8, width),
             f32(*short_weight.shape),
-            bf16(rows, width),
             f32(MODES, residues.shape[0]),
-            bf16(rows, width),
         ],
         scratch_shapes=[
             pltpu.VMEM((2, rows, width), BF16),
             pltpu.VMEM((2 * rows, rows), BF16),
             pltpu.VMEM(short_weight.shape, BF16),
             pltpu.VMEM((MODES, rates.shape[0]), F32),
-            pltpu.SemaphoreType.DMA((7,)),
+            pltpu.SemaphoreType.DMA((5,)),
             pltpu.SemaphoreType.DMA((2,)),
         ],
         compiler_params=params(),
         cost_estimate=cost(3),
         name="block_state",
-    )(kept(projected), kept(short_weight), kept(rates.T), kept(residues.T), kept(residual))
+    )(kept(projected), kept(short_weight), kept(rates.T), kept(residues.T))
 
     full_state, first = pl.pallas_call(
         lambda *refs: head_kernel(rows, *refs),
@@ -560,20 +558,25 @@
         name="head_tokens",
     )(place, before, head, weights, state, mode_rate)
 
-    inner, entering, carry_table, gate = pl.pallas_call(
+    inner, entering, carry_table, gate, residual_here = pl.pallas_call(
         prepare_kernel,
-        in_specs=[smem_spec] + [vmem_spec] * 5,
+        in_specs=[smem_spec] + [hbm_spec] * 2 + [vmem_spec] * 4,
         out_shape=[
             bf16(tiles, CHUNK + MODES, GROUPS * CHUNK),
             bf16(tiles, CHUNK, LANES),
             bf16(wides, rows, WIDE),
             f32(rows, width),
+            bf16(rows, width),
         ],
-        scratch_shapes=[pltpu.VMEM((2 * rows, rows), BF16)],
+        scratch_shapes=[
+            pltpu.VMEM((rows, width), BF16),
+            pltpu.VMEM((2 * rows, rows), BF16),
+            pltpu.SemaphoreType.DMA((2,)),
+        ],
         compiler_params=params(),
         cost_estimate=cost(2),
         name="prepare",
-    )(place, query, residue, before, weights, mode_rate)
+    )(place, kept(projected), kept(residual), residue, before, weights, mode_rate)
 
     group, entry, stride = full_state, jnp.zeros((MODES, width), F32), 1
     levels = radices(peers)

time: 28 us -> 28.1 us (level)
  Pallas kernels: 11.6 us -> 12 us
  waiting for transfers between devices: 4.53 us -> 4.16 us
    pallas_call x2, Pallas kernels: 6.04 us -> 6.34 us  [the longest x1 3.9 us: per_device(): pl.pallas_call(state_kernel, in_specs=[hbm_spec] * 4, out_shape=[bf16(row...]
    ppermute x4, waiting for transfers between devices: 2.82 us -> 2.52 us  [per_device(): lax.ppermute(group, 'ctx', route)]
  transfers between devices with their start and end apart: 8 -> 8, of which waited for: 5 -> 5; matrix products, arithmetic and copies ran while one was open for 0% -> 0% of each run, Pallas kernels for 34% -> 35%
where the time goes in v12:
time: 28.1 us; the launch traced here: 27.8 us
  Pallas kernels  12 us (43%)
  starting transfers between devices  10 us (36%)
  waiting for transfers between devices  4.16 us (15%)
  local copies, waits for them, and re-layouts  0.94 us (3%)
  between operations  0.69 us (2%)
    ppermute x4, starting transfers between devices, per_device(): lax.ppermute(group, 'ctx', route)  5.15 us
    pallas_call x1, Pallas kernels, per_device(): pl.pallas_call(state_kernel, in_specs=[hbm_spec] * 4, out_shape=[bf16(row...  3.9 us
    ppermute x1, starting transfers between devices, per_device(): lax.ppermute(projected[:, rows - (taps - 1):, :], 'ctx', ring(peers, 1))  2.99 us
    ppermute x4, waiting for transfers between devices, per_device(): lax.ppermute(group, 'ctx', route)  2.52 us
    pallas_call x1, Pallas kernels, per_device(): pl.pallas_call(prepare_kernel, in_specs=[smem_spec] + [hbm_spec] * 2 + [v...  2.44 us
    pallas_call x1, Pallas kernels, per_device(): pl.pallas_call(local_kernel, out_shape=f32(rows, width), compiler_params=...  2.43 us
    pallas_call x2, Pallas kernels, write(): pl.pallas_call(kernel, out_specs=hbm_spec, out_shape=bf16(rows, width), s...  2.21 us
    ppermute x3, starting transfers between devices, per_device(): lax.ppermute(squares, 'fsdp', route)  1.87 us
  transfers between devices with their start and end apart: 8, of which 5 were waited for; matrix products, arithmetic and copies ran while one was open for 0% of the time, Pallas kernels for 35%

profile of v12, /device:TPU:0, one launch (start us, length us, event | category | flops | bytes accessed | tf_op | source)
XLA Modules:
  0.0 27.8 jit_solution(9100465613240920212)
XLA Ops:
  0.6 0.9 %slice.3 = bf16[3,2,2048]{2,1,0:T(2,128)(2,1)S(1)} slice(bf16[3,256,2048]{2,1,0:T(8,128)(2,1)} %projected_ref.3), slice={[0:3], [254:256], [0:2048]} | slice | bytes 49152 | tf_op jit(solution)/shard_map/slice | solution.py:526
  1.6 3.0 %collective-permute-start = (bf16[3,2,2048]{2,1,0:T(2,128)(2,1)S(1)}, bf16[3,2,2048]{2,1,0:T(2,128)(2,1)S(1)}, u32[]{:S(2)}, u32[]{:S(2)}) collective-permute-start(bf16[3,2,2048]{2,1,0:T(2,128)(2,1)S(1)} %slice.3), channel_id=1, source_target_pairs={{0,4},{4,8},{8,12},{12,16},{16,20},{20,24},{24,28},{28,0},{1,5},{5... | collective-permute-start | bytes 73736 | tf_op jit(solution)/shard_map/ppermute | solution.py:526
  4.5 3.9 %block_state.1 = (bf16[256,2048]{1,0:T(8,128)(2,1)S(1)}, f32[16,2048]{1,0:T(8,128)S(1)}, f32[16,2048]{1,0:T(8,128)S(1)}, f32[2,8,2048]{2,1,0:T(8,128)S(1)}, f32[...) custom-call(bf16[3,256,2048]{2,1,0:T(8,128)(2,1)} %projected_ref.3, bf16[3,3,2048]{2,1,0:T(4,128)(2,1)} %weight_hbm.1, ...), custom_call_target="tpu_custom_call" | custom-call | bytes 9000000 | tf_op jit(solution)/shard_map/block_state/pallas_call | solution.py:528
  8.5 0.9 %collective-permute-done.before_ref.refs_1_ = bf16[3,2,2048]{2,1,0:T(2,128)(2,1)S(1)} collective-permute-done((bf16[3,2,2048]{2,1,0:T(2,128)(2,1)S(1)}, bf16[3,2,2048]{2,1,0:T(2,128)(2,1)S(1)}, u32[]{:S(2)}, u32[]{:S(2)}) %collective-permute-start) | collective-permute-done | bytes 24608 | tf_op jit(solution)/shard_map/ppermute | solution.py:526
  9.4 0.1 head_tokens.1
  9.5 0.7 %collective-permute-start.1 = (bf16[16,2048]{1,0:T(8,128)(2,1)S(1)}, bf16[16,2048]{1,0:T(8,128)(2,1)S(1)}, u32[]{:S(2)}, u32[]{:S(2)}) collective-permute-start(bf16[16,2048]{1,0:T(8,128)(2,1)S(1)} %get-tuple-element.30.refs_1_), channel_id=1, source_target_pairs={{4,0},{0,4},{12,8},{8,12},{20,16},{16,20},{28,24},{24,28},{5,1},{1... | collective-permute-start | bytes 196616 | tf_op jit(solution)/shard_map/ppermute | solution.py:587
  10.2 0.0 copy-start
  10.2 2.4 %prepare.1 = (bf16[16,48,256]{2,1,0:T(8,128)(2,1)S(1)}, bf16[16,32,128]{2,1,0:T(8,128)(2,1)S(1)}, bf16[8,256,256]{2,1,0:T(8,128)(2,1)S(1)}, f32[256,2048]{1,0:T(8,128)S(1)}, bf16[256,2048]{1,0:T(8,128)(2,1)S(1)}) custom-call(s32[1]{0:T(128)} %bitcast.place_ref.refs_0_, bf16[3,256,2048]{2,1,0:T(8,128)(2,1)} %projected_ref.3, bf16[256,2048]{1,0:T(8,128)(2,1)} %residual_hbm.1, ...), custom_call_target="tpu_custom_call" | custom-call | bytes 6000000 | tf_op jit(solution)/shard_map/prepare/pallas_call | solution.py:561
  12.7 1.2 %collective-permute-done.1.refs_4_ = bf16[16,2048]{1,0:T(8,128)(2,1)S(1)} collective-permute-done((bf16[16,2048]{1,0:T(8,128)(2,1)S(1)}, bf16[16,2048]{1,0:T(8,128)(2,1)S(1)}, u32[]{:S(2)}, u32[]{:S(2)}) %collective-permute-start.1) | collective-permute-done | bytes 65568 | tf_op jit(solution)/shard_map/ppermute | solution.py:587
  13.9 0.1 join.1
  14.0 2.7 %collective-permute-start.2 = (bf16[16,2048]{1,0:T(8,128)(2,1)S(1)}, bf16[16,2048]{1,0:T(8,128)(2,1)S(1)}, u32[]{:S(2)}, u32[]{:S(2)}) collective-permute-start(bf16[16,2048]{1,0:T(8,128)(2,1)S(1)} %get-tuple-element.37), channel_id=1, source_target_pairs={{24,0},{28,4},{16,8},{20,12},{8,16},{12,20},{0,24},{4,28},{25,1},{... | collective-permute-start | bytes 196616 | tf_op jit(solution)/shard_map/ppermute | solution.py:599
  16.7 0.0 collective-permute-start.3
  16.7 1.7 %collective-permute-start.4 = (bf16[16,2048]{1,0:T(8,128)(2,1)S(1)}, bf16[16,2048]{1,0:T(8,128)(2,1)S(1)}, u32[]{:S(2)}, u32[]{:S(2)}) collective-permute-start(bf16[16,2048]{1,0:T(8,128)(2,1)S(1)} %get-tuple-element.37), channel_id=1, source_target_pairs={{8,0},{12,4},{0,8},{4,12},{24,16},{28,20},{16,24},{20,28},{9,1},{1... | collective-permute-start | bytes 196616 | tf_op jit(solution)/shard_map/ppermute | solution.py:599
  18.4 0.0 copy-done
  18.4 2.4 %local_conv.1.refs_1_ = f32[256,2048]{1,0:T(8,128)S(1)} custom-call(f32[256,2048]{1,0:T(8,128)S(1)} %get-tuple-element.24.gate_ref.refs_2_, bf16[256,2048]{1,0:T(8,128)(2,1)S(1)} %get-tuple-element.25.residual_ref, bf16[256,2048]{1,0:T(8,128)(2,1)S(1)} %get-tuple-element.26.product_ref, f32[8,2048]{1,0:T(8,128)S(1)} %get-tuple-element.29.first_ref, ...), custom_call_target="tpu_custom_call" | custom-call | bytes 15000000 | tf_op jit(solution)/shard_map/local_conv/pallas_call | solution.py:601
  20.9 0.0 collective-permute-done.2.refs_6_
  20.9 1.3 %collective-permute-done.3.refs_7_ = bf16[16,2048]{1,0:T(8,128)(2,1)S(1)} collective-permute-done((bf16[16,2048]{1,0:T(8,128)(2,1)S(1)}, bf16[16,2048]{1,0:T(8,128)(2,1)S(1)}, u32[]{:S(2)}, u32[]{:S(2)}) %collective-permute-start.3) | collective-permute-done | bytes 65568 | tf_op jit(solution)/shard_map/ppermute | solution.py:599
  22.2 0.0 collective-permute-done.4.refs_8_
  22.2 0.7 %add_carry.1 = (f32[256,2048]{1,0:T(8,128)S(1)}, f32[1,256]{1,0:T(1,128)S(1)}) custom-call(s32[1]{0:T(128)} %bitcast.place_ref.refs_0_, f32[256,2048]{1,0:T(8,128)S(1)} %local_conv.1.refs_1_, f32[256,2048]{1,0:T(8,128)S(1)} %get-tuple-element.24.gate_ref.refs_2_, bf16[8,256,256]{2,1,0:T(8,128)(2,1)S(1)} %get-tuple-element.34.refs_3_, ...), custom_call_target="tpu_custom_call" | custom-call | bytes 3000000 | tf_op jit(solution)/shard_map/add_carry/pallas_call | solution.py:610
  23.0 0.0 copy-start.1
  23.0 0.0 collective-permute-start.5
  23.0 1.7 %collective-permute-start.6 = (f32[1,256]{1,0:T(1,128)S(1)}, f32[1,256]{1,0:T(1,128)S(1)}, u32[]{:S(2)}, u32[]{:S(2)}) collective-permute-start(f32[1,256]{1,0:T(1,128)S(1)} %get-tuple-element.39.refs_2_), channel_id=1, source_target_pairs={{2,0},{3,1},{0,2},{1,3},{6,4},{7,5},{4,6},{5,7},{10,8},{11,9},{8,1... | collective-permute-start | bytes 3080 | tf_op jit(solution)/shard_map/ppermute | solution.py:619
  24.7 0.2 collective-permute-start.7
  24.8 1.0 %new_residual.1 = bf16[256,2048]{1,0:T(8,128)(2,1)} custom-call(f32[256,2048]{1,0:T(8,128)S(1)} %get-tuple-element.38.summed_ref.refs_0_), custom_call_target="tpu_custom_call" | custom-call | bytes 3000000 | tf_op jit(solution)/shard_map/new_residual/pallas_call | solution.py:622
  25.9 0.1 collective-permute-done.5.refs_3_
  26.0 0.6 %collective-permute-done.6.refs_4_ = f32[1,256]{1,0:T(1,128)S(1)} collective-permute-done((f32[1,256]{1,0:T(1,128)S(1)}, f32[1,256]{1,0:T(1,128)S(1)}, u32[]{:S(2)}, u32[]{:S(2)}) %collective-permute-start.6) | collective-permute-done | bytes 1056 | tf_op jit(solution)/shard_map/ppermute | solution.py:619
  26.6 0.0 collective-permute-done.7.refs_5_
  26.6 0.0 copy-done.1
  26.6 1.2 %normed.1 = bf16[256,2048]{1,0:T(8,128)(2,1)} custom-call(f32[256,2048]{1,0:T(8,128)S(1)} %get-tuple-element.38.summed_ref.refs_0_, f32[1,2048]{1,0:T(1,128)S(1)} %bitcast.6, f32[1,256]{1,0:T(1,128)S(1)} %get-tuple-element.39.refs_2_, f32[1,256]{1,0:T(1,128)S(1)} %collective-permute-done.5.refs_3_, f32[1,256]{1,0:T(1,128)S(1)} %collective-permute-done.6.refs_4_, ...), custom_call_target="tpu_custom_call" | custom-call | bytes 3000000 | tf_op jit(solution)/shard_map/normed/pallas_call | solution.py:622
  (1 shorter events, 0.0 us)
Async XLA Ops:
  1.6 7.8 %collective-permute-start = (bf16[3,2,2048]{2,1,0:T(2,128)(2,1)S(1)}, bf16[3,2,2048]{2,1,0:T(2,128)(2,1)S(1)}, u32[]{:S(2)}, u32[]{:S(2)}) collective-permute-start(bf16[3,2,2048]{2,1,0:T(2,128)(2,1)S(1)} %slice.3), channel_id=1, source_target_pairs={{0,4},{4,8},{8,12},{12,16},{16,20},{20,24},{24,28},{28,0},{1,5},{5... | collective-permute-start | bytes 73736 | tf_op jit(solution)/shard_map/ppermute | solution.py:526
  9.5 4.3 %collective-permute-start.1 = (bf16[16,2048]{1,0:T(8,128)(2,1)S(1)}, bf16[16,2048]{1,0:T(8,128)(2,1)S(1)}, u32[]{:S(2)}, u32[]{:S(2)}) collective-permute-start(bf16[16,2048]{1,0:T(8,128)(2,1)S(1)} %get-tuple-element.30.refs_1_), channel_id=1, source_target_pairs={{4,0},{0,4},{12,8},{8,12},{20,16},{16,20},{28,24},{24,28},{5,1},{1... | collective-permute-start | bytes 196616 | tf_op jit(solution)/shard_map/ppermute | solution.py:587
  10.2 8.2 %copy-start = (f32[2048]{0:T(1024)S(1)}, f32[2048]{0:T(1024)}, u32[]{:S(2)}) copy-start(f32[2048]{0:T(1024)} %param.11) | copy-start | bytes 24580
  14.0 6.9 %collective-permute-start.2 = (bf16[16,2048]{1,0:T(8,128)(2,1)S(1)}, bf16[16,2048]{1,0:T(8,128)(2,1)S(1)}, u32[]{:S(2)}, u32[]{:S(2)}) collective-permute-start(bf16[16,2048]{1,0:T(8,128)(2,1)S(1)} %get-tuple-element.37), channel_id=1, source_target_pairs={{24,0},{28,4},{16,8},{20,12},{8,16},{12,20},{0,24},{4,28},{25,1},{... | collective-permute-start | bytes 196616 | tf_op jit(solution)/shard_map/ppermute | solution.py:599
  16.7 5.5 %collective-permute-start.3 = (bf16[16,2048]{1,0:T(8,128)(2,1)S(1)}, bf16[16,2048]{1,0:T(8,128)(2,1)S(1)}, u32[]{:S(2)}, u32[]{:S(2)}) collective-permute-start(bf16[16,2048]{1,0:T(8,128)(2,1)S(1)} %get-tuple-element.37), channel_id=1, source_target_pairs={{16,0},{20,4},{24,8},{28,12},{0,16},{4,20},{8,24},{12,28},{17,1},{... | collective-permute-start | bytes 196616 | tf_op jit(solution)/shard_map/ppermute | solution.py:599
  16.7 5.5 %collective-permute-start.4 = (bf16[16,2048]{1,0:T(8,128)(2,1)S(1)}, bf16[16,2048]{1,0:T(8,128)(2,1)S(1)}, u32[]{:S(2)}, u32[]{:S(2)}) collective-permute-start(bf16[16,2048]{1,0:T(8,128)(2,1)S(1)} %get-tuple-element.37), channel_id=1, source_target_pairs={{8,0},{12,4},{0,8},{4,12},{24,16},{28,20},{16,24},{20,28},{9,1},{1... | collective-permute-start | bytes 196616 | tf_op jit(solution)/shard_map/ppermute | solution.py:599
  23.0 3.6 %copy-start.1 = (f32[2048]{0:T(1024)S(1)}, f32[2048]{0:T(1024)}, u32[]{:S(2)}) copy-start(f32[2048]{0:T(1024)} %param.13) | copy-start | bytes 24580
  23.0 3.0 %collective-permute-start.5 = (f32[1,256]{1,0:T(1,128)S(1)}, f32[1,256]{1,0:T(1,128)S(1)}, u32[]{:S(2)}, u32[]{:S(2)}) collective-permute-start(f32[1,256]{1,0:T(1,128)S(1)} %get-tuple-element.39.refs_2_), channel_id=1, source_target_pairs={{3,0},{2,1},{1,2},{0,3},{7,4},{6,5},{5,6},{4,7},{11,8},{10,9},{9,1... | collective-permute-start | bytes 3080 | tf_op jit(solution)/shard_map/ppermute | solution.py:619
  23.0 3.6 %collective-permute-start.6 = (f32[1,256]{1,0:T(1,128)S(1)}, f32[1,256]{1,0:T(1,128)S(1)}, u32[]{:S(2)}, u32[]{:S(2)}) collective-permute-start(f32[1,256]{1,0:T(1,128)S(1)} %get-tuple-element.39.refs_2_), channel_id=1, source_target_pairs={{2,0},{3,1},{0,2},{1,3},{6,4},{7,5},{4,6},{5,7},{10,8},{11,9},{8,1... | collective-permute-start | bytes 3080 | tf_op jit(solution)/shard_map/ppermute | solution.py:619
  24.7 1.9 %collective-permute-start.7 = (f32[1,256]{1,0:T(1,128)S(1)}, f32[1,256]{1,0:T(1,128)S(1)}, u32[]{:S(2)}, u32[]{:S(2)}) collective-permute-start(f32[1,256]{1,0:T(1,128)S(1)} %get-tuple-element.39.refs_2_), channel_id=1, source_target_pairs={{1,0},{0,1},{3,2},{2,3},{5,4},{4,5},{7,6},{6,7},{9,8},{8,9},{11,10... | collective-permute-start | bytes 3080 | tf_op jit(solution)/shard_map/ppermute | solution.py:619

commit v13 on v7

--- a/solution.py
+++ b/solution.py
@@ -120,44 +120,39 @@
     return [weights[tap, feature : feature + 1, lanes] for tap in range(weights.shape[0])]
 
 
-def state_kernel(
+def fetch_kernel(
+    place_ref,
     projected_ref,
     weight_hbm,
     rate_hbm,
     residue_hbm,
-    residual_hbm,
-    product_ref,
-    state_ref,
+    block_ref,
+    tail_ref,
+    weight_ref,
     mode_rate_ref,
-    head_ref,
-    weight_ref,
-    query_ref,
-    residue_ref,
-    residual_ref,
-    buffer_ref,
     ending_ref,
     shift_ref,
+    residue_ref,
+    place_out_ref,
+    last_ref,
     short_ref,
     rate_ref,
     sems,
-    small_sems,
 ):
-    rows, width = product_ref.shape
-    wides = width // WIDE
-    rate_copy = pltpu.make_async_copy(rate_hbm, rate_ref, small_sems.at[0])
-    rate_copy.start()
-    weight_copy = pltpu.make_async_copy(weight_hbm, short_ref, small_sems.at[1])
-    weight_copy.start()
-    copies = [pltpu.make_async_copy(projected_ref.at[1 + c], buffer_ref.at[c], sems.at[c]) for c in (0, 1)]
-    later = [
-        pltpu.make_async_copy(residue_hbm, residue_ref, sems.at[2]),
-        pltpu.make_async_copy(projected_ref.at[0], query_ref, sems.at[3]),
-        pltpu.make_async_copy(residual_hbm, residual_ref, sems.at[4]),
+    rows, width = block_ref.shape[1:]
+    place_out_ref[0] = place_ref[0]
+    copies = [
+        pltpu.make_async_copy(rate_hbm, rate_ref, sems.at[0]),
+        pltpu.make_async_copy(projected_ref.at[:, pl.ds(rows - 16, 16), :], last_ref, sems.at[1]),
+        pltpu.make_async_copy(weight_hbm, short_ref, sems.at[2]),
+        pltpu.make_async_copy(projected_ref.at[1], block_ref.at[0], sems.at[3]),
+        pltpu.make_async_copy(projected_ref.at[2], block_ref.at[1], sems.at[4]),
+        pltpu.make_async_copy(residue_hbm, residue_ref, sems.at[5]),
     ]
     for copy in copies:
         copy.start()
     shift_ref[...] = shift_matrix(rows)
-    rate_copy.wait()
+    copies[0].wait()
     mode_rate = per_channel(rate_ref[...])
     mode_rate_ref[...] = mode_rate
     eye = own_mode(BF16)
@@ -173,24 +168,43 @@
         ending_ref[tile // 2, lanes_of(tile % 2), :] = jnp.exp(exponent).astype(BF16)
 
     pipelined(width // LANES, exponents, endings)
-    weight_copy.wait()
-    weights = short_ref[...].astype(F32)
-    weight_ref[...] = weights
+    copies[1].wait()
+    for c in range(3):
+        tail_ref[c] = last_ref[c].astype(F32)[14:].astype(BF16)
+    copies[2].wait()
+    weight_ref[...] = short_ref[...].astype(F32)
+    for copy in copies[3:]:
+        copy.wait()
+
+
+def state_kernel(
+    block_ref,
+    weight_ref,
+    ending_ref,
+    shift_ref,
+    projected_ref,
+    residual_hbm,
+    product_ref,
+    state_ref,
+    query_ref,
+    residual_ref,
+    sems,
+):
+    rows, width = product_ref.shape
+    copies = [
+        pltpu.make_async_copy(projected_ref.at[0], query_ref, sems.at[0]),
+        pltpu.make_async_copy(residual_hbm, residual_ref, sems.at[1]),
+    ]
+    for copy in copies:
+        copy.start()
     mask = group_mask(F32)
-    for copy in copies:
-        copy.wait()
-    for copy in later:
-        copy.start()
 
     def fetch(wide):
-        return [earlier_tokens(shift_ref[...], buffer_ref[c, :, lanes_of(wide, WIDE)]) for c in (0, 1)]
+        return [earlier_tokens(shift_ref[...], block_ref[c, :, lanes_of(wide, WIDE)]) for c in (0, 1)]
 
     def multiply(wide, *earlier):
         here = lanes_of(wide, WIDE)
-        parts = []
-        for c in (0, 1):
-            head_ref[c, :, here] = buffer_ref[c, 0:16, here].astype(F32)[:8]
-            parts.append(wide_conv(buffer_ref[c, :, here], earlier[c], taps_of(weights, c + 1, here)))
+        parts = [wide_conv(block_ref[c, :, here], earlier[c], taps_of(weight_ref, c + 1, here)) for c in (0, 1)]
         product = (parts[0] * parts[1]).astype(BF16)
         product_ref[:, here] = product
         return (jnp.dot(ending_ref[wide], product, preferred_element_type=F32),)
@@ -200,8 +214,8 @@
             own = every[lanes_of(half), lanes_of(half)].reshape(GROUPS, MODES, LANES)
             state_ref[:, lanes_of((WIDE // LANES) * wide + half)] = jnp.sum(own * mask, axis=0)
 
-    pipelined(wides, fetch, multiply, leave)
-    for copy in later:
+    pipelined(width // WIDE, fetch, multiply, leave)
+    for copy in copies:
         copy.wait()
 
 
@@ -209,10 +223,12 @@
     return jnp.where(place_ref[0] > 0, before_ref[...].astype(F32), 0.0)
 
 
-def head_kernel(rows, place_ref, before_ref, head_ref, weight_ref, state_ref, mode_rate_ref, full_ref, first_ref):
+def head_kernel(place_ref, before_ref, block_ref, weight_ref, state_ref, mode_rate_ref, full_ref, first_ref):
     before = halo(before_ref, place_ref)
-    everything = slice(0, head_ref.shape[2])
-    parts = [short_conv(head_ref[c], before[c + 1], taps_of(weight_ref, c + 1, everything)) for c in (0, 1)]
+    rows, width = block_ref.shape[1:]
+    everything = slice(0, width)
+    heads = [block_ref[c, 0:16, :].astype(F32)[:8] for c in (0, 1)]
+    parts = [short_conv(heads[c], before[c + 1], taps_of(weight_ref, c + 1, everything)) for c in (0, 1)]
     first = (parts[0] * parts[1]).astype(BF16).astype(F32)
     first_ref[...] = first
     rate = mode_rate_ref[...]
@@ -227,14 +243,13 @@
     before_ref,
     weight_ref,
     mode_rate_ref,
+    shift_ref,
     inner_ref,
     entering_ref,
     carry_ref,
     gate_ref,
-    shift_ref,
 ):
     rows, width = gate_ref.shape
-    shift_ref[...] = shift_matrix(rows)
     residue = per_channel(residue_ref[...])
     wide = GROUPS * CHUNK
     step = index_of((CHUNK, LANES), 0).astype(F32)
@@ -392,7 +407,7 @@
         rate = mode_rate_ref[:, here]
         step = float(rows * stride)
         outer = jnp.zeros_like(rate)
-        for k, ref in enumerate(entry_refs[::-1], 1):
+        for k, ref in enumerate(entry_refs, 1):
             source = partner(run, k, radix)
             lag = jnp.maximum(run - 1 - source, 0).astype(F32) * step
             outer = outer + jnp.where(source < run, jnp.exp(-lag * rate) * ref[:, here].astype(F32), 0.0)
@@ -443,12 +458,14 @@
     scale_row = lax.rsqrt(squares / full_width + 1e-05)
     scale = jnp.concatenate([as_column(scale_row[:, lanes_of(k)]) for k in range(rows // LANES)], axis=0)
     copies = []
-    for tile in range(width // WIDE):
-        for half in range(WIDE // LANES):
-            here = lanes_of(tile * (WIDE // LANES) + half)
-            rounded_ref[:, here] = (summed_ref[:, here] * scale * gain_ref[:, here]).astype(BF16)
-        span = pl.ds(tile * WIDE, WIDE)
-        copies.append(pltpu.make_async_copy(rounded_ref.at[:, span], out_hbm.at[:, span], sems.at[tile]))
+    block = rows // 8
+    for start in range(0, rows, block):
+        span = slice(start, start + block)
+        for tile in range(width // LANES):
+            here = lanes_of(tile)
+            rounded_ref[span, here] = (summed_ref[span, here] * scale[span] * gain_ref[:, here]).astype(BF16)
+        there = pl.ds(start, block)
+        copies.append(pltpu.make_async_copy(rounded_ref.at[there, :], out_hbm.at[there, :], sems.at[start // block]))
         copies[-1].start()
     for copy in copies:
         copy.wait()
@@ -513,58 +530,65 @@
     def bf16(*shape):
         return jax.ShapeDtypeStruct(shape, BF16)
 
-    before = lax.ppermute(projected[:, rows - (taps - 1) :, :], "ctx", ring(peers, 1))
-
-    product, state, mode_rate, head, weights, query, residue, residual_here = pl.pallas_call(
-        state_kernel,
-        in_specs=[hbm_spec] * 5,
+    block, tail, weights, mode_rate, ending, shift, residue, place = pl.pallas_call(
+        fetch_kernel,
+        in_specs=[smem_spec] + [hbm_spec] * 4,
+        out_specs=[vmem_spec] * 7 + [smem_spec],
         out_shape=[
-            bf16(rows, width),
+            bf16(2, rows, width),
+            bf16(3, taps - 1, width),
+            f32(*short_weight.shape),
             f32(MODES, width),
-            f32(MODES, width),
-            f32(2, 8, width),
-            f32(*short_weight.shape),
-            bf16(rows, width),
+            bf16(wides, WIDE, rows),
+            bf16(2 * rows, rows),
             f32(MODES, residues.shape[0]),
-            bf16(rows, width),
+            jax.ShapeDtypeStruct((1,), jnp.int32),
         ],
         scratch_shapes=[
-            pltpu.VMEM((2, rows, width), BF16),
-            pltpu.VMEM((wides, WIDE, rows), BF16),
-            pltpu.VMEM((2 * rows, rows), BF16),
+            pltpu.VMEM((3, 16, width), BF16),
             pltpu.VMEM(short_weight.shape, BF16),
             pltpu.VMEM((MODES, rates.shape[0]), F32),
-            pltpu.SemaphoreType.DMA((5,)),
-            pltpu.SemaphoreType.DMA((2,)),
+            pltpu.SemaphoreType.DMA((6,)),
         ],
         compiler_params=params(),
-        cost_estimate=cost(3),
+        cost_estimate=cost(2),
+        name="fetch",
+    )(place, kept(projected), kept(short_weight), kept(rates.T), kept(residues.T))
+
+    before = lax.ppermute(tail, "ctx", ring(peers, 1))
+
+    product, state, query, residual_here = pl.pallas_call(
+        state_kernel,
+        in_specs=[vmem_spec] * 4 + [hbm_spec] * 2,
+        out_shape=[bf16(rows, width), f32(MODES, width), bf16(rows, width), bf16(rows, width)],
+        scratch_shapes=[pltpu.SemaphoreType.DMA((2,))],
+        compiler_params=params(),
+        cost_estimate=cost(2),
         name="block_state",
-    )(kept(projected), kept(short_weight), kept(rates.T), kept(residues.T), kept(residual))
+    )(block, weights, ending, shift, kept(projected), kept(residual))
 
     full_state, first = pl.pallas_call(
-        lambda *refs: head_kernel(rows, *refs),
+        head_kernel,
         in_specs=[smem_spec] + [vmem_spec] * 5,
         out_shape=[bf16(MODES, width), f32(8, width)],
         compiler_params=params(),
         cost_estimate=cost(0.2),
         name="head_tokens",
-    )(place, before, head, weights, state, mode_rate)
+    )(place, before, block, weights, state, mode_rate)
 
     inner, entering, carry_table, gate = pl.pallas_call(
         prepare_kernel,
-        in_specs=[smem_spec] + [vmem_spec] * 5,
+        in_specs=[smem_spec] + [vmem_spec] * 6,
         out_shape=[
             bf16(tiles, CHUNK + MODES, GROUPS * CHUNK),
             bf16(tiles, CHUNK, LANES),
             bf16(wides, rows, WIDE),
             f32(rows, width),
         ],
-        scratch_shapes=[pltpu.VMEM((2 * rows, rows), BF16)],
         compiler_params=params(),
         cost_estimate=cost(2),
         name="prepare",
-    )(place, query, residue, before, weights, mode_rate)
+    )(place, query, residue, before, weights, mode_rate, shift)
 
     group, entry, stride = full_state, jnp.zeros((MODES, width), F32), 1
     levels = radices(peers)
@@ -584,7 +608,7 @@
             name="join",
         )(place, group, mode_rate, entry, *others)
         stride = size
-    received = [lax.ppermute(group, "ctx", route) for route in routes(peers, stride, levels[-1])[::-1]]
+    received = [lax.ppermute(group, "ctx", route) for route in routes(peers, stride, levels[-1])]
 
     base = pl.pallas_call(
         local_kernel,
@@ -604,14 +628,14 @@
         name="add_carry",
     )(place, base, gate, carry_table, mode_rate, entry, *received)
 
-    parts = [lax.ppermute(squares, "fsdp", route) for route in routes(count, 1, count)[::-1]]
+    parts = [lax.ppermute(squares, "fsdp", route) for route in routes(count, 1, count)]
 
     def write(kernel, operands, name):
         return pl.pallas_call(
             kernel,
             out_specs=hbm_spec,
             out_shape=bf16(rows, width),
-            scratch_shapes=[pltpu.VMEM((rows, width), BF16), pltpu.SemaphoreType.DMA((wides,))],
+            scratch_shapes=[pltpu.VMEM((rows, width), BF16), pltpu.SemaphoreType.DMA((max(8, wides),))],
             compiler_params=params(),
             cost_estimate=cost(1),
             name=name,

time: 27.8 us -> 30.8 us (1.11)
  Pallas kernels: 11.4 us -> 14.8 us
  local copies, waits for them, and re-layouts: 0.94 us -> 0.02 us
  waiting for transfers between devices: 4.94 us -> 5.49 us
    pallas_call x3 -> x4, Pallas kernels: 5.81 us -> 7.99 us  [the longest x1 2.94 us: per_device(): pl.pallas_call(prepare_kernel, in_specs=[smem_spec] + [vmem_spec] * 6, ou...]
    ppermute x1, waiting for transfers between devices: 1.36 us -> 2.85 us  [per_device(): before = lax.ppermute(tail, 'ctx', ring(peers, 1))]
    slice x1 -> x0, local copies, waits for them, and re-layouts: 0.92 us -> none  [per_device(): projected[:, rows - (taps - 1):, :]]
    ppermute x4, waiting for transfers between devices: 2.86 us -> 1.94 us  [per_device(): lax.ppermute(group, 'ctx', route)]
    pallas_call x1, Pallas kernels: 0.11 us -> 0.75 us  [per_device(): pl.pallas_call(lambda *refs, radix=radix, stride=stride: join_kernel(rows...]
    pallas_call x1, Pallas kernels: 0.74 us -> 1.38 us  [per_device(): pl.pallas_call(lambda *refs: carry_kernel(stride, levels[-1], *refs), in_...]
  transfers between devices with their start and end apart: 8 -> 8, of which waited for: 5 -> 5; matrix products, arithmetic and copies ran while one was open for 0% -> 0% of each run, Pallas kernels for 33% -> 28%
where the time goes in v13:
time: 30.8 us; the launch traced here: 30.4 us
  Pallas kernels  14.8 us (48%)
  starting transfers between devices  9.4 us (31%)
  waiting for transfers between devices  5.49 us (18%)
  between operations  0.71 us (2%)
    ppermute x4, starting transfers between devices, per_device(): lax.ppermute(group, 'ctx', route)  4.52 us
    ppermute x1, starting transfers between devices, per_device(): before = lax.ppermute(tail, 'ctx', ring(peers, 1))  2.99 us
    pallas_call x1, Pallas kernels, per_device(): pl.pallas_call(prepare_kernel, in_specs=[smem_spec] + [vmem_spec] * 6, ou...  2.94 us
    ppermute x1, waiting for transfers between devices, per_device(): before = lax.ppermute(tail, 'ctx', ring(peers, 1))  2.85 us
    pallas_call x1, Pallas kernels, per_device(): pl.pallas_call(local_kernel, out_shape=f32(rows, width), compiler_params=...  2.42 us
    pallas_call x1, Pallas kernels, per_device(): pl.pallas_call(fetch_kernel, in_specs=[smem_spec] + [hbm_spec] * 4, out_s...  2.27 us
    pallas_call x2, Pallas kernels, write(): pl.pallas_call(kernel, out_specs=hbm_spec, out_shape=bf16(rows, width), s...  2.21 us
    pallas_call x1, Pallas kernels, per_device(): pl.pallas_call(state_kernel, in_specs=[vmem_spec] * 4 + [hbm_spec] * 2, o...  1.99 us
  transfers between devices with their start and end apart: 8, of which 5 were waited for; matrix products, arithmetic and copies ran while one was open for 0% of the time, Pallas kernels for 28%

profile of v13, /device:TPU:0, one launch (start us, length us, event | category | flops | bytes accessed | tf_op | source)
XLA Modules:
  0.0 30.4 jit_solution(6681273237918460225)
XLA Ops:
  0.6 2.3 %fetch.1 = (bf16[2,256,2048]{2,1,0:T(8,128)(2,1)S(1)}, bf16[3,2,2048]{2,1,0:T(2,128)(2,1)S(1)}, f32[3,3,2048]{2,1,0:T(4,128)S(1)}, f32[16,2048]{1,0:T(8,128)S(1)...) custom-call(s32[1]{0:T(128)} %bitcast.place_ref, ...), custom_call_target="tpu_custom_call" | custom-call | bytes 6000000 | tf_op jit(solution)/shard_map/fetch/pallas_call | solution.py:533
  2.9 3.0 %collective-permute-start = (bf16[3,2,2048]{2,1,0:T(2,128)(2,1)S(1)}, bf16[3,2,2048]{2,1,0:T(2,128)(2,1)S(1)}, u32[]{:S(2)}, u32[]{:S(2)}) collective-permute-start(bf16[3,2,2048]{2,1,0:T(2,128)(2,1)S(1)} %get-tuple-element.33), channel_id=1, source_target_pairs={{0,4},{4,8},{8,12},{12,16},{16,20},{20,24},{24,28},{28,0},{1,5},{5... | collective-permute-start | bytes 73736 | tf_op jit(solution)/shard_map/ppermute | solution.py:558
  5.9 2.0 %block_state.1 = (bf16[256,2048]{1,0:T(8,128)(2,1)S(1)}, f32[16,2048]{1,0:T(8,128)S(1)}, bf16[256,2048]{1,0:T(8,128)(2,1)S(1)}, bf16[256,2048]{1,0:T(8,128)(2,1)S(1)}) custom-call(bf16[2,256,2048]{2,1,0:T(8,128)(2,1)S(1)} %get-tuple-element.27.block_ref, f32[3,3,2048]{2,1,0:T(4,128)S(1)} %get-tuple-element.28.weight_ref, ...), custom_call_target="tpu_custom_call" | custom-call | bytes 6000000 | tf_op jit(solution)/shard_map/block_state/pallas_call | solution.py:560
  7.9 2.8 %collective-permute-done.before_ref = bf16[3,2,2048]{2,1,0:T(2,128)(2,1)S(1)} collective-permute-done((bf16[3,2,2048]{2,1,0:T(2,128)(2,1)S(1)}, bf16[3,2,2048]{2,1,0:T(2,128)(2,1)S(1)}, u32[]{:S(2)}, u32[]{:S(2)}) %collective-permute-start) | collective-permute-done | bytes 24608 | tf_op jit(solution)/shard_map/ppermute | solution.py:558
  10.7 0.0 copy-start
  10.8 0.8 %head_tokens.1 = (bf16[16,2048]{1,0:T(8,128)(2,1)S(1)}, f32[8,2048]{1,0:T(8,128)S(1)}) custom-call(s32[1]{0:T(128)} %get-tuple-element.26.place_ref.refs_0_, bf16[3,2,2048]{2,1,0:T(2,128)(2,1)S(1)} %collective-permute-done.before_ref, bf16[2,256,2048]{2,1,0:T(8,128)(2,1)S(1)} %get-tuple-element.27.block_ref, f32[3,3,2048]{2,1,0:T(4,128)S(1)} %get-tuple-element.28.weight_ref, ...), custom_call_target="tpu_custom_call" | custom-call | bytes 600000 | tf_op jit(solution)/shard_map/head_tokens/pallas_call | solution.py:570
  11.5 0.1 collective-permute-start.1
  11.6 2.9 %prepare.1 = (bf16[16,48,256]{2,1,0:T(8,128)(2,1)S(1)}, bf16[16,32,128]{2,1,0:T(8,128)(2,1)S(1)}, bf16[8,256,256]{2,1,0:T(8,128)(2,1)S(1)}, f32[256,2048]{1,0:T(8,128)S(1)}) custom-call(s32[1]{0:T(128)} %get-tuple-element.26.place_ref.refs_0_, bf16[256,2048]{1,0:T(8,128)(2,1)S(1)} %get-tuple-element.31.query_ref, ...), custom_call_target="tpu_custom_call" | custom-call | bytes 6000000 | tf_op jit(solution)/shard_map/prepare/pallas_call | solution.py:579
  14.6 1.3 %collective-permute-done.1.refs_4_ = bf16[16,2048]{1,0:T(8,128)(2,1)S(1)} collective-permute-done((bf16[16,2048]{1,0:T(8,128)(2,1)S(1)}, bf16[16,2048]{1,0:T(8,128)(2,1)S(1)}, u32[]{:S(2)}, u32[]{:S(2)}) %collective-permute-start.1) | collective-permute-done | bytes 65568 | tf_op jit(solution)/shard_map/ppermute | solution.py:599
  15.9 0.8 %join.1 = (f32[16,2048]{1,0:T(8,128)S(1)}, bf16[16,2048]{1,0:T(8,128)(2,1)S(1)}) custom-call(s32[1]{0:T(128)} %get-tuple-element.26.place_ref.refs_0_, bf16[16,2048]{1,0:T(8,128)(2,1)S(1)} %get-tuple-element.40.refs_1_, f32[16,2048]{1,0:T(8,128)S(1)} %get-tuple-element.34.mode_rate_ref.refs_2_.refs_4_, f32[16,2048]{1,0:T(8,128)S(1)} %broadcast_in_dim.10.refs_3_, ...), custom_call_target="tpu_custom_call" | custom-call | bytes 600000 | tf_op jit(solution)/shard_map/join/pallas_call | solution.py:602
  16.6 2.1 %collective-permute-start.4 = (bf16[16,2048]{1,0:T(8,128)(2,1)S(1)}, bf16[16,2048]{1,0:T(8,128)(2,1)S(1)}, u32[]{:S(2)}, u32[]{:S(2)}) collective-permute-start(bf16[16,2048]{1,0:T(8,128)(2,1)S(1)} %get-tuple-element.47), channel_id=1, source_target_pairs={{24,0},{28,4},{16,8},{20,12},{8,16},{12,20},{0,24},{4,28},{25,1},{... | collective-permute-start | bytes 196616 | tf_op jit(solution)/shard_map/ppermute | solution.py:611
  18.7 0.0 collective-permute-start.3
  18.7 2.4 %collective-permute-start.2 = (bf16[16,2048]{1,0:T(8,128)(2,1)S(1)}, bf16[16,2048]{1,0:T(8,128)(2,1)S(1)}, u32[]{:S(2)}, u32[]{:S(2)}) collective-permute-start(bf16[16,2048]{1,0:T(8,128)(2,1)S(1)} %get-tuple-element.47), channel_id=1, source_target_pairs={{8,0},{12,4},{0,8},{4,12},{24,16},{28,20},{16,24},{20,28},{9,1},{1... | collective-permute-start | bytes 196616 | tf_op jit(solution)/shard_map/ppermute | solution.py:611
  21.1 0.0 copy-done
  21.1 2.4 %local_conv.1.refs_1_ = f32[256,2048]{1,0:T(8,128)S(1)} custom-call(f32[256,2048]{1,0:T(8,128)S(1)} %get-tuple-element.35.gate_ref.refs_2_, bf16[256,2048]{1,0:T(8,128)(2,1)S(1)} %get-tuple-element.36.residual_ref, bf16[256,2048]{1,0:T(8,128)(2,1)S(1)} %get-tuple-element.37.product_ref, f32[8,2048]{1,0:T(8,128)S(1)} %get-tuple-element.39.first_ref, ...), custom_call_target="tpu_custom_call" | custom-call | bytes 15000000 | tf_op jit(solution)/shard_map/local_conv/pallas_call | solution.py:613
  23.5 0.0 collective-permute-done.4.refs_8_
  23.5 0.6 %collective-permute-done.3.refs_7_ = bf16[16,2048]{1,0:T(8,128)(2,1)S(1)} collective-permute-done((bf16[16,2048]{1,0:T(8,128)(2,1)S(1)}, bf16[16,2048]{1,0:T(8,128)(2,1)S(1)}, u32[]{:S(2)}, u32[]{:S(2)}) %collective-permute-start.3) | collective-permute-done | bytes 65568 | tf_op jit(solution)/shard_map/ppermute | solution.py:611
  24.2 0.0 collective-permute-done.2.refs_6_
  24.2 1.4 %add_carry.1 = (f32[256,2048]{1,0:T(8,128)S(1)}, f32[1,256]{1,0:T(1,128)S(1)}) custom-call(s32[1]{0:T(128)} %get-tuple-element.26.place_ref.refs_0_, f32[256,2048]{1,0:T(8,128)S(1)} %local_conv.1.refs_1_, f32[256,2048]{1,0:T(8,128)S(1)} %get-tuple-element.35.gate_ref.refs_2_, bf16[8,256,256]{2,1,0:T(8,128)(2,1)S(1)} %get-tuple-element.44.refs_3_, ...), custom_call_target="tpu_custom_call" | custom-call | bytes 3000000 | tf_op jit(solution)/shard_map/add_carry/pallas_call | solution.py:622
  25.6 0.0 copy-start.1
  25.6 0.0 collective-permute-start.7
  25.6 1.8 %collective-permute-start.6 = (f32[1,256]{1,0:T(1,128)S(1)}, f32[1,256]{1,0:T(1,128)S(1)}, u32[]{:S(2)}, u32[]{:S(2)}) collective-permute-start(f32[1,256]{1,0:T(1,128)S(1)} %get-tuple-element.49.refs_2_), channel_id=1, source_target_pairs={{2,0},{3,1},{0,2},{1,3},{6,4},{7,5},{4,6},{5,7},{10,8},{11,9},{8,1... | collective-permute-start | bytes 3080 | tf_op jit(solution)/shard_map/ppermute | solution.py:631
  27.4 0.1 collective-permute-start.5
  27.5 1.0 %new_residual.1 = bf16[256,2048]{1,0:T(8,128)(2,1)} custom-call(f32[256,2048]{1,0:T(8,128)S(1)} %get-tuple-element.48.summed_ref.refs_0_), custom_call_target="tpu_custom_call" | custom-call | bytes 3000000 | tf_op jit(solution)/shard_map/new_residual/pallas_call | solution.py:634
  28.5 0.1 collective-permute-done.7.refs_5_
  28.6 0.6 %collective-permute-done.6.refs_4_ = f32[1,256]{1,0:T(1,128)S(1)} collective-permute-done((f32[1,256]{1,0:T(1,128)S(1)}, f32[1,256]{1,0:T(1,128)S(1)}, u32[]{:S(2)}, u32[]{:S(2)}) %collective-permute-start.6) | collective-permute-done | bytes 1056 | tf_op jit(solution)/shard_map/ppermute | solution.py:631
  29.2 0.0 collective-permute-done.5.refs_3_
  29.2 0.0 copy-done.1
  29.2 1.2 %normed.1 = bf16[256,2048]{1,0:T(8,128)(2,1)} custom-call(f32[256,2048]{1,0:T(8,128)S(1)} %get-tuple-element.48.summed_ref.refs_0_, f32[1,2048]{1,0:T(1,128)S(1)} %bitcast.6, f32[1,256]{1,0:T(1,128)S(1)} %get-tuple-element.49.refs_2_, f32[1,256]{1,0:T(1,128)S(1)} %collective-permute-done.5.refs_3_, f32[1,256]{1,0:T(1,128)S(1)} %collective-permute-done.6.refs_4_, ...), custom_call_target="tpu_custom_call" | custom-call | bytes 3000000 | tf_op jit(solution)/shard_map/normed/pallas_call | solution.py:634
  (1 shorter events, 0.0 us)
Async XLA Ops:
  2.9 7.8 %collective-permute-start = (bf16[3,2,2048]{2,1,0:T(2,128)(2,1)S(1)}, bf16[3,2,2048]{2,1,0:T(2,128)(2,1)S(1)}, u32[]{:S(2)}, u32[]{:S(2)}) collective-permute-start(bf16[3,2,2048]{2,1,0:T(2,128)(2,1)S(1)} %get-tuple-element.33), channel_id=1, source_target_pairs={{0,4},{4,8},{8,12},{12,16},{16,20},{20,24},{24,28},{28,0},{1,5},{5... | collective-permute-start | bytes 73736 | tf_op jit(solution)/shard_map/ppermute | solution.py:558
  10.7 10.4 %copy-start = (f32[2048]{0:T(1024)S(1)}, f32[2048]{0:T(1024)}, u32[]{:S(2)}) copy-start(f32[2048]{0:T(1024)} %param.11) | copy-start | bytes 24580
  11.5 4.3 %collective-permute-start.1 = (bf16[16,2048]{1,0:T(8,128)(2,1)S(1)}, bf16[16,2048]{1,0:T(8,128)(2,1)S(1)}, u32[]{:S(2)}, u32[]{:S(2)}) collective-permute-start(bf16[16,2048]{1,0:T(8,128)(2,1)S(1)} %get-tuple-element.40.refs_1_), channel_id=1, source_target_pairs={{4,0},{0,4},{12,8},{8,12},{20,16},{16,20},{28,24},{24,28},{5,1},{1... | collective-permute-start | bytes 196616 | tf_op jit(solution)/shard_map/ppermute | solution.py:599
  16.6 6.9 %collective-permute-start.4 = (bf16[16,2048]{1,0:T(8,128)(2,1)S(1)}, bf16[16,2048]{1,0:T(8,128)(2,1)S(1)}, u32[]{:S(2)}, u32[]{:S(2)}) collective-permute-start(bf16[16,2048]{1,0:T(8,128)(2,1)S(1)} %get-tuple-element.47), channel_id=1, source_target_pairs={{24,0},{28,4},{16,8},{20,12},{8,16},{12,20},{0,24},{4,28},{25,1},{... | collective-permute-start | bytes 196616 | tf_op jit(solution)/shard_map/ppermute | solution.py:611
  18.7 5.5 %collective-permute-start.3 = (bf16[16,2048]{1,0:T(8,128)(2,1)S(1)}, bf16[16,2048]{1,0:T(8,128)(2,1)S(1)}, u32[]{:S(2)}, u32[]{:S(2)}) collective-permute-start(bf16[16,2048]{1,0:T(8,128)(2,1)S(1)} %get-tuple-element.47), channel_id=1, source_target_pairs={{16,0},{20,4},{24,8},{28,12},{0,16},{4,20},{8,24},{12,28},{17,1},{... | collective-permute-start | bytes 196616 | tf_op jit(solution)/shard_map/ppermute | solution.py:611
  18.7 5.5 %collective-permute-start.2 = (bf16[16,2048]{1,0:T(8,128)(2,1)S(1)}, bf16[16,2048]{1,0:T(8,128)(2,1)S(1)}, u32[]{:S(2)}, u32[]{:S(2)}) collective-permute-start(bf16[16,2048]{1,0:T(8,128)(2,1)S(1)} %get-tuple-element.47), channel_id=1, source_target_pairs={{8,0},{12,4},{0,8},{4,12},{24,16},{28,20},{16,24},{20,28},{9,1},{1... | collective-permute-start | bytes 196616 | tf_op jit(solution)/shard_map/ppermute | solution.py:611
  25.6 3.6 %copy-start.1 = (f32[2048]{0:T(1024)S(1)}, f32[2048]{0:T(1024)}, u32[]{:S(2)}) copy-start(f32[2048]{0:T(1024)} %param.13) | copy-start | bytes 24580
  25.6 3.0 %collective-permute-start.7 = (f32[1,256]{1,0:T(1,128)S(1)}, f32[1,256]{1,0:T(1,128)S(1)}, u32[]{:S(2)}, u32[]{:S(2)}) collective-permute-start(f32[1,256]{1,0:T(1,128)S(1)} %get-tuple-element.49.refs_2_), channel_id=1, source_target_pairs={{3,0},{2,1},{1,2},{0,3},{7,4},{6,5},{5,6},{4,7},{11,8},{10,9},{9,1... | collective-permute-start | bytes 3080 | tf_op jit(solution)/shard_map/ppermute | solution.py:631
  25.6 3.6 %collective-permute-start.6 = (f32[1,256]{1,0:T(1,128)S(1)}, f32[1,256]{1,0:T(1,128)S(1)}, u32[]{:S(2)}, u32[]{:S(2)}) collective-permute-start(f32[1,256]{1,0:T(1,128)S(1)} %get-tuple-element.49.refs_2_), channel_id=1, source_target_pairs={{2,0},{3,1},{0,2},{1,3},{6,4},{7,5},{4,6},{5,7},{10,8},{11,9},{8,1... | collective-permute-start | bytes 3080 | tf_op jit(solution)/shard_map/ppermute | solution.py:631
  27.4 1.8 %collective-permute-start.5 = (f32[1,256]{1,0:T(1,128)S(1)}, f32[1,256]{1,0:T(1,128)S(1)}, u32[]{:S(2)}, u32[]{:S(2)}) collective-permute-start(f32[1,256]{1,0:T(1,128)S(1)} %get-tuple-element.49.refs_2_), channel_id=1, source_target_pairs={{1,0},{0,1},{3,2},{2,3},{5,4},{4,5},{7,6},{6,7},{9,8},{8,9},{11,10... | collective-permute-start | bytes 3080 | tf_op jit(solution)/shard_map/ppermute | solution.py:631

commit v14 on v7

--- a/solution.py
+++ b/solution.py
@@ -33,19 +33,24 @@
     return slice(tile * width, (tile + 1) * width)
 
 
-def per_channel(table):
-    groups = table.shape[1]
-    width = groups * CHANNELS_PER_GRP
+def selectors(groups):
+    shape = (groups, WIDE)
+    found = []
+    for tile in range(groups * CHANNELS_PER_GRP // WIDE):
+        own = index_of(shape, 0) == index_of(shape, 1) // CHANNELS_PER_GRP + tile * (WIDE // CHANNELS_PER_GRP)
+        found.append(jnp.where(own, 1.0, 0.0).astype(BF16))
+    return found
+
+
+def per_channel(table, chosen):
     high = table.astype(BF16)
     rest = table - high.astype(F32)
     middle = rest.astype(BF16)
     low = (rest - middle.astype(F32)).astype(BF16)
     terms = jnp.concatenate([high, middle, low], axis=0)
     parts = []
-    for tile in range(width // WIDE):
-        shape = (groups, WIDE)
-        own = index_of(shape, 0) == index_of(shape, 1) // CHANNELS_PER_GRP + tile * (WIDE // CHANNELS_PER_GRP)
-        three = jnp.dot(terms, jnp.where(own, 1.0, 0.0).astype(BF16), preferred_element_type=F32)
+    for selector in chosen:
+        three = jnp.dot(terms, selector, preferred_element_type=F32)
         parts.append(three[:MODES] + three[MODES : 2 * MODES] + three[2 * MODES :])
     return jnp.concatenate(parts, axis=1)
 
@@ -157,12 +162,14 @@
     for copy in copies:
         copy.start()
     shift_ref[...] = shift_matrix(rows)
-    rate_copy.wait()
-    mode_rate = per_channel(rate_ref[...])
-    mode_rate_ref[...] = mode_rate
+    chosen = selectors(rate_ref.shape[1])
     eye = own_mode(BF16)
+    mask = group_mask(F32)
     token = index_of((2 * LANES, rows), 1)
     left = jnp.where(token < 2, -1e30, (token - (rows - 1)).astype(F32)).astype(BF16)
+    rate_copy.wait()
+    mode_rate = per_channel(rate_ref[...], chosen)
+    mode_rate_ref[...] = mode_rate
 
     def exponents(tile):
         high, low = split(mode_rate[:, lanes_of(tile)])
@@ -176,7 +183,6 @@
     weight_copy.wait()
     weights = short_ref[...].astype(F32)
     weight_ref[...] = weights
-    mask = group_mask(F32)
     for copy in copies:
         copy.wait()
     for copy in later:
@@ -235,7 +241,7 @@
 ):
     rows, width = gate_ref.shape
     shift_ref[...] = shift_matrix(rows)
-    residue = per_channel(residue_ref[...])
+    residue = per_channel(residue_ref[...], selectors(residue_ref.shape[1]))
     wide = GROUPS * CHUNK
     step = index_of((CHUNK, LANES), 0).astype(F32)
     causal = (index_of((CHUNK, wide), 1) & (CHUNK - 1)) <= index_of((CHUNK, wide), 0)
@@ -443,12 +449,14 @@
     scale_row = lax.rsqrt(squares / full_width + 1e-05)
     scale = jnp.concatenate([as_column(scale_row[:, lanes_of(k)]) for k in range(rows // LANES)], axis=0)
     copies = []
-    for tile in range(width // WIDE):
-        for half in range(WIDE // LANES):
-            here = lanes_of(tile * (WIDE // LANES) + half)
-            rounded_ref[:, here] = (summed_ref[:, here] * scale * gain_ref[:, here]).astype(BF16)
-        span = pl.ds(tile * WIDE, WIDE)
-        copies.append(pltpu.make_async_copy(rounded_ref.at[:, span], out_hbm.at[:, span], sems.at[tile]))
+    block = rows // 8
+    for start in range(0, rows, block):
+        span = slice(start, start + block)
+        for tile in range(width // LANES):
+            here = lanes_of(tile)
+            rounded_ref[span, here] = (summed_ref[span, here] * scale[span] * gain_ref[:, here]).astype(BF16)
+        there = pl.ds(start, block)
+        copies.append(pltpu.make_async_copy(rounded_ref.at[there, :], out_hbm.at[there, :], sems.at[start // block]))
         copies[-1].start()
     for copy in copies:
         copy.wait()
@@ -611,7 +619,7 @@
             kernel,
             out_specs=hbm_spec,
             out_shape=bf16(rows, width),
-            scratch_shapes=[pltpu.VMEM((rows, width), BF16), pltpu.SemaphoreType.DMA((wides,))],
+            scratch_shapes=[pltpu.VMEM((rows, width), BF16), pltpu.SemaphoreType.DMA((max(8, wides),))],
             compiler_params=params(),
             cost_estimate=cost(1),
             name=name,

time: 27.8 us -> 27.7 us (level)
  no operation moved by 1% of the time
where the time goes in v14:
time: 27.7 us; the launch traced here: 27.4 us
  Pallas kernels  11.3 us (41%)
  starting transfers between devices  9.55 us (34%)
  waiting for transfers between devices  4.99 us (18%)
  local copies, waits for them, and re-layouts  0.94 us (3%)
  between operations  0.7 us (3%)
    ppermute x4, starting transfers between devices, per_device(): lax.ppermute(group, 'ctx', route)  4.69 us
    pallas_call x1, Pallas kernels, per_device(): pl.pallas_call(state_kernel, in_specs=[hbm_spec] * 5, out_shape=[bf16(row...  3.43 us
    ppermute x1, starting transfers between devices, per_device(): lax.ppermute(projected[:, rows - (taps - 1):, :], 'ctx', ring(peers, 1))  2.99 us
    ppermute x4, waiting for transfers between devices, per_device(): lax.ppermute(group, 'ctx', route)  2.88 us
    pallas_call x1, Pallas kernels, per_device(): pl.pallas_call(local_kernel, out_shape=f32(rows, width), compiler_params=...  2.42 us
    pallas_call x1, Pallas kernels, per_device(): pl.pallas_call(prepare_kernel, in_specs=[smem_spec] + [vmem_spec] * 5, ou...  2.22 us
    pallas_call x2, Pallas kernels, write(): pl.pallas_call(kernel, out_specs=hbm_spec, out_shape=bf16(rows, width), s...  2.21 us
    ppermute x3, starting transfers between devices, per_device(): lax.ppermute(squares, 'fsdp', route)  1.87 us
  transfers between devices with their start and end apart: 8, of which 5 were waited for; matrix products, arithmetic and copies ran while one was open for 0% of the time, Pallas kernels for 33%

profile of v14, /device:TPU:0, one launch (start us, length us, event | category | flops | bytes accessed | tf_op | source)
XLA Modules:
  0.0 27.4 jit_solution(11789146575677934373)
XLA Ops:
  0.6 0.9 %slice.3 = bf16[3,2,2048]{2,1,0:T(2,128)(2,1)S(1)} slice(bf16[3,256,2048]{2,1,0:T(8,128)(2,1)} %projected_ref.1), slice={[0:3], [254:256], [0:2048]} | slice | bytes 49152 | tf_op jit(solution)/shard_map/slice | solution.py:524
  1.6 3.0 %collective-permute-start = (bf16[3,2,2048]{2,1,0:T(2,128)(2,1)S(1)}, bf16[3,2,2048]{2,1,0:T(2,128)(2,1)S(1)}, u32[]{:S(2)}, u32[]{:S(2)}) collective-permute-start(bf16[3,2,2048]{2,1,0:T(2,128)(2,1)S(1)} %slice.3), channel_id=1, source_target_pairs={{0,4},{4,8},{8,12},{12,16},{16,20},{20,24},{24,28},{28,0},{1,5},{5... | collective-permute-start | bytes 73736 | tf_op jit(solution)/shard_map/ppermute | solution.py:524
  4.5 3.4 %block_state.1 = (bf16[256,2048]{1,0:T(8,128)(2,1)S(1)}, f32[16,2048]{1,0:T(8,128)S(1)}, f32[16,2048]{1,0:T(8,128)S(1)}, f32[2,8,2048]{2,1,0:T(8,128)S(1)}, f32[...) custom-call(bf16[3,256,2048]{2,1,0:T(8,128)(2,1)} %projected_ref.1, ...), custom_call_target="tpu_custom_call" | custom-call | bytes 9000000 | tf_op jit(solution)/shard_map/block_state/pallas_call | solution.py:526
  8.0 0.0 copy-start
  8.0 1.4 %collective-permute-done.before_ref.refs_1_ = bf16[3,2,2048]{2,1,0:T(2,128)(2,1)S(1)} collective-permute-done((bf16[3,2,2048]{2,1,0:T(2,128)(2,1)S(1)}, bf16[3,2,2048]{2,1,0:T(2,128)(2,1)S(1)}, u32[]{:S(2)}, u32[]{:S(2)}) %collective-permute-start) | collective-permute-done | bytes 24608 | tf_op jit(solution)/shard_map/ppermute | solution.py:524
  9.4 0.1 head_tokens.1
  9.5 0.2 collective-permute-start.1
  9.8 2.2 %prepare.1 = (bf16[16,48,256]{2,1,0:T(8,128)(2,1)S(1)}, bf16[16,32,128]{2,1,0:T(8,128)(2,1)S(1)}, bf16[8,256,256]{2,1,0:T(8,128)(2,1)S(1)}, f32[256,2048]{1,0:T(8,128)S(1)}) custom-call(s32[1]{0:T(128)} %bitcast.place_ref.refs_0_, bf16[256,2048]{1,0:T(8,128)(2,1)S(1)} %get-tuple-element.22.query_ref, f32[16,128]{1,0:T(8,128)S(1)} %get-tuple-element.23.residue_ref, ...), custom_call_target="tpu_custom_call" | custom-call | bytes 6000000 | tf_op jit(solution)/shard_map/prepare/pallas_call | solution.py:562
  12.0 1.9 %collective-permute-done.1.refs_4_ = bf16[16,2048]{1,0:T(8,128)(2,1)S(1)} collective-permute-done((bf16[16,2048]{1,0:T(8,128)(2,1)S(1)}, bf16[16,2048]{1,0:T(8,128)(2,1)S(1)}, u32[]{:S(2)}, u32[]{:S(2)}) %collective-permute-start.1) | collective-permute-done | bytes 65568 | tf_op jit(solution)/shard_map/ppermute | solution.py:583
  13.9 0.1 join.1
  14.0 2.3 %collective-permute-start.2 = (bf16[16,2048]{1,0:T(8,128)(2,1)S(1)}, bf16[16,2048]{1,0:T(8,128)(2,1)S(1)}, u32[]{:S(2)}, u32[]{:S(2)}) collective-permute-start(bf16[16,2048]{1,0:T(8,128)(2,1)S(1)} %get-tuple-element.39), channel_id=1, source_target_pairs={{24,0},{28,4},{16,8},{20,12},{8,16},{12,20},{0,24},{4,28},{25,1},{... | collective-permute-start | bytes 196616 | tf_op jit(solution)/shard_map/ppermute | solution.py:595
  16.3 0.0 collective-permute-start.3
  16.3 2.2 %collective-permute-start.4 = (bf16[16,2048]{1,0:T(8,128)(2,1)S(1)}, bf16[16,2048]{1,0:T(8,128)(2,1)S(1)}, u32[]{:S(2)}, u32[]{:S(2)}) collective-permute-start(bf16[16,2048]{1,0:T(8,128)(2,1)S(1)} %get-tuple-element.39), channel_id=1, source_target_pairs={{8,0},{12,4},{0,8},{4,12},{24,16},{28,20},{16,24},{20,28},{9,1},{1... | collective-permute-start | bytes 196616 | tf_op jit(solution)/shard_map/ppermute | solution.py:595
  18.4 0.0 copy-done
  18.4 2.4 %local_conv.1.refs_1_ = f32[256,2048]{1,0:T(8,128)S(1)} custom-call(f32[256,2048]{1,0:T(8,128)S(1)} %get-tuple-element.26.gate_ref.refs_2_, bf16[256,2048]{1,0:T(8,128)(2,1)S(1)} %get-tuple-element.27.residual_ref, bf16[256,2048]{1,0:T(8,128)(2,1)S(1)} %get-tuple-element.28.product_ref, f32[8,2048]{1,0:T(8,128)S(1)} %get-tuple-element.31.first_ref, ...), custom_call_target="tpu_custom_call" | custom-call | bytes 15000000 | tf_op jit(solution)/shard_map/local_conv/pallas_call | solution.py:597
  20.9 0.0 collective-permute-done.2.refs_6_
  20.9 1.0 %collective-permute-done.3.refs_7_ = bf16[16,2048]{1,0:T(8,128)(2,1)S(1)} collective-permute-done((bf16[16,2048]{1,0:T(8,128)(2,1)S(1)}, bf16[16,2048]{1,0:T(8,128)(2,1)S(1)}, u32[]{:S(2)}, u32[]{:S(2)}) %collective-permute-start.3) | collective-permute-done | bytes 65568 | tf_op jit(solution)/shard_map/ppermute | solution.py:595
  21.9 0.0 collective-permute-done.4.refs_8_
  21.9 0.7 %add_carry.1 = (f32[256,2048]{1,0:T(8,128)S(1)}, f32[1,256]{1,0:T(1,128)S(1)}) custom-call(s32[1]{0:T(128)} %bitcast.place_ref.refs_0_, f32[256,2048]{1,0:T(8,128)S(1)} %local_conv.1.refs_1_, f32[256,2048]{1,0:T(8,128)S(1)} %get-tuple-element.26.gate_ref.refs_2_, bf16[8,256,256]{2,1,0:T(8,128)(2,1)S(1)} %get-tuple-element.36.refs_3_, ...), custom_call_target="tpu_custom_call" | custom-call | bytes 3000000 | tf_op jit(solution)/shard_map/add_carry/pallas_call | solution.py:606
  22.6 0.0 copy-start.1
  22.6 0.0 collective-permute-start.5
  22.6 1.6 %collective-permute-start.6 = (f32[1,256]{1,0:T(1,128)S(1)}, f32[1,256]{1,0:T(1,128)S(1)}, u32[]{:S(2)}, u32[]{:S(2)}) collective-permute-start(f32[1,256]{1,0:T(1,128)S(1)} %get-tuple-element.41.refs_2_), channel_id=1, source_target_pairs={{2,0},{3,1},{0,2},{1,3},{6,4},{7,5},{4,6},{5,7},{10,8},{11,9},{8,1... | collective-permute-start | bytes 3080 | tf_op jit(solution)/shard_map/ppermute | solution.py:615
  24.2 0.3 %collective-permute-start.7 = (f32[1,256]{1,0:T(1,128)S(1)}, f32[1,256]{1,0:T(1,128)S(1)}, u32[]{:S(2)}, u32[]{:S(2)}) collective-permute-start(f32[1,256]{1,0:T(1,128)S(1)} %get-tuple-element.41.refs_2_), channel_id=1, source_target_pairs={{1,0},{0,1},{3,2},{2,3},{5,4},{4,5},{7,6},{6,7},{9,8},{8,9},{11,10... | collective-permute-start | bytes 3080 | tf_op jit(solution)/shard_map/ppermute | solution.py:615
  24.5 1.0 %new_residual.1 = bf16[256,2048]{1,0:T(8,128)(2,1)} custom-call(f32[256,2048]{1,0:T(8,128)S(1)} %get-tuple-element.40.summed_ref.refs_0_), custom_call_target="tpu_custom_call" | custom-call | bytes 3000000 | tf_op jit(solution)/shard_map/new_residual/pallas_call | solution.py:618
  25.6 0.1 collective-permute-done.5.refs_3_
  25.6 0.6 %collective-permute-done.6.refs_4_ = f32[1,256]{1,0:T(1,128)S(1)} collective-permute-done((f32[1,256]{1,0:T(1,128)S(1)}, f32[1,256]{1,0:T(1,128)S(1)}, u32[]{:S(2)}, u32[]{:S(2)}) %collective-permute-start.6) | collective-permute-done | bytes 1056 | tf_op jit(solution)/shard_map/ppermute | solution.py:615
  26.3 0.0 collective-permute-done.7.refs_5_
  26.3 0.0 copy-done.1
  26.3 1.2 %normed.1 = bf16[256,2048]{1,0:T(8,128)(2,1)} custom-call(f32[256,2048]{1,0:T(8,128)S(1)} %get-tuple-element.40.summed_ref.refs_0_, f32[1,2048]{1,0:T(1,128)S(1)} %bitcast.6, f32[1,256]{1,0:T(1,128)S(1)} %get-tuple-element.41.refs_2_, f32[1,256]{1,0:T(1,128)S(1)} %collective-permute-done.5.refs_3_, f32[1,256]{1,0:T(1,128)S(1)} %collective-permute-done.6.refs_4_, ...), custom_call_target="tpu_custom_call" | custom-call | bytes 3000000 | tf_op jit(solution)/shard_map/normed/pallas_call | solution.py:618
  (1 shorter events, 0.0 us)
Async XLA Ops:
  1.6 7.8 %collective-permute-start = (bf16[3,2,2048]{2,1,0:T(2,128)(2,1)S(1)}, bf16[3,2,2048]{2,1,0:T(2,128)(2,1)S(1)}, u32[]{:S(2)}, u32[]{:S(2)}) collective-permute-start(bf16[3,2,2048]{2,1,0:T(2,128)(2,1)S(1)} %slice.3), channel_id=1, source_target_pairs={{0,4},{4,8},{8,12},{12,16},{16,20},{20,24},{24,28},{28,0},{1,5},{5... | collective-permute-start | bytes 73736 | tf_op jit(solution)/shard_map/ppermute | solution.py:524
  8.0 10.5 %copy-start = (f32[2048]{0:T(1024)S(1)}, f32[2048]{0:T(1024)}, u32[]{:S(2)}) copy-start(f32[2048]{0:T(1024)} %param.11) | copy-start | bytes 24580
  9.5 4.3 %collective-permute-start.1 = (bf16[16,2048]{1,0:T(8,128)(2,1)S(1)}, bf16[16,2048]{1,0:T(8,128)(2,1)S(1)}, u32[]{:S(2)}, u32[]{:S(2)}) collective-permute-start(bf16[16,2048]{1,0:T(8,128)(2,1)S(1)} %get-tuple-element.32.refs_1_), channel_id=1, source_target_pairs={{4,0},{0,4},{12,8},{8,12},{20,16},{16,20},{28,24},{24,28},{5,1},{1... | collective-permute-start | bytes 196616 | tf_op jit(solution)/shard_map/ppermute | solution.py:583
  14.0 6.9 %collective-permute-start.2 = (bf16[16,2048]{1,0:T(8,128)(2,1)S(1)}, bf16[16,2048]{1,0:T(8,128)(2,1)S(1)}, u32[]{:S(2)}, u32[]{:S(2)}) collective-permute-start(bf16[16,2048]{1,0:T(8,128)(2,1)S(1)} %get-tuple-element.39), channel_id=1, source_target_pairs={{24,0},{28,4},{16,8},{20,12},{8,16},{12,20},{0,24},{4,28},{25,1},{... | collective-permute-start | bytes 196616 | tf_op jit(solution)/shard_map/ppermute | solution.py:595
  16.3 5.6 %collective-permute-start.3 = (bf16[16,2048]{1,0:T(8,128)(2,1)S(1)}, bf16[16,2048]{1,0:T(8,128)(2,1)S(1)}, u32[]{:S(2)}, u32[]{:S(2)}) collective-permute-start(bf16[16,2048]{1,0:T(8,128)(2,1)S(1)} %get-tuple-element.39), channel_id=1, source_target_pairs={{16,0},{20,4},{24,8},{28,12},{0,16},{4,20},{8,24},{12,28},{17,1},{... | collective-permute-start | bytes 196616 | tf_op jit(solution)/shard_map/ppermute | solution.py:595
  16.3 5.6 %collective-permute-start.4 = (bf16[16,2048]{1,0:T(8,128)(2,1)S(1)}, bf16[16,2048]{1,0:T(8,128)(2,1)S(1)}, u32[]{:S(2)}, u32[]{:S(2)}) collective-permute-start(bf16[16,2048]{1,0:T(8,128)(2,1)S(1)} %get-tuple-element.39), channel_id=1, source_target_pairs={{8,0},{12,4},{0,8},{4,12},{24,16},{28,20},{16,24},{20,28},{9,1},{1... | collective-permute-start | bytes 196616 | tf_op jit(solution)/shard_map/ppermute | solution.py:595
  22.6 3.6 %copy-start.1 = (f32[2048]{0:T(1024)S(1)}, f32[2048]{0:T(1024)}, u32[]{:S(2)}) copy-start(f32[2048]{0:T(1024)} %param.13) | copy-start | bytes 24580
  22.6 3.0 %collective-permute-start.5 = (f32[1,256]{1,0:T(1,128)S(1)}, f32[1,256]{1,0:T(1,128)S(1)}, u32[]{:S(2)}, u32[]{:S(2)}) collective-permute-start(f32[1,256]{1,0:T(1,128)S(1)} %get-tuple-element.41.refs_2_), channel_id=1, source_target_pairs={{3,0},{2,1},{1,2},{0,3},{7,4},{6,5},{5,6},{4,7},{11,8},{10,9},{9,1... | collective-permute-start | bytes 3080 | tf_op jit(solution)/shard_map/ppermute | solution.py:615
  22.6 3.6 %collective-permute-start.6 = (f32[1,256]{1,0:T(1,128)S(1)}, f32[1,256]{1,0:T(1,128)S(1)}, u32[]{:S(2)}, u32[]{:S(2)}) collective-permute-start(f32[1,256]{1,0:T(1,128)S(1)} %get-tuple-element.41.refs_2_), channel_id=1, source_target_pairs={{2,0},{3,1},{0,2},{1,3},{6,4},{7,5},{4,6},{5,7},{10,8},{11,9},{8,1... | collective-permute-start | bytes 3080 | tf_op jit(solution)/shard_map/ppermute | solution.py:615
  24.2 2.0 %collective-permute-start.7 = (f32[1,256]{1,0:T(1,128)S(1)}, f32[1,256]{1,0:T(1,128)S(1)}, u32[]{:S(2)}, u32[]{:S(2)}) collective-permute-start(f32[1,256]{1,0:T(1,128)S(1)} %get-tuple-element.41.refs_2_), channel_id=1, source_target_pairs={{1,0},{0,1},{3,2},{2,3},{5,4},{4,5},{7,6},{6,7},{9,8},{8,9},{11,10... | collective-permute-start | bytes 3080 | tf_op jit(solution)/shard_map/ppermute | solution.py:615

commit v15 on v14

--- a/solution.py
+++ b/solution.py
@@ -374,7 +374,7 @@
 
     found = jnp.zeros_like(rate)
     total = decayed(own_ref[...].astype(F32), radix - 1 - run)
-    for k, ref in enumerate(others, 1):
+    for k, ref in enumerate(others[::-1], 1):
         other = ref[...].astype(F32)
         source = partner(run, k, radix)
         found = found + jnp.where(source < run, decayed(other, jnp.maximum(run - 1 - source, 0)), 0.0)
@@ -472,7 +472,7 @@
 
 def radices(count):
     found = []
-    for radix in (2, 4, 4, 4, 3, 2, 5, 7):
+    for radix in (4, 4, 4, 3, 3, 2, 5, 7):
         if count % radix == 0:
             found.append(radix)
             count //= radix
@@ -580,7 +580,7 @@
         size = stride * radix
         if level == len(levels) - 1:
             break
-        others = [lax.ppermute(group, "ctx", route) for route in routes(peers, stride, radix)]
+        others = [lax.ppermute(group, "ctx", route) for route in routes(peers, stride, radix)[::-1]]
         if level == 0:
             others[0], inner = lax.optimization_barrier((others[0], inner))
         entry, group = pl.pallas_call(

time: 27.7 us -> 26.8 us (0.968)
  waiting for transfers between devices: 4.99 us -> 2.4 us
  starting transfers between devices: 9.55 us -> 11.1 us
    ppermute x4, waiting for transfers between devices: 2.88 us -> 0.31 us  [per_device(): lax.ppermute(group, 'ctx', route)]
    ppermute x4, starting transfers between devices: 4.69 us -> 6.21 us  [per_device(): lax.ppermute(group, 'ctx', route)]
  transfers between devices with their start and end apart: 8 -> 8, of which waited for: 5 -> 5; matrix products, arithmetic and copies ran while one was open for 0% -> 0% of each run, Pallas kernels for 33% -> 34%
where the time goes in v15:
time: 26.8 us; the launch traced here: 26.5 us
  Pallas kernels  11.3 us (42%)
  starting transfers between devices  11.1 us (41%)
  waiting for transfers between devices  2.4 us (9%)
  local copies, waits for them, and re-layouts  0.94 us (4%)
  between operations  0.71 us (3%)
    ppermute x4, starting transfers between devices, per_device(): lax.ppermute(group, 'ctx', route)  6.21 us
    pallas_call x1, Pallas kernels, per_device(): pl.pallas_call(state_kernel, in_specs=[hbm_spec] * 5, out_shape=[bf16(row...  3.43 us
    ppermute x1, starting transfers between devices, per_device(): lax.ppermute(projected[:, rows - (taps - 1):, :], 'ctx', ring(peers, 1))  2.99 us
    pallas_call x1, Pallas kernels, per_device(): pl.pallas_call(local_kernel, out_shape=f32(rows, width), compiler_params=...  2.43 us
    pallas_call x2, Pallas kernels, write(): pl.pallas_call(kernel, out_specs=hbm_spec, out_shape=bf16(rows, width), s...  2.21 us
    pallas_call x1, Pallas kernels, per_device(): pl.pallas_call(prepare_kernel, in_specs=[smem_spec] + [vmem_spec] * 5, ou...  2.21 us
    ppermute x3, starting transfers between devices, per_device(): lax.ppermute(squares, 'fsdp', route)  1.9 us
    ppermute x1, waiting for transfers between devices, per_device(): lax.ppermute(projected[:, rows - (taps - 1):, :], 'ctx', ring(peers, 1))  1.4 us
  transfers between devices with their start and end apart: 8, of which 5 were waited for; matrix products, arithmetic and copies ran while one was open for 0% of the time, Pallas kernels for 34%

profile of v15, /device:TPU:0, one launch (start us, length us, event | category | flops | bytes accessed | tf_op | source)
XLA Modules:
  0.0 26.5 jit_solution(15761358609908695734)
XLA Ops:
  0.6 0.9 %slice.3 = bf16[3,2,2048]{2,1,0:T(2,128)(2,1)S(1)} slice(bf16[3,256,2048]{2,1,0:T(8,128)(2,1)} %projected_ref.1), slice={[0:3], [254:256], [0:2048]} | slice | bytes 49152 | tf_op jit(solution)/shard_map/slice | solution.py:524
  1.6 3.0 %collective-permute-start = (bf16[3,2,2048]{2,1,0:T(2,128)(2,1)S(1)}, bf16[3,2,2048]{2,1,0:T(2,128)(2,1)S(1)}, u32[]{:S(2)}, u32[]{:S(2)}) collective-permute-start(bf16[3,2,2048]{2,1,0:T(2,128)(2,1)S(1)} %slice.3), channel_id=1, source_target_pairs={{0,4},{4,8},{8,12},{12,16},{16,20},{20,24},{24,28},{28,0},{1,5},{5... | collective-permute-start | bytes 73736 | tf_op jit(solution)/shard_map/ppermute | solution.py:524
  4.5 3.4 %block_state.1 = (bf16[256,2048]{1,0:T(8,128)(2,1)S(1)}, f32[16,2048]{1,0:T(8,128)S(1)}, f32[16,2048]{1,0:T(8,128)S(1)}, f32[2,8,2048]{2,1,0:T(8,128)S(1)}, f32[...) custom-call(bf16[3,256,2048]{2,1,0:T(8,128)(2,1)} %projected_ref.1, ...), custom_call_target="tpu_custom_call" | custom-call | bytes 9000000 | tf_op jit(solution)/shard_map/block_state/pallas_call | solution.py:526
  8.0 0.0 copy-start
  8.0 1.4 %collective-permute-done.before_ref.refs_1_ = bf16[3,2,2048]{2,1,0:T(2,128)(2,1)S(1)} collective-permute-done((bf16[3,2,2048]{2,1,0:T(2,128)(2,1)S(1)}, bf16[3,2,2048]{2,1,0:T(2,128)(2,1)S(1)}, u32[]{:S(2)}, u32[]{:S(2)}) %collective-permute-start) | collective-permute-done | bytes 24608 | tf_op jit(solution)/shard_map/ppermute | solution.py:524
  9.4 0.1 head_tokens.1
  9.5 1.2 %collective-permute-start.1 = (bf16[16,2048]{1,0:T(8,128)(2,1)S(1)}, bf16[16,2048]{1,0:T(8,128)(2,1)S(1)}, u32[]{:S(2)}, u32[]{:S(2)}) collective-permute-start(bf16[16,2048]{1,0:T(8,128)(2,1)S(1)} %get-tuple-element.32.refs_1_), channel_id=1, source_target_pairs={{12,0},{8,4},{4,8},{0,12},{28,16},{24,20},{20,24},{16,28},{13,1},{... | collective-permute-start | bytes 196616 | tf_op jit(solution)/shard_map/ppermute | solution.py:583
  10.8 0.4 %collective-permute-start.2 = (bf16[16,2048]{1,0:T(8,128)(2,1)S(1)}, bf16[16,2048]{1,0:T(8,128)(2,1)S(1)}, u32[]{:S(2)}, u32[]{:S(2)}) collective-permute-start(bf16[16,2048]{1,0:T(8,128)(2,1)S(1)} %get-tuple-element.32.refs_1_), channel_id=1, source_target_pairs={{8,0},{12,4},{0,8},{4,12},{24,16},{28,20},{16,24},{20,28},{9,1},{1... | collective-permute-start | bytes 196616 | tf_op jit(solution)/shard_map/ppermute | solution.py:583
  11.2 1.9 %collective-permute-start.3 = (bf16[16,2048]{1,0:T(8,128)(2,1)S(1)}, bf16[16,2048]{1,0:T(8,128)(2,1)S(1)}, u32[]{:S(2)}, u32[]{:S(2)}) collective-permute-start(bf16[16,2048]{1,0:T(8,128)(2,1)S(1)} %get-tuple-element.32.refs_1_), channel_id=1, source_target_pairs={{4,0},{0,4},{12,8},{8,12},{20,16},{16,20},{28,24},{24,28},{5,1},{1... | collective-permute-start | bytes 196616 | tf_op jit(solution)/shard_map/ppermute | solution.py:583
  13.1 2.2 %prepare.1 = (bf16[16,48,256]{2,1,0:T(8,128)(2,1)S(1)}, bf16[16,32,128]{2,1,0:T(8,128)(2,1)S(1)}, bf16[8,256,256]{2,1,0:T(8,128)(2,1)S(1)}, f32[256,2048]{1,0:T(8,128)S(1)}) custom-call(s32[1]{0:T(128)} %bitcast.place_ref.refs_0_, bf16[256,2048]{1,0:T(8,128)(2,1)S(1)} %get-tuple-element.22.query_ref, f32[16,128]{1,0:T(8,128)S(1)} %get-tuple-element.23.residue_ref, ...), custom_call_target="tpu_custom_call" | custom-call | bytes 6000000 | tf_op jit(solution)/shard_map/prepare/pallas_call | solution.py:562
  15.3 0.0 collective-permute-done.1.refs_4_
  15.3 0.0 collective-permute-done.2.refs_5_
  15.3 0.2 collective-permute-done.3.refs_6_
  15.5 0.2 join.1
  15.7 2.7 %collective-permute-start.4 = (bf16[16,2048]{1,0:T(8,128)(2,1)S(1)}, bf16[16,2048]{1,0:T(8,128)(2,1)S(1)}, u32[]{:S(2)}, u32[]{:S(2)}) collective-permute-start(bf16[16,2048]{1,0:T(8,128)(2,1)S(1)} %get-tuple-element.39), channel_id=1, source_target_pairs={{16,0},{20,4},{24,8},{28,12},{0,16},{4,20},{8,24},{12,28},{17,1},{... | collective-permute-start | bytes 196616 | tf_op jit(solution)/shard_map/ppermute | solution.py:595
  18.4 0.0 copy-done
  18.4 2.4 %local_conv.1.refs_1_ = f32[256,2048]{1,0:T(8,128)S(1)} custom-call(f32[256,2048]{1,0:T(8,128)S(1)} %get-tuple-element.26.gate_ref.refs_2_, bf16[256,2048]{1,0:T(8,128)(2,1)S(1)} %get-tuple-element.27.residual_ref, bf16[256,2048]{1,0:T(8,128)(2,1)S(1)} %get-tuple-element.28.product_ref, f32[8,2048]{1,0:T(8,128)S(1)} %get-tuple-element.31.first_ref, ...), custom_call_target="tpu_custom_call" | custom-call | bytes 15000000 | tf_op jit(solution)/shard_map/local_conv/pallas_call | solution.py:597
  20.8 0.1 collective-permute-done.4.refs_6_
  21.0 0.7 %add_carry.1 = (f32[256,2048]{1,0:T(8,128)S(1)}, f32[1,256]{1,0:T(1,128)S(1)}) custom-call(s32[1]{0:T(128)} %bitcast.place_ref.refs_0_, f32[256,2048]{1,0:T(8,128)S(1)} %local_conv.1.refs_1_, f32[256,2048]{1,0:T(8,128)S(1)} %get-tuple-element.26.gate_ref.refs_2_, bf16[8,256,256]{2,1,0:T(8,128)(2,1)S(1)} %get-tuple-element.36.refs_3_, ...), custom_call_target="tpu_custom_call" | custom-call | bytes 3000000 | tf_op jit(solution)/shard_map/add_carry/pallas_call | solution.py:606
  21.7 0.0 copy-start.1
  21.7 0.0 collective-permute-start.5
  21.7 1.7 %collective-permute-start.6 = (f32[1,256]{1,0:T(1,128)S(1)}, f32[1,256]{1,0:T(1,128)S(1)}, u32[]{:S(2)}, u32[]{:S(2)}) collective-permute-start(f32[1,256]{1,0:T(1,128)S(1)} %get-tuple-element.41.refs_2_), channel_id=1, source_target_pairs={{2,0},{3,1},{0,2},{1,3},{6,4},{7,5},{4,6},{5,7},{10,8},{11,9},{8,1... | collective-permute-start | bytes 3080 | tf_op jit(solution)/shard_map/ppermute | solution.py:615
  23.4 0.1 collective-permute-start.7
  23.6 1.0 %new_residual.1 = bf16[256,2048]{1,0:T(8,128)(2,1)} custom-call(f32[256,2048]{1,0:T(8,128)S(1)} %get-tuple-element.40.summed_ref.refs_0_), custom_call_target="tpu_custom_call" | custom-call | bytes 3000000 | tf_op jit(solution)/shard_map/new_residual/pallas_call | solution.py:618
  24.6 0.1 collective-permute-done.5.refs_3_
  24.7 0.6 %collective-permute-done.6.refs_4_ = f32[1,256]{1,0:T(1,128)S(1)} collective-permute-done((f32[1,256]{1,0:T(1,128)S(1)}, f32[1,256]{1,0:T(1,128)S(1)}, u32[]{:S(2)}, u32[]{:S(2)}) %collective-permute-start.6) | collective-permute-done | bytes 1056 | tf_op jit(solution)/shard_map/ppermute | solution.py:615
  25.3 0.0 collective-permute-done.7.refs_5_
  25.3 0.0 copy-done.1
  25.3 1.2 %normed.1 = bf16[256,2048]{1,0:T(8,128)(2,1)} custom-call(f32[256,2048]{1,0:T(8,128)S(1)} %get-tuple-element.40.summed_ref.refs_0_, f32[1,2048]{1,0:T(1,128)S(1)} %bitcast.6, f32[1,256]{1,0:T(1,128)S(1)} %get-tuple-element.41.refs_2_, f32[1,256]{1,0:T(1,128)S(1)} %collective-permute-done.5.refs_3_, f32[1,256]{1,0:T(1,128)S(1)} %collective-permute-done.6.refs_4_, ...), custom_call_target="tpu_custom_call" | custom-call | bytes 3000000 | tf_op jit(solution)/shard_map/normed/pallas_call | solution.py:618
  (1 shorter events, 0.0 us)
Async XLA Ops:
  1.6 7.8 %collective-permute-start = (bf16[3,2,2048]{2,1,0:T(2,128)(2,1)S(1)}, bf16[3,2,2048]{2,1,0:T(2,128)(2,1)S(1)}, u32[]{:S(2)}, u32[]{:S(2)}) collective-permute-start(bf16[3,2,2048]{2,1,0:T(2,128)(2,1)S(1)} %slice.3), channel_id=1, source_target_pairs={{0,4},{4,8},{8,12},{12,16},{16,20},{20,24},{24,28},{28,0},{1,5},{5... | collective-permute-start | bytes 73736 | tf_op jit(solution)/shard_map/ppermute | solution.py:524
  8.0 10.4 %copy-start = (f32[2048]{0:T(1024)S(1)}, f32[2048]{0:T(1024)}, u32[]{:S(2)}) copy-start(f32[2048]{0:T(1024)} %param.11) | copy-start | bytes 24580
  9.5 5.8 %collective-permute-start.1 = (bf16[16,2048]{1,0:T(8,128)(2,1)S(1)}, bf16[16,2048]{1,0:T(8,128)(2,1)S(1)}, u32[]{:S(2)}, u32[]{:S(2)}) collective-permute-start(bf16[16,2048]{1,0:T(8,128)(2,1)S(1)} %get-tuple-element.32.refs_1_), channel_id=1, source_target_pairs={{12,0},{8,4},{4,8},{0,12},{28,16},{24,20},{20,24},{16,28},{13,1},{... | collective-permute-start | bytes 196616 | tf_op jit(solution)/shard_map/ppermute | solution.py:583
  10.8 4.5 %collective-permute-start.2 = (bf16[16,2048]{1,0:T(8,128)(2,1)S(1)}, bf16[16,2048]{1,0:T(8,128)(2,1)S(1)}, u32[]{:S(2)}, u32[]{:S(2)}) collective-permute-start(bf16[16,2048]{1,0:T(8,128)(2,1)S(1)} %get-tuple-element.32.refs_1_), channel_id=1, source_target_pairs={{8,0},{12,4},{0,8},{4,12},{24,16},{28,20},{16,24},{20,28},{9,1},{1... | collective-permute-start | bytes 196616 | tf_op jit(solution)/shard_map/ppermute | solution.py:583
  11.2 4.3 %collective-permute-start.3 = (bf16[16,2048]{1,0:T(8,128)(2,1)S(1)}, bf16[16,2048]{1,0:T(8,128)(2,1)S(1)}, u32[]{:S(2)}, u32[]{:S(2)}) collective-permute-start(bf16[16,2048]{1,0:T(8,128)(2,1)S(1)} %get-tuple-element.32.refs_1_), channel_id=1, source_target_pairs={{4,0},{0,4},{12,8},{8,12},{20,16},{16,20},{28,24},{24,28},{5,1},{1... | collective-permute-start | bytes 196616 | tf_op jit(solution)/shard_map/ppermute | solution.py:583
  15.7 5.2 %collective-permute-start.4 = (bf16[16,2048]{1,0:T(8,128)(2,1)S(1)}, bf16[16,2048]{1,0:T(8,128)(2,1)S(1)}, u32[]{:S(2)}, u32[]{:S(2)}) collective-permute-start(bf16[16,2048]{1,0:T(8,128)(2,1)S(1)} %get-tuple-element.39), channel_id=1, source_target_pairs={{16,0},{20,4},{24,8},{28,12},{0,16},{4,20},{8,24},{12,28},{17,1},{... | collective-permute-start | bytes 196616 | tf_op jit(solution)/shard_map/ppermute | solution.py:595
  21.7 3.6 %copy-start.1 = (f32[2048]{0:T(1024)S(1)}, f32[2048]{0:T(1024)}, u32[]{:S(2)}) copy-start(f32[2048]{0:T(1024)} %param.13) | copy-start | bytes 24580
  21.7 3.0 %collective-permute-start.5 = (f32[1,256]{1,0:T(1,128)S(1)}, f32[1,256]{1,0:T(1,128)S(1)}, u32[]{:S(2)}, u32[]{:S(2)}) collective-permute-start(f32[1,256]{1,0:T(1,128)S(1)} %get-tuple-element.41.refs_2_), channel_id=1, source_target_pairs={{3,0},{2,1},{1,2},{0,3},{7,4},{6,5},{5,6},{4,7},{11,8},{10,9},{9,1... | collective-permute-start | bytes 3080 | tf_op jit(solution)/shard_map/ppermute | solution.py:615
  21.7 3.6 %collective-permute-start.6 = (f32[1,256]{1,0:T(1,128)S(1)}, f32[1,256]{1,0:T(1,128)S(1)}, u32[]{:S(2)}, u32[]{:S(2)}) collective-permute-start(f32[1,256]{1,0:T(1,128)S(1)} %get-tuple-element.41.refs_2_), channel_id=1, source_target_pairs={{2,0},{3,1},{0,2},{1,3},{6,4},{7,5},{4,6},{5,7},{10,8},{11,9},{8,1... | collective-permute-start | bytes 3080 | tf_op jit(solution)/shard_map/ppermute | solution.py:615
  23.4 1.9 %collective-permute-start.7 = (f32[1,256]{1,0:T(1,128)S(1)}, f32[1,256]{1,0:T(1,128)S(1)}, u32[]{:S(2)}, u32[]{:S(2)}) collective-permute-start(f32[1,256]{1,0:T(1,128)S(1)} %get-tuple-element.41.refs_2_), channel_id=1, source_target_pairs={{1,0},{0,1},{3,2},{2,3},{5,4},{4,5},{7,6},{6,7},{9,8},{8,9},{11,10... | collective-permute-start | bytes 3080 | tf_op jit(solution)/shard_map/ppermute | solution.py:615

commit v16 on v15

--- a/solution.py
+++ b/solution.py
@@ -118,7 +118,14 @@
 
 def wide_conv(block, earlier, weights):
     rows = block.shape[0]
-    return weights[0] * block.astype(F32) + weights[1] * earlier[:rows] + weights[2] * earlier[rows:]
+    wide = block.astype(F32)
+    if earlier.shape[0] == rows:
+        one = pltpu.roll(wide, 1, 0)
+        head = jnp.where(index_of((8, wide.shape[1]), 0) == 0, 0.0, one[:8])
+        one = jnp.concatenate([head, one[8:]], axis=0)
+    else:
+        one = earlier[:rows]
+    return weights[0] * wide + weights[1] * one + weights[2] * earlier[-rows:]
 
 
 def taps_of(weights, feature, lanes):
@@ -189,7 +196,11 @@
         copy.start()
 
     def fetch(wide):
-        return [earlier_tokens(shift_ref[...], buffer_ref[c, :, lanes_of(wide, WIDE)]) for c in (0, 1)]
+        here = lanes_of(wide, WIDE)
+        return (
+            earlier_tokens(shift_ref[...], buffer_ref[0, :, here]),
+            earlier_tokens(shift_ref[rows:, :], buffer_ref[1, :, here]),
+        )
 
     def multiply(wide, *earlier):
         here = lanes_of(wide, WIDE)
@@ -367,20 +378,21 @@
     others, (found_ref, group_ref) = refs[: radix - 1], refs[radix - 1 :]
     rate = mode_rate_ref[...]
     run = lax.rem(place_ref[0] // stride, radix)
-    step = float(tokens * stride)
-
-    def decayed(value, runs):
-        return jnp.exp(-step * runs.astype(F32) * rate) * value
-
+    decay = jnp.exp(-float(tokens * stride) * rate)
+    own = own_ref[...].astype(F32)
+    values = [ref[...].astype(F32) for ref in others[::-1]]
     found = jnp.zeros_like(rate)
-    total = decayed(own_ref[...].astype(F32), radix - 1 - run)
-    for k, ref in enumerate(others[::-1], 1):
-        other = ref[...].astype(F32)
-        source = partner(run, k, radix)
-        found = found + jnp.where(source < run, decayed(other, jnp.maximum(run - 1 - source, 0)), 0.0)
-        total = total + decayed(other, radix - 1 - source)
-    within = lax.rem(place_ref[0], stride).astype(F32) * float(tokens)
-    found_ref[...] = entry_ref[...] + jnp.exp(-within * rate) * found
+    total = jnp.zeros_like(rate)
+    for position in range(radix):
+        found = jnp.where(run == position, total, found)
+        state = own
+        for k, other in enumerate(values, 1):
+            state = jnp.where(partner(run, k, radix) == position, other, state)
+        total = decay * total + state
+    if stride > 1:
+        within = lax.rem(place_ref[0], stride).astype(F32) * float(tokens)
+        found = jnp.exp(-within * rate) * found
+    found_ref[...] = entry_ref[...] + found
     group_ref[...] = total.astype(BF16)
 
 

time: 26.8 us -> 26.8 us (level)
  no operation moved by 1% of the time
where the time goes in v16:
time: 26.8 us; the launch traced here: 26.4 us
  Pallas kernels  11.2 us (42%)
  starting transfers between devices  11.1 us (41%)
  waiting for transfers between devices  2.48 us (9%)
  local copies, waits for them, and re-layouts  0.94 us (4%)
  between operations  0.71 us (3%)
    ppermute x4, starting transfers between devices, per_device(): lax.ppermute(group, 'ctx', route)  6.18 us
    pallas_call x1, Pallas kernels, per_device(): pl.pallas_call(state_kernel, in_specs=[hbm_spec] * 5, out_shape=[bf16(row...  3.36 us
    ppermute x1, starting transfers between devices, per_device(): lax.ppermute(projected[:, rows - (taps - 1):, :], 'ctx', ring(peers, 1))  2.99 us
    pallas_call x1, Pallas kernels, per_device(): pl.pallas_call(local_kernel, out_shape=f32(rows, width), compiler_params=...  2.42 us
    pallas_call x2, Pallas kernels, write(): pl.pallas_call(kernel, out_specs=hbm_spec, out_shape=bf16(rows, width), s...  2.21 us
    pallas_call x1, Pallas kernels, per_device(): pl.pallas_call(prepare_kernel, in_specs=[smem_spec] + [vmem_spec] * 5, ou...  2.21 us
    ppermute x3, starting transfers between devices, per_device(): lax.ppermute(squares, 'fsdp', route)  1.89 us
    ppermute x1, waiting for transfers between devices, per_device(): lax.ppermute(projected[:, rows - (taps - 1):, :], 'ctx', ring(peers, 1))  1.46 us
  transfers between devices with their start and end apart: 8, of which 5 were waited for; matrix products, arithmetic and copies ran while one was open for 0% of the time, Pallas kernels for 34%

profile of v16, /device:TPU:0, one launch (start us, length us, event | category | flops | bytes accessed | tf_op | source)
XLA Modules:
  0.0 26.4 jit_solution(6678170466978426234)
XLA Ops:
  0.6 0.9 %slice.3 = bf16[3,2,2048]{2,1,0:T(2,128)(2,1)S(1)} slice(bf16[3,256,2048]{2,1,0:T(8,128)(2,1)} %projected_ref.1), slice={[0:3], [254:256], [0:2048]} | slice | bytes 49152 | tf_op jit(solution)/shard_map/slice | solution.py:536
  1.6 3.0 %collective-permute-start = (bf16[3,2,2048]{2,1,0:T(2,128)(2,1)S(1)}, bf16[3,2,2048]{2,1,0:T(2,128)(2,1)S(1)}, u32[]{:S(2)}, u32[]{:S(2)}) collective-permute-start(bf16[3,2,2048]{2,1,0:T(2,128)(2,1)S(1)} %slice.3), channel_id=1, source_target_pairs={{0,4},{4,8},{8,12},{12,16},{16,20},{20,24},{24,28},{28,0},{1,5},{5... | collective-permute-start | bytes 73736 | tf_op jit(solution)/shard_map/ppermute | solution.py:536
  4.5 3.4 %block_state.1 = (bf16[256,2048]{1,0:T(8,128)(2,1)S(1)}, f32[16,2048]{1,0:T(8,128)S(1)}, f32[16,2048]{1,0:T(8,128)S(1)}, f32[2,8,2048]{2,1,0:T(8,128)S(1)}, f32[...) custom-call(bf16[3,256,2048]{2,1,0:T(8,128)(2,1)} %projected_ref.1, ...), custom_call_target="tpu_custom_call" | custom-call | bytes 9000000 | tf_op jit(solution)/shard_map/block_state/pallas_call | solution.py:538
  7.9 0.0 copy-start
  7.9 1.5 %collective-permute-done.before_ref.refs_1_ = bf16[3,2,2048]{2,1,0:T(2,128)(2,1)S(1)} collective-permute-done((bf16[3,2,2048]{2,1,0:T(2,128)(2,1)S(1)}, bf16[3,2,2048]{2,1,0:T(2,128)(2,1)S(1)}, u32[]{:S(2)}, u32[]{:S(2)}) %collective-permute-start) | collective-permute-done | bytes 24608 | tf_op jit(solution)/shard_map/ppermute | solution.py:536
  9.4 0.1 head_tokens.1
  9.5 1.2 %collective-permute-start.1 = (bf16[16,2048]{1,0:T(8,128)(2,1)S(1)}, bf16[16,2048]{1,0:T(8,128)(2,1)S(1)}, u32[]{:S(2)}, u32[]{:S(2)}) collective-permute-start(bf16[16,2048]{1,0:T(8,128)(2,1)S(1)} %get-tuple-element.32.refs_1_), channel_id=1, source_target_pairs={{12,0},{8,4},{4,8},{0,12},{28,16},{24,20},{20,24},{16,28},{13,1},{... | collective-permute-start | bytes 196616 | tf_op jit(solution)/shard_map/ppermute | solution.py:595
  10.7 0.4 %collective-permute-start.2 = (bf16[16,2048]{1,0:T(8,128)(2,1)S(1)}, bf16[16,2048]{1,0:T(8,128)(2,1)S(1)}, u32[]{:S(2)}, u32[]{:S(2)}) collective-permute-start(bf16[16,2048]{1,0:T(8,128)(2,1)S(1)} %get-tuple-element.32.refs_1_), channel_id=1, source_target_pairs={{8,0},{12,4},{0,8},{4,12},{24,16},{28,20},{16,24},{20,28},{9,1},{1... | collective-permute-start | bytes 196616 | tf_op jit(solution)/shard_map/ppermute | solution.py:595
  11.2 1.9 %collective-permute-start.3 = (bf16[16,2048]{1,0:T(8,128)(2,1)S(1)}, bf16[16,2048]{1,0:T(8,128)(2,1)S(1)}, u32[]{:S(2)}, u32[]{:S(2)}) collective-permute-start(bf16[16,2048]{1,0:T(8,128)(2,1)S(1)} %get-tuple-element.32.refs_1_), channel_id=1, source_target_pairs={{4,0},{0,4},{12,8},{8,12},{20,16},{16,20},{28,24},{24,28},{5,1},{1... | collective-permute-start | bytes 196616 | tf_op jit(solution)/shard_map/ppermute | solution.py:595
  13.1 2.2 %prepare.1 = (bf16[16,48,256]{2,1,0:T(8,128)(2,1)S(1)}, bf16[16,32,128]{2,1,0:T(8,128)(2,1)S(1)}, bf16[8,256,256]{2,1,0:T(8,128)(2,1)S(1)}, f32[256,2048]{1,0:T(8,128)S(1)}) custom-call(s32[1]{0:T(128)} %bitcast.place_ref.refs_0_, bf16[256,2048]{1,0:T(8,128)(2,1)S(1)} %get-tuple-element.22.query_ref, f32[16,128]{1,0:T(8,128)S(1)} %get-tuple-element.23.residue_ref, ...), custom_call_target="tpu_custom_call" | custom-call | bytes 6000000 | tf_op jit(solution)/shard_map/prepare/pallas_call | solution.py:574
  15.3 0.0 collective-permute-done.1.refs_4_
  15.3 0.0 collective-permute-done.2.refs_5_
  15.3 0.1 collective-permute-done.3.refs_6_
  15.5 0.2 join.1
  15.6 2.6 %collective-permute-start.4 = (bf16[16,2048]{1,0:T(8,128)(2,1)S(1)}, bf16[16,2048]{1,0:T(8,128)(2,1)S(1)}, u32[]{:S(2)}, u32[]{:S(2)}) collective-permute-start(bf16[16,2048]{1,0:T(8,128)(2,1)S(1)} %get-tuple-element.39), channel_id=1, source_target_pairs={{16,0},{20,4},{24,8},{28,12},{0,16},{4,20},{8,24},{12,28},{17,1},{... | collective-permute-start | bytes 196616 | tf_op jit(solution)/shard_map/ppermute | solution.py:607
  18.2 0.0 copy-done
  18.3 2.4 %local_conv.1.refs_1_ = f32[256,2048]{1,0:T(8,128)S(1)} custom-call(f32[256,2048]{1,0:T(8,128)S(1)} %get-tuple-element.26.gate_ref.refs_2_, bf16[256,2048]{1,0:T(8,128)(2,1)S(1)} %get-tuple-element.27.residual_ref, bf16[256,2048]{1,0:T(8,128)(2,1)S(1)} %get-tuple-element.28.product_ref, f32[8,2048]{1,0:T(8,128)S(1)} %get-tuple-element.31.first_ref, ...), custom_call_target="tpu_custom_call" | custom-call | bytes 15000000 | tf_op jit(solution)/shard_map/local_conv/pallas_call | solution.py:609
  20.7 0.2 collective-permute-done.4.refs_6_
  20.9 0.7 %add_carry.1 = (f32[256,2048]{1,0:T(8,128)S(1)}, f32[1,256]{1,0:T(1,128)S(1)}) custom-call(s32[1]{0:T(128)} %bitcast.place_ref.refs_0_, f32[256,2048]{1,0:T(8,128)S(1)} %local_conv.1.refs_1_, f32[256,2048]{1,0:T(8,128)S(1)} %get-tuple-element.26.gate_ref.refs_2_, bf16[8,256,256]{2,1,0:T(8,128)(2,1)S(1)} %get-tuple-element.36.refs_3_, ...), custom_call_target="tpu_custom_call" | custom-call | bytes 3000000 | tf_op jit(solution)/shard_map/add_carry/pallas_call | solution.py:618
  21.6 0.0 copy-start.1
  21.6 0.0 collective-permute-start.5
  21.6 1.8 %collective-permute-start.6 = (f32[1,256]{1,0:T(1,128)S(1)}, f32[1,256]{1,0:T(1,128)S(1)}, u32[]{:S(2)}, u32[]{:S(2)}) collective-permute-start(f32[1,256]{1,0:T(1,128)S(1)} %get-tuple-element.41.refs_2_), channel_id=1, source_target_pairs={{2,0},{3,1},{0,2},{1,3},{6,4},{7,5},{4,6},{5,7},{10,8},{11,9},{8,1... | collective-permute-start | bytes 3080 | tf_op jit(solution)/shard_map/ppermute | solution.py:627
  23.4 0.1 collective-permute-start.7
  23.5 1.0 %new_residual.1 = bf16[256,2048]{1,0:T(8,128)(2,1)} custom-call(f32[256,2048]{1,0:T(8,128)S(1)} %get-tuple-element.40.summed_ref.refs_0_), custom_call_target="tpu_custom_call" | custom-call | bytes 3000000 | tf_op jit(solution)/shard_map/new_residual/pallas_call | solution.py:630
  24.5 0.1 collective-permute-done.5.refs_3_
  24.6 0.6 %collective-permute-done.6.refs_4_ = f32[1,256]{1,0:T(1,128)S(1)} collective-permute-done((f32[1,256]{1,0:T(1,128)S(1)}, f32[1,256]{1,0:T(1,128)S(1)}, u32[]{:S(2)}, u32[]{:S(2)}) %collective-permute-start.6) | collective-permute-done | bytes 1056 | tf_op jit(solution)/shard_map/ppermute | solution.py:627
  25.2 0.0 collective-permute-done.7.refs_5_
  25.2 0.0 copy-done.1
  25.2 1.2 %normed.1 = bf16[256,2048]{1,0:T(8,128)(2,1)} custom-call(f32[256,2048]{1,0:T(8,128)S(1)} %get-tuple-element.40.summed_ref.refs_0_, f32[1,2048]{1,0:T(1,128)S(1)} %bitcast.6, f32[1,256]{1,0:T(1,128)S(1)} %get-tuple-element.41.refs_2_, f32[1,256]{1,0:T(1,128)S(1)} %collective-permute-done.5.refs_3_, f32[1,256]{1,0:T(1,128)S(1)} %collective-permute-done.6.refs_4_, ...), custom_call_target="tpu_custom_call" | custom-call | bytes 3000000 | tf_op jit(solution)/shard_map/normed/pallas_call | solution.py:630
  (1 shorter events, 0.0 us)
Async XLA Ops:
  1.6 7.8 %collective-permute-start = (bf16[3,2,2048]{2,1,0:T(2,128)(2,1)S(1)}, bf16[3,2,2048]{2,1,0:T(2,128)(2,1)S(1)}, u32[]{:S(2)}, u32[]{:S(2)}) collective-permute-start(bf16[3,2,2048]{2,1,0:T(2,128)(2,1)S(1)} %slice.3), channel_id=1, source_target_pairs={{0,4},{4,8},{8,12},{12,16},{16,20},{20,24},{24,28},{28,0},{1,5},{5... | collective-permute-start | bytes 73736 | tf_op jit(solution)/shard_map/ppermute | solution.py:536
  7.9 10.3 %copy-start = (f32[2048]{0:T(1024)S(1)}, f32[2048]{0:T(1024)}, u32[]{:S(2)}) copy-start(f32[2048]{0:T(1024)} %param.11) | copy-start | bytes 24580
  9.5 5.8 %collective-permute-start.1 = (bf16[16,2048]{1,0:T(8,128)(2,1)S(1)}, bf16[16,2048]{1,0:T(8,128)(2,1)S(1)}, u32[]{:S(2)}, u32[]{:S(2)}) collective-permute-start(bf16[16,2048]{1,0:T(8,128)(2,1)S(1)} %get-tuple-element.32.refs_1_), channel_id=1, source_target_pairs={{12,0},{8,4},{4,8},{0,12},{28,16},{24,20},{20,24},{16,28},{13,1},{... | collective-permute-start | bytes 196616 | tf_op jit(solution)/shard_map/ppermute | solution.py:595
  10.7 4.6 %collective-permute-start.2 = (bf16[16,2048]{1,0:T(8,128)(2,1)S(1)}, bf16[16,2048]{1,0:T(8,128)(2,1)S(1)}, u32[]{:S(2)}, u32[]{:S(2)}) collective-permute-start(bf16[16,2048]{1,0:T(8,128)(2,1)S(1)} %get-tuple-element.32.refs_1_), channel_id=1, source_target_pairs={{8,0},{12,4},{0,8},{4,12},{24,16},{28,20},{16,24},{20,28},{9,1},{1... | collective-permute-start | bytes 196616 | tf_op jit(solution)/shard_map/ppermute | solution.py:595
  11.2 4.3 %collective-permute-start.3 = (bf16[16,2048]{1,0:T(8,128)(2,1)S(1)}, bf16[16,2048]{1,0:T(8,128)(2,1)S(1)}, u32[]{:S(2)}, u32[]{:S(2)}) collective-permute-start(bf16[16,2048]{1,0:T(8,128)(2,1)S(1)} %get-tuple-element.32.refs_1_), channel_id=1, source_target_pairs={{4,0},{0,4},{12,8},{8,12},{20,16},{16,20},{28,24},{24,28},{5,1},{1... | collective-permute-start | bytes 196616 | tf_op jit(solution)/shard_map/ppermute | solution.py:595
  15.6 5.2 %collective-permute-start.4 = (bf16[16,2048]{1,0:T(8,128)(2,1)S(1)}, bf16[16,2048]{1,0:T(8,128)(2,1)S(1)}, u32[]{:S(2)}, u32[]{:S(2)}) collective-permute-start(bf16[16,2048]{1,0:T(8,128)(2,1)S(1)} %get-tuple-element.39), channel_id=1, source_target_pairs={{16,0},{20,4},{24,8},{28,12},{0,16},{4,20},{8,24},{12,28},{17,1},{... | collective-permute-start | bytes 196616 | tf_op jit(solution)/shard_map/ppermute | solution.py:607
  21.6 3.6 %copy-start.1 = (f32[2048]{0:T(1024)S(1)}, f32[2048]{0:T(1024)}, u32[]{:S(2)}) copy-start(f32[2048]{0:T(1024)} %param.13) | copy-start | bytes 24580
  21.6 3.0 %collective-permute-start.5 = (f32[1,256]{1,0:T(1,128)S(1)}, f32[1,256]{1,0:T(1,128)S(1)}, u32[]{:S(2)}, u32[]{:S(2)}) collective-permute-start(f32[1,256]{1,0:T(1,128)S(1)} %get-tuple-element.41.refs_2_), channel_id=1, source_target_pairs={{3,0},{2,1},{1,2},{0,3},{7,4},{6,5},{5,6},{4,7},{11,8},{10,9},{9,1... | collective-permute-start | bytes 3080 | tf_op jit(solution)/shard_map/ppermute | solution.py:627
  21.6 3.6 %collective-permute-start.6 = (f32[1,256]{1,0:T(1,128)S(1)}, f32[1,256]{1,0:T(1,128)S(1)}, u32[]{:S(2)}, u32[]{:S(2)}) collective-permute-start(f32[1,256]{1,0:T(1,128)S(1)} %get-tuple-element.41.refs_2_), channel_id=1, source_target_pairs={{2,0},{3,1},{0,2},{1,3},{6,4},{7,5},{4,6},{5,7},{10,8},{11,9},{8,1... | collective-permute-start | bytes 3080 | tf_op jit(solution)/shard_map/ppermute | solution.py:627
  23.4 1.8 %collective-permute-start.7 = (f32[1,256]{1,0:T(1,128)S(1)}, f32[1,256]{1,0:T(1,128)S(1)}, u32[]{:S(2)}, u32[]{:S(2)}) collective-permute-start(f32[1,256]{1,0:T(1,128)S(1)} %get-tuple-element.41.refs_2_), channel_id=1, source_target_pairs={{1,0},{0,1},{3,2},{2,3},{5,4},{4,5},{7,6},{6,7},{9,8},{8,9},{11,10... | collective-permute-start | bytes 3080 | tf_op jit(solution)/shard_map/ppermute | solution.py:627

commit v17 on v16

--- a/solution.py
+++ b/solution.py
@@ -137,15 +137,12 @@
     weight_hbm,
     rate_hbm,
     residue_hbm,
-    residual_hbm,
     product_ref,
     state_ref,
     mode_rate_ref,
     head_ref,
     weight_ref,
-    query_ref,
     residue_ref,
-    residual_ref,
     buffer_ref,
     ending_ref,
     shift_ref,
@@ -160,14 +157,20 @@
     rate_copy.start()
     weight_copy = pltpu.make_async_copy(weight_hbm, short_ref, small_sems.at[1])
     weight_copy.start()
-    copies = [pltpu.make_async_copy(projected_ref.at[1 + c], buffer_ref.at[c], sems.at[c]) for c in (0, 1)]
-    later = [
-        pltpu.make_async_copy(residue_hbm, residue_ref, sems.at[2]),
-        pltpu.make_async_copy(projected_ref.at[0], query_ref, sems.at[3]),
-        pltpu.make_async_copy(residual_hbm, residual_ref, sems.at[4]),
+    part = width // 2
+    copies = [
+        pltpu.make_async_copy(
+            projected_ref.at[1 + c, :, pl.ds(side * part, part)],
+            buffer_ref.at[c, :, pl.ds(side * part, part)],
+            sems.at[2 * side + c],
+        )
+        for side in (0, 1)
+        for c in (0, 1)
     ]
+    residue_copy = pltpu.make_async_copy(residue_hbm, residue_ref, sems.at[4])
     for copy in copies:
         copy.start()
+    residue_copy.start()
     shift_ref[...] = shift_matrix(rows)
     chosen = selectors(rate_ref.shape[1])
     eye = own_mode(BF16)
@@ -190,12 +193,12 @@
     weight_copy.wait()
     weights = short_ref[...].astype(F32)
     weight_ref[...] = weights
-    for copy in copies:
-        copy.wait()
-    for copy in later:
-        copy.start()
 
     def fetch(wide):
+        if wide % (wides // 2) == 0:
+            first = 2 * (wide // (wides // 2))
+            for copy in copies[first : first + 2]:
+                copy.wait()
         here = lanes_of(wide, WIDE)
         return (
             earlier_tokens(shift_ref[...], buffer_ref[0, :, here]),
@@ -218,8 +221,7 @@
             state_ref[:, lanes_of((WIDE // LANES) * wide + half)] = jnp.sum(own * mask, axis=0)
 
     pipelined(wides, fetch, multiply, leave)
-    for copy in later:
-        copy.wait()
+    residue_copy.wait()
 
 
 def halo(before_ref, place_ref):
@@ -239,7 +241,8 @@
 
 def prepare_kernel(
     place_ref,
-    query_ref,
+    projected_ref,
+    residual_hbm,
     residue_ref,
     before_ref,
     weight_ref,
@@ -248,9 +251,16 @@
     entering_ref,
     carry_ref,
     gate_ref,
+    residual_ref,
+    query_ref,
     shift_ref,
+    sems,
 ):
     rows, width = gate_ref.shape
+    query_copy = pltpu.make_async_copy(projected_ref.at[0], query_ref, sems.at[0])
+    query_copy.start()
+    residual_copy = pltpu.make_async_copy(residual_hbm, residual_ref, sems.at[1])
+    residual_copy.start()
     shift_ref[...] = shift_matrix(rows)
     residue = per_channel(residue_ref[...], selectors(residue_ref.shape[1]))
     wide = GROUPS * CHUNK
@@ -302,6 +312,7 @@
 
     pipelined(width // LANES, exponents, products, finish)
     before = halo(before_ref, place_ref)
+    query_copy.wait()
 
     def fetch(part):
         return (earlier_tokens(shift_ref[...], query_ref[:, lanes_of(part, WIDE)]),)
@@ -314,6 +325,7 @@
         gate_ref[0:8, here] = short_conv(head, before[0, :, here], weights)
 
     pipelined(width // WIDE, fetch, convolve)
+    residual_copy.wait()
 
 
 def local_kernel(
@@ -535,18 +547,16 @@
 
     before = lax.ppermute(projected[:, rows - (taps - 1) :, :], "ctx", ring(peers, 1))
 
-    product, state, mode_rate, head, weights, query, residue, residual_here = pl.pallas_call(
+    product, state, mode_rate, head, weights, residue = pl.pallas_call(
         state_kernel,
-        in_specs=[hbm_spec] * 5,
+        in_specs=[hbm_spec] * 4,
         out_shape=[
             bf16(rows, width),
             f32(MODES, width),
             f32(MODES, width),
             f32(2, 8, width),
             f32(*short_weight.shape),
-            bf16(rows, width),
             f32(MODES, residues.shape[0]),
-            bf16(rows, width),
         ],
         scratch_shapes=[
             pltpu.VMEM((2, rows, width), BF16),
@@ -560,7 +570,7 @@
         compiler_params=params(),
         cost_estimate=cost(3),
         name="block_state",
-    )(kept(projected), kept(short_weight), kept(rates.T), kept(residues.T), kept(residual))
+    )(kept(projected), kept(short_weight), kept(rates.T), kept(residues.T))
 
     full_state, first = pl.pallas_call(
         lambda *refs: head_kernel(rows, *refs),
@@ -571,20 +581,25 @@
         name="head_tokens",
     )(place, before, head, weights, state, mode_rate)
 
-    inner, entering, carry_table, gate = pl.pallas_call(
+    inner, entering, carry_table, gate, residual_here = pl.pallas_call(
         prepare_kernel,
-        in_specs=[smem_spec] + [vmem_spec] * 5,
+        in_specs=[smem_spec] + [hbm_spec] * 2 + [vmem_spec] * 4,
         out_shape=[
             bf16(tiles, CHUNK + MODES, GROUPS * CHUNK),
             bf16(tiles, CHUNK, LANES),
             bf16(wides, rows, WIDE),
             f32(rows, width),
+            bf16(rows, width),
         ],
-        scratch_shapes=[pltpu.VMEM((2 * rows, rows), BF16)],
+        scratch_shapes=[
+            pltpu.VMEM((rows, width), BF16),
+            pltpu.VMEM((2 * rows, rows), BF16),
+            pltpu.SemaphoreType.DMA((2,)),
+        ],
         compiler_params=params(),
         cost_estimate=cost(2),
         name="prepare",
-    )(place, query, residue, before, weights, mode_rate)
+    )(place, kept(projected), kept(residual), residue, before, weights, mode_rate)
 
     group, entry, stride = full_state, jnp.zeros((MODES, width), F32), 1
     levels = radices(peers)

time: 26.8 us -> 27 us (level)
  Pallas kernels: 11.2 us -> 12 us
  waiting for transfers between devices: 2.48 us -> 2.17 us
    pallas_call x2, Pallas kernels: 5.57 us -> 6.3 us  [the longest x1 3.85 us: per_device(): pl.pallas_call(state_kernel, in_specs=[hbm_spec] * 4, out_shape=[bf16(row...]
    ppermute x1, waiting for transfers between devices: 1.46 us -> 0.98 us  [per_device(): lax.ppermute(projected[:, rows - (taps - 1):, :], 'ctx', ring(peers, 1))]
  transfers between devices with their start and end apart: 8 -> 8, of which waited for: 5 -> 5; matrix products, arithmetic and copies ran while one was open for 0% -> 0% of each run, Pallas kernels for 34% -> 36%
where the time goes in v17:
time: 27 us; the launch traced here: 26.9 us
  Pallas kernels  12 us (44%)
  starting transfers between devices  11.1 us (41%)
  waiting for transfers between devices  2.17 us (8%)
  local copies, waits for them, and re-layouts  0.94 us (3%)
  between operations  0.7 us (3%)
    ppermute x4, starting transfers between devices, per_device(): lax.ppermute(group, 'ctx', route)  6.21 us
    pallas_call x1, Pallas kernels, per_device(): pl.pallas_call(state_kernel, in_specs=[hbm_spec] * 4, out_shape=[bf16(row...  3.85 us
    ppermute x1, starting transfers between devices, per_device(): lax.ppermute(projected[:, rows - (taps - 1):, :], 'ctx', ring(peers, 1))  2.99 us
    pallas_call x1, Pallas kernels, per_device(): pl.pallas_call(prepare_kernel, in_specs=[smem_spec] + [hbm_spec] * 2 + [v...  2.45 us
    pallas_call x1, Pallas kernels, per_device(): pl.pallas_call(local_kernel, out_shape=f32(rows, width), compiler_params=...  2.43 us
    pallas_call x2, Pallas kernels, write(): pl.pallas_call(kernel, out_specs=hbm_spec, out_shape=bf16(rows, width), s...  2.21 us
    ppermute x3, starting transfers between devices, per_device(): lax.ppermute(squares, 'fsdp', route)  1.87 us
    ppermute x1, waiting for transfers between devices, per_device(): lax.ppermute(projected[:, rows - (taps - 1):, :], 'ctx', ring(peers, 1))  0.98 us
  transfers between devices with their start and end apart: 8, of which 5 were waited for; matrix products, arithmetic and copies ran while one was open for 0% of the time, Pallas kernels for 36%

profile of v17, /device:TPU:0, one launch (start us, length us, event | category | flops | bytes accessed | tf_op | source)
XLA Modules:
  0.0 26.9 jit_solution(5388179949726673805)
XLA Ops:
  0.6 0.9 %slice.3 = bf16[3,2,2048]{2,1,0:T(2,128)(2,1)S(1)} slice(bf16[3,256,2048]{2,1,0:T(8,128)(2,1)} %projected_ref.3), slice={[0:3], [254:256], [0:2048]} | slice | bytes 49152 | tf_op jit(solution)/shard_map/slice | solution.py:548
  1.6 3.0 %collective-permute-start = (bf16[3,2,2048]{2,1,0:T(2,128)(2,1)S(1)}, bf16[3,2,2048]{2,1,0:T(2,128)(2,1)S(1)}, u32[]{:S(2)}, u32[]{:S(2)}) collective-permute-start(bf16[3,2,2048]{2,1,0:T(2,128)(2,1)S(1)} %slice.3), channel_id=1, source_target_pairs={{0,4},{4,8},{8,12},{12,16},{16,20},{20,24},{24,28},{28,0},{1,5},{5... | collective-permute-start | bytes 73736 | tf_op jit(solution)/shard_map/ppermute | solution.py:548
  4.5 3.9 %block_state.1 = (bf16[256,2048]{1,0:T(8,128)(2,1)S(1)}, f32[16,2048]{1,0:T(8,128)S(1)}, f32[16,2048]{1,0:T(8,128)S(1)}, f32[2,8,2048]{2,1,0:T(8,128)S(1)}, f32[...) custom-call(bf16[3,256,2048]{2,1,0:T(8,128)(2,1)} %projected_ref.3, bf16[3,3,2048]{2,1,0:T(4,128)(2,1)} %weight_hbm.1, ...), custom_call_target="tpu_custom_call" | custom-call | bytes 9000000 | tf_op jit(solution)/shard_map/block_state/pallas_call | solution.py:550
  8.4 1.0 %collective-permute-done.before_ref.refs_1_ = bf16[3,2,2048]{2,1,0:T(2,128)(2,1)S(1)} collective-permute-done((bf16[3,2,2048]{2,1,0:T(2,128)(2,1)S(1)}, bf16[3,2,2048]{2,1,0:T(2,128)(2,1)S(1)}, u32[]{:S(2)}, u32[]{:S(2)}) %collective-permute-start) | collective-permute-done | bytes 24608 | tf_op jit(solution)/shard_map/ppermute | solution.py:548
  9.4 0.1 head_tokens.1
  9.5 1.7 %collective-permute-start.1 = (bf16[16,2048]{1,0:T(8,128)(2,1)S(1)}, bf16[16,2048]{1,0:T(8,128)(2,1)S(1)}, u32[]{:S(2)}, u32[]{:S(2)}) collective-permute-start(bf16[16,2048]{1,0:T(8,128)(2,1)S(1)} %get-tuple-element.30.refs_1_), channel_id=1, source_target_pairs={{12,0},{8,4},{4,8},{0,12},{28,16},{24,20},{20,24},{16,28},{13,1},{... | collective-permute-start | bytes 196616 | tf_op jit(solution)/shard_map/ppermute | solution.py:610
  11.2 0.4 %collective-permute-start.2 = (bf16[16,2048]{1,0:T(8,128)(2,1)S(1)}, bf16[16,2048]{1,0:T(8,128)(2,1)S(1)}, u32[]{:S(2)}, u32[]{:S(2)}) collective-permute-start(bf16[16,2048]{1,0:T(8,128)(2,1)S(1)} %get-tuple-element.30.refs_1_), channel_id=1, source_target_pairs={{8,0},{12,4},{0,8},{4,12},{24,16},{28,20},{16,24},{20,28},{9,1},{1... | collective-permute-start | bytes 196616 | tf_op jit(solution)/shard_map/ppermute | solution.py:610
  11.6 1.4 %collective-permute-start.3 = (bf16[16,2048]{1,0:T(8,128)(2,1)S(1)}, bf16[16,2048]{1,0:T(8,128)(2,1)S(1)}, u32[]{:S(2)}, u32[]{:S(2)}) collective-permute-start(bf16[16,2048]{1,0:T(8,128)(2,1)S(1)} %get-tuple-element.30.refs_1_), channel_id=1, source_target_pairs={{4,0},{0,4},{12,8},{8,12},{20,16},{16,20},{28,24},{24,28},{5,1},{1... | collective-permute-start | bytes 196616 | tf_op jit(solution)/shard_map/ppermute | solution.py:610
  13.1 0.0 copy-start
  13.1 2.4 %prepare.1 = (bf16[16,48,256]{2,1,0:T(8,128)(2,1)S(1)}, bf16[16,32,128]{2,1,0:T(8,128)(2,1)S(1)}, bf16[8,256,256]{2,1,0:T(8,128)(2,1)S(1)}, f32[256,2048]{1,0:T(8,128)S(1)}, bf16[256,2048]{1,0:T(8,128)(2,1)S(1)}) custom-call(s32[1]{0:T(128)} %bitcast.place_ref.refs_0_, bf16[3,256,2048]{2,1,0:T(8,128)(2,1)} %projected_ref.3, bf16[256,2048]{1,0:T(8,128)(2,1)} %residual_hbm.1, ...), custom_call_target="tpu_custom_call" | custom-call | bytes 6000000 | tf_op jit(solution)/shard_map/prepare/pallas_call | solution.py:584
  15.5 0.0 collective-permute-done.1.refs_4_
  15.5 0.0 collective-permute-done.2.refs_5_
  15.6 0.3 %collective-permute-done.3.refs_6_ = bf16[16,2048]{1,0:T(8,128)(2,1)S(1)} collective-permute-done((bf16[16,2048]{1,0:T(8,128)(2,1)S(1)}, bf16[16,2048]{1,0:T(8,128)(2,1)S(1)}, u32[]{:S(2)}, u32[]{:S(2)}) %collective-permute-start.3) | collective-permute-done | bytes 65568 | tf_op jit(solution)/shard_map/ppermute | solution.py:610
  15.9 0.2 join.1
  16.1 2.7 %collective-permute-start.4 = (bf16[16,2048]{1,0:T(8,128)(2,1)S(1)}, bf16[16,2048]{1,0:T(8,128)(2,1)S(1)}, u32[]{:S(2)}, u32[]{:S(2)}) collective-permute-start(bf16[16,2048]{1,0:T(8,128)(2,1)S(1)} %get-tuple-element.37), channel_id=1, source_target_pairs={{16,0},{20,4},{24,8},{28,12},{0,16},{4,20},{8,24},{12,28},{17,1},{... | collective-permute-start | bytes 196616 | tf_op jit(solution)/shard_map/ppermute | solution.py:622
  18.7 0.0 copy-done
  18.7 2.4 %local_conv.1.refs_1_ = f32[256,2048]{1,0:T(8,128)S(1)} custom-call(f32[256,2048]{1,0:T(8,128)S(1)} %get-tuple-element.24.gate_ref.refs_2_, bf16[256,2048]{1,0:T(8,128)(2,1)S(1)} %get-tuple-element.25.residual_ref, bf16[256,2048]{1,0:T(8,128)(2,1)S(1)} %get-tuple-element.26.product_ref, f32[8,2048]{1,0:T(8,128)S(1)} %get-tuple-element.29.first_ref, ...), custom_call_target="tpu_custom_call" | custom-call | bytes 15000000 | tf_op jit(solution)/shard_map/local_conv/pallas_call | solution.py:624
  21.2 0.1 collective-permute-done.4.refs_6_
  21.3 0.7 %add_carry.1 = (f32[256,2048]{1,0:T(8,128)S(1)}, f32[1,256]{1,0:T(1,128)S(1)}) custom-call(s32[1]{0:T(128)} %bitcast.place_ref.refs_0_, f32[256,2048]{1,0:T(8,128)S(1)} %local_conv.1.refs_1_, f32[256,2048]{1,0:T(8,128)S(1)} %get-tuple-element.24.gate_ref.refs_2_, bf16[8,256,256]{2,1,0:T(8,128)(2,1)S(1)} %get-tuple-element.34.refs_3_, ...), custom_call_target="tpu_custom_call" | custom-call | bytes 3000000 | tf_op jit(solution)/shard_map/add_carry/pallas_call | solution.py:633
  22.0 0.0 copy-start.1
  22.0 0.0 collective-permute-start.5
  22.0 1.6 %collective-permute-start.6 = (f32[1,256]{1,0:T(1,128)S(1)}, f32[1,256]{1,0:T(1,128)S(1)}, u32[]{:S(2)}, u32[]{:S(2)}) collective-permute-start(f32[1,256]{1,0:T(1,128)S(1)} %get-tuple-element.39.refs_2_), channel_id=1, source_target_pairs={{2,0},{3,1},{0,2},{1,3},{6,4},{7,5},{4,6},{5,7},{10,8},{11,9},{8,1... | collective-permute-start | bytes 3080 | tf_op jit(solution)/shard_map/ppermute | solution.py:642
  23.6 0.3 %collective-permute-start.7 = (f32[1,256]{1,0:T(1,128)S(1)}, f32[1,256]{1,0:T(1,128)S(1)}, u32[]{:S(2)}, u32[]{:S(2)}) collective-permute-start(f32[1,256]{1,0:T(1,128)S(1)} %get-tuple-element.39.refs_2_), channel_id=1, source_target_pairs={{1,0},{0,1},{3,2},{2,3},{5,4},{4,5},{7,6},{6,7},{9,8},{8,9},{11,10... | collective-permute-start | bytes 3080 | tf_op jit(solution)/shard_map/ppermute | solution.py:642
  23.9 1.0 %new_residual.1 = bf16[256,2048]{1,0:T(8,128)(2,1)} custom-call(f32[256,2048]{1,0:T(8,128)S(1)} %get-tuple-element.38.summed_ref.refs_0_), custom_call_target="tpu_custom_call" | custom-call | bytes 3000000 | tf_op jit(solution)/shard_map/new_residual/pallas_call | solution.py:645
  25.0 0.1 collective-permute-done.5.refs_3_
  25.0 0.6 %collective-permute-done.6.refs_4_ = f32[1,256]{1,0:T(1,128)S(1)} collective-permute-done((f32[1,256]{1,0:T(1,128)S(1)}, f32[1,256]{1,0:T(1,128)S(1)}, u32[]{:S(2)}, u32[]{:S(2)}) %collective-permute-start.6) | collective-permute-done | bytes 1056 | tf_op jit(solution)/shard_map/ppermute | solution.py:642
  25.7 0.0 collective-permute-done.7.refs_5_
  25.7 0.0 copy-done.1
  25.7 1.2 %normed.1 = bf16[256,2048]{1,0:T(8,128)(2,1)} custom-call(f32[256,2048]{1,0:T(8,128)S(1)} %get-tuple-element.38.summed_ref.refs_0_, f32[1,2048]{1,0:T(1,128)S(1)} %bitcast.6, f32[1,256]{1,0:T(1,128)S(1)} %get-tuple-element.39.refs_2_, f32[1,256]{1,0:T(1,128)S(1)} %collective-permute-done.5.refs_3_, f32[1,256]{1,0:T(1,128)S(1)} %collective-permute-done.6.refs_4_, ...), custom_call_target="tpu_custom_call" | custom-call | bytes 3000000 | tf_op jit(solution)/shard_map/normed/pallas_call | solution.py:645
  (1 shorter events, 0.0 us)
Async XLA Ops:
  1.6 7.8 %collective-permute-start = (bf16[3,2,2048]{2,1,0:T(2,128)(2,1)S(1)}, bf16[3,2,2048]{2,1,0:T(2,128)(2,1)S(1)}, u32[]{:S(2)}, u32[]{:S(2)}) collective-permute-start(bf16[3,2,2048]{2,1,0:T(2,128)(2,1)S(1)} %slice.3), channel_id=1, source_target_pairs={{0,4},{4,8},{8,12},{12,16},{16,20},{20,24},{24,28},{28,0},{1,5},{5... | collective-permute-start | bytes 73736 | tf_op jit(solution)/shard_map/ppermute | solution.py:548
  9.5 6.0 %collective-permute-start.1 = (bf16[16,2048]{1,0:T(8,128)(2,1)S(1)}, bf16[16,2048]{1,0:T(8,128)(2,1)S(1)}, u32[]{:S(2)}, u32[]{:S(2)}) collective-permute-start(bf16[16,2048]{1,0:T(8,128)(2,1)S(1)} %get-tuple-element.30.refs_1_), channel_id=1, source_target_pairs={{12,0},{8,4},{4,8},{0,12},{28,16},{24,20},{20,24},{16,28},{13,1},{... | collective-permute-start | bytes 196616 | tf_op jit(solution)/shard_map/ppermute | solution.py:610
  11.2 4.4 %collective-permute-start.2 = (bf16[16,2048]{1,0:T(8,128)(2,1)S(1)}, bf16[16,2048]{1,0:T(8,128)(2,1)S(1)}, u32[]{:S(2)}, u32[]{:S(2)}) collective-permute-start(bf16[16,2048]{1,0:T(8,128)(2,1)S(1)} %get-tuple-element.30.refs_1_), channel_id=1, source_target_pairs={{8,0},{12,4},{0,8},{4,12},{24,16},{28,20},{16,24},{20,28},{9,1},{1... | collective-permute-start | bytes 196616 | tf_op jit(solution)/shard_map/ppermute | solution.py:610
  11.6 4.3 %collective-permute-start.3 = (bf16[16,2048]{1,0:T(8,128)(2,1)S(1)}, bf16[16,2048]{1,0:T(8,128)(2,1)S(1)}, u32[]{:S(2)}, u32[]{:S(2)}) collective-permute-start(bf16[16,2048]{1,0:T(8,128)(2,1)S(1)} %get-tuple-element.30.refs_1_), channel_id=1, source_target_pairs={{4,0},{0,4},{12,8},{8,12},{20,16},{16,20},{28,24},{24,28},{5,1},{1... | collective-permute-start | bytes 196616 | tf_op jit(solution)/shard_map/ppermute | solution.py:610
  13.1 5.7 %copy-start = (f32[2048]{0:T(1024)S(1)}, f32[2048]{0:T(1024)}, u32[]{:S(2)}) copy-start(f32[2048]{0:T(1024)} %param.11) | copy-start | bytes 24580
  16.1 5.2 %collective-permute-start.4 = (bf16[16,2048]{1,0:T(8,128)(2,1)S(1)}, bf16[16,2048]{1,0:T(8,128)(2,1)S(1)}, u32[]{:S(2)}, u32[]{:S(2)}) collective-permute-start(bf16[16,2048]{1,0:T(8,128)(2,1)S(1)} %get-tuple-element.37), channel_id=1, source_target_pairs={{16,0},{20,4},{24,8},{28,12},{0,16},{4,20},{8,24},{12,28},{17,1},{... | collective-permute-start | bytes 196616 | tf_op jit(solution)/shard_map/ppermute | solution.py:622
  22.0 3.6 %copy-start.1 = (f32[2048]{0:T(1024)S(1)}, f32[2048]{0:T(1024)}, u32[]{:S(2)}) copy-start(f32[2048]{0:T(1024)} %param.13) | copy-start | bytes 24580
  22.0 3.0 %collective-permute-start.5 = (f32[1,256]{1,0:T(1,128)S(1)}, f32[1,256]{1,0:T(1,128)S(1)}, u32[]{:S(2)}, u32[]{:S(2)}) collective-permute-start(f32[1,256]{1,0:T(1,128)S(1)} %get-tuple-element.39.refs_2_), channel_id=1, source_target_pairs={{3,0},{2,1},{1,2},{0,3},{7,4},{6,5},{5,6},{4,7},{11,8},{10,9},{9,1... | collective-permute-start | bytes 3080 | tf_op jit(solution)/shard_map/ppermute | solution.py:642
  22.0 3.6 %collective-permute-start.6 = (f32[1,256]{1,0:T(1,128)S(1)}, f32[1,256]{1,0:T(1,128)S(1)}, u32[]{:S(2)}, u32[]{:S(2)}) collective-permute-start(f32[1,256]{1,0:T(1,128)S(1)} %get-tuple-element.39.refs_2_), channel_id=1, source_target_pairs={{2,0},{3,1},{0,2},{1,3},{6,4},{7,5},{4,6},{5,7},{10,8},{11,9},{8,1... | collective-permute-start | bytes 3080 | tf_op jit(solution)/shard_map/ppermute | solution.py:642
  23.6 2.1 %collective-permute-start.7 = (f32[1,256]{1,0:T(1,128)S(1)}, f32[1,256]{1,0:T(1,128)S(1)}, u32[]{:S(2)}, u32[]{:S(2)}) collective-permute-start(f32[1,256]{1,0:T(1,128)S(1)} %get-tuple-element.39.refs_2_), channel_id=1, source_target_pairs={{1,0},{0,1},{3,2},{2,3},{5,4},{4,5},{7,6},{6,7},{9,8},{8,9},{11,10... | collective-permute-start | bytes 3080 | tf_op jit(solution)/shard_map/ppermute | solution.py:642

commit v18 on v17

--- a/solution.py
+++ b/solution.py
@@ -157,17 +157,17 @@
     rate_copy.start()
     weight_copy = pltpu.make_async_copy(weight_hbm, short_ref, small_sems.at[1])
     weight_copy.start()
-    part = width // 2
+    part = rows // 4
     copies = [
         pltpu.make_async_copy(
-            projected_ref.at[1 + c, :, pl.ds(side * part, part)],
-            buffer_ref.at[c, :, pl.ds(side * part, part)],
+            projected_ref.at[1 + c, pl.ds(side * part, part), :],
+            buffer_ref.at[c, pl.ds(side * part, part), :],
             sems.at[2 * side + c],
         )
-        for side in (0, 1)
+        for side in range(4)
         for c in (0, 1)
     ]
-    residue_copy = pltpu.make_async_copy(residue_hbm, residue_ref, sems.at[4])
+    residue_copy = pltpu.make_async_copy(residue_hbm, residue_ref, sems.at[8])
     for copy in copies:
         copy.start()
     residue_copy.start()
@@ -193,12 +193,10 @@
     weight_copy.wait()
     weights = short_ref[...].astype(F32)
     weight_ref[...] = weights
+    for copy in copies:
+        copy.wait()
 
     def fetch(wide):
-        if wide % (wides // 2) == 0:
-            first = 2 * (wide // (wides // 2))
-            for copy in copies[first : first + 2]:
-                copy.wait()
         here = lanes_of(wide, WIDE)
         return (
             earlier_tokens(shift_ref[...], buffer_ref[0, :, here]),
@@ -564,7 +562,7 @@
             pltpu.VMEM((2 * rows, rows), BF16),
             pltpu.VMEM(short_weight.shape, BF16),
             pltpu.VMEM((MODES, rates.shape[0]), F32),
-            pltpu.SemaphoreType.DMA((5,)),
+            pltpu.SemaphoreType.DMA((9,)),
             pltpu.SemaphoreType.DMA((2,)),
         ],
         compiler_params=params(),

time: 27 us -> 26.9 us (level)
  no operation moved by 1% of the time
where the time goes in v18:
time: 26.9 us; the launch traced here: 26.7 us
  Pallas kernels  11.9 us (44%)
  starting transfers between devices  11.1 us (41%)
  waiting for transfers between devices  2.18 us (8%)
  local copies, waits for them, and re-layouts  0.94 us (3%)
  between operations  0.7 us (3%)
    ppermute x4, starting transfers between devices, per_device(): lax.ppermute(group, 'ctx', route)  6.2 us
    pallas_call x1, Pallas kernels, per_device(): pl.pallas_call(state_kernel, in_specs=[hbm_spec] * 4, out_shape=[bf16(row...  3.75 us
    ppermute x1, starting transfers between devices, per_device(): lax.ppermute(projected[:, rows - (taps - 1):, :], 'ctx', ring(peers, 1))  2.99 us
    pallas_call x1, Pallas kernels, per_device(): pl.pallas_call(prepare_kernel, in_specs=[smem_spec] + [hbm_spec] * 2 + [v...  2.45 us
    pallas_call x1, Pallas kernels, per_device(): pl.pallas_call(local_kernel, out_shape=f32(rows, width), compiler_params=...  2.44 us
    pallas_call x2, Pallas kernels, write(): pl.pallas_call(kernel, out_specs=hbm_spec, out_shape=bf16(rows, width), s...  2.21 us
    ppermute x3, starting transfers between devices, per_device(): lax.ppermute(squares, 'fsdp', route)  1.87 us
    ppermute x1, waiting for transfers between devices, per_device(): lax.ppermute(projected[:, rows - (taps - 1):, :], 'ctx', ring(peers, 1))  1.09 us
  transfers between devices with their start and end apart: 8, of which 5 were waited for; matrix products, arithmetic and copies ran while one was open for 0% of the time, Pallas kernels for 36%

profile of v18, /device:TPU:0, one launch (start us, length us, event | category | flops | bytes accessed | tf_op | source)
XLA Modules:
  0.0 26.7 jit_solution(4556696830208058138)
XLA Ops:
  0.6 0.9 %slice.3 = bf16[3,2,2048]{2,1,0:T(2,128)(2,1)S(1)} slice(bf16[3,256,2048]{2,1,0:T(8,128)(2,1)} %projected_ref.3), slice={[0:3], [254:256], [0:2048]} | slice | bytes 49152 | tf_op jit(solution)/shard_map/slice | solution.py:546
  1.6 3.0 %collective-permute-start = (bf16[3,2,2048]{2,1,0:T(2,128)(2,1)S(1)}, bf16[3,2,2048]{2,1,0:T(2,128)(2,1)S(1)}, u32[]{:S(2)}, u32[]{:S(2)}) collective-permute-start(bf16[3,2,2048]{2,1,0:T(2,128)(2,1)S(1)} %slice.3), channel_id=1, source_target_pairs={{0,4},{4,8},{8,12},{12,16},{16,20},{20,24},{24,28},{28,0},{1,5},{5... | collective-permute-start | bytes 73736 | tf_op jit(solution)/shard_map/ppermute | solution.py:546
  4.5 3.7 %block_state.1 = (bf16[256,2048]{1,0:T(8,128)(2,1)S(1)}, f32[16,2048]{1,0:T(8,128)S(1)}, f32[16,2048]{1,0:T(8,128)S(1)}, f32[2,8,2048]{2,1,0:T(8,128)S(1)}, f32[...) custom-call(bf16[3,256,2048]{2,1,0:T(8,128)(2,1)} %projected_ref.3, bf16[3,3,2048]{2,1,0:T(4,128)(2,1)} %weight_hbm.1, ...), custom_call_target="tpu_custom_call" | custom-call | bytes 9000000 | tf_op jit(solution)/shard_map/block_state/pallas_call | solution.py:548
  8.3 1.1 %collective-permute-done.before_ref.refs_1_ = bf16[3,2,2048]{2,1,0:T(2,128)(2,1)S(1)} collective-permute-done((bf16[3,2,2048]{2,1,0:T(2,128)(2,1)S(1)}, bf16[3,2,2048]{2,1,0:T(2,128)(2,1)S(1)}, u32[]{:S(2)}, u32[]{:S(2)}) %collective-permute-start) | collective-permute-done | bytes 24608 | tf_op jit(solution)/shard_map/ppermute | solution.py:546
  9.4 0.1 head_tokens.1
  9.5 1.6 %collective-permute-start.1 = (bf16[16,2048]{1,0:T(8,128)(2,1)S(1)}, bf16[16,2048]{1,0:T(8,128)(2,1)S(1)}, u32[]{:S(2)}, u32[]{:S(2)}) collective-permute-start(bf16[16,2048]{1,0:T(8,128)(2,1)S(1)} %get-tuple-element.30.refs_1_), channel_id=1, source_target_pairs={{12,0},{8,4},{4,8},{0,12},{28,16},{24,20},{20,24},{16,28},{13,1},{... | collective-permute-start | bytes 196616 | tf_op jit(solution)/shard_map/ppermute | solution.py:608
  11.1 0.4 %collective-permute-start.2 = (bf16[16,2048]{1,0:T(8,128)(2,1)S(1)}, bf16[16,2048]{1,0:T(8,128)(2,1)S(1)}, u32[]{:S(2)}, u32[]{:S(2)}) collective-permute-start(bf16[16,2048]{1,0:T(8,128)(2,1)S(1)} %get-tuple-element.30.refs_1_), channel_id=1, source_target_pairs={{8,0},{12,4},{0,8},{4,12},{24,16},{28,20},{16,24},{20,28},{9,1},{1... | collective-permute-start | bytes 196616 | tf_op jit(solution)/shard_map/ppermute | solution.py:608
  11.5 1.5 %collective-permute-start.3 = (bf16[16,2048]{1,0:T(8,128)(2,1)S(1)}, bf16[16,2048]{1,0:T(8,128)(2,1)S(1)}, u32[]{:S(2)}, u32[]{:S(2)}) collective-permute-start(bf16[16,2048]{1,0:T(8,128)(2,1)S(1)} %get-tuple-element.30.refs_1_), channel_id=1, source_target_pairs={{4,0},{0,4},{12,8},{8,12},{20,16},{16,20},{28,24},{24,28},{5,1},{1... | collective-permute-start | bytes 196616 | tf_op jit(solution)/shard_map/ppermute | solution.py:608
  13.1 0.0 copy-start
  13.1 2.4 %prepare.1 = (bf16[16,48,256]{2,1,0:T(8,128)(2,1)S(1)}, bf16[16,32,128]{2,1,0:T(8,128)(2,1)S(1)}, bf16[8,256,256]{2,1,0:T(8,128)(2,1)S(1)}, f32[256,2048]{1,0:T(8,128)S(1)}, bf16[256,2048]{1,0:T(8,128)(2,1)S(1)}) custom-call(s32[1]{0:T(128)} %bitcast.place_ref.refs_0_, bf16[3,256,2048]{2,1,0:T(8,128)(2,1)} %projected_ref.3, bf16[256,2048]{1,0:T(8,128)(2,1)} %residual_hbm.1, ...), custom_call_target="tpu_custom_call" | custom-call | bytes 6000000 | tf_op jit(solution)/shard_map/prepare/pallas_call | solution.py:582
  15.5 0.0 collective-permute-done.1.refs_4_
  15.5 0.0 collective-permute-done.2.refs_5_
  15.6 0.2 collective-permute-done.3.refs_6_
  15.8 0.2 join.1
  16.0 2.6 %collective-permute-start.4 = (bf16[16,2048]{1,0:T(8,128)(2,1)S(1)}, bf16[16,2048]{1,0:T(8,128)(2,1)S(1)}, u32[]{:S(2)}, u32[]{:S(2)}) collective-permute-start(bf16[16,2048]{1,0:T(8,128)(2,1)S(1)} %get-tuple-element.37), channel_id=1, source_target_pairs={{16,0},{20,4},{24,8},{28,12},{0,16},{4,20},{8,24},{12,28},{17,1},{... | collective-permute-start | bytes 196616 | tf_op jit(solution)/shard_map/ppermute | solution.py:620
  18.6 0.0 copy-done
  18.6 2.4 %local_conv.1.refs_1_ = f32[256,2048]{1,0:T(8,128)S(1)} custom-call(f32[256,2048]{1,0:T(8,128)S(1)} %get-tuple-element.24.gate_ref.refs_2_, bf16[256,2048]{1,0:T(8,128)(2,1)S(1)} %get-tuple-element.25.residual_ref, bf16[256,2048]{1,0:T(8,128)(2,1)S(1)} %get-tuple-element.26.product_ref, f32[8,2048]{1,0:T(8,128)S(1)} %get-tuple-element.29.first_ref, ...), custom_call_target="tpu_custom_call" | custom-call | bytes 15000000 | tf_op jit(solution)/shard_map/local_conv/pallas_call | solution.py:622
  21.1 0.1 collective-permute-done.4.refs_6_
  21.2 0.7 %add_carry.1 = (f32[256,2048]{1,0:T(8,128)S(1)}, f32[1,256]{1,0:T(1,128)S(1)}) custom-call(s32[1]{0:T(128)} %bitcast.place_ref.refs_0_, f32[256,2048]{1,0:T(8,128)S(1)} %local_conv.1.refs_1_, f32[256,2048]{1,0:T(8,128)S(1)} %get-tuple-element.24.gate_ref.refs_2_, bf16[8,256,256]{2,1,0:T(8,128)(2,1)S(1)} %get-tuple-element.34.refs_3_, ...), custom_call_target="tpu_custom_call" | custom-call | bytes 3000000 | tf_op jit(solution)/shard_map/add_carry/pallas_call | solution.py:631
  21.9 0.0 copy-start.1
  21.9 0.0 collective-permute-start.5
  21.9 1.6 %collective-permute-start.6 = (f32[1,256]{1,0:T(1,128)S(1)}, f32[1,256]{1,0:T(1,128)S(1)}, u32[]{:S(2)}, u32[]{:S(2)}) collective-permute-start(f32[1,256]{1,0:T(1,128)S(1)} %get-tuple-element.39.refs_2_), channel_id=1, source_target_pairs={{2,0},{3,1},{0,2},{1,3},{6,4},{7,5},{4,6},{5,7},{10,8},{11,9},{8,1... | collective-permute-start | bytes 3080 | tf_op jit(solution)/shard_map/ppermute | solution.py:640
  23.5 0.3 %collective-permute-start.7 = (f32[1,256]{1,0:T(1,128)S(1)}, f32[1,256]{1,0:T(1,128)S(1)}, u32[]{:S(2)}, u32[]{:S(2)}) collective-permute-start(f32[1,256]{1,0:T(1,128)S(1)} %get-tuple-element.39.refs_2_), channel_id=1, source_target_pairs={{1,0},{0,1},{3,2},{2,3},{5,4},{4,5},{7,6},{6,7},{9,8},{8,9},{11,10... | collective-permute-start | bytes 3080 | tf_op jit(solution)/shard_map/ppermute | solution.py:640
  23.8 1.0 %new_residual.1 = bf16[256,2048]{1,0:T(8,128)(2,1)} custom-call(f32[256,2048]{1,0:T(8,128)S(1)} %get-tuple-element.38.summed_ref.refs_0_), custom_call_target="tpu_custom_call" | custom-call | bytes 3000000 | tf_op jit(solution)/shard_map/new_residual/pallas_call | solution.py:643
  24.8 0.1 collective-permute-done.5.refs_3_
  24.9 0.6 %collective-permute-done.6.refs_4_ = f32[1,256]{1,0:T(1,128)S(1)} collective-permute-done((f32[1,256]{1,0:T(1,128)S(1)}, f32[1,256]{1,0:T(1,128)S(1)}, u32[]{:S(2)}, u32[]{:S(2)}) %collective-permute-start.6) | collective-permute-done | bytes 1056 | tf_op jit(solution)/shard_map/ppermute | solution.py:640
  25.6 0.0 collective-permute-done.7.refs_5_
  25.6 0.0 copy-done.1
  25.6 1.2 %normed.1 = bf16[256,2048]{1,0:T(8,128)(2,1)} custom-call(f32[256,2048]{1,0:T(8,128)S(1)} %get-tuple-element.38.summed_ref.refs_0_, f32[1,2048]{1,0:T(1,128)S(1)} %bitcast.6, f32[1,256]{1,0:T(1,128)S(1)} %get-tuple-element.39.refs_2_, f32[1,256]{1,0:T(1,128)S(1)} %collective-permute-done.5.refs_3_, f32[1,256]{1,0:T(1,128)S(1)} %collective-permute-done.6.refs_4_, ...), custom_call_target="tpu_custom_call" | custom-call | bytes 3000000 | tf_op jit(solution)/shard_map/normed/pallas_call | solution.py:643
  (1 shorter events, 0.0 us)
Async XLA Ops:
  1.6 7.8 %collective-permute-start = (bf16[3,2,2048]{2,1,0:T(2,128)(2,1)S(1)}, bf16[3,2,2048]{2,1,0:T(2,128)(2,1)S(1)}, u32[]{:S(2)}, u32[]{:S(2)}) collective-permute-start(bf16[3,2,2048]{2,1,0:T(2,128)(2,1)S(1)} %slice.3), channel_id=1, source_target_pairs={{0,4},{4,8},{8,12},{12,16},{16,20},{20,24},{24,28},{28,0},{1,5},{5... | collective-permute-start | bytes 73736 | tf_op jit(solution)/shard_map/ppermute | solution.py:546
  9.5 6.0 %collective-permute-start.1 = (bf16[16,2048]{1,0:T(8,128)(2,1)S(1)}, bf16[16,2048]{1,0:T(8,128)(2,1)S(1)}, u32[]{:S(2)}, u32[]{:S(2)}) collective-permute-start(bf16[16,2048]{1,0:T(8,128)(2,1)S(1)} %get-tuple-element.30.refs_1_), channel_id=1, source_target_pairs={{12,0},{8,4},{4,8},{0,12},{28,16},{24,20},{20,24},{16,28},{13,1},{... | collective-permute-start | bytes 196616 | tf_op jit(solution)/shard_map/ppermute | solution.py:608
  11.1 4.5 %collective-permute-start.2 = (bf16[16,2048]{1,0:T(8,128)(2,1)S(1)}, bf16[16,2048]{1,0:T(8,128)(2,1)S(1)}, u32[]{:S(2)}, u32[]{:S(2)}) collective-permute-start(bf16[16,2048]{1,0:T(8,128)(2,1)S(1)} %get-tuple-element.30.refs_1_), channel_id=1, source_target_pairs={{8,0},{12,4},{0,8},{4,12},{24,16},{28,20},{16,24},{20,28},{9,1},{1... | collective-permute-start | bytes 196616 | tf_op jit(solution)/shard_map/ppermute | solution.py:608
  11.5 4.3 %collective-permute-start.3 = (bf16[16,2048]{1,0:T(8,128)(2,1)S(1)}, bf16[16,2048]{1,0:T(8,128)(2,1)S(1)}, u32[]{:S(2)}, u32[]{:S(2)}) collective-permute-start(bf16[16,2048]{1,0:T(8,128)(2,1)S(1)} %get-tuple-element.30.refs_1_), channel_id=1, source_target_pairs={{4,0},{0,4},{12,8},{8,12},{20,16},{16,20},{28,24},{24,28},{5,1},{1... | collective-permute-start | bytes 196616 | tf_op jit(solution)/shard_map/ppermute | solution.py:608
  13.1 5.5 %copy-start = (f32[2048]{0:T(1024)S(1)}, f32[2048]{0:T(1024)}, u32[]{:S(2)}) copy-start(f32[2048]{0:T(1024)} %param.11) | copy-start | bytes 24580
  16.0 5.2 %collective-permute-start.4 = (bf16[16,2048]{1,0:T(8,128)(2,1)S(1)}, bf16[16,2048]{1,0:T(8,128)(2,1)S(1)}, u32[]{:S(2)}, u32[]{:S(2)}) collective-permute-start(bf16[16,2048]{1,0:T(8,128)(2,1)S(1)} %get-tuple-element.37), channel_id=1, source_target_pairs={{16,0},{20,4},{24,8},{28,12},{0,16},{4,20},{8,24},{12,28},{17,1},{... | collective-permute-start | bytes 196616 | tf_op jit(solution)/shard_map/ppermute | solution.py:620
  21.9 3.6 %copy-start.1 = (f32[2048]{0:T(1024)S(1)}, f32[2048]{0:T(1024)}, u32[]{:S(2)}) copy-start(f32[2048]{0:T(1024)} %param.13) | copy-start | bytes 24580
  21.9 3.0 %collective-permute-start.5 = (f32[1,256]{1,0:T(1,128)S(1)}, f32[1,256]{1,0:T(1,128)S(1)}, u32[]{:S(2)}, u32[]{:S(2)}) collective-permute-start(f32[1,256]{1,0:T(1,128)S(1)} %get-tuple-element.39.refs_2_), channel_id=1, source_target_pairs={{3,0},{2,1},{1,2},{0,3},{7,4},{6,5},{5,6},{4,7},{11,8},{10,9},{9,1... | collective-permute-start | bytes 3080 | tf_op jit(solution)/shard_map/ppermute | solution.py:640
  21.9 3.6 %collective-permute-start.6 = (f32[1,256]{1,0:T(1,128)S(1)}, f32[1,256]{1,0:T(1,128)S(1)}, u32[]{:S(2)}, u32[]{:S(2)}) collective-permute-start(f32[1,256]{1,0:T(1,128)S(1)} %get-tuple-element.39.refs_2_), channel_id=1, source_target_pairs={{2,0},{3,1},{0,2},{1,3},{6,4},{7,5},{4,6},{5,7},{10,8},{11,9},{8,1... | collective-permute-start | bytes 3080 | tf_op jit(solution)/shard_map/ppermute | solution.py:640
  23.5 2.1 %collective-permute-start.7 = (f32[1,256]{1,0:T(1,128)S(1)}, f32[1,256]{1,0:T(1,128)S(1)}, u32[]{:S(2)}, u32[]{:S(2)}) collective-permute-start(f32[1,256]{1,0:T(1,128)S(1)} %get-tuple-element.39.refs_2_), channel_id=1, source_target_pairs={{1,0},{0,1},{3,2},{2,3},{5,4},{4,5},{7,6},{6,7},{9,8},{8,9},{11,10... | collective-permute-start | bytes 3080 | tf_op jit(solution)/shard_map/ppermute | solution.py:640

commit v19 on v16

--- a/solution.py
+++ b/solution.py
@@ -317,6 +317,7 @@
 
 
 def local_kernel(
+    start,
     gate_ref,
     residual_ref,
     product_ref,
@@ -327,12 +328,13 @@
     skip_ref,
     base_ref,
 ):
-    rows, width = product_ref.shape
+    rows, width = base_ref.shape
     mask = group_mask(BF16)
     top = index_of((8, LANES), 0) < 2
     chunks = range(rows // CHUNK)
 
-    def inside(tile):
+    def inside(item):
+        tile = start + item
         here = lanes_of(tile)
         pieces = []
         for chunk in chunks:
@@ -348,7 +350,8 @@
             found.append(jnp.dot(inner_ref[tile], sources, preferred_element_type=F32))
         return found, pieces[0]
 
-    def across(tile, inner, first):
+    def across(item, inner, first):
+        tile = start + item
         decay = jnp.exp(-float(CHUNK) * mode_rate_ref[:, lanes_of(tile)])
         state = jnp.zeros((MODES, LANES), F32)
         states = []
@@ -361,15 +364,15 @@
             outer.append(jnp.dot(entering_ref[tile], two, preferred_element_type=F32))
         return [part[:CHUNK] for part in inner], outer, first
 
-    def finish(tile, inner, outer, first):
-        here = lanes_of(tile)
+    def finish(item, inner, outer, first):
+        here = lanes_of(start + item)
         skip = skip_ref[:, here]
         for chunk in chunks:
             span = slice(chunk * CHUNK, (chunk + 1) * CHUNK)
             piece = first if chunk == 0 else product_ref[span, here]
             conv = (inner[chunk // 2] + outer[chunk // 2])[:, lanes_of(chunk % 2)]
             whole = conv + skip * piece.astype(F32)
-            base_ref[span, here] = residual_ref[span, here].astype(F32) + gate_ref[span, here] * whole
+            base_ref[span, lanes_of(item)] = residual_ref[span, here].astype(F32) + gate_ref[span, here] * whole
 
     pipelined(width // LANES, inside, across, finish)
 
@@ -396,9 +399,12 @@
     group_ref[...] = total.astype(BF16)
 
 
-def carry_kernel(stride, radix, place_ref, base_ref, gate_ref, carry_ref, mode_rate_ref, inner_entry_ref, *refs):
+def carry_kernel(
+    stride, radix, place_ref, left_ref, right_ref, gate_ref, carry_ref, mode_rate_ref, inner_entry_ref, *refs
+):
     entry_refs, (summed_ref, squares_ref) = refs[:-2], refs[-2:]
-    rows, width = base_ref.shape
+    rows, width = gate_ref.shape
+    split_at = left_ref.shape[1] // WIDE
     run = place_ref[0] // stride
     within = lax.rem(place_ref[0], stride).astype(F32) * float(rows)
     mask = group_mask(BF16)
@@ -423,7 +429,11 @@
 
     def add(tile, carry):
         here = lanes_of(tile, WIDE)
-        summed = base_ref[:, here] + gate_ref[:, here] * carry
+        if tile < split_at:
+            base = left_ref[:, here]
+        else:
+            base = right_ref[:, lanes_of(tile - split_at, WIDE)]
+        summed = base + gate_ref[:, here] * carry
         summed_ref[:, here] = summed
         square = summed * summed
         totals[0] = totals[0] + (square[:, :LANES] + square[:, LANES:])
@@ -586,6 +596,18 @@
         name="prepare",
     )(place, query, residue, before, weights, mode_rate)
 
+    def local(start, count):
+        return pl.pallas_call(
+            lambda *refs: local_kernel(start, *refs),
+            out_shape=f32(rows, count * LANES),
+            compiler_params=params(),
+            cost_estimate=cost(0.15 * count),
+            name="local_conv",
+        )(gate, residual_here, product, first, mode_rate, inner, entering, skip[None])
+
+    early = max(2, tiles // 8 * 2)
+    left = local(0, early)
+
     group, entry, stride = full_state, jnp.zeros((MODES, width), F32), 1
     levels = radices(peers)
     for level, radix in enumerate(levels):
@@ -594,7 +616,7 @@
             break
         others = [lax.ppermute(group, "ctx", route) for route in routes(peers, stride, radix)[::-1]]
         if level == 0:
-            others[0], inner = lax.optimization_barrier((others[0], inner))
+            others[0], left = lax.optimization_barrier((others[0], left))
         entry, group = pl.pallas_call(
             lambda *refs, radix=radix, stride=stride: join_kernel(rows, radix, stride, *refs),
             in_specs=[smem_spec] + [vmem_spec] * (2 + radix),
@@ -606,23 +628,17 @@
         stride = size
     received = [lax.ppermute(group, "ctx", route) for route in routes(peers, stride, levels[-1])[::-1]]
 
-    base = pl.pallas_call(
-        local_kernel,
-        out_shape=f32(rows, width),
-        compiler_params=params(),
-        cost_estimate=cost(5),
-        name="local_conv",
-    )(gate, residual_here, product, first, mode_rate, inner, entering, skip[None])
+    right = local(early, tiles - early)
 
     count = lax.axis_size("fsdp")
     summed, squares = pl.pallas_call(
         lambda *refs: carry_kernel(stride, levels[-1], *refs),
-        in_specs=[smem_spec] + [vmem_spec] * (5 + len(received)),
+        in_specs=[smem_spec] + [vmem_spec] * (6 + len(received)),
         out_shape=[f32(rows, width), f32(1, rows)],
         compiler_params=params(),
         cost_estimate=cost(1),
         name="add_carry",
-    )(place, base, gate, carry_table, mode_rate, entry, *received)
+    )(place, left, right, gate, carry_table, mode_rate, entry, *received)
 
     parts = [lax.ppermute(squares, "fsdp", route) for route in routes(count, 1, count)[::-1]]
 

time: 26.8 us -> 28.1 us (1.049)
  waiting for transfers between devices: 2.48 us -> 4.27 us
  starting transfers between devices: 11.1 us -> 10.4 us
    ppermute x4, waiting for transfers between devices: 0.32 us -> 2.12 us  [per_device(): lax.ppermute(group, 'ctx', route)]
    ppermute x4, starting transfers between devices: 6.18 us -> 5.49 us  [per_device(): lax.ppermute(group, 'ctx', route)]
    pallas_call x1 -> x2, Pallas kernels: 2.42 us -> 2.64 us  [local(): pl.pallas_call(lambda *refs: local_kernel(start, *refs), out_shape=f32(ro...]
  transfers between devices with their start and end apart: 8 -> 8, of which waited for: 5 -> 4; matrix products, arithmetic and copies ran while one was open for 0% -> 0% of each run, Pallas kernels for 34% -> 34%
where the time goes in v19:
time: 28.1 us; the launch traced here: 27.7 us
  Pallas kernels  11.4 us (41%)
  starting transfers between devices  10.4 us (37%)
  waiting for transfers between devices  4.27 us (15%)
  local copies, waits for them, and re-layouts  0.94 us (3%)
  between operations  0.73 us (3%)
    ppermute x4, starting transfers between devices, per_device(): lax.ppermute(group, 'ctx', route)  5.49 us
    pallas_call x1, Pallas kernels, per_device(): pl.pallas_call(state_kernel, in_specs=[hbm_spec] * 5, out_shape=[bf16(row...  3.38 us
    ppermute x1, starting transfers between devices, per_device(): lax.ppermute(projected[:, rows - (taps - 1):, :], 'ctx', ring(peers, 1))  2.99 us
    pallas_call x2, Pallas kernels, local(): pl.pallas_call(lambda *refs: local_kernel(start, *refs), out_shape=f32(ro...  2.64 us
    pallas_call x1, Pallas kernels, per_device(): pl.pallas_call(prepare_kernel, in_specs=[smem_spec] + [vmem_spec] * 5, ou...  2.23 us
    pallas_call x2, Pallas kernels, write(): pl.pallas_call(kernel, out_specs=hbm_spec, out_shape=bf16(rows, width), s...  2.21 us
    ppermute x4, waiting for transfers between devices, per_device(): lax.ppermute(group, 'ctx', route)  2.12 us
    ppermute x3, starting transfers between devices, per_device(): lax.ppermute(squares, 'fsdp', route)  1.89 us
  transfers between devices with their start and end apart: 8, of which 4 were waited for; matrix products, arithmetic and copies ran while one was open for 0% of the time, Pallas kernels for 34%

profile of v19, /device:TPU:0, one launch (start us, length us, event | category | flops | bytes accessed | tf_op | source)
XLA Modules:
  0.0 27.7 jit_solution(15914469778050164051)
XLA Ops:
  0.6 0.9 %slice.3 = bf16[3,2,2048]{2,1,0:T(2,128)(2,1)S(1)} slice(bf16[3,256,2048]{2,1,0:T(8,128)(2,1)} %projected_ref.1), slice={[0:3], [254:256], [0:2048]} | slice | bytes 49152 | tf_op jit(solution)/shard_map/slice | solution.py:546
  1.6 3.0 %collective-permute-start = (bf16[3,2,2048]{2,1,0:T(2,128)(2,1)S(1)}, bf16[3,2,2048]{2,1,0:T(2,128)(2,1)S(1)}, u32[]{:S(2)}, u32[]{:S(2)}) collective-permute-start(bf16[3,2,2048]{2,1,0:T(2,128)(2,1)S(1)} %slice.3), channel_id=1, source_target_pairs={{0,4},{4,8},{8,12},{12,16},{16,20},{20,24},{24,28},{28,0},{1,5},{5... | collective-permute-start | bytes 73736 | tf_op jit(solution)/shard_map/ppermute | solution.py:546
  4.5 0.0 copy-start
  4.5 3.4 %block_state.1 = (bf16[256,2048]{1,0:T(8,128)(2,1)S(1)}, f32[16,2048]{1,0:T(8,128)S(1)}, f32[16,2048]{1,0:T(8,128)S(1)}, f32[2,8,2048]{2,1,0:T(8,128)S(1)}, f32[...) custom-call(bf16[3,256,2048]{2,1,0:T(8,128)(2,1)} %projected_ref.1, ...), custom_call_target="tpu_custom_call" | custom-call | bytes 9000000 | tf_op jit(solution)/shard_map/block_state/pallas_call | solution.py:548
  7.9 1.5 %collective-permute-done.refs_1_.before_ref = bf16[3,2,2048]{2,1,0:T(2,128)(2,1)S(1)} collective-permute-done((bf16[3,2,2048]{2,1,0:T(2,128)(2,1)S(1)}, bf16[3,2,2048]{2,1,0:T(2,128)(2,1)S(1)}, u32[]{:S(2)}, u32[]{:S(2)}) %collective-permute-start) | collective-permute-done | bytes 24608 | tf_op jit(solution)/shard_map/ppermute | solution.py:546
  9.4 0.1 head_tokens.1
  9.5 1.2 %collective-permute-start.1 = (bf16[16,2048]{1,0:T(8,128)(2,1)S(1)}, bf16[16,2048]{1,0:T(8,128)(2,1)S(1)}, u32[]{:S(2)}, u32[]{:S(2)}) collective-permute-start(bf16[16,2048]{1,0:T(8,128)(2,1)S(1)} %get-tuple-element.26.refs_1_), channel_id=1, source_target_pairs={{12,0},{8,4},{4,8},{0,12},{28,16},{24,20},{20,24},{16,28},{13,1},{... | collective-permute-start | bytes 196616 | tf_op jit(solution)/shard_map/ppermute | solution.py:617
  10.7 0.4 %collective-permute-start.2 = (bf16[16,2048]{1,0:T(8,128)(2,1)S(1)}, bf16[16,2048]{1,0:T(8,128)(2,1)S(1)}, u32[]{:S(2)}, u32[]{:S(2)}) collective-permute-start(bf16[16,2048]{1,0:T(8,128)(2,1)S(1)} %get-tuple-element.26.refs_1_), channel_id=1, source_target_pairs={{8,0},{12,4},{0,8},{4,12},{24,16},{28,20},{16,24},{20,28},{9,1},{1... | collective-permute-start | bytes 196616 | tf_op jit(solution)/shard_map/ppermute | solution.py:617
  11.2 1.9 %collective-permute-start.3 = (bf16[16,2048]{1,0:T(8,128)(2,1)S(1)}, bf16[16,2048]{1,0:T(8,128)(2,1)S(1)}, u32[]{:S(2)}, u32[]{:S(2)}) collective-permute-start(bf16[16,2048]{1,0:T(8,128)(2,1)S(1)} %get-tuple-element.26.refs_1_), channel_id=1, source_target_pairs={{4,0},{0,4},{12,8},{8,12},{20,16},{16,20},{28,24},{24,28},{5,1},{1... | collective-permute-start | bytes 196616 | tf_op jit(solution)/shard_map/ppermute | solution.py:617
  13.1 2.2 %prepare.1 = (bf16[16,48,256]{2,1,0:T(8,128)(2,1)S(1)}, bf16[16,32,128]{2,1,0:T(8,128)(2,1)S(1)}, bf16[8,256,256]{2,1,0:T(8,128)(2,1)S(1)}, f32[256,2048]{1,0:T(8,128)S(1)}) custom-call(s32[1]{0:T(128)} %bitcast.refs_0_.place_ref, bf16[256,2048]{1,0:T(8,128)(2,1)S(1)} %get-tuple-element.27.query_ref, f32[16,128]{1,0:T(8,128)S(1)} %get-tuple-element.28.residue_ref, ...), custom_call_target="tpu_custom_call" | custom-call | bytes 6000000 | tf_op jit(solution)/shard_map/prepare/pallas_call | solution.py:584
  15.3 0.0 copy-done
  15.3 0.8 %local_conv.2.refs_1_ = f32[256,512]{1,0:T(8,128)S(1)} custom-call(f32[256,2048]{1,0:T(8,128)S(1)} %get-tuple-element.29.refs_0_.refs_3_, bf16[256,2048]{1,0:T(8,128)(2,1)S(1)} %get-tuple-element.30.refs_1_, bf16[256,2048]{1,0:T(8,128)(2,1)S(1)} %get-tuple-element.31.refs_2_, f32[8,2048]{1,0:T(8,128)S(1)} %get-tuple-element.32.refs_3_, ...), custom_call_target="tpu_custom_call" | custom-call | bytes 1800000 | tf_op jit(solution)/shard_map/local_conv/pallas_call | solution.py:600
  16.1 0.0 collective-permute-done.1.refs_4_
  16.1 0.0 collective-permute-done.2.refs_5_
  16.1 0.0 collective-permute-done.3.refs_6_
  16.2 0.2 join.1
  16.3 1.9 %collective-permute-start.4 = (bf16[16,2048]{1,0:T(8,128)(2,1)S(1)}, bf16[16,2048]{1,0:T(8,128)(2,1)S(1)}, u32[]{:S(2)}, u32[]{:S(2)}) collective-permute-start(bf16[16,2048]{1,0:T(8,128)(2,1)S(1)} %get-tuple-element.39), channel_id=1, source_target_pairs={{16,0},{20,4},{24,8},{28,12},{0,16},{4,20},{8,24},{12,28},{17,1},{... | collective-permute-start | bytes 196616 | tf_op jit(solution)/shard_map/ppermute | solution.py:629
  18.2 1.9 %local_conv.3.refs_2_ = f32[256,1536]{1,0:T(8,128)S(1)} custom-call(f32[256,2048]{1,0:T(8,128)S(1)} %get-tuple-element.29.refs_0_.refs_3_, bf16[256,2048]{1,0:T(8,128)(2,1)S(1)} %get-tuple-element.30.refs_1_, bf16[256,2048]{1,0:T(8,128)(2,1)S(1)} %get-tuple-element.31.refs_2_, f32[8,2048]{1,0:T(8,128)S(1)} %get-tuple-element.32.refs_3_, ...), custom_call_target="tpu_custom_call" | custom-call | bytes 5399999 | tf_op jit(solution)/shard_map/local_conv/pallas_call | solution.py:600
  20.1 2.1 %collective-permute-done.4.refs_7_ = bf16[16,2048]{1,0:T(8,128)(2,1)S(1)} collective-permute-done((bf16[16,2048]{1,0:T(8,128)(2,1)S(1)}, bf16[16,2048]{1,0:T(8,128)(2,1)S(1)}, u32[]{:S(2)}, u32[]{:S(2)}) %collective-permute-start.4) | collective-permute-done | bytes 65568 | tf_op jit(solution)/shard_map/ppermute | solution.py:629
  22.2 0.7 %add_carry.1 = (f32[256,2048]{1,0:T(8,128)S(1)}, f32[1,256]{1,0:T(1,128)S(1)}) custom-call(s32[1]{0:T(128)} %bitcast.refs_0_.place_ref, f32[256,512]{1,0:T(8,128)S(1)} %local_conv.2.refs_1_, f32[256,1536]{1,0:T(8,128)S(1)} %local_conv.3.refs_2_, f32[256,2048]{1,0:T(8,128)S(1)} %get-tuple-element.29.refs_0_.refs_3_, ...), custom_call_target="tpu_custom_call" | custom-call | bytes 3000000 | tf_op jit(solution)/shard_map/add_carry/pallas_call | solution.py:634
  22.9 0.0 copy-start.1
  22.9 0.0 collective-permute-start.5
  22.9 1.8 %collective-permute-start.6 = (f32[1,256]{1,0:T(1,128)S(1)}, f32[1,256]{1,0:T(1,128)S(1)}, u32[]{:S(2)}, u32[]{:S(2)}) collective-permute-start(f32[1,256]{1,0:T(1,128)S(1)} %get-tuple-element.41.refs_2_), channel_id=1, source_target_pairs={{2,0},{3,1},{0,2},{1,3},{6,4},{7,5},{4,6},{5,7},{10,8},{11,9},{8,1... | collective-permute-start | bytes 3080 | tf_op jit(solution)/shard_map/ppermute | solution.py:643
  24.7 0.1 collective-permute-start.7
  24.8 1.0 %new_residual.1 = bf16[256,2048]{1,0:T(8,128)(2,1)} custom-call(f32[256,2048]{1,0:T(8,128)S(1)} %get-tuple-element.40.summed_ref.refs_0_), custom_call_target="tpu_custom_call" | custom-call | bytes 3000000 | tf_op jit(solution)/shard_map/new_residual/pallas_call | solution.py:646
  25.9 0.1 collective-permute-done.5.refs_3_
  25.9 0.6 %collective-permute-done.6.refs_4_ = f32[1,256]{1,0:T(1,128)S(1)} collective-permute-done((f32[1,256]{1,0:T(1,128)S(1)}, f32[1,256]{1,0:T(1,128)S(1)}, u32[]{:S(2)}, u32[]{:S(2)}) %collective-permute-start.6) | collective-permute-done | bytes 1056 | tf_op jit(solution)/shard_map/ppermute | solution.py:643
  26.6 0.0 collective-permute-done.7.refs_5_
  26.6 0.0 copy-done.1
  26.6 1.2 %normed.1 = bf16[256,2048]{1,0:T(8,128)(2,1)} custom-call(f32[256,2048]{1,0:T(8,128)S(1)} %get-tuple-element.40.summed_ref.refs_0_, f32[1,2048]{1,0:T(1,128)S(1)} %bitcast.7, f32[1,256]{1,0:T(1,128)S(1)} %get-tuple-element.41.refs_2_, f32[1,256]{1,0:T(1,128)S(1)} %collective-permute-done.5.refs_3_, f32[1,256]{1,0:T(1,128)S(1)} %collective-permute-done.6.refs_4_, ...), custom_call_target="tpu_custom_call" | custom-call | bytes 3000000 | tf_op jit(solution)/shard_map/normed/pallas_call | solution.py:646
  (1 shorter events, 0.0 us)
Async XLA Ops:
  1.6 7.8 %collective-permute-start = (bf16[3,2,2048]{2,1,0:T(2,128)(2,1)S(1)}, bf16[3,2,2048]{2,1,0:T(2,128)(2,1)S(1)}, u32[]{:S(2)}, u32[]{:S(2)}) collective-permute-start(bf16[3,2,2048]{2,1,0:T(2,128)(2,1)S(1)} %slice.3), channel_id=1, source_target_pairs={{0,4},{4,8},{8,12},{12,16},{16,20},{20,24},{24,28},{28,0},{1,5},{5... | collective-permute-start | bytes 73736 | tf_op jit(solution)/shard_map/ppermute | solution.py:546
  4.5 10.8 %copy-start = (f32[2048]{0:T(1024)S(1)}, f32[2048]{0:T(1024)}, u32[]{:S(2)}) copy-start(f32[2048]{0:T(1024)} %param.11) | copy-start | bytes 24580
  9.5 6.6 %collective-permute-start.1 = (bf16[16,2048]{1,0:T(8,128)(2,1)S(1)}, bf16[16,2048]{1,0:T(8,128)(2,1)S(1)}, u32[]{:S(2)}, u32[]{:S(2)}) collective-permute-start(bf16[16,2048]{1,0:T(8,128)(2,1)S(1)} %get-tuple-element.26.refs_1_), channel_id=1, source_target_pairs={{12,0},{8,4},{4,8},{0,12},{28,16},{24,20},{20,24},{16,28},{13,1},{... | collective-permute-start | bytes 196616 | tf_op jit(solution)/shard_map/ppermute | solution.py:617
  10.7 5.4 %collective-permute-start.2 = (bf16[16,2048]{1,0:T(8,128)(2,1)S(1)}, bf16[16,2048]{1,0:T(8,128)(2,1)S(1)}, u32[]{:S(2)}, u32[]{:S(2)}) collective-permute-start(bf16[16,2048]{1,0:T(8,128)(2,1)S(1)} %get-tuple-element.26.refs_1_), channel_id=1, source_target_pairs={{8,0},{12,4},{0,8},{4,12},{24,16},{28,20},{16,24},{20,28},{9,1},{1... | collective-permute-start | bytes 196616 | tf_op jit(solution)/shard_map/ppermute | solution.py:617
  11.2 5.0 %collective-permute-start.3 = (bf16[16,2048]{1,0:T(8,128)(2,1)S(1)}, bf16[16,2048]{1,0:T(8,128)(2,1)S(1)}, u32[]{:S(2)}, u32[]{:S(2)}) collective-permute-start(bf16[16,2048]{1,0:T(8,128)(2,1)S(1)} %get-tuple-element.26.refs_1_), channel_id=1, source_target_pairs={{4,0},{0,4},{12,8},{8,12},{20,16},{16,20},{28,24},{24,28},{5,1},{1... | collective-permute-start | bytes 196616 | tf_op jit(solution)/shard_map/ppermute | solution.py:617
  16.3 5.9 %collective-permute-start.4 = (bf16[16,2048]{1,0:T(8,128)(2,1)S(1)}, bf16[16,2048]{1,0:T(8,128)(2,1)S(1)}, u32[]{:S(2)}, u32[]{:S(2)}) collective-permute-start(bf16[16,2048]{1,0:T(8,128)(2,1)S(1)} %get-tuple-element.39), channel_id=1, source_target_pairs={{16,0},{20,4},{24,8},{28,12},{0,16},{4,20},{8,24},{12,28},{17,1},{... | collective-permute-start | bytes 196616 | tf_op jit(solution)/shard_map/ppermute | solution.py:629
  22.9 3.6 %copy-start.1 = (f32[2048]{0:T(1024)S(1)}, f32[2048]{0:T(1024)}, u32[]{:S(2)}) copy-start(f32[2048]{0:T(1024)} %param.13) | copy-start | bytes 24580
  22.9 3.0 %collective-permute-start.5 = (f32[1,256]{1,0:T(1,128)S(1)}, f32[1,256]{1,0:T(1,128)S(1)}, u32[]{:S(2)}, u32[]{:S(2)}) collective-permute-start(f32[1,256]{1,0:T(1,128)S(1)} %get-tuple-element.41.refs_2_), channel_id=1, source_target_pairs={{3,0},{2,1},{1,2},{0,3},{7,4},{6,5},{5,6},{4,7},{11,8},{10,9},{9,1... | collective-permute-start | bytes 3080 | tf_op jit(solution)/shard_map/ppermute | solution.py:643
  22.9 3.6 %collective-permute-start.6 = (f32[1,256]{1,0:T(1,128)S(1)}, f32[1,256]{1,0:T(1,128)S(1)}, u32[]{:S(2)}, u32[]{:S(2)}) collective-permute-start(f32[1,256]{1,0:T(1,128)S(1)} %get-tuple-element.41.refs_2_), channel_id=1, source_target_pairs={{2,0},{3,1},{0,2},{1,3},{6,4},{7,5},{4,6},{5,7},{10,8},{11,9},{8,1... | collective-permute-start | bytes 3080 | tf_op jit(solution)/shard_map/ppermute | solution.py:643
  24.7 1.8 %collective-permute-start.7 = (f32[1,256]{1,0:T(1,128)S(1)}, f32[1,256]{1,0:T(1,128)S(1)}, u32[]{:S(2)}, u32[]{:S(2)}) collective-permute-start(f32[1,256]{1,0:T(1,128)S(1)} %get-tuple-element.41.refs_2_), channel_id=1, source_target_pairs={{1,0},{0,1},{3,2},{2,3},{5,4},{4,5},{7,6},{6,7},{9,8},{8,9},{11,10... | collective-permute-start | bytes 3080 | tf_op jit(solution)/shard_map/ppermute | solution.py:643

commit v20 on v16

--- a/solution.py
+++ b/solution.py
@@ -137,7 +137,6 @@
     weight_hbm,
     rate_hbm,
     residue_hbm,
-    residual_hbm,
     product_ref,
     state_ref,
     mode_rate_ref,
@@ -145,7 +144,6 @@
     weight_ref,
     query_ref,
     residue_ref,
-    residual_ref,
     buffer_ref,
     ending_ref,
     shift_ref,
@@ -164,7 +162,6 @@
     later = [
         pltpu.make_async_copy(residue_hbm, residue_ref, sems.at[2]),
         pltpu.make_async_copy(projected_ref.at[0], query_ref, sems.at[3]),
-        pltpu.make_async_copy(residual_hbm, residual_ref, sems.at[4]),
     ]
     for copy in copies:
         copy.start()
@@ -239,6 +236,7 @@
 
 def prepare_kernel(
     place_ref,
+    residual_hbm,
     query_ref,
     residue_ref,
     before_ref,
@@ -248,9 +246,13 @@
     entering_ref,
     carry_ref,
     gate_ref,
+    residual_ref,
     shift_ref,
+    sem,
 ):
     rows, width = gate_ref.shape
+    residual_copy = pltpu.make_async_copy(residual_hbm, residual_ref, sem)
+    residual_copy.start()
     shift_ref[...] = shift_matrix(rows)
     residue = per_channel(residue_ref[...], selectors(residue_ref.shape[1]))
     wide = GROUPS * CHUNK
@@ -314,6 +316,7 @@
         gate_ref[0:8, here] = short_conv(head, before[0, :, here], weights)
 
     pipelined(width // WIDE, fetch, convolve)
+    residual_copy.wait()
 
 
 def local_kernel(
@@ -535,9 +538,9 @@
 
     before = lax.ppermute(projected[:, rows - (taps - 1) :, :], "ctx", ring(peers, 1))
 
-    product, state, mode_rate, head, weights, query, residue, residual_here = pl.pallas_call(
+    product, state, mode_rate, head, weights, query, residue = pl.pallas_call(
         state_kernel,
-        in_specs=[hbm_spec] * 5,
+        in_specs=[hbm_spec] * 4,
         out_shape=[
             bf16(rows, width),
             f32(MODES, width),
@@ -546,7 +549,6 @@
             f32(*short_weight.shape),
             bf16(rows, width),
             f32(MODES, residues.shape[0]),
-            bf16(rows, width),
         ],
         scratch_shapes=[
             pltpu.VMEM((2, rows, width), BF16),
@@ -554,13 +556,13 @@
             pltpu.VMEM((2 * rows, rows), BF16),
             pltpu.VMEM(short_weight.shape, BF16),
             pltpu.VMEM((MODES, rates.shape[0]), F32),
-            pltpu.SemaphoreType.DMA((5,)),
+            pltpu.SemaphoreType.DMA((4,)),
             pltpu.SemaphoreType.DMA((2,)),
         ],
         compiler_params=params(),
         cost_estimate=cost(3),
         name="block_state",
-    )(kept(projected), kept(short_weight), kept(rates.T), kept(residues.T), kept(residual))
+    )(kept(projected), kept(short_weight), kept(rates.T), kept(residues.T))
 
     full_state, first = pl.pallas_call(
         lambda *refs: head_kernel(rows, *refs),
@@ -571,20 +573,21 @@
         name="head_tokens",
     )(place, before, head, weights, state, mode_rate)
 
-    inner, entering, carry_table, gate = pl.pallas_call(
+    inner, entering, carry_table, gate, residual_here = pl.pallas_call(
         prepare_kernel,
-        in_specs=[smem_spec] + [vmem_spec] * 5,
+        in_specs=[smem_spec, hbm_spec] + [vmem_spec] * 5,
         out_shape=[
             bf16(tiles, CHUNK + MODES, GROUPS * CHUNK),
             bf16(tiles, CHUNK, LANES),
             bf16(wides, rows, WIDE),
             f32(rows, width),
+            bf16(rows, width),
         ],
-        scratch_shapes=[pltpu.VMEM((2 * rows, rows), BF16)],
+        scratch_shapes=[pltpu.VMEM((2 * rows, rows), BF16), pltpu.SemaphoreType.DMA],
         compiler_params=params(),
         cost_estimate=cost(2),
         name="prepare",
-    )(place, query, residue, before, weights, mode_rate)
+    )(place, kept(residual), query, residue, before, weights, mode_rate)
 
     group, entry, stride = full_state, jnp.zeros((MODES, width), F32), 1
     levels = radices(peers)

time: 26.8 us -> 26.8 us (level)
  no operation moved by 1% of the time
where the time goes in v20:
time: 26.8 us; the launch traced here: 26.4 us
  Pallas kernels  11.2 us (42%)
  starting transfers between devices  11 us (41%)
  waiting for transfers between devices  2.48 us (9%)
  local copies, waits for them, and re-layouts  0.94 us (4%)
  between operations  0.71 us (3%)
    ppermute x4, starting transfers between devices, per_device(): lax.ppermute(group, 'ctx', route)  6.16 us
    pallas_call x1, Pallas kernels, per_device(): pl.pallas_call(state_kernel, in_specs=[hbm_spec] * 4, out_shape=[bf16(row...  3.35 us
    ppermute x1, starting transfers between devices, per_device(): lax.ppermute(projected[:, rows - (taps - 1):, :], 'ctx', ring(peers, 1))  2.99 us
    pallas_call x1, Pallas kernels, per_device(): pl.pallas_call(local_kernel, out_shape=f32(rows, width), compiler_params=...  2.42 us
    pallas_call x1, Pallas kernels, per_device(): pl.pallas_call(prepare_kernel, in_specs=[smem_spec, hbm_spec] + [vmem_spe...  2.24 us
    pallas_call x2, Pallas kernels, write(): pl.pallas_call(kernel, out_specs=hbm_spec, out_shape=bf16(rows, width), s...  2.21 us
    ppermute x3, starting transfers between devices, per_device(): lax.ppermute(squares, 'fsdp', route)  1.87 us
    ppermute x1, waiting for transfers between devices, per_device(): lax.ppermute(projected[:, rows - (taps - 1):, :], 'ctx', ring(peers, 1))  1.47 us
  transfers between devices with their start and end apart: 8, of which 5 were waited for; matrix products, arithmetic and copies ran while one was open for 0% of the time, Pallas kernels for 34%

profile of v20, /device:TPU:0, one launch (start us, length us, event | category | flops | bytes accessed | tf_op | source)
XLA Modules:
  0.0 26.4 jit_solution(11491294054542584488)
XLA Ops:
  0.6 0.9 %slice.3 = bf16[3,2,2048]{2,1,0:T(2,128)(2,1)S(1)} slice(bf16[3,256,2048]{2,1,0:T(8,128)(2,1)} %projected_ref.1), slice={[0:3], [254:256], [0:2048]} | slice | bytes 49152 | tf_op jit(solution)/shard_map/slice | solution.py:539
  1.6 3.0 %collective-permute-start = (bf16[3,2,2048]{2,1,0:T(2,128)(2,1)S(1)}, bf16[3,2,2048]{2,1,0:T(2,128)(2,1)S(1)}, u32[]{:S(2)}, u32[]{:S(2)}) collective-permute-start(bf16[3,2,2048]{2,1,0:T(2,128)(2,1)S(1)} %slice.3), channel_id=1, source_target_pairs={{0,4},{4,8},{8,12},{12,16},{16,20},{20,24},{24,28},{28,0},{1,5},{5... | collective-permute-start | bytes 73736 | tf_op jit(solution)/shard_map/ppermute | solution.py:539
  4.5 3.4 %block_state.1 = (bf16[256,2048]{1,0:T(8,128)(2,1)S(1)}, f32[16,2048]{1,0:T(8,128)S(1)}, f32[16,2048]{1,0:T(8,128)S(1)}, f32[2,8,2048]{2,1,0:T(8,128)S(1)}, f32[...) custom-call(bf16[3,256,2048]{2,1,0:T(8,128)(2,1)} %projected_ref.1, ...), custom_call_target="tpu_custom_call" | custom-call | bytes 9000000 | tf_op jit(solution)/shard_map/block_state/pallas_call | solution.py:541
  7.9 0.0 copy-start
  7.9 1.5 %collective-permute-done.before_ref.refs_1_ = bf16[3,2,2048]{2,1,0:T(2,128)(2,1)S(1)} collective-permute-done((bf16[3,2,2048]{2,1,0:T(2,128)(2,1)S(1)}, bf16[3,2,2048]{2,1,0:T(2,128)(2,1)S(1)}, u32[]{:S(2)}, u32[]{:S(2)}) %collective-permute-start) | collective-permute-done | bytes 24608 | tf_op jit(solution)/shard_map/ppermute | solution.py:539
  9.4 0.1 head_tokens.1
  9.5 1.2 %collective-permute-start.1 = (bf16[16,2048]{1,0:T(8,128)(2,1)S(1)}, bf16[16,2048]{1,0:T(8,128)(2,1)S(1)}, u32[]{:S(2)}, u32[]{:S(2)}) collective-permute-start(bf16[16,2048]{1,0:T(8,128)(2,1)S(1)} %get-tuple-element.32.refs_1_), channel_id=1, source_target_pairs={{12,0},{8,4},{4,8},{0,12},{28,16},{24,20},{20,24},{16,28},{13,1},{... | collective-permute-start | bytes 196616 | tf_op jit(solution)/shard_map/ppermute | solution.py:598
  10.7 0.4 %collective-permute-start.2 = (bf16[16,2048]{1,0:T(8,128)(2,1)S(1)}, bf16[16,2048]{1,0:T(8,128)(2,1)S(1)}, u32[]{:S(2)}, u32[]{:S(2)}) collective-permute-start(bf16[16,2048]{1,0:T(8,128)(2,1)S(1)} %get-tuple-element.32.refs_1_), channel_id=1, source_target_pairs={{8,0},{12,4},{0,8},{4,12},{24,16},{28,20},{16,24},{20,28},{9,1},{1... | collective-permute-start | bytes 196616 | tf_op jit(solution)/shard_map/ppermute | solution.py:598
  11.1 1.9 %collective-permute-start.3 = (bf16[16,2048]{1,0:T(8,128)(2,1)S(1)}, bf16[16,2048]{1,0:T(8,128)(2,1)S(1)}, u32[]{:S(2)}, u32[]{:S(2)}) collective-permute-start(bf16[16,2048]{1,0:T(8,128)(2,1)S(1)} %get-tuple-element.32.refs_1_), channel_id=1, source_target_pairs={{4,0},{0,4},{12,8},{8,12},{20,16},{16,20},{28,24},{24,28},{5,1},{1... | collective-permute-start | bytes 196616 | tf_op jit(solution)/shard_map/ppermute | solution.py:598
  13.1 2.2 %prepare.1 = (bf16[16,48,256]{2,1,0:T(8,128)(2,1)S(1)}, bf16[16,32,128]{2,1,0:T(8,128)(2,1)S(1)}, bf16[8,256,256]{2,1,0:T(8,128)(2,1)S(1)}, f32[256,2048]{1,0:T(8,128)S(1)}, bf16[256,2048]{1,0:T(8,128)(2,1)S(1)}) custom-call(s32[1]{0:T(128)} %bitcast.place_ref.refs_0_, bf16[256,2048]{1,0:T(8,128)(2,1)} %residual_hbm.1, ...), custom_call_target="tpu_custom_call" | custom-call | bytes 6000000 | tf_op jit(solution)/shard_map/prepare/pallas_call | solution.py:576
  15.3 0.0 collective-permute-done.1.refs_4_
  15.3 0.0 collective-permute-done.2.refs_5_
  15.4 0.1 collective-permute-done.3.refs_6_
  15.5 0.2 join.1
  15.6 2.6 %collective-permute-start.4 = (bf16[16,2048]{1,0:T(8,128)(2,1)S(1)}, bf16[16,2048]{1,0:T(8,128)(2,1)S(1)}, u32[]{:S(2)}, u32[]{:S(2)}) collective-permute-start(bf16[16,2048]{1,0:T(8,128)(2,1)S(1)} %get-tuple-element.39), channel_id=1, source_target_pairs={{16,0},{20,4},{24,8},{28,12},{0,16},{4,20},{8,24},{12,28},{17,1},{... | collective-permute-start | bytes 196616 | tf_op jit(solution)/shard_map/ppermute | solution.py:610
  18.2 0.0 copy-done
  18.2 2.4 %local_conv.1.refs_1_ = f32[256,2048]{1,0:T(8,128)S(1)} custom-call(f32[256,2048]{1,0:T(8,128)S(1)} %get-tuple-element.26.gate_ref.refs_2_, bf16[256,2048]{1,0:T(8,128)(2,1)S(1)} %get-tuple-element.27.residual_ref, bf16[256,2048]{1,0:T(8,128)(2,1)S(1)} %get-tuple-element.28.product_ref, f32[8,2048]{1,0:T(8,128)S(1)} %get-tuple-element.31.first_ref, ...), custom_call_target="tpu_custom_call" | custom-call | bytes 15000000 | tf_op jit(solution)/shard_map/local_conv/pallas_call | solution.py:612
  20.7 0.2 collective-permute-done.4.refs_6_
  20.9 0.7 %add_carry.1 = (f32[256,2048]{1,0:T(8,128)S(1)}, f32[1,256]{1,0:T(1,128)S(1)}) custom-call(s32[1]{0:T(128)} %bitcast.place_ref.refs_0_, f32[256,2048]{1,0:T(8,128)S(1)} %local_conv.1.refs_1_, f32[256,2048]{1,0:T(8,128)S(1)} %get-tuple-element.26.gate_ref.refs_2_, bf16[8,256,256]{2,1,0:T(8,128)(2,1)S(1)} %get-tuple-element.36.refs_3_, ...), custom_call_target="tpu_custom_call" | custom-call | bytes 3000000 | tf_op jit(solution)/shard_map/add_carry/pallas_call | solution.py:621
  21.6 0.0 copy-start.1
  21.6 0.0 collective-permute-start.5
  21.6 1.8 %collective-permute-start.6 = (f32[1,256]{1,0:T(1,128)S(1)}, f32[1,256]{1,0:T(1,128)S(1)}, u32[]{:S(2)}, u32[]{:S(2)}) collective-permute-start(f32[1,256]{1,0:T(1,128)S(1)} %get-tuple-element.41.refs_2_), channel_id=1, source_target_pairs={{2,0},{3,1},{0,2},{1,3},{6,4},{7,5},{4,6},{5,7},{10,8},{11,9},{8,1... | collective-permute-start | bytes 3080 | tf_op jit(solution)/shard_map/ppermute | solution.py:630
  23.4 0.1 collective-permute-start.7
  23.5 1.0 %new_residual.1 = bf16[256,2048]{1,0:T(8,128)(2,1)} custom-call(f32[256,2048]{1,0:T(8,128)S(1)} %get-tuple-element.40.summed_ref.refs_0_), custom_call_target="tpu_custom_call" | custom-call | bytes 3000000 | tf_op jit(solution)/shard_map/new_residual/pallas_call | solution.py:633
  24.5 0.1 collective-permute-done.5.refs_3_
  24.6 0.6 %collective-permute-done.6.refs_4_ = f32[1,256]{1,0:T(1,128)S(1)} collective-permute-done((f32[1,256]{1,0:T(1,128)S(1)}, f32[1,256]{1,0:T(1,128)S(1)}, u32[]{:S(2)}, u32[]{:S(2)}) %collective-permute-start.6) | collective-permute-done | bytes 1056 | tf_op jit(solution)/shard_map/ppermute | solution.py:630
  25.2 0.0 collective-permute-done.7.refs_5_
  25.2 0.0 copy-done.1
  25.2 1.2 %normed.1 = bf16[256,2048]{1,0:T(8,128)(2,1)} custom-call(f32[256,2048]{1,0:T(8,128)S(1)} %get-tuple-element.40.summed_ref.refs_0_, f32[1,2048]{1,0:T(1,128)S(1)} %bitcast.6, f32[1,256]{1,0:T(1,128)S(1)} %get-tuple-element.41.refs_2_, f32[1,256]{1,0:T(1,128)S(1)} %collective-permute-done.5.refs_3_, f32[1,256]{1,0:T(1,128)S(1)} %collective-permute-done.6.refs_4_, ...), custom_call_target="tpu_custom_call" | custom-call | bytes 3000000 | tf_op jit(solution)/shard_map/normed/pallas_call | solution.py:633
  (1 shorter events, 0.0 us)
Async XLA Ops:
  1.6 7.8 %collective-permute-start = (bf16[3,2,2048]{2,1,0:T(2,128)(2,1)S(1)}, bf16[3,2,2048]{2,1,0:T(2,128)(2,1)S(1)}, u32[]{:S(2)}, u32[]{:S(2)}) collective-permute-start(bf16[3,2,2048]{2,1,0:T(2,128)(2,1)S(1)} %slice.3), channel_id=1, source_target_pairs={{0,4},{4,8},{8,12},{12,16},{16,20},{20,24},{24,28},{28,0},{1,5},{5... | collective-permute-start | bytes 73736 | tf_op jit(solution)/shard_map/ppermute | solution.py:539
  7.9 10.3 %copy-start = (f32[2048]{0:T(1024)S(1)}, f32[2048]{0:T(1024)}, u32[]{:S(2)}) copy-start(f32[2048]{0:T(1024)} %param.11) | copy-start | bytes 24580
  9.5 5.8 %collective-permute-start.1 = (bf16[16,2048]{1,0:T(8,128)(2,1)S(1)}, bf16[16,2048]{1,0:T(8,128)(2,1)S(1)}, u32[]{:S(2)}, u32[]{:S(2)}) collective-permute-start(bf16[16,2048]{1,0:T(8,128)(2,1)S(1)} %get-tuple-element.32.refs_1_), channel_id=1, source_target_pairs={{12,0},{8,4},{4,8},{0,12},{28,16},{24,20},{20,24},{16,28},{13,1},{... | collective-permute-start | bytes 196616 | tf_op jit(solution)/shard_map/ppermute | solution.py:598
  10.7 4.6 %collective-permute-start.2 = (bf16[16,2048]{1,0:T(8,128)(2,1)S(1)}, bf16[16,2048]{1,0:T(8,128)(2,1)S(1)}, u32[]{:S(2)}, u32[]{:S(2)}) collective-permute-start(bf16[16,2048]{1,0:T(8,128)(2,1)S(1)} %get-tuple-element.32.refs_1_), channel_id=1, source_target_pairs={{8,0},{12,4},{0,8},{4,12},{24,16},{28,20},{16,24},{20,28},{9,1},{1... | collective-permute-start | bytes 196616 | tf_op jit(solution)/shard_map/ppermute | solution.py:598
  11.1 4.3 %collective-permute-start.3 = (bf16[16,2048]{1,0:T(8,128)(2,1)S(1)}, bf16[16,2048]{1,0:T(8,128)(2,1)S(1)}, u32[]{:S(2)}, u32[]{:S(2)}) collective-permute-start(bf16[16,2048]{1,0:T(8,128)(2,1)S(1)} %get-tuple-element.32.refs_1_), channel_id=1, source_target_pairs={{4,0},{0,4},{12,8},{8,12},{20,16},{16,20},{28,24},{24,28},{5,1},{1... | collective-permute-start | bytes 196616 | tf_op jit(solution)/shard_map/ppermute | solution.py:598
  15.6 5.2 %collective-permute-start.4 = (bf16[16,2048]{1,0:T(8,128)(2,1)S(1)}, bf16[16,2048]{1,0:T(8,128)(2,1)S(1)}, u32[]{:S(2)}, u32[]{:S(2)}) collective-permute-start(bf16[16,2048]{1,0:T(8,128)(2,1)S(1)} %get-tuple-element.39), channel_id=1, source_target_pairs={{16,0},{20,4},{24,8},{28,12},{0,16},{4,20},{8,24},{12,28},{17,1},{... | collective-permute-start | bytes 196616 | tf_op jit(solution)/shard_map/ppermute | solution.py:610
  21.6 3.6 %copy-start.1 = (f32[2048]{0:T(1024)S(1)}, f32[2048]{0:T(1024)}, u32[]{:S(2)}) copy-start(f32[2048]{0:T(1024)} %param.13) | copy-start | bytes 24580
  21.6 3.0 %collective-permute-start.5 = (f32[1,256]{1,0:T(1,128)S(1)}, f32[1,256]{1,0:T(1,128)S(1)}, u32[]{:S(2)}, u32[]{:S(2)}) collective-permute-start(f32[1,256]{1,0:T(1,128)S(1)} %get-tuple-element.41.refs_2_), channel_id=1, source_target_pairs={{3,0},{2,1},{1,2},{0,3},{7,4},{6,5},{5,6},{4,7},{11,8},{10,9},{9,1... | collective-permute-start | bytes 3080 | tf_op jit(solution)/shard_map/ppermute | solution.py:630
  21.6 3.6 %collective-permute-start.6 = (f32[1,256]{1,0:T(1,128)S(1)}, f32[1,256]{1,0:T(1,128)S(1)}, u32[]{:S(2)}, u32[]{:S(2)}) collective-permute-start(f32[1,256]{1,0:T(1,128)S(1)} %get-tuple-element.41.refs_2_), channel_id=1, source_target_pairs={{2,0},{3,1},{0,2},{1,3},{6,4},{7,5},{4,6},{5,7},{10,8},{11,9},{8,1... | collective-permute-start | bytes 3080 | tf_op jit(solution)/shard_map/ppermute | solution.py:630
  23.4 1.8 %collective-permute-start.7 = (f32[1,256]{1,0:T(1,128)S(1)}, f32[1,256]{1,0:T(1,128)S(1)}, u32[]{:S(2)}, u32[]{:S(2)}) collective-permute-start(f32[1,256]{1,0:T(1,128)S(1)} %get-tuple-element.41.refs_2_), channel_id=1, source_target_pairs={{1,0},{0,1},{3,2},{2,3},{5,4},{4,5},{7,6},{6,7},{9,8},{8,9},{11,10... | collective-permute-start | bytes 3080 | tf_op jit(solution)/shard_map/ppermute | solution.py:630

commit v21 on v20

--- a/solution.py
+++ b/solution.py
@@ -157,14 +157,14 @@
     rate_copy = pltpu.make_async_copy(rate_hbm, rate_ref, small_sems.at[0])
     rate_copy.start()
     weight_copy = pltpu.make_async_copy(weight_hbm, short_ref, small_sems.at[1])
-    weight_copy.start()
-    copies = [pltpu.make_async_copy(projected_ref.at[1 + c], buffer_ref.at[c], sems.at[c]) for c in (0, 1)]
+    copies = [pltpu.make_async_copy(projected_ref.at[pl.ds(1, 2)], buffer_ref, sems.at[0])]
     later = [
         pltpu.make_async_copy(residue_hbm, residue_ref, sems.at[2]),
         pltpu.make_async_copy(projected_ref.at[0], query_ref, sems.at[3]),
     ]
     for copy in copies:
         copy.start()
+    weight_copy.start()
     shift_ref[...] = shift_matrix(rows)
     chosen = selectors(rate_ref.shape[1])
     eye = own_mode(BF16)

time: 26.8 us -> 26.8 us (level)
  no operation moved by 1% of the time
where the time goes in v21:
time: 26.8 us; the launch traced here: 26.4 us
  Pallas kernels  11.3 us (42%)
  starting transfers between devices  11.1 us (41%)
  waiting for transfers between devices  2.41 us (9%)
  local copies, waits for them, and re-layouts  0.94 us (4%)
  between operations  0.71 us (3%)
    ppermute x4, starting transfers between devices, per_device(): lax.ppermute(group, 'ctx', route)  6.2 us
    pallas_call x1, Pallas kernels, per_device(): pl.pallas_call(state_kernel, in_specs=[hbm_spec] * 4, out_shape=[bf16(row...  3.39 us
    ppermute x1, starting transfers between devices, per_device(): lax.ppermute(projected[:, rows - (taps - 1):, :], 'ctx', ring(peers, 1))  2.99 us
    pallas_call x1, Pallas kernels, per_device(): pl.pallas_call(local_kernel, out_shape=f32(rows, width), compiler_params=...  2.42 us
    pallas_call x1, Pallas kernels, per_device(): pl.pallas_call(prepare_kernel, in_specs=[smem_spec, hbm_spec] + [vmem_spe...  2.24 us
    pallas_call x2, Pallas kernels, write(): pl.pallas_call(kernel, out_specs=hbm_spec, out_shape=bf16(rows, width), s...  2.21 us
    ppermute x3, starting transfers between devices, per_device(): lax.ppermute(squares, 'fsdp', route)  1.87 us
    ppermute x1, waiting for transfers between devices, per_device(): lax.ppermute(projected[:, rows - (taps - 1):, :], 'ctx', ring(peers, 1))  1.44 us
  transfers between devices with their start and end apart: 8, of which 5 were waited for; matrix products, arithmetic and copies ran while one was open for 0% of the time, Pallas kernels for 34%

profile of v21, /device:TPU:0, one launch (start us, length us, event | category | flops | bytes accessed | tf_op | source)
XLA Modules:
  0.0 26.4 jit_solution(16385546422060714312)
XLA Ops:
  0.6 0.9 %slice.3 = bf16[3,2,2048]{2,1,0:T(2,128)(2,1)S(1)} slice(bf16[3,256,2048]{2,1,0:T(8,128)(2,1)} %projected_ref.1), slice={[0:3], [254:256], [0:2048]} | slice | bytes 49152 | tf_op jit(solution)/shard_map/slice | solution.py:539
  1.6 3.0 %collective-permute-start = (bf16[3,2,2048]{2,1,0:T(2,128)(2,1)S(1)}, bf16[3,2,2048]{2,1,0:T(2,128)(2,1)S(1)}, u32[]{:S(2)}, u32[]{:S(2)}) collective-permute-start(bf16[3,2,2048]{2,1,0:T(2,128)(2,1)S(1)} %slice.3), channel_id=1, source_target_pairs={{0,4},{4,8},{8,12},{12,16},{16,20},{20,24},{24,28},{28,0},{1,5},{5... | collective-permute-start | bytes 73736 | tf_op jit(solution)/shard_map/ppermute | solution.py:539
  4.5 3.4 %block_state.1 = (bf16[256,2048]{1,0:T(8,128)(2,1)S(1)}, f32[16,2048]{1,0:T(8,128)S(1)}, f32[16,2048]{1,0:T(8,128)S(1)}, f32[2,8,2048]{2,1,0:T(8,128)S(1)}, f32[...) custom-call(bf16[3,256,2048]{2,1,0:T(8,128)(2,1)} %projected_ref.1, ...), custom_call_target="tpu_custom_call" | custom-call | bytes 9000000 | tf_op jit(solution)/shard_map/block_state/pallas_call | solution.py:541
  7.9 0.0 copy-start
  8.0 1.4 %collective-permute-done.before_ref.refs_1_ = bf16[3,2,2048]{2,1,0:T(2,128)(2,1)S(1)} collective-permute-done((bf16[3,2,2048]{2,1,0:T(2,128)(2,1)S(1)}, bf16[3,2,2048]{2,1,0:T(2,128)(2,1)S(1)}, u32[]{:S(2)}, u32[]{:S(2)}) %collective-permute-start) | collective-permute-done | bytes 24608 | tf_op jit(solution)/shard_map/ppermute | solution.py:539
  9.4 0.1 head_tokens.1
  9.5 1.2 %collective-permute-start.1 = (bf16[16,2048]{1,0:T(8,128)(2,1)S(1)}, bf16[16,2048]{1,0:T(8,128)(2,1)S(1)}, u32[]{:S(2)}, u32[]{:S(2)}) collective-permute-start(bf16[16,2048]{1,0:T(8,128)(2,1)S(1)} %get-tuple-element.32.refs_1_), channel_id=1, source_target_pairs={{12,0},{8,4},{4,8},{0,12},{28,16},{24,20},{20,24},{16,28},{13,1},{... | collective-permute-start | bytes 196616 | tf_op jit(solution)/shard_map/ppermute | solution.py:598
  10.7 0.4 %collective-permute-start.2 = (bf16[16,2048]{1,0:T(8,128)(2,1)S(1)}, bf16[16,2048]{1,0:T(8,128)(2,1)S(1)}, u32[]{:S(2)}, u32[]{:S(2)}) collective-permute-start(bf16[16,2048]{1,0:T(8,128)(2,1)S(1)} %get-tuple-element.32.refs_1_), channel_id=1, source_target_pairs={{8,0},{12,4},{0,8},{4,12},{24,16},{28,20},{16,24},{20,28},{9,1},{1... | collective-permute-start | bytes 196616 | tf_op jit(solution)/shard_map/ppermute | solution.py:598
  11.2 1.9 %collective-permute-start.3 = (bf16[16,2048]{1,0:T(8,128)(2,1)S(1)}, bf16[16,2048]{1,0:T(8,128)(2,1)S(1)}, u32[]{:S(2)}, u32[]{:S(2)}) collective-permute-start(bf16[16,2048]{1,0:T(8,128)(2,1)S(1)} %get-tuple-element.32.refs_1_), channel_id=1, source_target_pairs={{4,0},{0,4},{12,8},{8,12},{20,16},{16,20},{28,24},{24,28},{5,1},{1... | collective-permute-start | bytes 196616 | tf_op jit(solution)/shard_map/ppermute | solution.py:598
  13.1 2.2 %prepare.1 = (bf16[16,48,256]{2,1,0:T(8,128)(2,1)S(1)}, bf16[16,32,128]{2,1,0:T(8,128)(2,1)S(1)}, bf16[8,256,256]{2,1,0:T(8,128)(2,1)S(1)}, f32[256,2048]{1,0:T(8,128)S(1)}, bf16[256,2048]{1,0:T(8,128)(2,1)S(1)}) custom-call(s32[1]{0:T(128)} %bitcast.place_ref.refs_0_, bf16[256,2048]{1,0:T(8,128)(2,1)} %residual_hbm.1, ...), custom_call_target="tpu_custom_call" | custom-call | bytes 6000000 | tf_op jit(solution)/shard_map/prepare/pallas_call | solution.py:576
  15.3 0.0 collective-permute-done.1.refs_4_
  15.3 0.0 collective-permute-done.2.refs_5_
  15.4 0.1 collective-permute-done.3.refs_6_
  15.5 0.2 join.1
  15.6 2.6 %collective-permute-start.4 = (bf16[16,2048]{1,0:T(8,128)(2,1)S(1)}, bf16[16,2048]{1,0:T(8,128)(2,1)S(1)}, u32[]{:S(2)}, u32[]{:S(2)}) collective-permute-start(bf16[16,2048]{1,0:T(8,128)(2,1)S(1)} %get-tuple-element.39), channel_id=1, source_target_pairs={{16,0},{20,4},{24,8},{28,12},{0,16},{4,20},{8,24},{12,28},{17,1},{... | collective-permute-start | bytes 196616 | tf_op jit(solution)/shard_map/ppermute | solution.py:610
  18.3 0.0 copy-done
  18.3 2.4 %local_conv.1.refs_1_ = f32[256,2048]{1,0:T(8,128)S(1)} custom-call(f32[256,2048]{1,0:T(8,128)S(1)} %get-tuple-element.26.gate_ref.refs_2_, bf16[256,2048]{1,0:T(8,128)(2,1)S(1)} %get-tuple-element.27.residual_ref, bf16[256,2048]{1,0:T(8,128)(2,1)S(1)} %get-tuple-element.28.product_ref, f32[8,2048]{1,0:T(8,128)S(1)} %get-tuple-element.31.first_ref, ...), custom_call_target="tpu_custom_call" | custom-call | bytes 15000000 | tf_op jit(solution)/shard_map/local_conv/pallas_call | solution.py:612
  20.7 0.2 collective-permute-done.4.refs_6_
  20.9 0.7 %add_carry.1 = (f32[256,2048]{1,0:T(8,128)S(1)}, f32[1,256]{1,0:T(1,128)S(1)}) custom-call(s32[1]{0:T(128)} %bitcast.place_ref.refs_0_, f32[256,2048]{1,0:T(8,128)S(1)} %local_conv.1.refs_1_, f32[256,2048]{1,0:T(8,128)S(1)} %get-tuple-element.26.gate_ref.refs_2_, bf16[8,256,256]{2,1,0:T(8,128)(2,1)S(1)} %get-tuple-element.36.refs_3_, ...), custom_call_target="tpu_custom_call" | custom-call | bytes 3000000 | tf_op jit(solution)/shard_map/add_carry/pallas_call | solution.py:621
  21.6 0.0 copy-start.1
  21.6 0.0 collective-permute-start.5
  21.6 1.8 %collective-permute-start.6 = (f32[1,256]{1,0:T(1,128)S(1)}, f32[1,256]{1,0:T(1,128)S(1)}, u32[]{:S(2)}, u32[]{:S(2)}) collective-permute-start(f32[1,256]{1,0:T(1,128)S(1)} %get-tuple-element.41.refs_2_), channel_id=1, source_target_pairs={{2,0},{3,1},{0,2},{1,3},{6,4},{7,5},{4,6},{5,7},{10,8},{11,9},{8,1... | collective-permute-start | bytes 3080 | tf_op jit(solution)/shard_map/ppermute | solution.py:630
  23.4 0.1 collective-permute-start.7
  23.5 1.0 %new_residual.1 = bf16[256,2048]{1,0:T(8,128)(2,1)} custom-call(f32[256,2048]{1,0:T(8,128)S(1)} %get-tuple-element.40.summed_ref.refs_0_), custom_call_target="tpu_custom_call" | custom-call | bytes 3000000 | tf_op jit(solution)/shard_map/new_residual/pallas_call | solution.py:633
  24.5 0.1 collective-permute-done.5.refs_3_
  24.6 0.6 %collective-permute-done.6.refs_4_ = f32[1,256]{1,0:T(1,128)S(1)} collective-permute-done((f32[1,256]{1,0:T(1,128)S(1)}, f32[1,256]{1,0:T(1,128)S(1)}, u32[]{:S(2)}, u32[]{:S(2)}) %collective-permute-start.6) | collective-permute-done | bytes 1056 | tf_op jit(solution)/shard_map/ppermute | solution.py:630
  25.2 0.0 collective-permute-done.7.refs_5_
  25.2 0.0 copy-done.1
  25.2 1.2 %normed.1 = bf16[256,2048]{1,0:T(8,128)(2,1)} custom-call(f32[256,2048]{1,0:T(8,128)S(1)} %get-tuple-element.40.summed_ref.refs_0_, f32[1,2048]{1,0:T(1,128)S(1)} %bitcast.6, f32[1,256]{1,0:T(1,128)S(1)} %get-tuple-element.41.refs_2_, f32[1,256]{1,0:T(1,128)S(1)} %collective-permute-done.5.refs_3_, f32[1,256]{1,0:T(1,128)S(1)} %collective-permute-done.6.refs_4_, ...), custom_call_target="tpu_custom_call" | custom-call | bytes 3000000 | tf_op jit(solution)/shard_map/normed/pallas_call | solution.py:633
  (1 shorter events, 0.0 us)
Async XLA Ops:
  1.6 7.8 %collective-permute-start = (bf16[3,2,2048]{2,1,0:T(2,128)(2,1)S(1)}, bf16[3,2,2048]{2,1,0:T(2,128)(2,1)S(1)}, u32[]{:S(2)}, u32[]{:S(2)}) collective-permute-start(bf16[3,2,2048]{2,1,0:T(2,128)(2,1)S(1)} %slice.3), channel_id=1, source_target_pairs={{0,4},{4,8},{8,12},{12,16},{16,20},{20,24},{24,28},{28,0},{1,5},{5... | collective-permute-start | bytes 73736 | tf_op jit(solution)/shard_map/ppermute | solution.py:539
  7.9 10.3 %copy-start = (f32[2048]{0:T(1024)S(1)}, f32[2048]{0:T(1024)}, u32[]{:S(2)}) copy-start(f32[2048]{0:T(1024)} %param.11) | copy-start | bytes 24580
  9.5 5.8 %collective-permute-start.1 = (bf16[16,2048]{1,0:T(8,128)(2,1)S(1)}, bf16[16,2048]{1,0:T(8,128)(2,1)S(1)}, u32[]{:S(2)}, u32[]{:S(2)}) collective-permute-start(bf16[16,2048]{1,0:T(8,128)(2,1)S(1)} %get-tuple-element.32.refs_1_), channel_id=1, source_target_pairs={{12,0},{8,4},{4,8},{0,12},{28,16},{24,20},{20,24},{16,28},{13,1},{... | collective-permute-start | bytes 196616 | tf_op jit(solution)/shard_map/ppermute | solution.py:598
  10.7 4.6 %collective-permute-start.2 = (bf16[16,2048]{1,0:T(8,128)(2,1)S(1)}, bf16[16,2048]{1,0:T(8,128)(2,1)S(1)}, u32[]{:S(2)}, u32[]{:S(2)}) collective-permute-start(bf16[16,2048]{1,0:T(8,128)(2,1)S(1)} %get-tuple-element.32.refs_1_), channel_id=1, source_target_pairs={{8,0},{12,4},{0,8},{4,12},{24,16},{28,20},{16,24},{20,28},{9,1},{1... | collective-permute-start | bytes 196616 | tf_op jit(solution)/shard_map/ppermute | solution.py:598
  11.2 4.3 %collective-permute-start.3 = (bf16[16,2048]{1,0:T(8,128)(2,1)S(1)}, bf16[16,2048]{1,0:T(8,128)(2,1)S(1)}, u32[]{:S(2)}, u32[]{:S(2)}) collective-permute-start(bf16[16,2048]{1,0:T(8,128)(2,1)S(1)} %get-tuple-element.32.refs_1_), channel_id=1, source_target_pairs={{4,0},{0,4},{12,8},{8,12},{20,16},{16,20},{28,24},{24,28},{5,1},{1... | collective-permute-start | bytes 196616 | tf_op jit(solution)/shard_map/ppermute | solution.py:598
  15.6 5.2 %collective-permute-start.4 = (bf16[16,2048]{1,0:T(8,128)(2,1)S(1)}, bf16[16,2048]{1,0:T(8,128)(2,1)S(1)}, u32[]{:S(2)}, u32[]{:S(2)}) collective-permute-start(bf16[16,2048]{1,0:T(8,128)(2,1)S(1)} %get-tuple-element.39), channel_id=1, source_target_pairs={{16,0},{20,4},{24,8},{28,12},{0,16},{4,20},{8,24},{12,28},{17,1},{... | collective-permute-start | bytes 196616 | tf_op jit(solution)/shard_map/ppermute | solution.py:610
  21.6 3.6 %copy-start.1 = (f32[2048]{0:T(1024)S(1)}, f32[2048]{0:T(1024)}, u32[]{:S(2)}) copy-start(f32[2048]{0:T(1024)} %param.13) | copy-start | bytes 24580
  21.6 3.0 %collective-permute-start.5 = (f32[1,256]{1,0:T(1,128)S(1)}, f32[1,256]{1,0:T(1,128)S(1)}, u32[]{:S(2)}, u32[]{:S(2)}) collective-permute-start(f32[1,256]{1,0:T(1,128)S(1)} %get-tuple-element.41.refs_2_), channel_id=1, source_target_pairs={{3,0},{2,1},{1,2},{0,3},{7,4},{6,5},{5,6},{4,7},{11,8},{10,9},{9,1... | collective-permute-start | bytes 3080 | tf_op jit(solution)/shard_map/ppermute | solution.py:630
  21.6 3.6 %collective-permute-start.6 = (f32[1,256]{1,0:T(1,128)S(1)}, f32[1,256]{1,0:T(1,128)S(1)}, u32[]{:S(2)}, u32[]{:S(2)}) collective-permute-start(f32[1,256]{1,0:T(1,128)S(1)} %get-tuple-element.41.refs_2_), channel_id=1, source_target_pairs={{2,0},{3,1},{0,2},{1,3},{6,4},{7,5},{4,6},{5,7},{10,8},{11,9},{8,1... | collective-permute-start | bytes 3080 | tf_op jit(solution)/shard_map/ppermute | solution.py:630
  23.4 1.8 %collective-permute-start.7 = (f32[1,256]{1,0:T(1,128)S(1)}, f32[1,256]{1,0:T(1,128)S(1)}, u32[]{:S(2)}, u32[]{:S(2)}) collective-permute-start(f32[1,256]{1,0:T(1,128)S(1)} %get-tuple-element.41.refs_2_), channel_id=1, source_target_pairs={{1,0},{0,1},{3,2},{2,3},{5,4},{4,5},{7,6},{6,7},{9,8},{8,9},{11,10... | collective-permute-start | bytes 3080 | tf_op jit(solution)/shard_map/ppermute | solution.py:630

commit v22 on v21

--- a/solution.py
+++ b/solution.py
@@ -144,9 +144,9 @@
     weight_ref,
     query_ref,
     residue_ref,
+    shift_ref,
     buffer_ref,
     ending_ref,
-    shift_ref,
     short_ref,
     rate_ref,
     sems,
@@ -242,18 +242,17 @@
     before_ref,
     weight_ref,
     mode_rate_ref,
+    shift_ref,
     inner_ref,
     entering_ref,
     carry_ref,
     gate_ref,
     residual_ref,
-    shift_ref,
     sem,
 ):
     rows, width = gate_ref.shape
     residual_copy = pltpu.make_async_copy(residual_hbm, residual_ref, sem)
     residual_copy.start()
-    shift_ref[...] = shift_matrix(rows)
     residue = per_channel(residue_ref[...], selectors(residue_ref.shape[1]))
     wide = GROUPS * CHUNK
     step = index_of((CHUNK, LANES), 0).astype(F32)
@@ -442,22 +441,24 @@
     squares_ref[...] = squares[0:1]
 
 
-def write_kernel(summed_ref, out_hbm, rounded_ref, sems):
+def write_kernel(summed_ref, gain_ref, out_hbm, gained_ref, rounded_ref, sems):
     width = summed_ref.shape[1]
     copies = []
     for tile in range(width // WIDE):
         here = lanes_of(tile, WIDE)
-        rounded_ref[:, here] = summed_ref[:, here].astype(BF16)
+        summed = summed_ref[:, here]
+        rounded_ref[:, here] = summed.astype(BF16)
         span = pl.ds(tile * WIDE, WIDE)
         copies.append(pltpu.make_async_copy(rounded_ref.at[:, span], out_hbm.at[:, span], sems.at[tile]))
         copies[-1].start()
+        gained_ref[:, here] = summed * gain_ref[:, here]
     for copy in copies:
         copy.wait()
 
 
-def norm_kernel(full_width, summed_ref, gain_ref, *refs):
+def norm_kernel(full_width, gained_ref, *refs):
     squares_refs, (out_hbm, rounded_ref, sems) = refs[:-3], refs[-3:]
-    rows, width = summed_ref.shape
+    rows, width = gained_ref.shape
     squares = squares_refs[0][...]
     for ref in squares_refs[1:]:
         squares = squares + ref[...]
@@ -469,7 +470,7 @@
         span = slice(start, start + block)
         for tile in range(width // LANES):
             here = lanes_of(tile)
-            rounded_ref[span, here] = (summed_ref[span, here] * scale[span] * gain_ref[:, here]).astype(BF16)
+            rounded_ref[span, here] = (gained_ref[span, here] * scale[span]).astype(BF16)
         there = pl.ds(start, block)
         copies.append(pltpu.make_async_copy(rounded_ref.at[there, :], out_hbm.at[there, :], sems.at[start // block]))
         copies[-1].start()
@@ -538,7 +539,7 @@
 
     before = lax.ppermute(projected[:, rows - (taps - 1) :, :], "ctx", ring(peers, 1))
 
-    product, state, mode_rate, head, weights, query, residue = pl.pallas_call(
+    product, state, mode_rate, head, weights, query, residue, shift = pl.pallas_call(
         state_kernel,
         in_specs=[hbm_spec] * 4,
         out_shape=[
@@ -549,11 +550,11 @@
             f32(*short_weight.shape),
             bf16(rows, width),
             f32(MODES, residues.shape[0]),
+            bf16(2 * rows, rows),
         ],
         scratch_shapes=[
             pltpu.VMEM((2, rows, width), BF16),
             pltpu.VMEM((wides, WIDE, rows), BF16),
-            pltpu.VMEM((2 * rows, rows), BF16),
             pltpu.VMEM(short_weight.shape, BF16),
             pltpu.VMEM((MODES, rates.shape[0]), F32),
             pltpu.SemaphoreType.DMA((4,)),
@@ -575,7 +576,7 @@
 
     inner, entering, carry_table, gate, residual_here = pl.pallas_call(
         prepare_kernel,
-        in_specs=[smem_spec, hbm_spec] + [vmem_spec] * 5,
+        in_specs=[smem_spec, hbm_spec] + [vmem_spec] * 6,
         out_shape=[
             bf16(tiles, CHUNK + MODES, GROUPS * CHUNK),
             bf16(tiles, CHUNK, LANES),
@@ -583,11 +584,11 @@
             f32(rows, width),
             bf16(rows, width),
         ],
-        scratch_shapes=[pltpu.VMEM((2 * rows, rows), BF16), pltpu.SemaphoreType.DMA],
+        scratch_shapes=[pltpu.SemaphoreType.DMA],
         compiler_params=params(),
         cost_estimate=cost(2),
         name="prepare",
-    )(place, kept(residual), query, residue, before, weights, mode_rate)
+    )(place, kept(residual), query, residue, before, weights, mode_rate, shift)
 
     group, entry, stride = full_state, jnp.zeros((MODES, width), F32), 1
     levels = radices(peers)
@@ -629,21 +630,21 @@
 
     parts = [lax.ppermute(squares, "fsdp", route) for route in routes(count, 1, count)[::-1]]
 
-    def write(kernel, operands, name):
+    def write(kernel, operands, name, more_specs=(), more_shapes=()):
         return pl.pallas_call(
             kernel,
-            out_specs=hbm_spec,
-            out_shape=bf16(rows, width),
+            out_specs=[hbm_spec, *more_specs],
+            out_shape=[bf16(rows, width), *more_shapes],
             scratch_shapes=[pltpu.VMEM((rows, width), BF16), pltpu.SemaphoreType.DMA((max(8, wides),))],
             compiler_params=params(),
             cost_estimate=cost(1),
             name=name,
         )(*operands)
 
-    new_residual = write(write_kernel, (summed,), "new_residual")
-    normed = write(
-        lambda *refs: norm_kernel(full_width, *refs), (summed, gain[None], squares, *parts), "normed"
+    new_residual, gained = write(
+        write_kernel, (summed, gain[None]), "new_residual", [vmem_spec], [f32(rows, width)]
     )
+    (normed,) = write(lambda *refs: norm_kernel(full_width, *refs), (gained, squares, *parts), "normed")
     return (new_residual, normed)
 
 

time: 26.8 us -> 26.7 us (level)
  transfers between devices with their start and end apart: 8 -> 8, of which waited for: 5 -> 5; matrix products, arithmetic and copies ran while one was open for 0% -> 0% of each run, Pallas kernels for 34% -> 35%
where the time goes in v22:
time: 26.7 us; the launch traced here: 26.4 us
  Pallas kernels  11.4 us (43%)
  starting transfers between devices  11.1 us (42%)
  waiting for transfers between devices  2.31 us (9%)
  local copies, waits for them, and re-layouts  0.94 us (4%)
  between operations  0.71 us (3%)
    ppermute x4, starting transfers between devices, per_device(): lax.ppermute(group, 'ctx', route)  6.21 us
    pallas_call x1, Pallas kernels, per_device(): pl.pallas_call(state_kernel, in_specs=[hbm_spec] * 4, out_shape=[bf16(row...  3.45 us
    ppermute x1, starting transfers between devices, per_device(): lax.ppermute(projected[:, rows - (taps - 1):, :], 'ctx', ring(peers, 1))  2.99 us
    pallas_call x1, Pallas kernels, per_device(): pl.pallas_call(local_kernel, out_shape=f32(rows, width), compiler_params=...  2.42 us
    pallas_call x1, Pallas kernels, per_device(): pl.pallas_call(prepare_kernel, in_specs=[smem_spec, hbm_spec] + [vmem_spe...  2.3 us
    pallas_call x2, Pallas kernels, write(): pl.pallas_call(kernel, out_specs=[hbm_spec, *more_specs], out_shape=[bf16...  2.18 us
    ppermute x3, starting transfers between devices, per_device(): lax.ppermute(squares, 'fsdp', route)  1.87 us
    ppermute x1, waiting for transfers between devices, per_device(): lax.ppermute(projected[:, rows - (taps - 1):, :], 'ctx', ring(peers, 1))  1.37 us
  transfers between devices with their start and end apart: 8, of which 5 were waited for; matrix products, arithmetic and copies ran while one was open for 0% of the time, Pallas kernels for 35%

profile of v22, /device:TPU:0, one launch (start us, length us, event | category | flops | bytes accessed | tf_op | source)
XLA Modules:
  0.0 26.4 jit_solution(8475914595895117376)
XLA Ops:
  0.6 0.9 %slice.3 = bf16[3,2,2048]{2,1,0:T(2,128)(2,1)S(1)} slice(bf16[3,256,2048]{2,1,0:T(8,128)(2,1)} %projected_ref.1), slice={[0:3], [254:256], [0:2048]} | slice | bytes 49152 | tf_op jit(solution)/shard_map/slice | solution.py:540
  1.6 3.0 %collective-permute-start = (bf16[3,2,2048]{2,1,0:T(2,128)(2,1)S(1)}, bf16[3,2,2048]{2,1,0:T(2,128)(2,1)S(1)}, u32[]{:S(2)}, u32[]{:S(2)}) collective-permute-start(bf16[3,2,2048]{2,1,0:T(2,128)(2,1)S(1)} %slice.3), channel_id=1, source_target_pairs={{0,4},{4,8},{8,12},{12,16},{16,20},{20,24},{24,28},{28,0},{1,5},{5... | collective-permute-start | bytes 73736 | tf_op jit(solution)/shard_map/ppermute | solution.py:540
  4.5 3.5 %block_state.1 = (bf16[256,2048]{1,0:T(8,128)(2,1)S(1)}, f32[16,2048]{1,0:T(8,128)S(1)}, f32[16,2048]{1,0:T(8,128)S(1)}, f32[2,8,2048]{2,1,0:T(8,128)S(1)}, f32[...) custom-call(bf16[3,256,2048]{2,1,0:T(8,128)(2,1)} %projected_ref.1, ...), custom_call_target="tpu_custom_call" | custom-call | bytes 9000000 | tf_op jit(solution)/shard_map/block_state/pallas_call | solution.py:542
  8.0 0.0 copy-start
  8.0 1.4 %collective-permute-done.before_ref.refs_1_ = bf16[3,2,2048]{2,1,0:T(2,128)(2,1)S(1)} collective-permute-done((bf16[3,2,2048]{2,1,0:T(2,128)(2,1)S(1)}, bf16[3,2,2048]{2,1,0:T(2,128)(2,1)S(1)}, u32[]{:S(2)}, u32[]{:S(2)}) %collective-permute-start) | collective-permute-done | bytes 24608 | tf_op jit(solution)/shard_map/ppermute | solution.py:540
  9.4 0.1 head_tokens.1
  9.5 1.3 %collective-permute-start.1 = (bf16[16,2048]{1,0:T(8,128)(2,1)S(1)}, bf16[16,2048]{1,0:T(8,128)(2,1)S(1)}, u32[]{:S(2)}, u32[]{:S(2)}) collective-permute-start(bf16[16,2048]{1,0:T(8,128)(2,1)S(1)} %get-tuple-element.36.refs_1_), channel_id=1, source_target_pairs={{12,0},{8,4},{4,8},{0,12},{28,16},{24,20},{20,24},{16,28},{13,1},{... | collective-permute-start | bytes 196616 | tf_op jit(solution)/shard_map/ppermute | solution.py:599
  10.8 0.4 %collective-permute-start.2 = (bf16[16,2048]{1,0:T(8,128)(2,1)S(1)}, bf16[16,2048]{1,0:T(8,128)(2,1)S(1)}, u32[]{:S(2)}, u32[]{:S(2)}) collective-permute-start(bf16[16,2048]{1,0:T(8,128)(2,1)S(1)} %get-tuple-element.36.refs_1_), channel_id=1, source_target_pairs={{8,0},{12,4},{0,8},{4,12},{24,16},{28,20},{16,24},{20,28},{9,1},{1... | collective-permute-start | bytes 196616 | tf_op jit(solution)/shard_map/ppermute | solution.py:599
  11.2 1.8 %collective-permute-start.3 = (bf16[16,2048]{1,0:T(8,128)(2,1)S(1)}, bf16[16,2048]{1,0:T(8,128)(2,1)S(1)}, u32[]{:S(2)}, u32[]{:S(2)}) collective-permute-start(bf16[16,2048]{1,0:T(8,128)(2,1)S(1)} %get-tuple-element.36.refs_1_), channel_id=1, source_target_pairs={{4,0},{0,4},{12,8},{8,12},{20,16},{16,20},{28,24},{24,28},{5,1},{1... | collective-permute-start | bytes 196616 | tf_op jit(solution)/shard_map/ppermute | solution.py:599
  13.1 2.3 %prepare.1 = (bf16[16,48,256]{2,1,0:T(8,128)(2,1)S(1)}, bf16[16,32,128]{2,1,0:T(8,128)(2,1)S(1)}, bf16[8,256,256]{2,1,0:T(8,128)(2,1)S(1)}, f32[256,2048]{1,0:T(8,128)S(1)}, bf16[256,2048]{1,0:T(8,128)(2,1)S(1)}) custom-call(s32[1]{0:T(128)} %bitcast.place_ref.refs_0_, bf16[256,2048]{1,0:T(8,128)(2,1)} %residual_hbm.1, ...), custom_call_target="tpu_custom_call" | custom-call | bytes 6000000 | tf_op jit(solution)/shard_map/prepare/pallas_call | solution.py:577
  15.4 0.0 collective-permute-done.1.refs_4_
  15.4 0.0 collective-permute-done.2.refs_5_
  15.4 0.1 collective-permute-done.3.refs_6_
  15.5 0.2 join.1
  15.7 2.7 %collective-permute-start.4 = (bf16[16,2048]{1,0:T(8,128)(2,1)S(1)}, bf16[16,2048]{1,0:T(8,128)(2,1)S(1)}, u32[]{:S(2)}, u32[]{:S(2)}) collective-permute-start(bf16[16,2048]{1,0:T(8,128)(2,1)S(1)} %get-tuple-element.43), channel_id=1, source_target_pairs={{16,0},{20,4},{24,8},{28,12},{0,16},{4,20},{8,24},{12,28},{17,1},{... | collective-permute-start | bytes 196616 | tf_op jit(solution)/shard_map/ppermute | solution.py:611
  18.3 0.0 copy-done
  18.3 2.4 %local_conv.1.refs_1_ = f32[256,2048]{1,0:T(8,128)S(1)} custom-call(f32[256,2048]{1,0:T(8,128)S(1)} %get-tuple-element.30.gate_ref.refs_2_, bf16[256,2048]{1,0:T(8,128)(2,1)S(1)} %get-tuple-element.31.residual_ref, bf16[256,2048]{1,0:T(8,128)(2,1)S(1)} %get-tuple-element.32.product_ref, f32[8,2048]{1,0:T(8,128)S(1)} %get-tuple-element.35.first_ref, ...), custom_call_target="tpu_custom_call" | custom-call | bytes 15000000 | tf_op jit(solution)/shard_map/local_conv/pallas_call | solution.py:613
  20.8 0.1 collective-permute-done.4.refs_6_
  20.9 0.0 copy-start.1
  20.9 0.7 %add_carry.1 = (f32[256,2048]{1,0:T(8,128)S(1)}, f32[1,256]{1,0:T(1,128)S(1)}) custom-call(s32[1]{0:T(128)} %bitcast.place_ref.refs_0_, f32[256,2048]{1,0:T(8,128)S(1)} %local_conv.1.refs_1_, f32[256,2048]{1,0:T(8,128)S(1)} %get-tuple-element.30.gate_ref.refs_2_, bf16[8,256,256]{2,1,0:T(8,128)(2,1)S(1)} %get-tuple-element.40.refs_3_, ...), custom_call_target="tpu_custom_call" | custom-call | bytes 3000000 | tf_op jit(solution)/shard_map/add_carry/pallas_call | solution.py:622
  21.6 0.0 collective-permute-start.5
  21.6 1.7 %collective-permute-start.6 = (f32[1,256]{1,0:T(1,128)S(1)}, f32[1,256]{1,0:T(1,128)S(1)}, u32[]{:S(2)}, u32[]{:S(2)}) collective-permute-start(f32[1,256]{1,0:T(1,128)S(1)} %get-tuple-element.47.refs_1_), channel_id=1, source_target_pairs={{2,0},{3,1},{0,2},{1,3},{6,4},{7,5},{4,6},{5,7},{10,8},{11,9},{8,1... | collective-permute-start | bytes 3080 | tf_op jit(solution)/shard_map/ppermute | solution.py:631
  23.3 0.2 collective-permute-start.7
  23.5 0.0 copy-done.1
  23.5 1.0 %new_residual.1 = (bf16[256,2048]{1,0:T(8,128)(2,1)}, f32[256,2048]{1,0:T(8,128)S(1)}) custom-call(f32[256,2048]{1,0:T(8,128)S(1)} %get-tuple-element.44.summed_ref, f32[1,2048]{1,0:T(1,128)S(1)} %bitcast.6), custom_call_target="tpu_custom_call" | custom-call | bytes 3000000 | tf_op jit(solution)/shard_map/new_residual/pallas_call | solution.py:634
  24.6 0.1 collective-permute-done.5.refs_2_
  24.7 0.6 %collective-permute-done.6.refs_3_ = f32[1,256]{1,0:T(1,128)S(1)} collective-permute-done((f32[1,256]{1,0:T(1,128)S(1)}, f32[1,256]{1,0:T(1,128)S(1)}, u32[]{:S(2)}, u32[]{:S(2)}) %collective-permute-start.6) | collective-permute-done | bytes 1056 | tf_op jit(solution)/shard_map/ppermute | solution.py:631
  25.3 0.0 collective-permute-done.7.refs_4_
  25.3 1.1 %normed.1 = bf16[256,2048]{1,0:T(8,128)(2,1)} custom-call(f32[256,2048]{1,0:T(8,128)S(1)} %get-tuple-element.46.refs_0_, f32[1,256]{1,0:T(1,128)S(1)} %get-tuple-element.47.refs_1_, f32[1,256]{1,0:T(1,128)S(1)} %collective-permute-done.5.refs_2_, f32[1,256]{1,0:T(1,128)S(1)} %collective-permute-done.6.refs_3_, f32[1,256]{1,0:T(1,128)S(1)} %collective-permute-done.7.refs_4_), custom_call_target="tpu_custom_call" | custom-call | bytes 3000000 | tf_op jit(solution)/shard_map/normed/pallas_call | solution.py:634
  (1 shorter events, 0.0 us)
Async XLA Ops:
  1.6 7.8 %collective-permute-start = (bf16[3,2,2048]{2,1,0:T(2,128)(2,1)S(1)}, bf16[3,2,2048]{2,1,0:T(2,128)(2,1)S(1)}, u32[]{:S(2)}, u32[]{:S(2)}) collective-permute-start(bf16[3,2,2048]{2,1,0:T(2,128)(2,1)S(1)} %slice.3), channel_id=1, source_target_pairs={{0,4},{4,8},{8,12},{12,16},{16,20},{20,24},{24,28},{28,0},{1,5},{5... | collective-permute-start | bytes 73736 | tf_op jit(solution)/shard_map/ppermute | solution.py:540
  8.0 10.3 %copy-start = (f32[2048]{0:T(1024)S(1)}, f32[2048]{0:T(1024)}, u32[]{:S(2)}) copy-start(f32[2048]{0:T(1024)} %param.11) | copy-start | bytes 24580
  9.5 5.9 %collective-permute-start.1 = (bf16[16,2048]{1,0:T(8,128)(2,1)S(1)}, bf16[16,2048]{1,0:T(8,128)(2,1)S(1)}, u32[]{:S(2)}, u32[]{:S(2)}) collective-permute-start(bf16[16,2048]{1,0:T(8,128)(2,1)S(1)} %get-tuple-element.36.refs_1_), channel_id=1, source_target_pairs={{12,0},{8,4},{4,8},{0,12},{28,16},{24,20},{20,24},{16,28},{13,1},{... | collective-permute-start | bytes 196616 | tf_op jit(solution)/shard_map/ppermute | solution.py:599
  10.8 4.6 %collective-permute-start.2 = (bf16[16,2048]{1,0:T(8,128)(2,1)S(1)}, bf16[16,2048]{1,0:T(8,128)(2,1)S(1)}, u32[]{:S(2)}, u32[]{:S(2)}) collective-permute-start(bf16[16,2048]{1,0:T(8,128)(2,1)S(1)} %get-tuple-element.36.refs_1_), channel_id=1, source_target_pairs={{8,0},{12,4},{0,8},{4,12},{24,16},{28,20},{16,24},{20,28},{9,1},{1... | collective-permute-start | bytes 196616 | tf_op jit(solution)/shard_map/ppermute | solution.py:599
  11.2 4.3 %collective-permute-start.3 = (bf16[16,2048]{1,0:T(8,128)(2,1)S(1)}, bf16[16,2048]{1,0:T(8,128)(2,1)S(1)}, u32[]{:S(2)}, u32[]{:S(2)}) collective-permute-start(bf16[16,2048]{1,0:T(8,128)(2,1)S(1)} %get-tuple-element.36.refs_1_), channel_id=1, source_target_pairs={{4,0},{0,4},{12,8},{8,12},{20,16},{16,20},{28,24},{24,28},{5,1},{1... | collective-permute-start | bytes 196616 | tf_op jit(solution)/shard_map/ppermute | solution.py:599
  15.7 5.2 %collective-permute-start.4 = (bf16[16,2048]{1,0:T(8,128)(2,1)S(1)}, bf16[16,2048]{1,0:T(8,128)(2,1)S(1)}, u32[]{:S(2)}, u32[]{:S(2)}) collective-permute-start(bf16[16,2048]{1,0:T(8,128)(2,1)S(1)} %get-tuple-element.43), channel_id=1, source_target_pairs={{16,0},{20,4},{24,8},{28,12},{0,16},{4,20},{8,24},{12,28},{17,1},{... | collective-permute-start | bytes 196616 | tf_op jit(solution)/shard_map/ppermute | solution.py:611
  20.9 2.6 %copy-start.1 = (f32[2048]{0:T(1024)S(1)}, f32[2048]{0:T(1024)}, u32[]{:S(2)}) copy-start(f32[2048]{0:T(1024)} %param.13) | copy-start | bytes 24580
  21.6 3.0 %collective-permute-start.5 = (f32[1,256]{1,0:T(1,128)S(1)}, f32[1,256]{1,0:T(1,128)S(1)}, u32[]{:S(2)}, u32[]{:S(2)}) collective-permute-start(f32[1,256]{1,0:T(1,128)S(1)} %get-tuple-element.47.refs_1_), channel_id=1, source_target_pairs={{3,0},{2,1},{1,2},{0,3},{7,4},{6,5},{5,6},{4,7},{11,8},{10,9},{9,1... | collective-permute-start | bytes 3080 | tf_op jit(solution)/shard_map/ppermute | solution.py:631
  21.6 3.6 %collective-permute-start.6 = (f32[1,256]{1,0:T(1,128)S(1)}, f32[1,256]{1,0:T(1,128)S(1)}, u32[]{:S(2)}, u32[]{:S(2)}) collective-permute-start(f32[1,256]{1,0:T(1,128)S(1)} %get-tuple-element.47.refs_1_), channel_id=1, source_target_pairs={{2,0},{3,1},{0,2},{1,3},{6,4},{7,5},{4,6},{5,7},{10,8},{11,9},{8,1... | collective-permute-start | bytes 3080 | tf_op jit(solution)/shard_map/ppermute | solution.py:631
  23.3 1.9 %collective-permute-start.7 = (f32[1,256]{1,0:T(1,128)S(1)}, f32[1,256]{1,0:T(1,128)S(1)}, u32[]{:S(2)}, u32[]{:S(2)}) collective-permute-start(f32[1,256]{1,0:T(1,128)S(1)} %get-tuple-element.47.refs_1_), channel_id=1, source_target_pairs={{1,0},{0,1},{3,2},{2,3},{5,4},{4,5},{7,6},{6,7},{9,8},{8,9},{11,10... | collective-permute-start | bytes 3080 | tf_op jit(solution)/shard_map/ppermute | solution.py:631

commit v23 on v22

--- a/solution.py
+++ b/solution.py
@@ -207,6 +207,9 @@
             parts.append(wide_conv(buffer_ref[c, :, here], earlier[c], taps_of(weights, c + 1, here)))
         product = (parts[0] * parts[1]).astype(BF16)
         product_ref[:, here] = product
+        return (product,)
+
+    def reach(wide, product):
         return (jnp.dot(ending_ref[wide], product, preferred_element_type=F32),)
 
     def leave(wide, every):
@@ -214,7 +217,7 @@
             own = every[lanes_of(half), lanes_of(half)].reshape(GROUPS, MODES, LANES)
             state_ref[:, lanes_of((WIDE // LANES) * wide + half)] = jnp.sum(own * mask, axis=0)
 
-    pipelined(wides, fetch, multiply, leave)
+    pipelined(wides, fetch, multiply, reach, leave)
     for copy in later:
         copy.wait()
 

time: 26.7 us -> 26.7 us (level)
  no operation moved by 1% of the time
where the time goes in v23:
time: 26.7 us; the launch traced here: 26.4 us
  Pallas kernels  11.4 us (43%)
  starting transfers between devices  11.1 us (42%)
  waiting for transfers between devices  2.32 us (9%)
  local copies, waits for them, and re-layouts  0.94 us (4%)
  between operations  0.71 us (3%)
    ppermute x4, starting transfers between devices, per_device(): lax.ppermute(group, 'ctx', route)  6.21 us
    pallas_call x1, Pallas kernels, per_device(): pl.pallas_call(state_kernel, in_specs=[hbm_spec] * 4, out_shape=[bf16(row...  3.45 us
    ppermute x1, starting transfers between devices, per_device(): lax.ppermute(projected[:, rows - (taps - 1):, :], 'ctx', ring(peers, 1))  2.99 us
    pallas_call x1, Pallas kernels, per_device(): pl.pallas_call(local_kernel, out_shape=f32(rows, width), compiler_params=...  2.42 us
    pallas_call x1, Pallas kernels, per_device(): pl.pallas_call(prepare_kernel, in_specs=[smem_spec, hbm_spec] + [vmem_spe...  2.3 us
    pallas_call x2, Pallas kernels, write(): pl.pallas_call(kernel, out_specs=[hbm_spec, *more_specs], out_shape=[bf16...  2.18 us
    ppermute x3, starting transfers between devices, per_device(): lax.ppermute(squares, 'fsdp', route)  1.87 us
    ppermute x1, waiting for transfers between devices, per_device(): lax.ppermute(projected[:, rows - (taps - 1):, :], 'ctx', ring(peers, 1))  1.38 us
  transfers between devices with their start and end apart: 8, of which 5 were waited for; matrix products, arithmetic and copies ran while one was open for 0% of the time, Pallas kernels for 35%

profile of v23, /device:TPU:0, one launch (start us, length us, event | category | flops | bytes accessed | tf_op | source)
XLA Modules:
  0.0 26.4 jit_solution(14755795815344301489)
XLA Ops:
  0.6 0.9 %slice.3 = bf16[3,2,2048]{2,1,0:T(2,128)(2,1)S(1)} slice(bf16[3,256,2048]{2,1,0:T(8,128)(2,1)} %projected_ref.1), slice={[0:3], [254:256], [0:2048]} | slice | bytes 49152 | tf_op jit(solution)/shard_map/slice | solution.py:543
  1.6 3.0 %collective-permute-start = (bf16[3,2,2048]{2,1,0:T(2,128)(2,1)S(1)}, bf16[3,2,2048]{2,1,0:T(2,128)(2,1)S(1)}, u32[]{:S(2)}, u32[]{:S(2)}) collective-permute-start(bf16[3,2,2048]{2,1,0:T(2,128)(2,1)S(1)} %slice.3), channel_id=1, source_target_pairs={{0,4},{4,8},{8,12},{12,16},{16,20},{20,24},{24,28},{28,0},{1,5},{5... | collective-permute-start | bytes 73736 | tf_op jit(solution)/shard_map/ppermute | solution.py:543
  4.5 3.4 %block_state.1 = (bf16[256,2048]{1,0:T(8,128)(2,1)S(1)}, f32[16,2048]{1,0:T(8,128)S(1)}, f32[16,2048]{1,0:T(8,128)S(1)}, f32[2,8,2048]{2,1,0:T(8,128)S(1)}, f32[...) custom-call(bf16[3,256,2048]{2,1,0:T(8,128)(2,1)} %projected_ref.1, ...), custom_call_target="tpu_custom_call" | custom-call | bytes 9000000 | tf_op jit(solution)/shard_map/block_state/pallas_call | solution.py:545
  8.0 0.0 copy-start
  8.0 1.4 %collective-permute-done.before_ref.refs_1_ = bf16[3,2,2048]{2,1,0:T(2,128)(2,1)S(1)} collective-permute-done((bf16[3,2,2048]{2,1,0:T(2,128)(2,1)S(1)}, bf16[3,2,2048]{2,1,0:T(2,128)(2,1)S(1)}, u32[]{:S(2)}, u32[]{:S(2)}) %collective-permute-start) | collective-permute-done | bytes 24608 | tf_op jit(solution)/shard_map/ppermute | solution.py:543
  9.4 0.1 head_tokens.1
  9.5 1.3 %collective-permute-start.1 = (bf16[16,2048]{1,0:T(8,128)(2,1)S(1)}, bf16[16,2048]{1,0:T(8,128)(2,1)S(1)}, u32[]{:S(2)}, u32[]{:S(2)}) collective-permute-start(bf16[16,2048]{1,0:T(8,128)(2,1)S(1)} %get-tuple-element.36.refs_1_), channel_id=1, source_target_pairs={{12,0},{8,4},{4,8},{0,12},{28,16},{24,20},{20,24},{16,28},{13,1},{... | collective-permute-start | bytes 196616 | tf_op jit(solution)/shard_map/ppermute | solution.py:602
  10.8 0.4 %collective-permute-start.2 = (bf16[16,2048]{1,0:T(8,128)(2,1)S(1)}, bf16[16,2048]{1,0:T(8,128)(2,1)S(1)}, u32[]{:S(2)}, u32[]{:S(2)}) collective-permute-start(bf16[16,2048]{1,0:T(8,128)(2,1)S(1)} %get-tuple-element.36.refs_1_), channel_id=1, source_target_pairs={{8,0},{12,4},{0,8},{4,12},{24,16},{28,20},{16,24},{20,28},{9,1},{1... | collective-permute-start | bytes 196616 | tf_op jit(solution)/shard_map/ppermute | solution.py:602
  11.2 1.8 %collective-permute-start.3 = (bf16[16,2048]{1,0:T(8,128)(2,1)S(1)}, bf16[16,2048]{1,0:T(8,128)(2,1)S(1)}, u32[]{:S(2)}, u32[]{:S(2)}) collective-permute-start(bf16[16,2048]{1,0:T(8,128)(2,1)S(1)} %get-tuple-element.36.refs_1_), channel_id=1, source_target_pairs={{4,0},{0,4},{12,8},{8,12},{20,16},{16,20},{28,24},{24,28},{5,1},{1... | collective-permute-start | bytes 196616 | tf_op jit(solution)/shard_map/ppermute | solution.py:602
  13.1 2.3 %prepare.1 = (bf16[16,48,256]{2,1,0:T(8,128)(2,1)S(1)}, bf16[16,32,128]{2,1,0:T(8,128)(2,1)S(1)}, bf16[8,256,256]{2,1,0:T(8,128)(2,1)S(1)}, f32[256,2048]{1,0:T(8,128)S(1)}, bf16[256,2048]{1,0:T(8,128)(2,1)S(1)}) custom-call(s32[1]{0:T(128)} %bitcast.place_ref.refs_0_, bf16[256,2048]{1,0:T(8,128)(2,1)} %residual_hbm.1, ...), custom_call_target="tpu_custom_call" | custom-call | bytes 6000000 | tf_op jit(solution)/shard_map/prepare/pallas_call | solution.py:580
  15.4 0.0 collective-permute-done.1.refs_4_
  15.4 0.0 collective-permute-done.2.refs_5_
  15.4 0.1 collective-permute-done.3.refs_6_
  15.5 0.2 join.1
  15.7 2.7 %collective-permute-start.4 = (bf16[16,2048]{1,0:T(8,128)(2,1)S(1)}, bf16[16,2048]{1,0:T(8,128)(2,1)S(1)}, u32[]{:S(2)}, u32[]{:S(2)}) collective-permute-start(bf16[16,2048]{1,0:T(8,128)(2,1)S(1)} %get-tuple-element.43), channel_id=1, source_target_pairs={{16,0},{20,4},{24,8},{28,12},{0,16},{4,20},{8,24},{12,28},{17,1},{... | collective-permute-start | bytes 196616 | tf_op jit(solution)/shard_map/ppermute | solution.py:614
  18.3 0.0 copy-done
  18.3 2.4 %local_conv.1.refs_1_ = f32[256,2048]{1,0:T(8,128)S(1)} custom-call(f32[256,2048]{1,0:T(8,128)S(1)} %get-tuple-element.30.gate_ref.refs_2_, bf16[256,2048]{1,0:T(8,128)(2,1)S(1)} %get-tuple-element.31.residual_ref, bf16[256,2048]{1,0:T(8,128)(2,1)S(1)} %get-tuple-element.32.product_ref, f32[8,2048]{1,0:T(8,128)S(1)} %get-tuple-element.35.first_ref, ...), custom_call_target="tpu_custom_call" | custom-call | bytes 15000000 | tf_op jit(solution)/shard_map/local_conv/pallas_call | solution.py:616
  20.8 0.1 collective-permute-done.4.refs_6_
  20.9 0.0 copy-start.1
  20.9 0.7 %add_carry.1 = (f32[256,2048]{1,0:T(8,128)S(1)}, f32[1,256]{1,0:T(1,128)S(1)}) custom-call(s32[1]{0:T(128)} %bitcast.place_ref.refs_0_, f32[256,2048]{1,0:T(8,128)S(1)} %local_conv.1.refs_1_, f32[256,2048]{1,0:T(8,128)S(1)} %get-tuple-element.30.gate_ref.refs_2_, bf16[8,256,256]{2,1,0:T(8,128)(2,1)S(1)} %get-tuple-element.40.refs_3_, ...), custom_call_target="tpu_custom_call" | custom-call | bytes 3000000 | tf_op jit(solution)/shard_map/add_carry/pallas_call | solution.py:625
  21.6 0.0 collective-permute-start.5
  21.6 1.7 %collective-permute-start.6 = (f32[1,256]{1,0:T(1,128)S(1)}, f32[1,256]{1,0:T(1,128)S(1)}, u32[]{:S(2)}, u32[]{:S(2)}) collective-permute-start(f32[1,256]{1,0:T(1,128)S(1)} %get-tuple-element.47.refs_1_), channel_id=1, source_target_pairs={{2,0},{3,1},{0,2},{1,3},{6,4},{7,5},{4,6},{5,7},{10,8},{11,9},{8,1... | collective-permute-start | bytes 3080 | tf_op jit(solution)/shard_map/ppermute | solution.py:634
  23.3 0.2 collective-permute-start.7
  23.5 0.0 copy-done.1
  23.5 1.0 %new_residual.1 = (bf16[256,2048]{1,0:T(8,128)(2,1)}, f32[256,2048]{1,0:T(8,128)S(1)}) custom-call(f32[256,2048]{1,0:T(8,128)S(1)} %get-tuple-element.44.summed_ref, f32[1,2048]{1,0:T(1,128)S(1)} %bitcast.6), custom_call_target="tpu_custom_call" | custom-call | bytes 3000000 | tf_op jit(solution)/shard_map/new_residual/pallas_call | solution.py:637
  24.6 0.1 collective-permute-done.5.refs_2_
  24.6 0.6 %collective-permute-done.6.refs_3_ = f32[1,256]{1,0:T(1,128)S(1)} collective-permute-done((f32[1,256]{1,0:T(1,128)S(1)}, f32[1,256]{1,0:T(1,128)S(1)}, u32[]{:S(2)}, u32[]{:S(2)}) %collective-permute-start.6) | collective-permute-done | bytes 1056 | tf_op jit(solution)/shard_map/ppermute | solution.py:634
  25.3 0.0 collective-permute-done.7.refs_4_
  25.3 1.1 %normed.1 = bf16[256,2048]{1,0:T(8,128)(2,1)} custom-call(f32[256,2048]{1,0:T(8,128)S(1)} %get-tuple-element.46.refs_0_, f32[1,256]{1,0:T(1,128)S(1)} %get-tuple-element.47.refs_1_, f32[1,256]{1,0:T(1,128)S(1)} %collective-permute-done.5.refs_2_, f32[1,256]{1,0:T(1,128)S(1)} %collective-permute-done.6.refs_3_, f32[1,256]{1,0:T(1,128)S(1)} %collective-permute-done.7.refs_4_), custom_call_target="tpu_custom_call" | custom-call | bytes 3000000 | tf_op jit(solution)/shard_map/normed/pallas_call | solution.py:637
  (1 shorter events, 0.0 us)
Async XLA Ops:
  1.6 7.8 %collective-permute-start = (bf16[3,2,2048]{2,1,0:T(2,128)(2,1)S(1)}, bf16[3,2,2048]{2,1,0:T(2,128)(2,1)S(1)}, u32[]{:S(2)}, u32[]{:S(2)}) collective-permute-start(bf16[3,2,2048]{2,1,0:T(2,128)(2,1)S(1)} %slice.3), channel_id=1, source_target_pairs={{0,4},{4,8},{8,12},{12,16},{16,20},{20,24},{24,28},{28,0},{1,5},{5... | collective-permute-start | bytes 73736 | tf_op jit(solution)/shard_map/ppermute | solution.py:543
  8.0 10.3 %copy-start = (f32[2048]{0:T(1024)S(1)}, f32[2048]{0:T(1024)}, u32[]{:S(2)}) copy-start(f32[2048]{0:T(1024)} %param.11) | copy-start | bytes 24580
  9.5 5.9 %collective-permute-start.1 = (bf16[16,2048]{1,0:T(8,128)(2,1)S(1)}, bf16[16,2048]{1,0:T(8,128)(2,1)S(1)}, u32[]{:S(2)}, u32[]{:S(2)}) collective-permute-start(bf16[16,2048]{1,0:T(8,128)(2,1)S(1)} %get-tuple-element.36.refs_1_), channel_id=1, source_target_pairs={{12,0},{8,4},{4,8},{0,12},{28,16},{24,20},{20,24},{16,28},{13,1},{... | collective-permute-start | bytes 196616 | tf_op jit(solution)/shard_map/ppermute | solution.py:602
  10.8 4.6 %collective-permute-start.2 = (bf16[16,2048]{1,0:T(8,128)(2,1)S(1)}, bf16[16,2048]{1,0:T(8,128)(2,1)S(1)}, u32[]{:S(2)}, u32[]{:S(2)}) collective-permute-start(bf16[16,2048]{1,0:T(8,128)(2,1)S(1)} %get-tuple-element.36.refs_1_), channel_id=1, source_target_pairs={{8,0},{12,4},{0,8},{4,12},{24,16},{28,20},{16,24},{20,28},{9,1},{1... | collective-permute-start | bytes 196616 | tf_op jit(solution)/shard_map/ppermute | solution.py:602
  11.2 4.3 %collective-permute-start.3 = (bf16[16,2048]{1,0:T(8,128)(2,1)S(1)}, bf16[16,2048]{1,0:T(8,128)(2,1)S(1)}, u32[]{:S(2)}, u32[]{:S(2)}) collective-permute-start(bf16[16,2048]{1,0:T(8,128)(2,1)S(1)} %get-tuple-element.36.refs_1_), channel_id=1, source_target_pairs={{4,0},{0,4},{12,8},{8,12},{20,16},{16,20},{28,24},{24,28},{5,1},{1... | collective-permute-start | bytes 196616 | tf_op jit(solution)/shard_map/ppermute | solution.py:602
  15.7 5.2 %collective-permute-start.4 = (bf16[16,2048]{1,0:T(8,128)(2,1)S(1)}, bf16[16,2048]{1,0:T(8,128)(2,1)S(1)}, u32[]{:S(2)}, u32[]{:S(2)}) collective-permute-start(bf16[16,2048]{1,0:T(8,128)(2,1)S(1)} %get-tuple-element.43), channel_id=1, source_target_pairs={{16,0},{20,4},{24,8},{28,12},{0,16},{4,20},{8,24},{12,28},{17,1},{... | collective-permute-start | bytes 196616 | tf_op jit(solution)/shard_map/ppermute | solution.py:614
  20.9 2.6 %copy-start.1 = (f32[2048]{0:T(1024)S(1)}, f32[2048]{0:T(1024)}, u32[]{:S(2)}) copy-start(f32[2048]{0:T(1024)} %param.13) | copy-start | bytes 24580
  21.6 3.0 %collective-permute-start.5 = (f32[1,256]{1,0:T(1,128)S(1)}, f32[1,256]{1,0:T(1,128)S(1)}, u32[]{:S(2)}, u32[]{:S(2)}) collective-permute-start(f32[1,256]{1,0:T(1,128)S(1)} %get-tuple-element.47.refs_1_), channel_id=1, source_target_pairs={{3,0},{2,1},{1,2},{0,3},{7,4},{6,5},{5,6},{4,7},{11,8},{10,9},{9,1... | collective-permute-start | bytes 3080 | tf_op jit(solution)/shard_map/ppermute | solution.py:634
  21.6 3.6 %collective-permute-start.6 = (f32[1,256]{1,0:T(1,128)S(1)}, f32[1,256]{1,0:T(1,128)S(1)}, u32[]{:S(2)}, u32[]{:S(2)}) collective-permute-start(f32[1,256]{1,0:T(1,128)S(1)} %get-tuple-element.47.refs_1_), channel_id=1, source_target_pairs={{2,0},{3,1},{0,2},{1,3},{6,4},{7,5},{4,6},{5,7},{10,8},{11,9},{8,1... | collective-permute-start | bytes 3080 | tf_op jit(solution)/shard_map/ppermute | solution.py:634
  23.3 1.9 %collective-permute-start.7 = (f32[1,256]{1,0:T(1,128)S(1)}, f32[1,256]{1,0:T(1,128)S(1)}, u32[]{:S(2)}, u32[]{:S(2)}) collective-permute-start(f32[1,256]{1,0:T(1,128)S(1)} %get-tuple-element.47.refs_1_), channel_id=1, source_target_pairs={{1,0},{0,1},{3,2},{2,3},{5,4},{4,5},{7,6},{6,7},{9,8},{8,9},{11,10... | collective-permute-start | bytes 3080 | tf_op jit(solution)/shard_map/ppermute | solution.py:634

commit v24 on v22

--- a/solution.py
+++ b/solution.py
@@ -465,7 +465,7 @@
     scale_row = lax.rsqrt(squares / full_width + 1e-05)
     scale = jnp.concatenate([as_column(scale_row[:, lanes_of(k)]) for k in range(rows // LANES)], axis=0)
     copies = []
-    block = rows // 8
+    block = rows // 4
     for start in range(0, rows, block):
         span = slice(start, start + block)
         for tile in range(width // LANES):

time: 26.7 us -> 26.8 us (level)
  no operation moved by 1% of the time
where the time goes in v24:
time: 26.8 us; the launch traced here: 26.4 us
  Pallas kernels  11.4 us (43%)
  starting transfers between devices  11.1 us (41%)
  waiting for transfers between devices  2.31 us (9%)
  local copies, waits for them, and re-layouts  0.94 us (4%)
  between operations  0.71 us (3%)
    ppermute x4, starting transfers between devices, per_device(): lax.ppermute(group, 'ctx', route)  6.21 us
    pallas_call x1, Pallas kernels, per_device(): pl.pallas_call(state_kernel, in_specs=[hbm_spec] * 4, out_shape=[bf16(row...  3.45 us
    ppermute x1, starting transfers between devices, per_device(): lax.ppermute(projected[:, rows - (taps - 1):, :], 'ctx', ring(peers, 1))  2.99 us
    pallas_call x1, Pallas kernels, per_device(): pl.pallas_call(local_kernel, out_shape=f32(rows, width), compiler_params=...  2.42 us
    pallas_call x1, Pallas kernels, per_device(): pl.pallas_call(prepare_kernel, in_specs=[smem_spec, hbm_spec] + [vmem_spe...  2.3 us
    pallas_call x2, Pallas kernels, write(): pl.pallas_call(kernel, out_specs=[hbm_spec, *more_specs], out_shape=[bf16...  2.22 us
    ppermute x3, starting transfers between devices, per_device(): lax.ppermute(squares, 'fsdp', route)  1.87 us
    ppermute x1, waiting for transfers between devices, per_device(): lax.ppermute(projected[:, rows - (taps - 1):, :], 'ctx', ring(peers, 1))  1.37 us
  transfers between devices with their start and end apart: 8, of which 5 were waited for; matrix products, arithmetic and copies ran while one was open for 0% of the time, Pallas kernels for 35%

profile of v24, /device:TPU:0, one launch (start us, length us, event | category | flops | bytes accessed | tf_op | source)
XLA Modules:
  0.0 26.4 jit_solution(5046959698647144890)
XLA Ops:
  0.6 0.9 %slice.3 = bf16[3,2,2048]{2,1,0:T(2,128)(2,1)S(1)} slice(bf16[3,256,2048]{2,1,0:T(8,128)(2,1)} %projected_ref.1), slice={[0:3], [254:256], [0:2048]} | slice | bytes 49152 | tf_op jit(solution)/shard_map/slice | solution.py:540
  1.6 3.0 %collective-permute-start = (bf16[3,2,2048]{2,1,0:T(2,128)(2,1)S(1)}, bf16[3,2,2048]{2,1,0:T(2,128)(2,1)S(1)}, u32[]{:S(2)}, u32[]{:S(2)}) collective-permute-start(bf16[3,2,2048]{2,1,0:T(2,128)(2,1)S(1)} %slice.3), channel_id=1, source_target_pairs={{0,4},{4,8},{8,12},{12,16},{16,20},{20,24},{24,28},{28,0},{1,5},{5... | collective-permute-start | bytes 73736 | tf_op jit(solution)/shard_map/ppermute | solution.py:540
  4.5 3.5 %block_state.1 = (bf16[256,2048]{1,0:T(8,128)(2,1)S(1)}, f32[16,2048]{1,0:T(8,128)S(1)}, f32[16,2048]{1,0:T(8,128)S(1)}, f32[2,8,2048]{2,1,0:T(8,128)S(1)}, f32[...) custom-call(bf16[3,256,2048]{2,1,0:T(8,128)(2,1)} %projected_ref.1, ...), custom_call_target="tpu_custom_call" | custom-call | bytes 9000000 | tf_op jit(solution)/shard_map/block_state/pallas_call | solution.py:542
  8.0 0.0 copy-start
  8.0 1.4 %collective-permute-done.before_ref.refs_1_ = bf16[3,2,2048]{2,1,0:T(2,128)(2,1)S(1)} collective-permute-done((bf16[3,2,2048]{2,1,0:T(2,128)(2,1)S(1)}, bf16[3,2,2048]{2,1,0:T(2,128)(2,1)S(1)}, u32[]{:S(2)}, u32[]{:S(2)}) %collective-permute-start) | collective-permute-done | bytes 24608 | tf_op jit(solution)/shard_map/ppermute | solution.py:540
  9.4 0.1 head_tokens.1
  9.5 1.3 %collective-permute-start.1 = (bf16[16,2048]{1,0:T(8,128)(2,1)S(1)}, bf16[16,2048]{1,0:T(8,128)(2,1)S(1)}, u32[]{:S(2)}, u32[]{:S(2)}) collective-permute-start(bf16[16,2048]{1,0:T(8,128)(2,1)S(1)} %get-tuple-element.36.refs_1_), channel_id=1, source_target_pairs={{12,0},{8,4},{4,8},{0,12},{28,16},{24,20},{20,24},{16,28},{13,1},{... | collective-permute-start | bytes 196616 | tf_op jit(solution)/shard_map/ppermute | solution.py:599
  10.8 0.4 %collective-permute-start.2 = (bf16[16,2048]{1,0:T(8,128)(2,1)S(1)}, bf16[16,2048]{1,0:T(8,128)(2,1)S(1)}, u32[]{:S(2)}, u32[]{:S(2)}) collective-permute-start(bf16[16,2048]{1,0:T(8,128)(2,1)S(1)} %get-tuple-element.36.refs_1_), channel_id=1, source_target_pairs={{8,0},{12,4},{0,8},{4,12},{24,16},{28,20},{16,24},{20,28},{9,1},{1... | collective-permute-start | bytes 196616 | tf_op jit(solution)/shard_map/ppermute | solution.py:599
  11.2 1.8 %collective-permute-start.3 = (bf16[16,2048]{1,0:T(8,128)(2,1)S(1)}, bf16[16,2048]{1,0:T(8,128)(2,1)S(1)}, u32[]{:S(2)}, u32[]{:S(2)}) collective-permute-start(bf16[16,2048]{1,0:T(8,128)(2,1)S(1)} %get-tuple-element.36.refs_1_), channel_id=1, source_target_pairs={{4,0},{0,4},{12,8},{8,12},{20,16},{16,20},{28,24},{24,28},{5,1},{1... | collective-permute-start | bytes 196616 | tf_op jit(solution)/shard_map/ppermute | solution.py:599
  13.1 2.3 %prepare.1 = (bf16[16,48,256]{2,1,0:T(8,128)(2,1)S(1)}, bf16[16,32,128]{2,1,0:T(8,128)(2,1)S(1)}, bf16[8,256,256]{2,1,0:T(8,128)(2,1)S(1)}, f32[256,2048]{1,0:T(8,128)S(1)}, bf16[256,2048]{1,0:T(8,128)(2,1)S(1)}) custom-call(s32[1]{0:T(128)} %bitcast.place_ref.refs_0_, bf16[256,2048]{1,0:T(8,128)(2,1)} %residual_hbm.1, ...), custom_call_target="tpu_custom_call" | custom-call | bytes 6000000 | tf_op jit(solution)/shard_map/prepare/pallas_call | solution.py:577
  15.4 0.0 collective-permute-done.1.refs_4_
  15.4 0.0 collective-permute-done.2.refs_5_
  15.4 0.1 collective-permute-done.3.refs_6_
  15.5 0.2 join.1
  15.7 2.7 %collective-permute-start.4 = (bf16[16,2048]{1,0:T(8,128)(2,1)S(1)}, bf16[16,2048]{1,0:T(8,128)(2,1)S(1)}, u32[]{:S(2)}, u32[]{:S(2)}) collective-permute-start(bf16[16,2048]{1,0:T(8,128)(2,1)S(1)} %get-tuple-element.43), channel_id=1, source_target_pairs={{16,0},{20,4},{24,8},{28,12},{0,16},{4,20},{8,24},{12,28},{17,1},{... | collective-permute-start | bytes 196616 | tf_op jit(solution)/shard_map/ppermute | solution.py:611
  18.3 0.0 copy-done
  18.3 2.4 %local_conv.1.refs_1_ = f32[256,2048]{1,0:T(8,128)S(1)} custom-call(f32[256,2048]{1,0:T(8,128)S(1)} %get-tuple-element.30.gate_ref.refs_2_, bf16[256,2048]{1,0:T(8,128)(2,1)S(1)} %get-tuple-element.31.residual_ref, bf16[256,2048]{1,0:T(8,128)(2,1)S(1)} %get-tuple-element.32.product_ref, f32[8,2048]{1,0:T(8,128)S(1)} %get-tuple-element.35.first_ref, ...), custom_call_target="tpu_custom_call" | custom-call | bytes 15000000 | tf_op jit(solution)/shard_map/local_conv/pallas_call | solution.py:613
  20.8 0.1 collective-permute-done.4.refs_6_
  20.9 0.0 copy-start.1
  20.9 0.7 %add_carry.1 = (f32[256,2048]{1,0:T(8,128)S(1)}, f32[1,256]{1,0:T(1,128)S(1)}) custom-call(s32[1]{0:T(128)} %bitcast.place_ref.refs_0_, f32[256,2048]{1,0:T(8,128)S(1)} %local_conv.1.refs_1_, f32[256,2048]{1,0:T(8,128)S(1)} %get-tuple-element.30.gate_ref.refs_2_, bf16[8,256,256]{2,1,0:T(8,128)(2,1)S(1)} %get-tuple-element.40.refs_3_, ...), custom_call_target="tpu_custom_call" | custom-call | bytes 3000000 | tf_op jit(solution)/shard_map/add_carry/pallas_call | solution.py:622
  21.6 0.0 collective-permute-start.5
  21.6 1.7 %collective-permute-start.6 = (f32[1,256]{1,0:T(1,128)S(1)}, f32[1,256]{1,0:T(1,128)S(1)}, u32[]{:S(2)}, u32[]{:S(2)}) collective-permute-start(f32[1,256]{1,0:T(1,128)S(1)} %get-tuple-element.47.refs_1_), channel_id=1, source_target_pairs={{2,0},{3,1},{0,2},{1,3},{6,4},{7,5},{4,6},{5,7},{10,8},{11,9},{8,1... | collective-permute-start | bytes 3080 | tf_op jit(solution)/shard_map/ppermute | solution.py:631
  23.3 0.2 collective-permute-start.7
  23.5 0.0 copy-done.1
  23.5 1.0 %new_residual.1 = (bf16[256,2048]{1,0:T(8,128)(2,1)}, f32[256,2048]{1,0:T(8,128)S(1)}) custom-call(f32[256,2048]{1,0:T(8,128)S(1)} %get-tuple-element.44.summed_ref, f32[1,2048]{1,0:T(1,128)S(1)} %bitcast.6), custom_call_target="tpu_custom_call" | custom-call | bytes 3000000 | tf_op jit(solution)/shard_map/new_residual/pallas_call | solution.py:634
  24.6 0.1 collective-permute-done.5.refs_2_
  24.7 0.6 %collective-permute-done.6.refs_3_ = f32[1,256]{1,0:T(1,128)S(1)} collective-permute-done((f32[1,256]{1,0:T(1,128)S(1)}, f32[1,256]{1,0:T(1,128)S(1)}, u32[]{:S(2)}, u32[]{:S(2)}) %collective-permute-start.6) | collective-permute-done | bytes 1056 | tf_op jit(solution)/shard_map/ppermute | solution.py:631
  25.3 0.0 collective-permute-done.7.refs_4_
  25.3 1.2 %normed.1 = bf16[256,2048]{1,0:T(8,128)(2,1)} custom-call(f32[256,2048]{1,0:T(8,128)S(1)} %get-tuple-element.46.refs_0_, f32[1,256]{1,0:T(1,128)S(1)} %get-tuple-element.47.refs_1_, f32[1,256]{1,0:T(1,128)S(1)} %collective-permute-done.5.refs_2_, f32[1,256]{1,0:T(1,128)S(1)} %collective-permute-done.6.refs_3_, f32[1,256]{1,0:T(1,128)S(1)} %collective-permute-done.7.refs_4_), custom_call_target="tpu_custom_call" | custom-call | bytes 3000000 | tf_op jit(solution)/shard_map/normed/pallas_call | solution.py:634
  (1 shorter events, 0.0 us)
Async XLA Ops:
  1.6 7.8 %collective-permute-start = (bf16[3,2,2048]{2,1,0:T(2,128)(2,1)S(1)}, bf16[3,2,2048]{2,1,0:T(2,128)(2,1)S(1)}, u32[]{:S(2)}, u32[]{:S(2)}) collective-permute-start(bf16[3,2,2048]{2,1,0:T(2,128)(2,1)S(1)} %slice.3), channel_id=1, source_target_pairs={{0,4},{4,8},{8,12},{12,16},{16,20},{20,24},{24,28},{28,0},{1,5},{5... | collective-permute-start | bytes 73736 | tf_op jit(solution)/shard_map/ppermute | solution.py:540
  8.0 10.3 %copy-start = (f32[2048]{0:T(1024)S(1)}, f32[2048]{0:T(1024)}, u32[]{:S(2)}) copy-start(f32[2048]{0:T(1024)} %param.11) | copy-start | bytes 24580
  9.5 5.9 %collective-permute-start.1 = (bf16[16,2048]{1,0:T(8,128)(2,1)S(1)}, bf16[16,2048]{1,0:T(8,128)(2,1)S(1)}, u32[]{:S(2)}, u32[]{:S(2)}) collective-permute-start(bf16[16,2048]{1,0:T(8,128)(2,1)S(1)} %get-tuple-element.36.refs_1_), channel_id=1, source_target_pairs={{12,0},{8,4},{4,8},{0,12},{28,16},{24,20},{20,24},{16,28},{13,1},{... | collective-permute-start | bytes 196616 | tf_op jit(solution)/shard_map/ppermute | solution.py:599
  10.8 4.6 %collective-permute-start.2 = (bf16[16,2048]{1,0:T(8,128)(2,1)S(1)}, bf16[16,2048]{1,0:T(8,128)(2,1)S(1)}, u32[]{:S(2)}, u32[]{:S(2)}) collective-permute-start(bf16[16,2048]{1,0:T(8,128)(2,1)S(1)} %get-tuple-element.36.refs_1_), channel_id=1, source_target_pairs={{8,0},{12,4},{0,8},{4,12},{24,16},{28,20},{16,24},{20,28},{9,1},{1... | collective-permute-start | bytes 196616 | tf_op jit(solution)/shard_map/ppermute | solution.py:599
  11.2 4.3 %collective-permute-start.3 = (bf16[16,2048]{1,0:T(8,128)(2,1)S(1)}, bf16[16,2048]{1,0:T(8,128)(2,1)S(1)}, u32[]{:S(2)}, u32[]{:S(2)}) collective-permute-start(bf16[16,2048]{1,0:T(8,128)(2,1)S(1)} %get-tuple-element.36.refs_1_), channel_id=1, source_target_pairs={{4,0},{0,4},{12,8},{8,12},{20,16},{16,20},{28,24},{24,28},{5,1},{1... | collective-permute-start | bytes 196616 | tf_op jit(solution)/shard_map/ppermute | solution.py:599
  15.7 5.2 %collective-permute-start.4 = (bf16[16,2048]{1,0:T(8,128)(2,1)S(1)}, bf16[16,2048]{1,0:T(8,128)(2,1)S(1)}, u32[]{:S(2)}, u32[]{:S(2)}) collective-permute-start(bf16[16,2048]{1,0:T(8,128)(2,1)S(1)} %get-tuple-element.43), channel_id=1, source_target_pairs={{16,0},{20,4},{24,8},{28,12},{0,16},{4,20},{8,24},{12,28},{17,1},{... | collective-permute-start | bytes 196616 | tf_op jit(solution)/shard_map/ppermute | solution.py:611
  20.9 2.6 %copy-start.1 = (f32[2048]{0:T(1024)S(1)}, f32[2048]{0:T(1024)}, u32[]{:S(2)}) copy-start(f32[2048]{0:T(1024)} %param.13) | copy-start | bytes 24580
  21.6 3.0 %collective-permute-start.5 = (f32[1,256]{1,0:T(1,128)S(1)}, f32[1,256]{1,0:T(1,128)S(1)}, u32[]{:S(2)}, u32[]{:S(2)}) collective-permute-start(f32[1,256]{1,0:T(1,128)S(1)} %get-tuple-element.47.refs_1_), channel_id=1, source_target_pairs={{3,0},{2,1},{1,2},{0,3},{7,4},{6,5},{5,6},{4,7},{11,8},{10,9},{9,1... | collective-permute-start | bytes 3080 | tf_op jit(solution)/shard_map/ppermute | solution.py:631
  21.6 3.6 %collective-permute-start.6 = (f32[1,256]{1,0:T(1,128)S(1)}, f32[1,256]{1,0:T(1,128)S(1)}, u32[]{:S(2)}, u32[]{:S(2)}) collective-permute-start(f32[1,256]{1,0:T(1,128)S(1)} %get-tuple-element.47.refs_1_), channel_id=1, source_target_pairs={{2,0},{3,1},{0,2},{1,3},{6,4},{7,5},{4,6},{5,7},{10,8},{11,9},{8,1... | collective-permute-start | bytes 3080 | tf_op jit(solution)/shard_map/ppermute | solution.py:631
  23.3 1.9 %collective-permute-start.7 = (f32[1,256]{1,0:T(1,128)S(1)}, f32[1,256]{1,0:T(1,128)S(1)}, u32[]{:S(2)}, u32[]{:S(2)}) collective-permute-start(f32[1,256]{1,0:T(1,128)S(1)} %get-tuple-element.47.refs_1_), channel_id=1, source_target_pairs={{1,0},{0,1},{3,2},{2,3},{5,4},{4,5},{7,6},{6,7},{9,8},{8,9},{11,10... | collective-permute-start | bytes 3080 | tf_op jit(solution)/shard_map/ppermute | solution.py:631
